TPU v7x, 32 devices: a whole 2x2x4 slice. The times are simulated.
32 devices in a mesh: dp: 8 (over z, y), seq: 4 (over x, core).
Axes of the slice: x: 2, y: 2, z: 4, core: 2. Of those that a mesh axis runs over, the one named last changes fastest.
Arguments:
- tokens: bfloat16 [8, 2048, 768], P('dp', 'seq'), may hold values from -6 to 6
- cotangent: bfloat16 [8, 2048, 768], P('dp', 'seq'), may hold values from -6 to 6
- segments: int32 [8, 2048], P('dp', 'seq'), may hold values from 0 to 3, as said below
- w_query: bfloat16 [768, 768], P(('dp', 'seq')), may hold values from -0.3125 to 0.3125
- w_key: bfloat16 [768, 768], P(('dp', 'seq')), may hold values from -0.3125 to 0.3125
- w_value: bfloat16 [768, 768], P(('dp', 'seq')), may hold values from -0.21875 to 0.21875
- w_out: bfloat16 [768, 768], P(('dp', 'seq')), may hold values from -1.25 to 1.25
- w_up: bfloat16 [768, 3072], P(('dp', 'seq')), may hold values from -0.21875 to 0.21875
- w_down: bfloat16 [3072, 768], P(('dp', 'seq')), may hold values from -0.109375 to 0.109375
- ln1_gain: bfloat16 [768], P(('dp', 'seq')), may hold values from 0.25 to 1.75
- ln1_shift: bfloat16 [768], P(('dp', 'seq')), may hold values from -4 to 4
- query_bias: bfloat16 [768], P(('dp', 'seq')), may hold values from -4 to 4
- value_bias: bfloat16 [768], P(('dp', 'seq')), may hold values from -4 to 4
- out_bias: bfloat16 [768], P(('dp', 'seq')), may hold values from -4 to 4
- ln2_gain: bfloat16 [768], P(('dp', 'seq')), may hold values from 0.25 to 1.75
- ln2_shift: bfloat16 [768], P(('dp', 'seq')), may hold values from -4 to 4
- up_bias: bfloat16 [3072], P(('dp', 'seq')), may hold values from -4 to 4
- down_bias: bfloat16 [768], P(('dp', 'seq')), may hold values from -4 to 4
Outputs:
- output: float32 [8, 2048, 768], P('dp', 'seq')
- grad_tokens: float32 [8, 2048, 768], P('dp', 'seq')
- grad_w_query: float32 [768, 768], P(('dp', 'seq'))
- grad_w_key: float32 [768, 768], P(('dp', 'seq'))
- grad_w_value: float32 [768, 768], P(('dp', 'seq'))
- grad_w_out: float32 [768, 768], P(('dp', 'seq'))
- grad_w_up: float32 [768, 3072], P(('dp', 'seq'))
- grad_w_down: float32 [3072, 768], P(('dp', 'seq'))
- grad_ln1_gain: float32 [768], P(('dp', 'seq'))
- grad_ln1_shift: float32 [768], P(('dp', 'seq'))
- grad_query_bias: float32 [768], P(('dp', 'seq'))
- grad_value_bias: float32 [768], P(('dp', 'seq'))
- grad_out_bias: float32 [768], P(('dp', 'seq'))
- grad_ln2_gain: float32 [768], P(('dp', 'seq'))
- grad_ln2_shift: float32 [768], P(('dp', 'seq'))
- grad_up_bias: float32 [3072], P(('dp', 'seq'))
- grad_down_bias: float32 [768], P(('dp', 'seq'))
Inputs may be any that keep to these rules, and one draw needn't show every extreme that they name: `segments`: along each sequence the numbers start at 0 and rise by one at each document boundary; each document has 200 to 2048 tokens; in every sequence document 0 ends within the first 2048 // 4 positions and document 1 reaches into the last 2048 // 4 positions.
All inputs are finite; a program needn't handle non-finite values.
Results may differ from a plain program's by a relative error of at most 0.015.
Values may be sent and summed in bfloat16 or wider, within the bound.
No kernel may reach another device: no remote copies, remote signals or barrier semaphores. Data moves between devices by JAX's collectives and lax.ppermute only.
A program may use at most 256 MiB of HBM per device.

v0:
```python
import math

import jax
import jax.numpy as jnp
from jax import lax
from jax.sharding import PartitionSpec as P

H = 12


EPSILON = 1e-05
MASKED = -1e30


def normalize(value, gain, shift):
    mean = jnp.mean(value, -1, keepdims=True)
    centred = value - mean
    inv_std = lax.rsqrt(jnp.mean(centred * centred, -1, keepdims=True) + EPSILON)
    normed = centred * inv_std
    return (normed * gain + shift, normed, inv_std)


def normalize_back(grad_in, normed, inv_std, gain):
    scaled = grad_in * gain
    return inv_std * (
        scaled
        - jnp.mean(scaled, -1, keepdims=True)
        - normed * jnp.mean(scaled * normed, -1, keepdims=True)
    )


def gelu_slope(value):
    cumul = 0.5 * (1.0 + lax.erf(value * (1.0 / math.sqrt(2.0))))
    return cumul + value * jnp.exp(-0.5 * value * value) * (1.0 / math.sqrt(2.0 * math.pi))


def pair_mask(q_seg, q_pos, k_seg, k_pos):
    same_doc = q_seg[:, :, None] == k_seg[:, None, :]
    causal = k_pos[None, :] <= q_pos[:, None]
    return same_doc & causal[None]


def back_terms(query4, grad_att4, log_total, row_dot, k4, v4, allowed, score_scale):
    scores = (
        jnp.einsum("sqhd,skhd->shqk", query4, k4, preferred_element_type=jnp.float32) * score_scale
    )
    scores = jnp.where(allowed[:, None], scores, MASKED)
    attn_weights = jnp.exp(scores - log_total[..., None])
    weights_low = attn_weights.astype(jnp.bfloat16)
    grad_weights = jnp.einsum("sqhd,skhd->shqk", grad_att4, v4, preferred_element_type=jnp.float32)
    grad_scores = (attn_weights * (grad_weights - row_dot[..., None])).astype(jnp.bfloat16)
    return (weights_low, grad_scores)


def body(
    tokens,
    cotangent,
    segments,
    w_query,
    w_key,
    w_value,
    w_out,
    w_up,
    w_down,
    ln1_gain,
    ln1_shift,
    query_bias,
    value_bias,
    out_bias,
    ln2_gain,
    ln2_shift,
    up_bias,
    down_bias,
):
    f32 = jnp.float32
    bf16 = jnp.bfloat16
    seq_count, block_len, model_width = tokens.shape
    head_count = H
    head_dim = model_width // head_count
    score_scale = 1.0 / math.sqrt(head_dim)
    row_count = seq_count * block_len
    (
        query_full,
        key_full,
        value_full,
        out_full,
        up_full,
        down_full,
        gain_one,
        shift_one,
        query_add,
        value_add,
        out_add,
        gain_two,
        shift_two,
        up_add,
        down_add,
    ) = (
        lax.all_gather(w_query, ("dp", "seq"), axis=0, tiled=True),
        lax.all_gather(w_key, ("dp", "seq"), axis=0, tiled=True),
        lax.all_gather(w_value, ("dp", "seq"), axis=0, tiled=True),
        lax.all_gather(w_out, ("dp", "seq"), axis=0, tiled=True),
        lax.all_gather(w_up, ("dp", "seq"), axis=0, tiled=True),
        lax.all_gather(w_down, ("dp", "seq"), axis=0, tiled=True),
        lax.all_gather(ln1_gain, ("dp", "seq"), axis=0, tiled=True),
        lax.all_gather(ln1_shift, ("dp", "seq"), axis=0, tiled=True),
        lax.all_gather(query_bias, ("dp", "seq"), axis=0, tiled=True),
        lax.all_gather(value_bias, ("dp", "seq"), axis=0, tiled=True),
        lax.all_gather(out_bias, ("dp", "seq"), axis=0, tiled=True),
        lax.all_gather(ln2_gain, ("dp", "seq"), axis=0, tiled=True),
        lax.all_gather(ln2_shift, ("dp", "seq"), axis=0, tiled=True),
        lax.all_gather(up_bias, ("dp", "seq"), axis=0, tiled=True),
        lax.all_gather(down_bias, ("dp", "seq"), axis=0, tiled=True),
    )
    gain_one_f = gain_one.astype(f32)
    gain_two_f = gain_two.astype(f32)
    inputs = tokens.astype(f32).reshape(row_count, model_width)
    first, normed_one, inv_one = normalize(inputs, gain_one_f, shift_one.astype(f32))
    first_low = first.astype(bf16)
    query = (
        jnp.dot(first_low, query_full, preferred_element_type=f32) + query_add.astype(f32)
    ).astype(bf16)
    key_rows = jnp.dot(first_low, key_full, preferred_element_type=f32).astype(bf16)
    value_rows = (
        jnp.dot(first_low, value_full, preferred_element_type=f32) + value_add.astype(f32)
    ).astype(bf16)
    query4 = query.reshape(seq_count, block_len, head_count, head_dim)
    key_send = key_rows.reshape(seq_count, block_len, model_width)
    value_send = value_rows.reshape(seq_count, block_len, model_width)
    seg_send = segments.astype(bf16)
    q_seg = segments.astype(f32)
    own_start = lax.axis_index("seq") * block_len
    q_pos = own_start + jnp.arange(block_len)
    start_state = (
        jnp.full((seq_count, head_count, block_len), MASKED, f32),
        jnp.zeros((seq_count, head_count, block_len), f32),
        jnp.zeros((seq_count, head_count, block_len, head_dim), f32),
    )
    k_piece = lax.all_gather(key_send, "seq", axis=1, tiled=True)
    v_piece = lax.all_gather(value_send, "seq", axis=1, tiled=True)
    s_piece = lax.all_gather(seg_send, "seq", axis=1, tiled=True)
    key_count = k_piece.shape[1]
    allowed = pair_mask(q_seg, q_pos, s_piece.astype(f32), jnp.arange(key_count))

    def block_work(running):
        row_max, row_sum, weighted = running
        k4 = k_piece.reshape(seq_count, -1, head_count, head_dim)
        v4 = v_piece.reshape(seq_count, -1, head_count, head_dim)
        scores = jnp.einsum("sqhd,skhd->shqk", query4, k4, preferred_element_type=f32) * score_scale
        scores = jnp.where(allowed[:, None], scores, MASKED)
        new_max = jnp.maximum(row_max, jnp.max(scores, -1))
        attn_weights = jnp.exp(scores - new_max[..., None])
        row_sum = jnp.sum(attn_weights, -1)
        weighted = jnp.einsum(
            "shqk,skhd->shqd", attn_weights.astype(bf16), v4, preferred_element_type=f32
        )
        return (new_max, row_sum, weighted)

    row_max, row_sum, weighted = block_work(start_state)
    log_total = row_max + jnp.log(row_sum)
    attended4 = jnp.transpose(weighted / row_sum[..., None], (0, 2, 1, 3))
    attended = attended4.reshape(row_count, model_width)
    attended_low = attended.astype(bf16)
    resid = (
        inputs + jnp.dot(attended_low, out_full, preferred_element_type=f32) + out_add.astype(f32)
    )
    second, normed_two, inv_two = normalize(resid, gain_two_f, shift_two.astype(f32))
    second_low = second.astype(bf16)
    hidden_pre = jnp.dot(second_low, up_full, preferred_element_type=f32) + up_add.astype(f32)
    hidden_low = jax.nn.gelu(hidden_pre, approximate=False).astype(bf16)
    final = (
        resid + jnp.dot(hidden_low, down_full, preferred_element_type=f32) + down_add.astype(f32)
    )
    output = final.reshape(seq_count, block_len, model_width)
    query_full, key_full, value_full, out_full, up_full, down_full, gain_one, gain_two = (
        lax.all_gather(w_query, ("dp", "seq"), axis=0, tiled=True),
        lax.all_gather(w_key, ("dp", "seq"), axis=0, tiled=True),
        lax.all_gather(w_value, ("dp", "seq"), axis=0, tiled=True),
        lax.all_gather(w_out, ("dp", "seq"), axis=0, tiled=True),
        lax.all_gather(w_up, ("dp", "seq"), axis=0, tiled=True),
        lax.all_gather(w_down, ("dp", "seq"), axis=0, tiled=True),
        lax.all_gather(ln1_gain, ("dp", "seq"), axis=0, tiled=True),
        lax.all_gather(ln2_gain, ("dp", "seq"), axis=0, tiled=True),
    )
    gain_one_f = gain_one.astype(f32)
    gain_two_f = gain_two.astype(f32)
    grad_final = cotangent.reshape(row_count, model_width)
    grad_final_f = grad_final.astype(f32)
    grad_down = jnp.dot(hidden_low.T, grad_final, preferred_element_type=f32)
    grad_down_bias = jnp.sum(grad_final_f, 0)
    grad_hidden = jnp.dot(grad_final, down_full.T, preferred_element_type=f32)
    grad_pre = (grad_hidden * gelu_slope(hidden_pre)).astype(bf16)
    grad_up = jnp.dot(second_low.T, grad_pre, preferred_element_type=f32)
    grad_up_bias = jnp.sum(grad_pre.astype(f32), 0)
    grad_second = jnp.dot(grad_pre, up_full.T, preferred_element_type=f32)
    grad_gain_two = jnp.sum(grad_second * normed_two, 0)
    grad_shift_two = jnp.sum(grad_second, 0)
    grad_resid = grad_final_f + normalize_back(grad_second, normed_two, inv_two, gain_two_f)
    grad_branch = grad_resid.astype(bf16)
    grad_out = jnp.dot(attended_low.T, grad_branch, preferred_element_type=f32)
    grad_out_bias = jnp.sum(grad_branch.astype(f32), 0)
    grad_attended = jnp.dot(grad_branch, out_full.T, preferred_element_type=f32).astype(bf16)
    grad_att4 = grad_attended.reshape(seq_count, block_len, head_count, head_dim)
    row_dot = jnp.transpose(jnp.sum(grad_att4.astype(f32) * attended4, -1), (0, 2, 1))
    q_zero = jnp.zeros((seq_count, block_len, head_count, head_dim), f32)
    attend_k_piece = lax.all_gather(key_send, "seq", axis=1, tiled=True)
    attend_v_piece = lax.all_gather(value_send, "seq", axis=1, tiled=True)
    s_piece = lax.all_gather(seg_send, "seq", axis=1, tiled=True)
    key_count = attend_k_piece.shape[1]
    attend_allowed = pair_mask(q_seg, q_pos, s_piece.astype(f32), jnp.arange(key_count))

    def block_work(running):
        k4 = attend_k_piece.reshape(seq_count, -1, head_count, head_dim)
        v4 = attend_v_piece.reshape(seq_count, -1, head_count, head_dim)
        weights_low, grad_scores = back_terms(
            query4, grad_att4, log_total, row_dot, k4, v4, attend_allowed, score_scale
        )
        part_q = score_scale * jnp.einsum(
            "shqk,skhd->sqhd", grad_scores, k4, preferred_element_type=f32
        )
        return part_q

    back_result = block_work(q_zero)
    lse_all, dot_all = (
        lax.all_gather(jnp.transpose(log_total, (0, 2, 1)), "seq", axis=1, tiled=True),
        lax.all_gather(jnp.transpose(row_dot, (0, 2, 1)), "seq", axis=1, tiled=True),
    )
    key4 = key_rows.reshape(seq_count, block_len, head_count, head_dim)
    value4 = value_rows.reshape(seq_count, block_len, head_count, head_dim)
    k_pos = own_start + jnp.arange(block_len)
    query_piece = lax.all_gather(
        query.reshape(seq_count, block_len, model_width), "seq", axis=1, tiled=True
    )
    grad_piece = lax.all_gather(
        grad_attended.reshape(seq_count, block_len, model_width), "seq", axis=1, tiled=True
    )
    seg_piece = lax.all_gather(seg_send, "seq", axis=1, tiled=True)
    count = query_piece.shape[1]
    keys_allowed = pair_mask(seg_piece.astype(f32), jnp.arange(count), q_seg, k_pos)

    def block_work(running):
        q4 = query_piece.reshape(seq_count, -1, head_count, head_dim)
        g4 = grad_piece.reshape(seq_count, -1, head_count, head_dim)
        lse_piece = jnp.transpose(lse_all, (0, 2, 1))
        dot_piece = jnp.transpose(dot_all, (0, 2, 1))
        weights_low, grad_scores = back_terms(
            q4, g4, lse_piece, dot_piece, key4, value4, keys_allowed, score_scale
        )
        grad_k = score_scale * jnp.einsum(
            "shqk,sqhd->skhd", grad_scores, q4, preferred_element_type=f32
        )
        grad_v = jnp.einsum("shqk,sqhd->skhd", weights_low, g4, preferred_element_type=f32)
        return (grad_k, grad_v)

    grad_k_mine, grad_v_mine = block_work((q_zero, q_zero))
    grad_q_low = back_result.reshape(row_count, model_width).astype(bf16)
    grad_k_low = grad_k_mine.reshape(row_count, model_width).astype(bf16)
    grad_v_low = grad_v_mine.reshape(row_count, model_width).astype(bf16)
    grad_query = jnp.dot(first_low.T, grad_q_low, preferred_element_type=f32)
    grad_key = jnp.dot(first_low.T, grad_k_low, preferred_element_type=f32)
    grad_value = jnp.dot(first_low.T, grad_v_low, preferred_element_type=f32)
    grad_q_bias = jnp.sum(grad_q_low.astype(f32), 0)
    grad_v_bias = jnp.sum(grad_v_low.astype(f32), 0)
    grad_first = (
        jnp.dot(grad_q_low, query_full.T, preferred_element_type=f32)
        + jnp.dot(grad_k_low, key_full.T, preferred_element_type=f32)
        + jnp.dot(grad_v_low, value_full.T, preferred_element_type=f32)
    )
    grad_gain_one = jnp.sum(grad_first * normed_one, 0)
    grad_shift_one = jnp.sum(grad_first, 0)
    grad_inputs = grad_resid + normalize_back(grad_first, normed_one, inv_one, gain_one_f)
    (
        sh_query,
        sh_key,
        sh_value,
        sh_out,
        sh_up,
        sh_down,
        sh_gain1,
        sh_shift1,
        sh_qbias,
        sh_vbias,
        sh_obias,
        sh_gain2,
        sh_shift2,
        sh_upbias,
        sh_downbias,
    ) = (
        lax.psum_scatter(grad_query, ("dp", "seq"), scatter_dimension=0, tiled=True),
        lax.psum_scatter(grad_key, ("dp", "seq"), scatter_dimension=0, tiled=True),
        lax.psum_scatter(grad_value, ("dp", "seq"), scatter_dimension=0, tiled=True),
        lax.psum_scatter(grad_out, ("dp", "seq"), scatter_dimension=0, tiled=True),
        lax.psum_scatter(grad_up, ("dp", "seq"), scatter_dimension=0, tiled=True),
        lax.psum_scatter(grad_down, ("dp", "seq"), scatter_dimension=0, tiled=True),
        lax.psum_scatter(grad_gain_one, ("dp", "seq"), scatter_dimension=0, tiled=True),
        lax.psum_scatter(grad_shift_one, ("dp", "seq"), scatter_dimension=0, tiled=True),
        lax.psum_scatter(grad_q_bias, ("dp", "seq"), scatter_dimension=0, tiled=True),
        lax.psum_scatter(grad_v_bias, ("dp", "seq"), scatter_dimension=0, tiled=True),
        lax.psum_scatter(grad_out_bias, ("dp", "seq"), scatter_dimension=0, tiled=True),
        lax.psum_scatter(grad_gain_two, ("dp", "seq"), scatter_dimension=0, tiled=True),
        lax.psum_scatter(grad_shift_two, ("dp", "seq"), scatter_dimension=0, tiled=True),
        lax.psum_scatter(grad_up_bias, ("dp", "seq"), scatter_dimension=0, tiled=True),
        lax.psum_scatter(grad_down_bias, ("dp", "seq"), scatter_dimension=0, tiled=True),
    )
    return (
        output,
        grad_inputs.reshape(seq_count, block_len, model_width),
        sh_query,
        sh_key,
        sh_value,
        sh_out,
        sh_up,
        sh_down,
        sh_gain1,
        sh_shift1,
        sh_qbias,
        sh_vbias,
        sh_obias,
        sh_gain2,
        sh_shift2,
        sh_upbias,
        sh_downbias,
    )


def solution(mesh):
    placed = (
        P("dp", "seq", None),
        P("dp", "seq", None),
        P("dp", "seq"),
        P(("dp", "seq"), None),
        P(("dp", "seq"), None),
        P(("dp", "seq"), None),
        P(("dp", "seq"), None),
        P(("dp", "seq"), None),
        P(("dp", "seq"), None),
        P(("dp", "seq")),
        P(("dp", "seq")),
        P(("dp", "seq")),
        P(("dp", "seq")),
        P(("dp", "seq")),
        P(("dp", "seq")),
        P(("dp", "seq")),
        P(("dp", "seq")),
        P(("dp", "seq")),
    )
    return jax.shard_map(
        body,
        mesh=mesh,
        in_specs=placed,
        out_specs=(
            P("dp", "seq", None),
            P("dp", "seq", None),
            P(("dp", "seq"), None),
            P(("dp", "seq"), None),
            P(("dp", "seq"), None),
            P(("dp", "seq"), None),
            P(("dp", "seq"), None),
            P(("dp", "seq"), None),
            P(("dp", "seq")),
            P(("dp", "seq")),
            P(("dp", "seq")),
            P(("dp", "seq")),
            P(("dp", "seq")),
            P(("dp", "seq")),
            P(("dp", "seq")),
            P(("dp", "seq")),
            P(("dp", "seq")),
        ),
        check_vma=False,
    )
```

profile of v0, /device:TPU:0, one launch (start us, length us, event | category | flops | bytes accessed | tf_op | source)
XLA Modules:
  0.0 1192.8 jit_solution(10302343069604853596)
XLA Ops:
  17.0 42.6 %all-reduce.19 = (bf16[768]{0:T(1024)(128)(2,1)S(1)}, bf16[768]{0:T(1024)(128)(2,1)S(1)}, bf16[768]{0:T(1024)(128)(2,1)S(1)}, bf16[768]{0:T(1024)(128)(2,1)S(1)}...) all-reduce(bf16[768]{0:T(1024)(128)(2,1)S(1)} %dynamic-update-slice, ...), channel_id=1, replica_groups=mesh['dp'=8,'seq'=4] {'dp','seq'}, use_global_device_ids=true, to_apply=%add.2 | all-reduce | flops 9216 | bytes 36864
  62.5 5.5 all-gather.18.cloned.1.call-done
  68.1 3.3 convolution_convert_fusion.1
  71.5 52.3 %all-gather.20.cloned.1.call-done = bf16[768,768]{1,0:T(8,128)(2,1)} async-done(((bf16[24,768]{1,0:T(8,128)(2,1)}), bf16[768,768]{1,0:T(8,128)(2,1)}) %all-gather.20.cloned.1.call-update) | async-done | bytes 1179664 | tf_op jit(solution)/shard_map/all_gather | solution.py:101
  123.8 3.1 add_convert_fusion.1
  129.1 5.2 all_gather.78
  136.5 43.2 %all-gather.16.cloned.1.call-done = bf16[768,768]{1,0:T(8,128)(2,1)} async-done(((bf16[24,768]{1,0:T(8,128)(2,1)}), bf16[768,768]{1,0:T(8,128)(2,1)}) %all-gather.16.cloned.1.call-update) | async-done | bytes 1179664 | tf_op jit(solution)/shard_map/all_gather | solution.py:99
  183.3 25.2 %all-gather.28.cloned.1.call-done = bf16[2048,768]{1,0:T(8,128)(2,1)} async-done(((bf16[512,768]{1,0:T(8,128)(2,1)}), bf16[2048,768]{1,0:T(8,128)(2,1)}) %all-gather.28.cloned.1.call-update) | async-done | bytes 3145744 | tf_op jit(solution)/shard_map/all_gather | solution.py:139
  208.6 3.2 copy.54
  211.8 22.2 %fusion.3 = (f32[12,512]{1,0:T(8,128)S(1)}, f32[12,512,2048]{2,1,0:T(8,128)}) fusion(pred[512,2048]{1,0:T(8,128)(4,1)} %fusion.34, bf16[512,12,64]{0,2,1:T(8,128)(2,1)} %bitcast.158, bf16[2048,12,64]{0,2,1:T(8,128)(2,1)S(1)} %bitcast.153), kind=kOutput, calls=%fused_computation.8 | convolution fusion | flops 1648355328 | bytes 55336960 | tf_op jit(solution)/shard_map/sqhd,skhd->shqk/dot_general | solution.py:149
  234.0 22.1 %fusion = f32[12,512]{1,0:T(8,128)S(1)} fusion(f32[12,512,2048]{2,1,0:T(8,128)} %get-tuple-element.49, f32[12,512]{1,0:T(8,128)S(1)} %broadcast_maximum_fusion, pred[512,2048]{1,0:T(8,128)(4,1)} %fusion.34), kind=kLoop, calls=%fused_computation.5 | loop fusion | flops 50325504 | bytes 51429376 | tf_op jit(solution)/shard_map/reduce_sum | solution.py:153
  256.1 4.7 copy.55
  260.8 21.6 %bitcast_convert_fusion = (bf16[1,512,12,64]{1,3,2,0:T(8,128)(2,1)}, f32[12,512,64]{1,2,0:T(8,128)}) fusion(f32[12,512]{1,0:T(8,128)S(1)} %fusion, bf16[2048,12,64]{0,2,1:T(8,128)(2,1)} %bitcast.160, f32[12,512,2048]{2,1,0:T(8,128)} %get-tuple-element.49, f32[12,512]{1,0:T(8,128)S(1)} %broadcast_maximum_fusion, pred[512,2048]{1,0:T(8,128)(4,1)} %fusion.34), kind=kOutput, calls=%fused_computation.78 | convolution fusion | flops 1661730816 | bytes 56934400 | tf_op jit(solution)/shard_map/shqk,skhd->shqd/dot_general | solution.py:154
  282.4 13.0 %all-gather.22.cloned.1.call-done = bf16[768,768]{1,0:T(8,128)(2,1)} async-done(((bf16[24,768]{1,0:T(8,128)(2,1)}), bf16[768,768]{1,0:T(8,128)(2,1)}) %all-gather.22.cloned.1.call-update) | async-done | bytes 1179664 | tf_op jit(solution)/shard_map/all_gather | solution.py:102
  295.4 2.6 fusion.91
  299.5 61.4 %all-gather.24.cloned.1.call-done = bf16[768,3072]{1,0:T(8,128)(2,1)} async-done(((bf16[24,3072]{1,0:T(8,128)(2,1)}), bf16[768,3072]{1,0:T(8,128)(2,1)}) %all-gather.24.cloned.1.call-update) | async-done | bytes 4718608 | tf_op jit(solution)/shard_map/all_gather | solution.py:103
  360.9 20.5 %fusion.20 = (bf16[512,3072]{1,0:T(8,128)(2,1)}, f32[512,3072]{1,0:T(8,128)}) fusion(f32[3072]{0:T(1024)S(1)} %convert_element_type.199, bf16[768,3072]{1,0:T(8,128)(2,1)} %all-gather.24.cloned.1.call-done, f32[512,768]{1,0:T(8,128)} %copy-done.4, f32[768]{0:T(1024)S(1)} %convert_element_type.197, f32[768]{0:T(1024)S(1)} %convert_element_type.196, ...), kind=kOutput, calls=%fused_computation.23 | convolution fusion | flops 2521694208 | bytes 15751168 | tf_op jit(solution)/shard_map/dot_general | solution.py:169
  381.4 44.9 %all-gather.26.cloned.1.call-done = bf16[3072,768]{1,0:T(8,128)(2,1)} async-done(((bf16[96,768]{1,0:T(8,128)(2,1)}), bf16[3072,768]{1,0:T(8,128)(2,1)}) %all-gather.26.cloned.1.call-update) | async-done | bytes 4718608 | tf_op jit(solution)/shard_map/all_gather | solution.py:104
  426.3 8.2 convert_reduce_fusion
  434.5 3.6 multiply_reduce_fusion
  442.4 2.6 copy.57
  444.9 2.3 copy.56
  447.2 2.3 fusion.58
  449.6 28.9 %convert_reduce_fusion.5 = (f32[12,64]{1,0:T(8,128)S(1)}, bf16[12,64,512]{2,1,0:T(8,128)(2,1)}) fusion(bf16[2048,12,64]{0,2,1:T(8,128)(2,1)S(1)} %bitcast.154, f32[12,512,2048]{2,1,0:T(8,128)} %get-tuple-element.49, f32[12,512]{1,0:T(8,128)S(1)} %bitcast.170, f32[12,512]{1,0:T(8,128)S(1)} %log_add_fusion, pred[512,2048]{1,0:T(8,128)(4,1)} %fusion.34, ...), kind=kOutput, calls=%fused_computation.83 | convolution fusion | flops 3298295040 | bytes 59296768 | tf_op jit(solution)/shard_map/shqk,skhd->sqhd/dot_general | solution.py:218
  478.6 3.9 fusion.85
  487.3 3.2 copy.58
  490.4 5.4 all_gather.97
  495.9 21.2 %fusion.93 = f32[12,2048,512]{2,1,0:T(8,128)} fusion(bf16[2048,12,64]{0,2,1:T(8,128)(2,1)S(1)} %bitcast.155, bf16[512,12,64]{0,2,1:T(8,128)(2,1)} %bitcast.159), kind=kOutput, calls=%fused_computation.134 | convolution fusion | flops 1610612736 | bytes 54263808 | tf_op jit(solution)/shard_map/sqhd,skhd->shqk/dot_general | solution.py:45
  517.1 5.4 all-gather.4
  522.5 3.9 fusion.68
  526.5 4.8 copy.60
  531.2 26.5 %multiply_convert_fusion.4 = bf16[12,64,512]{2,1,0:T(8,128)(2,1)} fusion(bf16[2048,12,64]{0,2,1:T(8,128)(2,1)S(1)} %bitcast.156, f32[12,2048,512]{2,1,0:T(8,128)} %fusion.93, f32[12,2048]{1,0:T(8,128)S(1)} %bitcast.174, f32[12,2048]{1,0:T(8,128)S(1)} %bitcast.172, pred[2048,512]{1,0:T(8,128)(4,1)} %fusion.35, bf16[2048,12,64]{0,2,1:T(8,128)(2,1)} %bitcast.162, ...), kind=kOutput, calls=%fused_computation.85 | convolution fusion | flops 3297509376 | bytes 59441152 | tf_op jit(solution)/shard_map/shqk,sqhd->skhd/dot_general | solution.py:249
  557.8 3.9 fusion.83
  561.8 21.3 %convert_reduce_fusion.4 = (f32[12,64]{1,0:T(8,128)}, bf16[12,64,512]{2,1,0:T(8,128)(2,1)S(1)}) fusion(bf16[2048,12,64]{0,2,1:T(8,128)(2,1)} %bitcast.163, f32[12,2048,512]{2,1,0:T(8,128)} %fusion.93, f32[12,2048]{1,0:T(8,128)S(1)} %bitcast.173, pred[2048,512]{1,0:T(8,128)(4,1)S(1)} %copy-done.11), kind=kOutput, calls=%fused_computation.82 | convolution fusion | flops 1662123264 | bytes 55413760 | tf_op jit(solution)/shard_map/shqk,sqhd->skhd/dot_general | solution.py:252
  583.9 2.6 fusion.81
  586.7 7.2 fusion.79
  595.1 8.2 fusion.63
  604.6 3.4 fusion.92
  608.0 6.2 add_bitcast_fusion
  615.6 2.4 fusion.94
  618.0 4.9 fusion.51
  622.9 41.2 %all-reduce.18 = (f32[768]{0:T(1024)S(1)}, f32[768]{0:T(1024)S(1)}, f32[768]{0:T(1024)S(1)}, f32[768]{0:T(1024)S(1)}, f32[768]{0:T(1024)S(1)}, /*index=5*/f32[76...) all-reduce(f32[768]{0:T(1024)} %get-tuple-element.19, ...), channel_id=13, replica_groups=mesh['dp'=8,'seq'=4] {'dp','seq'}, use_global_device_ids=true, to_apply=%region_18.19.clone | all-reduce | flops 9216 | bytes 73728
  670.7 3.1 fusion.50
  673.8 20.9 %reduce-scatter.13.cloned.1.call-done = f32[24,768]{1,0:T(8,128)} async-done(((f32[768,768]{1,0:T(8,128)}), f32[24,768]{1,0:T(8,128)}) %reduce-scatter.13.cloned.1.call-update) | async-done | bytes 73744 | tf_op jit(solution)/shard_map/reduce_scatter | solution.py:292
  694.7 104.0 %reduce-scatter.9.cloned.1.call-done = f32[24,768]{1,0:T(8,128)} async-done(((f32[768,768]{1,0:T(8,128)}), f32[24,768]{1,0:T(8,128)}) %reduce-scatter.9.cloned.1.call-update) | async-done | bytes 73744 | tf_op jit(solution)/shard_map/reduce_scatter | solution.py:290
  798.7 104.6 %reduce-scatter.11.cloned.1.call-done = f32[24,768]{1,0:T(8,128)} async-done(((f32[768,768]{1,0:T(8,128)}), f32[24,768]{1,0:T(8,128)}) %reduce-scatter.11.cloned.1.call-update) | async-done | bytes 73744 | tf_op jit(solution)/shard_map/reduce_scatter | solution.py:291
  903.2 141.0 %reduce-scatter.15.cloned.1.call-done = f32[24,3072]{1,0:T(8,128)} async-done(((f32[768,3072]{1,0:T(8,128)}), f32[24,3072]{1,0:T(8,128)}) %reduce-scatter.15.cloned.1.call-update) | async-done | bytes 294928 | tf_op jit(solution)/shard_map/reduce_scatter | solution.py:293
  1044.3 141.8 %reduce-scatter.17.cloned.1.call-done = f32[96,768]{1,0:T(8,128)} async-done(((f32[3072,768]{1,0:T(8,128)}), f32[96,768]{1,0:T(8,128)}) %reduce-scatter.17.cloned.1.call-update) | async-done | bytes 294928 | tf_op jit(solution)/shard_map/reduce_scatter | solution.py:294
  (169 shorter events, 42.8 us)
Async XLA Ops:
  7.2 60.9 %all-gather.18.cloned.1.call-start = ((), (), s32[]{:S(2)}) async-start(), calls=%async_computation.7 | async-start | bytes 1216512 | tf_op jit(solution)/shard_map/all_gather | solution.py:100
  7.9 115.9 %all-gather.20.cloned.1.call-start = ((), (), s32[]{:S(2)}) async-start(), calls=%async_computation.8 | async-start | bytes 1216512 | tf_op jit(solution)/shard_map/all_gather | solution.py:101
  8.7 171.0 %all-gather.16.cloned.1.call-start = ((), (), s32[]{:S(2)}) async-start(), calls=%async_computation.6 | async-start | bytes 1216512 | tf_op jit(solution)/shard_map/all_gather | solution.py:99
  9.4 199.2 %all-gather.28.cloned.1.call-start = ((), (), s32[]{:S(2)}) async-start(), calls=%async_computation.18 | async-start | bytes 3932160 | tf_op jit(solution)/shard_map/all_gather | solution.py:139
  59.7 120.0 %copy-start.27 = (f32[768]{0:T(1024)}, f32[768]{0:T(1024)S(1)}, u32[]{:S(2)}) copy-start(f32[768]{0:T(1024)S(1)} %convert_element_type.185) | copy-start | bytes 9220
  59.7 120.0 %copy-start.17 = (f32[768]{0:T(1024)}, f32[768]{0:T(1024)S(1)}, u32[]{:S(2)}) copy-start(f32[768]{0:T(1024)S(1)} %convert_element_type.184) | copy-start | bytes 9220
  61.0 118.7 %copy-start.19 = (f32[512]{0:T(512)}, f32[512]{0:T(512)S(1)}, u32[]{:S(2)}) copy-start(f32[512]{0:T(512)S(1)} %broadcast_multiply_fusion.5) | copy-start | bytes 6148
  62.5 61.3 %copy-start.2 = (bf16[1,512,768]{2,1,0:T(8,128)(2,1)S(1)}, bf16[1,512,768]{2,1,0:T(8,128)(2,1)}, u32[]{:S(2)}) copy-start(bf16[1,512,768]{2,1,0:T(8,128)(2,1)} %param.18) | copy-start | bytes 2359300
  62.5 117.2 %copy-start.25 = (f32[512]{0:T(512)}, f32[512]{0:T(512)S(1)}, u32[]{:S(2)}) copy-start(f32[512]{0:T(512)S(1)} %add_rsqrt_fusion.1) | copy-start | bytes 6148
  71.4 184.7 %all-gather.30.cloned.1.call-start = ((), (), s32[]{:S(2)}) async-start(), calls=%async_computation.19 | async-start | bytes 3932160 | tf_op jit(solution)/shard_map/all_gather | solution.py:140
  71.5 57.6 %copy-start.29 = (s32[1,512]{1,0:T(1,128)S(1)}, s32[1,512]{1,0:T(1,128)}, u32[]{:S(2)}) copy-start(s32[1,512]{1,0:T(1,128)} %param.20) | copy-start | bytes 6148
  126.9 168.5 %all-gather.22.cloned.1.call-start = ((), (), s32[]{:S(2)}) async-start(), calls=%async_computation.9 | async-start | bytes 1216512 | tf_op jit(solution)/shard_map/all_gather | solution.py:102
  127.5 233.4 %all-gather.24.cloned.1.call-start = ((), (), s32[]{:S(2)}) async-start(), calls=%async_computation.10 | async-start | bytes 4866048 | tf_op jit(solution)/shard_map/all_gather | solution.py:103
  128.2 298.1 %all-gather.26.cloned.1.call-start = ((), (), s32[]{:S(2)}) async-start(), calls=%async_computation.11 | async-start | bytes 4866048 | tf_op jit(solution)/shard_map/all_gather | solution.py:104
  129.0 358.3 %all-gather.32.cloned.1.call-start = ((), (), s32[]{:S(2)}) async-start(), calls=%async_computation.20 | async-start | bytes 3932160 | tf_op jit(solution)/shard_map/all_gather | solution.py:231
  129.1 7.4 copy-start.21
  134.2 2.3 copy-start.15
  134.3 2.2 copy-start.23
  181.9 1.2 copy-start.9
  183.1 343.4 %all-gather.34.cloned.1.call-start = ((), (), s32[]{:S(2)}) async-start(), calls=%async_computation.21 | async-start | bytes 3932160 | tf_op jit(solution)/shard_map/all_gather | solution.py:234
  298.1 1.1 copy-start.4
  426.3 8.2 copy-start.5
  426.3 8.2 copy-start.31
  434.5 3.6 copy-start.35
  434.5 3.6 copy-start.12
  438.1 2.5 copy-start.32
  442.3 231.5 %reduce-scatter.7.cloned.1.call-start = ((), (), s32[]{:S(2)}) async-start(), calls=%async_computation.12 | async-start | bytes 2433024 | tf_op jit(solution)/shard_map/reduce_scatter | solution.py:289
  449.6 29.0 %copy-start.18 = (f32[768]{0:T(1024)S(1)}, f32[768]{0:T(1024)}, u32[]{:S(2)}) copy-start(f32[768]{0:T(1024)} %copy-done.17) | copy-start | bytes 9220
  449.6 28.9 %copy-start.20 = (f32[512]{0:T(512)S(1)}, f32[512]{0:T(512)}, u32[]{:S(2)}) copy-start(f32[512]{0:T(512)} %copy-done.19) | copy-start | bytes 6148
  449.6 28.9 %copy-start.26 = (f32[512]{0:T(512)S(1)}, f32[512]{0:T(512)}, u32[]{:S(2)}) copy-start(f32[512]{0:T(512)} %copy-done.25) | copy-start | bytes 6148
  449.6 28.9 %copy-start.28 = (f32[768]{0:T(1024)S(1)}, f32[768]{0:T(1024)}, u32[]{:S(2)}) copy-start(f32[768]{0:T(1024)} %copy-done.27) | copy-start | bytes 9220
  478.5 4.4 copy-start.16
  478.5 4.4 copy-start.22
  478.6 4.4 copy-start.24
  478.6 6.3 copy-start.7
  482.5 3.6 copy-start.8
  482.5 212.2 %reduce-scatter.13.cloned.1.call-start = ((), (), s32[]{:S(2)}) async-start(), calls=%async_computation.15 | async-start | bytes 2433024 | tf_op jit(solution)/shard_map/reduce_scatter | solution.py:292
  526.4 272.3 %reduce-scatter.9.cloned.1.call-start = ((), (), s32[]{:S(2)}) async-start(), calls=%async_computation.13 | async-start | bytes 2433024 | tf_op jit(solution)/shard_map/reduce_scatter | solution.py:290
  557.8 4.0 copy-start.11
  561.7 22.2 %copy-start.3 = (bf16[1,512,768]{2,1,0:T(8,128)(2,1)S(1)}, bf16[1,512,768]{2,1,0:T(8,128)(2,1)}, u32[]{:S(2)}) copy-start(bf16[1,512,768]{2,1,0:T(8,128)(2,1)} %param.18) | copy-start | bytes 2359300
  561.7 341.5 %reduce-scatter.11.cloned.1.call-start = ((), (), s32[]{:S(2)}) async-start(), calls=%async_computation.14 | async-start | bytes 2433024 | tf_op jit(solution)/shard_map/reduce_scatter | solution.py:291
  583.9 2.8 copy-start.6
  586.5 457.8 %reduce-scatter.15.cloned.1.call-start = ((), (), s32[]{:S(2)}) async-start(), calls=%async_computation.16 | async-start | bytes 9732096 | tf_op jit(solution)/shard_map/reduce_scatter | solution.py:293
  594.0 592.1 %reduce-scatter.17.cloned.1.call-start = ((), (), s32[]{:S(2)}) async-start(), calls=%async_computation.17 | async-start | bytes 9732096 | tf_op jit(solution)/shard_map/reduce_scatter | solution.py:294
  603.3 1.3 copy-start.33
  604.6 3.4 copy-start.34
  614.2 3.8 copy-start.10
  618.0 52.7 %copy-start.1 = (f32[512,768]{1,0:T(8,128)S(1)}, f32[512,768]{1,0:T(8,128)}, u32[]{:S(2)}) copy-start(f32[512,768]{1,0:T(8,128)} %copy-done) | copy-start | bytes 4718596
  (4 other events, 3.8 us)
Sparse Core Ops, SparseCore 0:
  10.9 57.0 all-gather.17
  71.0 52.7 all-gather.19
  126.7 52.9 all-gather.15
  181.1 27.4 all-gather.27
  210.0 28.5 all-gather.29
  241.3 54.0 all-gather.21
  298.3 62.5 all-gather.23
  363.8 62.4 all-gather.25
  427.9 27.3 all-gather.31
  456.6 28.5 all-gather.33
  491.1 99.0 reduce-scatter.6
  596.7 97.9 reduce-scatter.12
  700.6 98.0 reduce-scatter.8
  805.2 97.9 reduce-scatter.10
  909.5 134.6 reduce-scatter.14
  1051.6 134.4 reduce-scatter.16
where the time goes:
time: 1200 us; the launch traced here: 1190 us
  waiting for transfers between devices  762 us (64%)
  matrix products  233 us (19%)
  blocking collectives  99.9 us (8%)
  local copies, waits for them, and re-layouts  44.2 us (4%)
  other arithmetic  37.3 us (3%)
  between operations  14.6 us (1%)
    reduce_scatter x1, waiting for transfers between devices, body(): lax.psum_scatter(grad_down, ('dp', 'seq'), scatter_dimension=0, tiled=True)  142 us
    reduce_scatter x1, waiting for transfers between devices, body(): lax.psum_scatter(grad_up, ('dp', 'seq'), scatter_dimension=0, tiled=True)  141 us
    reduce_scatter x1, waiting for transfers between devices, body(): lax.psum_scatter(grad_value, ('dp', 'seq'), scatter_dimension=0, tiled=True)  105 us
    reduce_scatter x1, waiting for transfers between devices, body(): lax.psum_scatter(grad_key, ('dp', 'seq'), scatter_dimension=0, tiled=True)  104 us
    unnamed x2, blocking collectives  83.9 us
    all_gather x1, waiting for transfers between devices, body(): lax.all_gather(w_up, ('dp', 'seq'), axis=0, tiled=True)  61.4 us
    all_gather x1, waiting for transfers between devices, body(): lax.all_gather(w_value, ('dp', 'seq'), axis=0, tiled=True)  52.3 us
    all_gather x1, waiting for transfers between devices, body(): lax.all_gather(w_down, ('dp', 'seq'), axis=0, tiled=True)  44.9 us
  transfers between devices with their start and end apart: 16, of which 12 were waited for; matrix products, arithmetic and copies ran while one was open for 26% of the time, Pallas kernels for 0%

commit v1 on v0

v1 whole, which is shorter than its diff:
```python
import functools
import math

import jax
import jax.numpy as jnp
from jax import lax
from jax.experimental import pallas as pl
from jax.experimental.pallas import tpu as pltpu
from jax.sharding import PartitionSpec as P

H = 12
EPSILON = 1e-05
MASKED = -1e30
F32 = jnp.float32
BF16 = jnp.bfloat16
LANES = 128


def dot_nt(a, b):
    return lax.dot_general(a, b, (((1,), (1,)), ((), ())), preferred_element_type=F32)


def dot_tn(a, b):
    return lax.dot_general(a, b, (((0,), (0,)), ((), ())), preferred_element_type=F32)


def dot_nn(a, b):
    return jnp.dot(a, b, preferred_element_type=F32)


def attend_kernel(me_ref, qkv_ref, seg_row_ref, seg_col_ref, low_ref, full_ref, lse_ref, *, heads, hd):
    me = me_ref[0]
    qi = pl.program_id(0)
    rq = qi ^ me
    block = qkv_ref.shape[1]
    width = heads * hd
    scale = jnp.asarray(1.0 / math.sqrt(hd), BF16)
    queries = [qkv_ref[rq, :, h * hd : (h + 1) * hd] * scale for h in range(heads)]
    seg_q = seg_row_ref[rq]

    def step(rk, state, causal):
        allowed = seg_col_ref[rk] == seg_q
        if causal:
            k_pos = lax.broadcasted_iota(jnp.int32, (block, block), 0)
            q_pos = lax.broadcasted_iota(jnp.int32, (block, block), 1)
            allowed = allowed & (k_pos <= q_pos)
        new = []
        for h in range(heads):
            top, total, mixed = state[h]
            key = qkv_ref[rk, :, width + h * hd : width + (h + 1) * hd]
            value = qkv_ref[rk, :, 2 * width + h * hd : 2 * width + (h + 1) * hd]
            scores = jnp.where(allowed, dot_nt(key, queries[h]), MASKED)
            higher = jnp.maximum(top, jnp.max(scores, 0, keepdims=True))
            weights = jnp.exp(scores - higher)
            fade = jnp.exp(top - higher)
            total = total * fade + jnp.sum(weights, 0, keepdims=True)
            mixed = mixed * fade + dot_tn(value, weights.astype(BF16))
            new.append((higher, total, mixed))
        return tuple(new)

    start = tuple(
        (jnp.full((1, block), MASKED, F32), jnp.zeros((1, block), F32), jnp.zeros((hd, block), F32))
        for _ in range(heads)
    )
    state = lax.fori_loop(0, qi, lambda kj, c: step(kj ^ me, c, False), start)
    state = step(rq, state, True)
    rows = []
    for h in range(heads):
        top, total, mixed = state[h]
        rows.append(mixed / total)
        lse_ref[0, h : h + 1, :] = top + jnp.log(total)
    full = jnp.concatenate(rows, 0)
    full_ref[0] = full
    low_ref[0] = full.T.astype(BF16)


def attend(me, qkv, seg_row, seg_col, heads, hd):
    n, block, _ = qkv.shape
    width = heads * hd

    def whole(shape):
        return pl.BlockSpec(shape, lambda i, me: (0,) * len(shape))

    def own(shape):
        return pl.BlockSpec(shape, lambda i, me: (i ^ me[0], 0, 0))

    return pl.pallas_call(
        functools.partial(attend_kernel, heads=heads, hd=hd),
        grid_spec=pltpu.PrefetchScalarGridSpec(
            num_scalar_prefetch=1,
            grid=(n,),
            in_specs=[whole(qkv.shape), whole(seg_row.shape), whole(seg_col.shape)],
            out_specs=[own((1, block, width)), own((1, width, block)), own((1, 8, block))],
        ),
        out_shape=[
            jax.ShapeDtypeStruct((n, block, width), BF16),
            jax.ShapeDtypeStruct((n, width, block), F32),
            jax.ShapeDtypeStruct((n, 8, block), F32),
        ],
        compiler_params=pltpu.CompilerParams(vmem_limit_bytes=40 * 1024 * 1024),
        cost_estimate=pl.CostEstimate(
            flops=20 * 1000**3, bytes_accessed=8 * 1000**2, transcendentals=8 * 1000**2
        ),
        name="attend",
    )(me, qkv, seg_row, seg_col)


def attend_back_kernel(
    me_ref, qkv_ref, go_ref, full_ref, lse_ref, seg_row_ref, seg_col_ref, grad_ref, gq_ref, dot_ref, *, heads, hd
):
    me = me_ref[0]
    kj = pl.program_id(0)
    rk = kj ^ me
    n, block, _ = qkv_ref.shape
    width = heads * hd
    scale = 1.0 / math.sqrt(hd)
    low_scale = jnp.asarray(scale, BF16)

    @pl.when(kj == 0)
    def _():
        gq_ref[...] = jnp.zeros_like(gq_ref)
        for b in range(n):
            prod = go_ref[b].astype(F32).T * full_ref[b]
            for h in range(heads):
                dot_ref[b, h : h + 1, :] = jnp.sum(prod[h * hd : (h + 1) * hd], 0, keepdims=True)

    keys = [qkv_ref[rk, :, width + h * hd : width + (h + 1) * hd] for h in range(heads)]
    values = [qkv_ref[rk, :, 2 * width + h * hd : 2 * width + (h + 1) * hd] for h in range(heads)]
    seg_k = seg_col_ref[rk]

    def step(rq, state, causal):
        allowed = seg_k == seg_row_ref[rq]
        if causal:
            k_pos = lax.broadcasted_iota(jnp.int32, (block, block), 0)
            q_pos = lax.broadcasted_iota(jnp.int32, (block, block), 1)
            allowed = allowed & (k_pos <= q_pos)
        new = []
        for h in range(heads):
            gk, gv = state[h]
            query = qkv_ref[rq, :, h * hd : (h + 1) * hd] * low_scale
            go = go_ref[rq, :, h * hd : (h + 1) * hd]
            scores = jnp.where(allowed, dot_nt(keys[h], query), MASKED)
            weights = jnp.exp(scores - lse_ref[rq, h : h + 1, :])
            gw = dot_nt(values[h], go)
            ds = (weights * (gw - dot_ref[rq, h : h + 1, :])).astype(BF16)
            gv = gv + dot_nn(weights.astype(BF16), go)
            gk = gk + dot_nn(ds, query)
            gq_ref[rq, h * hd : (h + 1) * hd, :] += dot_tn(keys[h], ds)
            new.append((gk, gv))
        return tuple(new)

    zero = jnp.zeros((block, hd), F32)
    state = step(rk, tuple((zero, zero) for _ in range(heads)), True)
    state = lax.fori_loop(kj + 1, n, lambda qi, c: step(qi ^ me, c, False), state)
    grad_ref[0, :, :width] = (gq_ref[rk] * scale).T.astype(BF16)
    for h in range(heads):
        gk, gv = state[h]
        grad_ref[0, :, width + h * hd : width + (h + 1) * hd] = gk.astype(BF16)
        grad_ref[0, :, 2 * width + h * hd : 2 * width + (h + 1) * hd] = gv.astype(BF16)


def attend_back(me, qkv, go, full, lse, seg_row, seg_col, heads, hd):
    n, block, wide = qkv.shape
    width = heads * hd

    def whole(shape):
        return pl.BlockSpec(shape, lambda i, me: (0,) * len(shape))

    return pl.pallas_call(
        functools.partial(attend_back_kernel, heads=heads, hd=hd),
        grid_spec=pltpu.PrefetchScalarGridSpec(
            num_scalar_prefetch=1,
            grid=(n,),
            in_specs=[whole(a.shape) for a in (qkv, go, full, lse, seg_row, seg_col)],
            out_specs=pl.BlockSpec((1, block, wide), lambda i, me: (i ^ me[0], 0, 0)),
            scratch_shapes=[pltpu.VMEM((n, width, block), F32), pltpu.VMEM((n, 8, block), F32)],
        ),
        out_shape=jax.ShapeDtypeStruct((n, block, wide), BF16),
        compiler_params=pltpu.CompilerParams(vmem_limit_bytes=40 * 1024 * 1024),
        cost_estimate=pl.CostEstimate(
            flops=40 * 1000**3, bytes_accessed=12 * 1000**2, transcendentals=8 * 1000**2
        ),
        name="attend_back",
    )(me, qkv, go, full, lse, seg_row, seg_col)


def normed_parts(value):
    mean = jnp.mean(value, -1, keepdims=True)
    centred = value - mean
    inv_std = lax.rsqrt(jnp.mean(centred * centred, -1, keepdims=True) + EPSILON)
    return centred * inv_std, inv_std


def normalize_back(grad_in, normed, inv_std, gain):
    scaled = grad_in * gain
    return inv_std * (
        scaled
        - jnp.mean(scaled, -1, keepdims=True)
        - normed * jnp.mean(scaled * normed, -1, keepdims=True)
    )


def gelu_and_slope(value):
    cumul = 0.5 * (1.0 + lax.erf(value * (1.0 / math.sqrt(2.0))))
    slope = cumul + value * jnp.exp(-0.5 * value * value) * (1.0 / math.sqrt(2.0 * math.pi))
    return value * cumul, slope


def swap(value, axis, size, mask):
    return lax.ppermute(value, axis, [(i, i ^ mask) for i in range(size)])


def bits_of(size):
    count = size.bit_length() - 1
    return [1 << b for b in range(count)]


def ordered(parts, index):
    parts = [part[None] for part in parts]
    bit = 1
    while len(parts) > 1:
        on = (index & bit) != 0
        parts = [
            jnp.where(on, jnp.concatenate([b, a], 0), jnp.concatenate([a, b], 0))
            for a, b in zip(parts[::2], parts[1::2])
        ]
        bit *= 2
    return parts[0]


def spread_dp(value, index, size):
    masks = bits_of(size)[::-1]
    shape = value.shape
    value = value.reshape((1,) * len(masks) + shape)
    for axis, mask in enumerate(masks):
        other = swap(value, "dp", size, mask)
        on = (index & mask) != 0
        value = jnp.where(
            on, jnp.concatenate([other, value], axis), jnp.concatenate([value, other], axis)
        )
    return value.reshape((size,) + shape)


def collect_dp(value, index, size, last=F32):
    masks = bits_of(size)
    shape = value.shape[1:]
    value = value.reshape((2,) * len(masks) + shape)
    for step, mask in enumerate(masks):
        axis = len(masks) - 1 - step
        on = ((index & mask) != 0).astype(jnp.int32)
        keep = lax.dynamic_index_in_dim(value, on, axis, False)
        send = lax.dynamic_index_in_dim(value, 1 - on, axis, False)
        got = swap(send, "dp", size, mask)
        value = keep.astype(F32) + got.astype(F32)
        value = value.astype(BF16 if step < len(masks) - 1 else last)
    return value


def collect_seq(parts, size, last=BF16):
    mask = 1
    while len(parts) > 1:
        sent = [swap(b, "seq", size, mask) for b in parts[1::2]]
        kind = BF16 if len(parts) > 2 else last
        parts = [(a.astype(F32) + b.astype(F32)).astype(kind) for a, b in zip(parts[::2], sent)]
        mask *= 2
    return parts[0]


def spread_seq(value, size):
    got = {0: value}
    for mask in bits_of(size)[::-1]:
        for p in list(got):
            got[p | mask] = swap(got[p], "seq", size, mask)
    return [got[p] for p in range(size)]


def trade_seq(pieces, index, size):
    return [
        swap(lax.dynamic_index_in_dim(pieces, index ^ p, 0, False), "seq", size, p)
        if p
        else lax.dynamic_index_in_dim(pieces, index, 0, False)
        for p in range(size)
    ]


def body(
    nd,
    ns,
    tokens,
    cotangent,
    segments,
    w_query,
    w_key,
    w_value,
    w_out,
    w_up,
    w_down,
    ln1_gain,
    ln1_shift,
    query_bias,
    value_bias,
    out_bias,
    ln2_gain,
    ln2_shift,
    up_bias,
    down_bias,
):
    d = lax.axis_index("dp")
    s = lax.axis_index("seq")
    me = s.astype(jnp.int32).reshape(1)
    _, block, dm = tokens.shape
    hd = dm // H
    heads = H // ns
    width = heads * hd
    rows = w_query.shape[0]
    ff_rows, ff = w_down.shape[0], w_up.shape[1]
    ratio = ff_rows // rows
    part = ff // ns

    x_own = tokens.reshape(block, dm)
    x_all = jnp.stack(spread_seq(x_own, ns))
    segs = jnp.stack(spread_seq(segments.reshape(block), ns))
    seg_row = segs.reshape(ns, 1, block)
    seg_col = segs.reshape(ns, block, 1)

    cols = jnp.concatenate([w.reshape(rows, ns, width) for w in (w_query, w_key, w_value)], 2)
    vectors = [ln1_gain, ln1_shift, ln2_gain, ln2_shift, out_bias, down_bias, query_bias, value_bias]
    vec = jnp.concatenate([jnp.stack(vectors), up_bias.reshape(ratio, rows)], 0).T
    vec = jnp.pad(vec, ((0, 0), (0, LANES - vec.shape[1])))
    vec = jnp.broadcast_to(vec[:, None], (rows, ns, LANES))
    pieces = jnp.concatenate([cols, vec], 2).transpose(1, 0, 2)
    got = spread_dp(ordered(trade_seq(pieces, s, ns), s), d, nd)
    got = got.reshape(dm, 3 * width + LANES)
    w_qkv = got[:, : 3 * width]
    vecs = got[:, 3 * width :].T.astype(F32)
    gain_one, shift_one, gain_two, shift_two, out_add, down_add, q_add, v_add = [vecs[i] for i in range(8)]
    up_add = vecs[8 : 8 + ratio].reshape(ratio, nd, ns, rows).transpose(2, 1, 0, 3).reshape(ns, part)
    up_add = jnp.stack([lax.dynamic_index_in_dim(up_add, s ^ p, 0, False) for p in range(ns)])

    up_cols = w_up.reshape(rows, nd, ns, ff_rows).transpose(2, 0, 1, 3).reshape(ns, rows, part)
    up_piece = ordered(trade_seq(up_cols, s, ns), s).reshape(ns * rows, part)
    up_out = spread_dp(jnp.concatenate([w_out, up_piece], 0), d, nd)
    up_out = spread_seq(up_out, ns)
    w_ups = [piece[:, rows:].reshape(dm, part) for piece in up_out]
    w_outs = ordered([piece[:, :rows] for piece in up_out], s)
    w_outs = w_outs.transpose(1, 0, 2, 3).reshape(ns, width, dm)
    w_outs = jnp.concatenate([lax.dynamic_index_in_dim(w_outs, s ^ p, 0, False) for p in range(ns)], 0)
    down = spread_dp(w_down, d, nd).reshape(part, dm)
    w_downs = spread_seq(down, ns)

    x_all_f = x_all.astype(F32)
    n_one, inv_one = normed_parts(x_all_f)
    h_one = (n_one * gain_one + shift_one).astype(BF16)
    add = jnp.concatenate(
        [
            lax.dynamic_slice_in_dim(q_add, s * width, width),
            jnp.zeros((width,), F32),
            lax.dynamic_slice_in_dim(v_add, s * width, width),
        ]
    )
    qkv = (jnp.einsum("nbk,kc->nbc", h_one, w_qkv, preferred_element_type=F32) + add).astype(BF16)
    o_low, o_full, lse = attend(me, qkv, seg_row, seg_col, heads, hd)
    ol = jnp.concatenate([o_low[0]] + [swap(o_low[p], "seq", ns, p) for p in range(1, ns)], 1)
    x_f = x_own.astype(F32)
    x_two = x_f + dot_nn(ol, w_outs) + out_add
    n_two, inv_two = normed_parts(x_two)
    h_two = (n_two * gain_two + shift_two).astype(BF16)
    g = cotangent.reshape(block, dm)
    g_f = g.astype(F32)
    out = x_two + down_add
    gh_two = jnp.zeros((block, dm), F32)
    gus, d_downs, d_ups, d_up_adds = [], [], [], []
    for p in range(ns):
        u = dot_nn(h_two, w_ups[p]) + up_add[p]
        act, slope = gelu_and_slope(u)
        act = act.astype(BF16)
        out = out + dot_nn(act, w_downs[p])
        gu = (dot_nt(g, w_downs[p]) * slope).astype(BF16)
        d_downs.append(dot_tn(act, g).astype(BF16))
        gus.append(gu)
    for p in range(ns):
        d_ups.append(dot_tn(h_two, gus[p]).astype(BF16))
        d_up_adds.append(jnp.sum(gus[p].astype(F32), 0))
        gh_two = gh_two + dot_nt(gus[p], w_ups[p])
    gx_two = g_f + normalize_back(gh_two, n_two, inv_two, gain_two)
    gb = gx_two.astype(BF16)
    go = dot_nt(gb, w_outs).astype(BF16)
    d_out = dot_tn(ol, gb).astype(BF16).reshape(ns, width, dm)
    gos = [go[:, p * width : (p + 1) * width] for p in range(ns)]
    go_all = jnp.stack([gos[0]] + [swap(gos[p], "seq", ns, p) for p in range(1, ns)])

    sum_down = collect_seq(d_downs, ns).reshape(nd, ff_rows, dm)
    sum_down = collect_dp(sum_down, d, nd)
    d_out = ordered([d_out[p] for p in range(ns)], s).reshape(nd, ns, rows, dm)
    d_outs = [lax.dynamic_index_in_dim(d_out, s ^ p, 1, False) for p in range(ns)]
    mixed = [
        jnp.concatenate([d_outs[p], d_ups[p].reshape(nd, ns * rows, part)], 1) for p in range(ns)
    ]
    sum_up = collect_dp(collect_seq(mixed, ns), d, nd)
    sum_out = sum_up[:rows]
    sum_up = ordered(trade_seq(sum_up[rows:].reshape(ns, rows, part), s, ns), s)
    sum_up = sum_up.reshape(ns, rows, nd, ff_rows).transpose(1, 2, 0, 3).reshape(rows, ff)

    grads = attend_back(me, qkv, go_all, o_full, lse, seg_row, seg_col, heads, hd)
    gh_part = jnp.einsum("nbc,kc->nbk", grads, w_qkv, preferred_element_type=F32)
    d_qkv = jnp.einsum("nbk,nbc->kc", h_one, grads, preferred_element_type=F32)
    d_add = jnp.sum(grads.astype(F32), (0, 1))
    gh_low = gh_part.astype(BF16)
    gh_one = collect_seq([gh_low[p] for p in range(ns)], ns, F32)
    n_own, inv_own = normed_parts(x_f)
    grad_x = gx_two + normalize_back(gh_one, n_own, inv_own, gain_one)

    def at_heads(v):
        return lax.dynamic_update_slice_in_dim(jnp.zeros((dm,), F32), v, s * width, 0)

    d_vecs = jnp.stack(
        [
            jnp.sum(gh_part * n_one, (0, 1)),
            jnp.sum(gh_part, (0, 1)),
            jnp.sum(gh_two * n_two, 0),
            jnp.sum(gh_two, 0),
            jnp.sum(gb.astype(F32), 0),
            jnp.sum(g_f, 0),
            at_heads(d_add[:width]),
            at_heads(d_add[2 * width :]),
        ]
    )
    d_up_add = ordered(d_up_adds, s).reshape(ns, nd, ratio, rows).transpose(2, 1, 0, 3).reshape(ratio, dm)
    d_vecs = jnp.concatenate([d_vecs, d_up_add], 0)
    count = d_vecs.shape[0]
    d_vecs = jnp.pad(d_vecs, ((0, LANES - count), (0, 0))).T
    blob = jnp.concatenate([d_qkv, d_vecs], 1).astype(BF16)
    blob = collect_dp(blob.reshape(nd, ns * rows, 3 * width + LANES), d, nd)
    blobs = trade_seq(blob.reshape(ns, rows, 3 * width + LANES), s, ns)
    vec_sum = sum(b[:, 3 * width :] for b in blobs).T
    sums = ordered([b[:, : 3 * width] for b in blobs], s).reshape(ns, rows, 3, width)
    sums = sums.transpose(2, 1, 0, 3).reshape(3, rows, dm)
    v = [vec_sum[i] for i in range(8)]
    sum_up_bias = vec_sum[8 : 8 + ratio].reshape(ff_rows)
    return (
        out.reshape(1, block, dm),
        grad_x.reshape(1, block, dm),
        sums[0],
        sums[1],
        sums[2],
        sum_out,
        sum_up,
        sum_down,
        v[0],
        v[1],
        v[6],
        v[7],
        v[4],
        v[2],
        v[3],
        sum_up_bias,
        v[5],
    )


def solution(mesh):
    act = P("dp", "seq", None)
    weight = P(("dp", "seq"), None)
    vector = P(("dp", "seq"))
    return jax.shard_map(
        functools.partial(body, mesh.shape["dp"], mesh.shape["seq"]),
        mesh=mesh,
        in_specs=(act, act, P("dp", "seq")) + (weight,) * 6 + (vector,) * 9,
        out_specs=(act, act) + (weight,) * 6 + (vector,) * 9,
        check_vma=False,
    )
```

time: 1200 us -> 459 us (0.38)
  waiting for transfers between devices: 762 us -> 185 us
  matrix products: 233 us -> 72.9 us
  blocking collectives: 99.9 us -> 0 us
  starting transfers between devices: 1.43 us -> 51.4 us
  Pallas kernels: 0 us -> 44.3 us
    reduce_scatter x6 -> x0, waiting for transfers between devices: 512 us -> none  [the longest x1 142 us: body(): lax.psum_scatter(grad_down, ('dp', 'seq'), scatter_dimension=0, tiled=True)]
    all_gather x10 -> x0, waiting for transfers between devices: 246 us -> none  [the longest x1 61.4 us: body(): lax.all_gather(w_up, ('dp', 'seq'), axis=0, tiled=True)]
    ppermute x0 -> x57, waiting for transfers between devices: none -> 185 us  [swap(): return lax.ppermute(value, axis, [(i, i ^ mask) for i in range(size)])]
    dot_general x24 -> x30, matrix products: 233 us -> 72.9 us  [the longest x9 21 us: dot_nt(): lax.dot_general(a, b, (((1,), (1,)), ((), ())), preferred_element_type=F32)]
    unnamed x2 -> x0, blocking collectives: 83.9 us -> none
    ppermute x0 -> x57, starting transfers between devices: none -> 51.4 us  [swap(): return lax.ppermute(value, axis, [(i, i ^ mask) for i in range(size)])]
    pallas_call x0 -> x2, Pallas kernels: none -> 44.3 us  [the longest x1 26.5 us: attend_back(): pl.pallas_call(functools.partial(attend_back_kernel, heads=heads, hd=hd),...]
    reduce_sum x6 -> x9, other arithmetic: 28.8 us -> 9 us  [the longest x3 3.08 us: normed_parts(): jnp.mean(centred * centred, -1, keepdims=True) + EPSILON]
  transfers between devices with their start and end apart: 16 -> 57, of which waited for: 12 -> 22; matrix products, arithmetic and copies ran while one was open for 26% -> 31% of each run, Pallas kernels for 0% -> 10%
where the time goes in v1:
time: 459 us; the launch traced here: 451 us
  waiting for transfers between devices  185 us (40%)
  matrix products  72.9 us (16%)
  starting transfers between devices  51.4 us (11%)
  local copies, waits for them, and re-layouts  47.3 us (10%)
  other arithmetic  47 us (10%)
  Pallas kernels  44.3 us (10%)
    ppermute x57, waiting for transfers between devices, swap(): return lax.ppermute(value, axis, [(i, i ^ mask) for i in range(size)])  185 us
    ppermute x57, starting transfers between devices, swap(): return lax.ppermute(value, axis, [(i, i ^ mask) for i in range(size)])  51.4 us
    pallas_call x1, Pallas kernels, attend_back(): pl.pallas_call(functools.partial(attend_back_kernel, heads=heads, hd=hd),...  26.5 us
    dot_general x9, matrix products, dot_nt(): lax.dot_general(a, b, (((1,), (1,)), ((), ())), preferred_element_type=F32)  21 us
    dot_general x9, matrix products, dot_nn(): return jnp.dot(a, b, preferred_element_type=F32)  20 us
    pallas_call x1, Pallas kernels, attend(): pl.pallas_call(functools.partial(attend_kernel, heads=heads, hd=hd), grid...  17.8 us
    dot_general x9, matrix products, dot_tn(): lax.dot_general(a, b, (((0,), (0,)), ((), ())), preferred_element_type=F32)  17.6 us
    select_n x9, other arithmetic, spread_dp(): jnp.where(on, jnp.concatenate([other, value], axis), jnp.concatenate([val...  13.7 us
  transfers between devices with their start and end apart: 57, of which 22 were waited for; matrix products, arithmetic and copies ran while one was open for 31% of the time, Pallas kernels for 10%

profile of v1, /device:TPU:0, one launch (start us, length us, event | category | flops | bytes accessed | tf_op | source)
XLA Modules:
  0.0 450.9 jit_solution(16550125264361989442)
XLA Ops:
  0.7 3.0 collective-permute-start.1
  13.7 8.2 %collective-permute-done.3 = bf16[24,704]{1,0:T(8,128)(2,1)S(1)} collective-permute-done((bf16[24,704]{1,0:T(8,128)(2,1)S(1)}, bf16[24,704]{1,0:T(8,128)(2,1)S(1)}, u32[]{:S(2)}, u32[]{:S(2)}) %collective-permute-start.3) | collective-permute-done | bytes 33824 | tf_op jit(solution)/shard_map/ppermute | solution.py:210
  27.8 2.6 collective-permute-start.24
  30.9 11.5 %collective-permute-done.6 = bf16[1,1,1,4,24,704]{5,4,3,0,2,1:T(8,128)(2,1)S(1)} collective-permute-done((bf16[1,1,1,4,24,704]{5,4,3,0,2,1:T(8,128)(2,1)S(1)}, bf16[1,1,1,4,24,704]{5,4,3,0,2,1:T(8,128)(2,1)S(1)}, u32[]{:S(2)}, u32[]{:S(2)}) %collective-permute-start.6) | collective-permute-done | bytes 135200 | tf_op jit(solution)/shard_map/ppermute | solution.py:210
  42.4 4.1 collective-permute-start.7
  47.4 5.4 %collective-permute-done.18 = bf16[1,1,1,120,768]{4,3,0,2,1:T(8,128)(2,1)S(1)} collective-permute-done((bf16[1,1,1,120,768]{4,3,0,2,1:T(8,128)(2,1)S(1)}, bf16[1,1,1,120,768]{4,3,0,2,1:T(8,128)(2,1)S(1)}, u32[]{:S(2)}, u32[]{:S(2)}) %collective-permute-start.18) | collective-permute-done | bytes 184352 | tf_op jit(solution)/shard_map/ppermute | solution.py:210
  60.3 5.3 %collective-permute-done.25 = bf16[2,1,1,96,768]{4,3,2,1,0:T(8,128)(2,1)} collective-permute-done((bf16[2,1,1,96,768]{4,3,2,1,0:T(8,128)(2,1)}, bf16[2,1,1,96,768]{4,3,2,1,0:T(8,128)(2,1)}, u32[]{:S(2)}, u32[]{:S(2)}) %collective-permute-start.25) | collective-permute-done | bytes 294944 | tf_op jit(solution)/shard_map/ppermute | solution.py:210
  69.1 2.6 collective-permute-done.19
  75.3 2.1 maximum_select_fusion.1
  81.1 6.5 %collective-permute-done.26 = bf16[2,2,1,96,768]{4,3,2,1,0:T(8,128)(2,1)} collective-permute-done((bf16[2,2,1,96,768]{4,3,2,1,0:T(8,128)(2,1)}, bf16[2,2,1,96,768]{4,3,2,1,0:T(8,128)(2,1)}, u32[]{:S(2)}, u32[]{:S(2)}) %collective-permute-start.26) | collective-permute-done | bytes 589856 | tf_op jit(solution)/shard_map/ppermute | solution.py:210
  87.6 2.9 maximum_select_fusion.3
  91.9 9.1 %collective-permute-done.20 = bf16[2,2,1,120,768]{4,3,0,2,1:T(8,128)(2,1)} collective-permute-done((bf16[2,2,1,120,768]{4,3,0,2,1:T(8,128)(2,1)}, bf16[2,2,1,120,768]{4,3,0,2,1:T(8,128)(2,1)}, u32[]{:S(2)}, u32[]{:S(2)}) %collective-permute-start.20) | collective-permute-done | bytes 737312 | tf_op jit(solution)/shard_map/ppermute | solution.py:210
  101.0 2.2 maximum_select_fusion
  107.0 2.4 fusion.7
  109.5 4.3 add_convert_fusion.qkv_ref
  113.8 36.8 %collective-permute-done.21 = bf16[8,120,768]{2,1,0:T(8,128)(2,1)S(1)} collective-permute-done((bf16[8,120,768]{2,1,0:T(8,128)(2,1)S(1)}, bf16[8,120,768]{2,1,0:T(8,128)(2,1)S(1)}, u32[]{:S(2)}, u32[]{:S(2)}) %collective-permute-start.21) | collective-permute-done | bytes 1474592 | tf_op jit(solution)/shard_map/ppermute | solution.py:210
  150.6 17.8 %attend.1 = (bf16[4,512,192]{2,1,0:T(8,128)(2,1)S(1)}, f32[4,192,512]{2,1,0:T(8,128)S(1)}, f32[4,8,512]{2,1,0:T(8,128)S(1)}) custom-call(s32[1]{0:T(128)} %bitcast.1.me_ref, bf16[4,512,576]{2,1,0:T(8,128)(2,1)S(1)} %add_convert_fusion.qkv_ref, s32[4,1,512]{2,1,0:T(1,128)S(1)} %reshape.1520.seg_row_ref, s32[4,512,1]{2,1,0:T(8,128)S(1)} %copy.129.seg_col_ref), custom_call_target="tpu_custom_call" | custom-call | flops 20000000000 | bytes 8000000 | tf_op jit(solution)/shard_map/attend/pallas_call | solution.py:87
  174.2 5.2 %collective-permute-done.13 = bf16[512,192]{1,0:T(8,128)(2,1)S(1)} collective-permute-done((bf16[512,192]{1,0:T(8,128)(2,1)S(1)}, bf16[512,192]{1,0:T(8,128)(2,1)S(1)}, u32[]{:S(2)}, u32[]{:S(2)}) %collective-permute-start.13) | collective-permute-done | bytes 196640 | tf_op jit(solution)/shard_map/ppermute | solution.py:210
  179.4 3.7 collective-permute-done.14
  187.1 3.3 convert_reduce_fusion.3
  190.5 3.4 multiply_convert_fusion.2
  193.9 3.3 convert_reduce_fusion.4
  205.9 3.3 convert_reduce_fusion.6
  209.2 3.4 multiply_convert_fusion.1
  212.6 3.3 convert_reduce_fusion.5
  216.0 2.9 fusion.104
  236.9 2.1 fusion.102
  239.1 2.2 fusion.103
  241.3 3.5 add_bitcast_fusion
  245.0 2.8 pad_maximum_fusion.2
  249.6 26.5 %attend_back.1 = bf16[4,512,576]{2,1,0:T(8,128)(2,1)S(1)} custom-call(s32[1]{0:T(128)} %bitcast.1.me_ref, bf16[4,512,576]{2,1,0:T(8,128)(2,1)S(1)} %copy-done.1, bf16[4,512,192]{2,1,0:T(8,128)(2,1)S(1)} %pad_maximum_fusion.4.go_ref, f32[4,192,512]{2,1,0:T(8,128)S(1)} %get-tuple-element.21.full_ref, f32[4,8,512]{2,1,0:T(8,128)S(1)} %get-tuple-element.22.lse_ref, ...), custom_call_target="tpu_custom_call" | custom-call | flops 40000000000 | bytes 12000000 | tf_op jit(solution)/shard_map/attend_back/pallas_call | solution.py:169
  276.1 5.9 %fusion.96 = (bf16[768]{0:T(1024)(128)(2,1)S(1)}, bf16[768]{0:T(1024)(128)(2,1)S(1)}, bf16[4,512,768]{2,1,0:T(8,128)(2,1)}) fusion(f32[4,512]{1,0:T(4,128)S(1)} %copy-done.61, f32[4,512]{1,0:T(4,128)S(1)} %broadcast_multiply_fusion, bf16[1,512,768]{2,1,0:T(8,128)(2,1)} %bitcast.4, bf16[1,512,768]{2,1,0:T(8,128)(2,1)S(1)} %bitcast.355, ...), kind=kOutput, calls=%fused_computation.301 | convolution fusion | flops 1833957888 | bytes 9915392 | tf_op jit(solution)/shard_map/nbc,kc->nbk/dot_general | solution.py:405
  282.7 4.0 bitcast_convert_fusion
  292.9 11.1 %collective-permute-done.36 = bf16[2,2,96,704]{3,2,1,0:T(8,128)(2,1)S(1)} collective-permute-done((bf16[2,2,96,704]{3,2,1,0:T(8,128)(2,1)S(1)}, bf16[2,2,96,704]{3,2,1,0:T(8,128)(2,1)S(1)}, u32[]{:S(2)}, u32[]{:S(2)}) %collective-permute-start.36) | collective-permute-done | bytes 540704 | tf_op jit(solution)/shard_map/ppermute | solution.py:210
  307.5 5.2 %collective-permute-done.37 = bf16[2,96,704]{2,1,0:T(8,128)(2,1)S(1)} collective-permute-done((bf16[2,96,704]{2,1,0:T(8,128)(2,1)S(1)}, bf16[2,96,704]{2,1,0:T(8,128)(2,1)S(1)}, u32[]{:S(2)}, u32[]{:S(2)}) %collective-permute-start.37) | collective-permute-done | bytes 270368 | tf_op jit(solution)/shard_map/ppermute | solution.py:210
  312.8 2.3 collective-permute-start.38
  316.3 6.9 %collective-permute-done.38 = bf16[96,704]{1,0:T(8,128)(2,1)S(1)} collective-permute-done((bf16[96,704]{1,0:T(8,128)(2,1)S(1)}, bf16[96,704]{1,0:T(8,128)(2,1)S(1)}, u32[]{:S(2)}, u32[]{:S(2)}) %collective-permute-start.38) | collective-permute-done | bytes 135200 | tf_op jit(solution)/shard_map/ppermute | solution.py:210
  326.6 2.3 add_convert_fusion.6
  329.0 3.1 add_convert_fusion.2
  333.3 3.1 add_convert_fusion.5
  362.3 22.0 %collective-permute-done.35 = bf16[512,768]{1,0:T(8,128)(2,1)S(1)} collective-permute-done((bf16[512,768]{1,0:T(8,128)(2,1)}, bf16[512,768]{1,0:T(8,128)(2,1)S(1)}, u32[]{:S(2)}, u32[]{:S(2)}) %collective-permute-start.35) | collective-permute-done | bytes 786464 | tf_op jit(solution)/shard_map/ppermute | solution.py:210
  386.2 2.4 add_convert_fusion.1
  390.3 18.9 %collective-permute-done.53 = bf16[768,768]{1,0:T(8,128)(2,1)} collective-permute-done((bf16[768,768]{1,0:T(8,128)(2,1)}, bf16[768,768]{1,0:T(8,128)(2,1)}, u32[]{:S(2)}, u32[]{:S(2)}) %collective-permute-start.53) | collective-permute-done | bytes 1179680 | tf_op jit(solution)/shard_map/ppermute | solution.py:210
  412.6 3.0 fusion.19
  416.3 9.7 %collective-permute-done.54 = bf16[2,2,96,768]{3,2,0,1:T(8,128)(2,1)S(1)} collective-permute-done((bf16[2,2,96,768]{3,2,0,1:T(8,128)(2,1)S(1)}, bf16[2,2,96,768]{3,2,0,1:T(8,128)(2,1)S(1)}, u32[]{:S(2)}, u32[]{:S(2)}) %collective-permute-start.54) | collective-permute-done | bytes 589856 | tf_op jit(solution)/shard_map/ppermute | solution.py:210
  426.8 3.4 collective-permute-start.47
  430.2 7.7 %collective-permute-done.55 = bf16[2,96,768]{2,1,0:T(8,128)(2,1)S(1)} collective-permute-done((bf16[2,96,768]{2,1,0:T(8,128)(2,1)S(1)}, bf16[2,96,768]{2,1,0:T(8,128)(2,1)S(1)}, u32[]{:S(2)}, u32[]{:S(2)}) %collective-permute-start.55) | collective-permute-done | bytes 294944 | tf_op jit(solution)/shard_map/ppermute | solution.py:210
  440.4 5.5 %collective-permute-done.56 = bf16[96,768]{1,0:T(8,128)(2,1)S(1)} collective-permute-done((bf16[96,768]{1,0:T(8,128)(2,1)S(1)}, bf16[96,768]{1,0:T(8,128)(2,1)S(1)}, u32[]{:S(2)}, u32[]{:S(2)}) %collective-permute-start.56) | collective-permute-done | bytes 147488 | tf_op jit(solution)/shard_map/ppermute | solution.py:210
  (433 shorter events, 136.2 us)
Async XLA Ops:
  0.7 74.7 %collective-permute-start.1 = (bf16[512,768]{1,0:T(8,128)(2,1)}, bf16[512,768]{1,0:T(8,128)(2,1)S(1)}, u32[]{:S(2)}, u32[]{:S(2)}) collective-permute-start(bf16[512,768]{1,0:T(8,128)(2,1)} %bitcast.337), channel_id=1, source_target_pairs={{0,2},{1,3},{2,0},{3,1},{4,6},{5,7},{6,4},{7,5},{8,10},{9,11},{10,... | collective-permute-start | bytes 2359304 | tf_op jit(solution)/shard_map/ppermute | solution.py:210
  3.7 101.2 %collective-permute-start = (bf16[512,768]{1,0:T(8,128)(2,1)}, bf16[512,768]{1,0:T(8,128)(2,1)}, u32[]{:S(2)}, u32[]{:S(2)}) collective-permute-start(bf16[512,768]{1,0:T(8,128)(2,1)} %bitcast.338), channel_id=1, source_target_pairs={{0,1},{1,0},{2,3},{3,2},{4,5},{5,4},{6,7},{7,6},{8,9},{9,8},{10,11... | collective-permute-start | bytes 2359304 | tf_op jit(solution)/shard_map/ppermute | solution.py:210
  9.1 12.8 %collective-permute-start.3 = (bf16[24,704]{1,0:T(8,128)(2,1)S(1)}, bf16[24,704]{1,0:T(8,128)(2,1)S(1)}, u32[]{:S(2)}, u32[]{:S(2)}) collective-permute-start(bf16[24,704]{1,0:T(8,128)(2,1)S(1)} %bitcast.389), channel_id=1, source_target_pairs={{0,3},{1,2},{2,1},{3,0},{4,7},{5,6},{6,5},{7,4},{8,11},{9,10},{10,... | collective-permute-start | bytes 101384 | tf_op jit(solution)/shard_map/ppermute | solution.py:210
  9.1 14.7 %collective-permute-start.4 = (bf16[24,704]{1,0:T(8,128)(2,1)S(1)}, bf16[24,704]{1,0:T(8,128)(2,1)S(1)}, u32[]{:S(2)}, u32[]{:S(2)}) collective-permute-start(bf16[24,704]{1,0:T(8,128)(2,1)S(1)} %bitcast.388), channel_id=1, source_target_pairs={{0,2},{1,3},{2,0},{3,1},{4,6},{5,7},{6,4},{7,5},{8,10},{9,11},{10,... | collective-permute-start | bytes 101384 | tf_op jit(solution)/shard_map/ppermute | solution.py:210
  13.3 34.0 %collective-permute-start.10 = (s32[512]{0:T(512)S(1)}, s32[512]{0:T(512)S(1)}, u32[]{:S(2)}, u32[]{:S(2)}) collective-permute-start(s32[512]{0:T(512)S(1)} %bitcast.398), channel_id=1, source_target_pairs={{0,2},{1,3},{2,0},{3,1},{4,6},{5,7},{6,4},{7,5},{8,10},{9,11},{10,... | collective-permute-start | bytes 6152 | tf_op jit(solution)/shard_map/ppermute | solution.py:210
  27.8 14.6 %collective-permute-start.24 = (bf16[1,1,1,96,768]{4,3,2,1,0:T(8,128)(2,1)S(1)}, bf16[1,1,1,96,768]{4,3,2,1,0:T(8,128)(2,1)S(1)}, u32[]{:S(2)}, u32[]{:S(2)}) collective-permute-start(bf16[1,1,1,96,768]{4,3,2,1,0:T(8,128)(2,1)S(1)} %bitcast.379), channel_id=1, source_target_pairs={{0,16},{4,20},{8,24},{12,28},{16,0},{20,4},{24,8},{28,12},{1,17},{... | collective-permute-start | bytes 442376 | tf_op jit(solution)/shard_map/ppermute | solution.py:210
  30.4 12.0 %collective-permute-start.6 = (bf16[1,1,1,4,24,704]{5,4,3,0,2,1:T(8,128)(2,1)S(1)}, bf16[1,1,1,4,24,704]{5,4,3,0,2,1:T(8,128)(2,1)S(1)}, u32[]{:S(2)}, u32[]{:S(2)}) collective-permute-start(bf16[1,1,1,4,24,704]{5,4,3,0,2,1:T(8,128)(2,1)S(1)} %maximum_select_fusion.23), channel_id=1, source_target_pairs={{0,16},{4,20},{8,24},{12,28},{16,0},{20,4},{24,8},{28,12},{1,17},{... | collective-permute-start | bytes 405512 | tf_op jit(solution)/shard_map/ppermute | solution.py:210
  42.3 10.4 %collective-permute-start.18 = (bf16[1,1,1,120,768]{4,3,0,2,1:T(8,128)(2,1)S(1)}, bf16[1,1,1,120,768]{4,3,0,2,1:T(8,128)(2,1)S(1)}, u32[]{:S(2)}, u32[]{:S(2)}) collective-permute-start(bf16[1,1,1,120,768]{4,3,0,2,1:T(8,128)(2,1)S(1)} %get-tuple-element.97), channel_id=1, source_target_pairs={{0,16},{4,20},{8,24},{12,28},{16,0},{20,4},{24,8},{28,12},{1,17},{... | collective-permute-start | bytes 552968 | tf_op jit(solution)/shard_map/ppermute | solution.py:210
  42.4 13.0 %collective-permute-start.7 = (bf16[2,1,1,4,24,704]{5,4,3,0,2,1:T(8,128)(2,1)S(1)}, bf16[2,1,1,4,24,704]{5,4,3,0,2,1:T(8,128)(2,1)S(1)}, u32[]{:S(2)}, u32[]{:S(2)}) collective-permute-start(bf16[2,1,1,4,24,704]{5,4,3,0,2,1:T(8,128)(2,1)S(1)} %maximum_select_fusion.15), channel_id=1, source_target_pairs={{0,8},{4,12},{8,0},{12,4},{16,24},{20,28},{24,16},{28,20},{1,9},{5... | collective-permute-start | bytes 811016 | tf_op jit(solution)/shard_map/ppermute | solution.py:210
  47.3 9.0 %collective-permute-start.9 = (s32[512]{0:T(512)S(1)}, s32[512]{0:T(512)S(1)}, u32[]{:S(2)}, u32[]{:S(2)}) collective-permute-start(s32[512]{0:T(512)S(1)} %bitcast.399), channel_id=1, source_target_pairs={{0,1},{1,0},{2,3},{3,2},{4,5},{5,4},{6,7},{7,6},{8,9},{9,8},{10,11... | collective-permute-start | bytes 6152 | tf_op jit(solution)/shard_map/ppermute | solution.py:210
  55.4 10.3 %collective-permute-start.25 = (bf16[2,1,1,96,768]{4,3,2,1,0:T(8,128)(2,1)}, bf16[2,1,1,96,768]{4,3,2,1,0:T(8,128)(2,1)}, u32[]{:S(2)}, u32[]{:S(2)}) collective-permute-start(bf16[2,1,1,96,768]{4,3,2,1,0:T(8,128)(2,1)} %maximum_select_fusion.17), channel_id=1, source_target_pairs={{0,8},{4,12},{8,0},{12,4},{16,24},{20,28},{24,16},{28,20},{1,9},{5... | collective-permute-start | bytes 884744 | tf_op jit(solution)/shard_map/ppermute | solution.py:210
  56.3 15.4 %collective-permute-start.19 = (bf16[2,1,1,120,768]{4,3,0,2,1:T(8,128)(2,1)}, bf16[2,1,1,120,768]{4,3,0,2,1:T(8,128)(2,1)}, u32[]{:S(2)}, u32[]{:S(2)}) collective-permute-start(bf16[2,1,1,120,768]{4,3,0,2,1:T(8,128)(2,1)} %maximum_select_fusion.13), channel_id=1, source_target_pairs={{0,8},{4,12},{8,0},{12,4},{16,24},{20,28},{24,16},{28,20},{1,9},{5... | collective-permute-start | bytes 1105928 | tf_op jit(solution)/shard_map/ppermute | solution.py:210
  58.3 17.0 %collective-permute-start.8 = (bf16[2,2,1,4,24,704]{5,4,3,0,2,1:T(8,128)(2,1)}, bf16[2,2,1,4,24,704]{5,4,3,0,2,1:T(8,128)(2,1)}, u32[]{:S(2)}, u32[]{:S(2)}) collective-permute-start(bf16[2,2,1,4,24,704]{5,4,3,0,2,1:T(8,128)(2,1)} %maximum_select_fusion.6), channel_id=1, source_target_pairs={{0,4},{4,0},{8,12},{12,8},{16,20},{20,16},{24,28},{28,24},{1,5},{5... | collective-permute-start | bytes 1622024 | tf_op jit(solution)/shard_map/ppermute | solution.py:210
  67.6 20.0 %collective-permute-start.26 = (bf16[2,2,1,96,768]{4,3,2,1,0:T(8,128)(2,1)}, bf16[2,2,1,96,768]{4,3,2,1,0:T(8,128)(2,1)}, u32[]{:S(2)}, u32[]{:S(2)}) collective-permute-start(bf16[2,2,1,96,768]{4,3,2,1,0:T(8,128)(2,1)} %maximum_select_fusion.8), channel_id=1, source_target_pairs={{0,4},{4,0},{8,12},{12,8},{16,20},{20,16},{24,28},{28,24},{1,5},{5... | collective-permute-start | bytes 1769480 | tf_op jit(solution)/shard_map/ppermute | solution.py:210
  73.8 27.2 %collective-permute-start.20 = (bf16[2,2,1,120,768]{4,3,0,2,1:T(8,128)(2,1)}, bf16[2,2,1,120,768]{4,3,0,2,1:T(8,128)(2,1)}, u32[]{:S(2)}, u32[]{:S(2)}) collective-permute-start(bf16[2,2,1,120,768]{4,3,0,2,1:T(8,128)(2,1)} %maximum_select_fusion.5), channel_id=1, source_target_pairs={{0,4},{4,0},{8,12},{12,8},{16,20},{20,16},{24,28},{28,24},{1,5},{5... | collective-permute-start | bytes 2211848 | tf_op jit(solution)/shard_map/ppermute | solution.py:210
  75.3 29.7 %collective-permute-start.2 = (bf16[512,768]{1,0:T(8,128)(2,1)S(1)}, bf16[512,768]{1,0:T(8,128)(2,1)}, u32[]{:S(2)}, u32[]{:S(2)}) collective-permute-start(bf16[512,768]{1,0:T(8,128)(2,1)S(1)} %collective-permute-done.1), channel_id=1, source_target_pairs={{0,1},{1,0},{2,3},{3,2},{4,5},{5,4},{6,7},{7,6},{8,9},{9,8},{10,11... | collective-permute-start | bytes 2359304 | tf_op jit(solution)/shard_map/ppermute | solution.py:210
  90.4 103.5 %collective-permute-start.27 = (bf16[768,768]{1,0:T(8,128)(2,1)}, bf16[768,768]{1,0:T(8,128)(2,1)}, u32[]{:S(2)}, u32[]{:S(2)}) collective-permute-start(bf16[768,768]{1,0:T(8,128)(2,1)} %bitcast.68), channel_id=1, source_target_pairs={{0,1},{1,0},{2,3},{3,2},{4,5},{5,4},{6,7},{7,6},{8,9},{9,8},{10,11... | collective-permute-start | bytes 3538952 | tf_op jit(solution)/shard_map/ppermute | solution.py:210
  90.4 82.5 %collective-permute-start.28 = (bf16[768,768]{1,0:T(8,128)(2,1)}, bf16[768,768]{1,0:T(8,128)(2,1)}, u32[]{:S(2)}, u32[]{:S(2)}) collective-permute-start(bf16[768,768]{1,0:T(8,128)(2,1)} %bitcast.68), channel_id=1, source_target_pairs={{0,2},{1,3},{2,0},{3,1},{4,6},{5,7},{6,4},{7,5},{8,10},{9,11},{10,... | collective-permute-start | bytes 3538952 | tf_op jit(solution)/shard_map/ppermute | solution.py:210
  103.3 47.3 %collective-permute-start.21 = (bf16[8,120,768]{2,1,0:T(8,128)(2,1)S(1)}, bf16[8,120,768]{2,1,0:T(8,128)(2,1)S(1)}, u32[]{:S(2)}, u32[]{:S(2)}) collective-permute-start(bf16[8,120,768]{2,1,0:T(8,128)(2,1)S(1)} %bitcast.341), channel_id=1, source_target_pairs={{0,2},{1,3},{2,0},{3,1},{4,6},{5,7},{6,4},{7,5},{8,10},{9,11},{10,... | collective-permute-start | bytes 4423688 | tf_op jit(solution)/shard_map/ppermute | solution.py:210
  104.9 65.3 %collective-permute-start.23 = (bf16[8,120,768]{2,1,0:T(8,128)(2,1)S(1)}, bf16[8,120,768]{2,1,0:T(8,128)(2,1)S(1)}, u32[]{:S(2)}, u32[]{:S(2)}) collective-permute-start(bf16[8,120,768]{2,1,0:T(8,128)(2,1)S(1)} %bitcast.344), channel_id=1, source_target_pairs={{0,1},{1,0},{2,3},{3,2},{4,5},{5,4},{6,7},{7,6},{8,9},{9,8},{10,11... | collective-permute-start | bytes 4423688 | tf_op jit(solution)/shard_map/ppermute | solution.py:210
  150.6 22.4 %collective-permute-start.22 = (bf16[8,120,768]{2,1,0:T(8,128)(2,1)S(1)}, bf16[8,120,768]{2,1,0:T(8,128)(2,1)S(1)}, u32[]{:S(2)}, u32[]{:S(2)}) collective-permute-start(bf16[8,120,768]{2,1,0:T(8,128)(2,1)S(1)} %collective-permute-done.21), channel_id=1, source_target_pairs={{0,1},{1,0},{2,3},{3,2},{4,5},{5,4},{6,7},{7,6},{8,9},{9,8},{10,11... | collective-permute-start | bytes 4423688 | tf_op jit(solution)/shard_map/ppermute | solution.py:210
  170.2 9.2 %collective-permute-start.13 = (bf16[512,192]{1,0:T(8,128)(2,1)S(1)}, bf16[512,192]{1,0:T(8,128)(2,1)S(1)}, u32[]{:S(2)}, u32[]{:S(2)}) collective-permute-start(bf16[512,192]{1,0:T(8,128)(2,1)S(1)} %get-tuple-element.70), channel_id=1, source_target_pairs={{0,2},{1,3},{2,0},{3,1},{4,6},{5,7},{6,4},{7,5},{8,10},{9,11},{10,... | collective-permute-start | bytes 589832 | tf_op jit(solution)/shard_map/ppermute | solution.py:210
  172.9 10.2 %collective-permute-start.14 = (bf16[512,192]{1,0:T(8,128)(2,1)S(1)}, bf16[512,192]{1,0:T(8,128)(2,1)S(1)}, u32[]{:S(2)}, u32[]{:S(2)}) collective-permute-start(bf16[512,192]{1,0:T(8,128)(2,1)S(1)} %get-tuple-element.69), channel_id=1, source_target_pairs={{0,3},{1,2},{2,1},{3,0},{4,7},{5,6},{6,5},{7,4},{8,11},{9,10},{10,... | collective-permute-start | bytes 589832 | tf_op jit(solution)/shard_map/ppermute | solution.py:210
  173.0 32.8 %collective-permute-start.29 = (bf16[768,768]{1,0:T(8,128)(2,1)}, bf16[768,768]{1,0:T(8,128)(2,1)}, u32[]{:S(2)}, u32[]{:S(2)}) collective-permute-start(bf16[768,768]{1,0:T(8,128)(2,1)} %collective-permute-done.28), channel_id=1, source_target_pairs={{0,1},{1,0},{2,3},{3,2},{4,5},{5,4},{6,7},{7,6},{8,9},{9,8},{10,11... | collective-permute-start | bytes 3538952 | tf_op jit(solution)/shard_map/ppermute | solution.py:210
  226.8 20.9 %collective-permute-start.30 = (bf16[512,192]{1,0:T(8,128)(2,1)}, bf16[512,192]{1,0:T(8,128)(2,1)}, u32[]{:S(2)}, u32[]{:S(2)}) collective-permute-start(bf16[512,192]{1,0:T(8,128)(2,1)} %get-tuple-element.75), channel_id=1, source_target_pairs={{0,1},{1,0},{2,3},{3,2},{4,5},{5,4},{6,7},{7,6},{8,9},{9,8},{10,11... | collective-permute-start | bytes 589832 | tf_op jit(solution)/shard_map/ppermute | solution.py:210
  227.6 20.6 %collective-permute-start.31 = (bf16[512,192]{1,0:T(8,128)(2,1)}, bf16[512,192]{1,0:T(8,128)(2,1)}, u32[]{:S(2)}, u32[]{:S(2)}) collective-permute-start(bf16[512,192]{1,0:T(8,128)(2,1)} %get-tuple-element.74), channel_id=1, source_target_pairs={{0,2},{1,3},{2,0},{3,1},{4,6},{5,7},{6,4},{7,5},{8,10},{9,11},{10,... | collective-permute-start | bytes 589832 | tf_op jit(solution)/shard_map/ppermute | solution.py:210
  229.1 19.2 %collective-permute-start.32 = (bf16[512,192]{1,0:T(8,128)(2,1)}, bf16[512,192]{1,0:T(8,128)(2,1)}, u32[]{:S(2)}, u32[]{:S(2)}) collective-permute-start(bf16[512,192]{1,0:T(8,128)(2,1)} %get-tuple-element.73), channel_id=1, source_target_pairs={{0,3},{1,2},{2,1},{3,0},{4,7},{5,6},{6,5},{7,4},{8,11},{9,10},{10,... | collective-permute-start | bytes 589832 | tf_op jit(solution)/shard_map/ppermute | solution.py:210
  230.9 94.4 %collective-permute-start.51 = (bf16[768,768]{1,0:T(8,128)(2,1)}, bf16[768,768]{1,0:T(8,128)(2,1)}, u32[]{:S(2)}, u32[]{:S(2)}) collective-permute-start(bf16[768,768]{1,0:T(8,128)(2,1)} %convolution_convert_fusion.2), channel_id=1, source_target_pairs={{0,1},{1,0},{2,3},{3,2},{4,5},{5,4},{6,7},{7,6},{8,9},{9,8},{10,11... | collective-permute-start | bytes 3538952 | tf_op jit(solution)/shard_map/ppermute | solution.py:210
  231.6 100.5 %collective-permute-start.52 = (bf16[768,768]{1,0:T(8,128)(2,1)}, bf16[768,768]{1,0:T(8,128)(2,1)}, u32[]{:S(2)}, u32[]{:S(2)}) collective-permute-start(bf16[768,768]{1,0:T(8,128)(2,1)} %convolution_convert_fusion), channel_id=1, source_target_pairs={{0,1},{1,0},{2,3},{3,2},{4,5},{5,4},{6,7},{7,6},{8,9},{9,8},{10,11... | collective-permute-start | bytes 3538952 | tf_op jit(solution)/shard_map/ppermute | solution.py:210
  247.7 81.2 %collective-permute-start.43 = (bf16[8,120,768]{2,1,0:T(8,128)(2,1)}, bf16[8,120,768]{2,1,0:T(8,128)(2,1)}, u32[]{:S(2)}, u32[]{:S(2)}) collective-permute-start(bf16[8,120,768]{2,1,0:T(8,128)(2,1)} %pad_maximum_fusion.2), channel_id=1, source_target_pairs={{0,1},{1,0},{2,3},{3,2},{4,5},{5,4},{6,7},{7,6},{8,9},{9,8},{10,11... | collective-permute-start | bytes 4423688 | tf_op jit(solution)/shard_map/ppermute | solution.py:210
  288.5 15.5 %collective-permute-start.36 = (bf16[2,2,96,704]{3,2,1,0:T(8,128)(2,1)S(1)}, bf16[2,2,96,704]{3,2,1,0:T(8,128)(2,1)S(1)}, u32[]{:S(2)}, u32[]{:S(2)}) collective-permute-start(bf16[2,2,96,704]{3,2,1,0:T(8,128)(2,1)S(1)} %fusion.65), channel_id=1, source_target_pairs={{0,4},{4,0},{8,12},{12,8},{16,20},{20,16},{24,28},{28,24},{1,5},{5... | collective-permute-start | bytes 1622024 | tf_op jit(solution)/shard_map/ppermute | solution.py:210
  292.9 19.9 %collective-permute-start.34 = (bf16[512,768]{1,0:T(8,128)(2,1)S(1)}, bf16[512,768]{1,0:T(8,128)(2,1)S(1)}, u32[]{:S(2)}, u32[]{:S(2)}) collective-permute-start(bf16[512,768]{1,0:T(8,128)(2,1)S(1)} %get-tuple-element.53), channel_id=1, source_target_pairs={{0,1},{1,0},{2,3},{3,2},{4,5},{5,4},{6,7},{7,6},{8,9},{9,8},{10,11... | collective-permute-start | bytes 2359304 | tf_op jit(solution)/shard_map/ppermute | solution.py:210
  304.3 8.4 %collective-permute-start.37 = (bf16[2,96,704]{2,1,0:T(8,128)(2,1)S(1)}, bf16[2,96,704]{2,1,0:T(8,128)(2,1)S(1)}, u32[]{:S(2)}, u32[]{:S(2)}) collective-permute-start(bf16[2,96,704]{2,1,0:T(8,128)(2,1)S(1)} %dynamic-slice_bitcast_fusion.7), channel_id=1, source_target_pairs={{0,8},{4,12},{8,0},{12,4},{16,24},{20,28},{24,16},{28,20},{1,9},{5... | collective-permute-start | bytes 811016 | tf_op jit(solution)/shard_map/ppermute | solution.py:210
  312.7 73.5 %collective-permute-start.42 = (bf16[8,120,768]{2,1,0:T(8,128)(2,1)}, bf16[8,120,768]{2,1,0:T(8,128)(2,1)}, u32[]{:S(2)}, u32[]{:S(2)}) collective-permute-start(bf16[8,120,768]{2,1,0:T(8,128)(2,1)} %pad_maximum_fusion.1), channel_id=1, source_target_pairs={{0,1},{1,0},{2,3},{3,2},{4,5},{5,4},{6,7},{7,6},{8,9},{9,8},{10,11... | collective-permute-start | bytes 4423688 | tf_op jit(solution)/shard_map/ppermute | solution.py:210
  312.8 10.4 %collective-permute-start.38 = (bf16[96,704]{1,0:T(8,128)(2,1)S(1)}, bf16[96,704]{1,0:T(8,128)(2,1)S(1)}, u32[]{:S(2)}, u32[]{:S(2)}) collective-permute-start(bf16[96,704]{1,0:T(8,128)(2,1)S(1)} %dynamic-slice_bitcast_fusion.14), channel_id=1, source_target_pairs={{0,16},{4,20},{8,24},{12,28},{16,0},{20,4},{24,8},{28,12},{1,17},{... | collective-permute-start | bytes 405512 | tf_op jit(solution)/shard_map/ppermute | solution.py:210
  323.9 12.5 %collective-permute-start.39 = (f32[24,704]{1,0:T(8,128)S(1)}, f32[24,704]{1,0:T(8,128)S(1)}, u32[]{:S(2)}, u32[]{:S(2)}) collective-permute-start(f32[24,704]{1,0:T(8,128)S(1)} %get-tuple-element.93), channel_id=1, source_target_pairs={{0,3},{1,2},{2,1},{3,0},{4,7},{5,6},{6,5},{7,4},{8,11},{9,10},{10,... | collective-permute-start | bytes 202760 | tf_op jit(solution)/shard_map/ppermute | solution.py:210
  325.3 11.9 %collective-permute-start.40 = (f32[24,704]{1,0:T(8,128)S(1)}, f32[24,704]{1,0:T(8,128)}, u32[]{:S(2)}, u32[]{:S(2)}) collective-permute-start(f32[24,704]{1,0:T(8,128)S(1)} %get-tuple-element.96), channel_id=1, source_target_pairs={{0,2},{1,3},{2,0},{3,1},{4,6},{5,7},{6,4},{7,5},{8,10},{9,11},{10,... | collective-permute-start | bytes 202760 | tf_op jit(solution)/shard_map/ppermute | solution.py:210
  328.9 12.3 %collective-permute-start.41 = (f32[24,704]{1,0:T(8,128)}, f32[24,704]{1,0:T(8,128)}, u32[]{:S(2)}, u32[]{:S(2)}) collective-permute-start(f32[24,704]{1,0:T(8,128)} %get-tuple-element.95), channel_id=1, source_target_pairs={{0,1},{1,0},{2,3},{3,2},{4,5},{5,4},{6,7},{7,6},{8,9},{9,8},{10,11... | collective-permute-start | bytes 202760 | tf_op jit(solution)/shard_map/ppermute | solution.py:210
  332.1 54.1 %collective-permute-start.44 = (bf16[8,120,768]{2,1,0:T(8,128)(2,1)}, bf16[8,120,768]{2,1,0:T(8,128)(2,1)}, u32[]{:S(2)}, u32[]{:S(2)}) collective-permute-start(bf16[8,120,768]{2,1,0:T(8,128)(2,1)} %add_convert_fusion.2), channel_id=1, source_target_pairs={{0,2},{1,3},{2,0},{3,1},{4,6},{5,7},{6,4},{7,5},{8,10},{9,11},{10,... | collective-permute-start | bytes 4423688 | tf_op jit(solution)/shard_map/ppermute | solution.py:210
  336.5 25.8 %collective-permute-start.33 = (bf16[512,768]{1,0:T(8,128)(2,1)}, bf16[512,768]{1,0:T(8,128)(2,1)S(1)}, u32[]{:S(2)}, u32[]{:S(2)}) collective-permute-start(bf16[512,768]{1,0:T(8,128)(2,1)} %get-tuple-element.52), channel_id=1, source_target_pairs={{0,1},{1,0},{2,3},{3,2},{4,5},{5,4},{6,7},{7,6},{8,9},{9,8},{10,11... | collective-permute-start | bytes 2359304 | tf_op jit(solution)/shard_map/ppermute | solution.py:210
  337.2 47.0 %collective-permute-start.35 = (bf16[512,768]{1,0:T(8,128)(2,1)}, bf16[512,768]{1,0:T(8,128)(2,1)S(1)}, u32[]{:S(2)}, u32[]{:S(2)}) collective-permute-start(bf16[512,768]{1,0:T(8,128)(2,1)} %fusion.46), channel_id=1, source_target_pairs={{0,2},{1,3},{2,0},{3,1},{4,6},{5,7},{6,4},{7,5},{8,10},{9,11},{10,... | collective-permute-start | bytes 2359304 | tf_op jit(solution)/shard_map/ppermute | solution.py:210
  341.2 68.0 %collective-permute-start.53 = (bf16[768,768]{1,0:T(8,128)(2,1)}, bf16[768,768]{1,0:T(8,128)(2,1)}, u32[]{:S(2)}, u32[]{:S(2)}) collective-permute-start(bf16[768,768]{1,0:T(8,128)(2,1)} %add_convert_fusion.5), channel_id=1, source_target_pairs={{0,2},{1,3},{2,0},{3,1},{4,6},{5,7},{6,4},{7,5},{8,10},{9,11},{10,... | collective-permute-start | bytes 3538952 | tf_op jit(solution)/shard_map/ppermute | solution.py:210
  388.7 27.0 %collective-permute-start.45 = (bf16[2,2,120,768]{3,2,1,0:T(8,128)(2,1)S(1)}, bf16[2,2,120,768]{3,2,1,0:T(8,128)(2,1)S(1)}, u32[]{:S(2)}, u32[]{:S(2)}) collective-permute-start(bf16[2,2,120,768]{3,2,1,0:T(8,128)(2,1)S(1)} %dynamic-slice_bitcast_fusion), channel_id=1, source_target_pairs={{0,4},{4,0},{8,12},{12,8},{16,20},{20,16},{24,28},{28,24},{1,5},{5... | collective-permute-start | bytes 2211848 | tf_op jit(solution)/shard_map/ppermute | solution.py:210
  411.0 15.0 %collective-permute-start.54 = (bf16[2,2,96,768]{3,2,0,1:T(8,128)(2,1)S(1)}, bf16[2,2,96,768]{3,2,0,1:T(8,128)(2,1)S(1)}, u32[]{:S(2)}, u32[]{:S(2)}) collective-permute-start(bf16[2,2,96,768]{3,2,0,1:T(8,128)(2,1)S(1)} %bitcast.377), channel_id=1, source_target_pairs={{0,4},{4,0},{8,12},{12,8},{16,20},{20,16},{24,28},{28,24},{1,5},{5... | collective-permute-start | bytes 1769480 | tf_op jit(solution)/shard_map/ppermute | solution.py:210
  415.9 10.8 %collective-permute-start.46 = (bf16[2,120,768]{2,1,0:T(8,128)(2,1)S(1)}, bf16[2,120,768]{2,1,0:T(8,128)(2,1)S(1)}, u32[]{:S(2)}, u32[]{:S(2)}) collective-permute-start(bf16[2,120,768]{2,1,0:T(8,128)(2,1)S(1)} %dynamic-slice_bitcast_fusion.1), channel_id=1, source_target_pairs={{0,8},{4,12},{8,0},{12,4},{16,24},{20,28},{24,16},{28,20},{1,9},{5... | collective-permute-start | bytes 1105928 | tf_op jit(solution)/shard_map/ppermute | solution.py:210
  426.2 11.7 %collective-permute-start.55 = (bf16[2,96,768]{2,1,0:T(8,128)(2,1)S(1)}, bf16[2,96,768]{2,1,0:T(8,128)(2,1)S(1)}, u32[]{:S(2)}, u32[]{:S(2)}) collective-permute-start(bf16[2,96,768]{2,1,0:T(8,128)(2,1)S(1)} %dynamic-slice_bitcast_fusion.2), channel_id=1, source_target_pairs={{0,8},{4,12},{8,0},{12,4},{16,24},{20,28},{24,16},{28,20},{1,9},{5... | collective-permute-start | bytes 884744 | tf_op jit(solution)/shard_map/ppermute | solution.py:210
  426.8 12.6 %collective-permute-start.47 = (bf16[120,768]{1,0:T(8,128)(2,1)S(1)}, bf16[120,768]{1,0:T(8,128)(2,1)S(1)}, u32[]{:S(2)}, u32[]{:S(2)}) collective-permute-start(bf16[120,768]{1,0:T(8,128)(2,1)S(1)} %dynamic-slice_bitcast_fusion.12), channel_id=1, source_target_pairs={{0,16},{4,20},{8,24},{12,28},{16,0},{20,4},{24,8},{28,12},{1,17},{... | collective-permute-start | bytes 552968 | tf_op jit(solution)/shard_map/ppermute | solution.py:210
  439.6 8.2 %collective-permute-start.49 = (f32[24,768]{1,0:T(8,128)S(1)}, f32[24,768]{1,0:T(8,128)S(1)}, u32[]{:S(2)}, u32[]{:S(2)}) collective-permute-start(f32[24,768]{1,0:T(8,128)S(1)} %get-tuple-element.92), channel_id=1, source_target_pairs={{0,2},{1,3},{2,0},{3,1},{4,6},{5,7},{6,4},{7,5},{8,10},{9,11},{10,... | collective-permute-start | bytes 221192 | tf_op jit(solution)/shard_map/ppermute | solution.py:210
  (88 other events, 660.1 us)

commit v2 on v1

v2 whole, which is shorter than its diff:
```python
import functools
import math

import jax
import jax.numpy as jnp
from jax import lax
from jax.experimental import pallas as pl
from jax.experimental.pallas import tpu as pltpu
from jax.sharding import PartitionSpec as P

H = 12
EPSILON = 1e-05
MASKED = -1e30
F32 = jnp.float32
BF16 = jnp.bfloat16
LANES = 128


def dot_nt(a, b):
    return lax.dot_general(a, b, (((1,), (1,)), ((), ())), preferred_element_type=F32)


def dot_tn(a, b):
    return lax.dot_general(a, b, (((0,), (0,)), ((), ())), preferred_element_type=F32)


def dot_nn(a, b):
    return jnp.dot(a, b, preferred_element_type=F32)


def attend_kernel(me_ref, qkv_ref, seg_row_ref, seg_col_ref, low_ref, full_ref, lse_ref, *, heads, hd):
    me = me_ref[0]
    qi = pl.program_id(0)
    rq = qi ^ me
    block = qkv_ref.shape[1]
    width = heads * hd
    scale = jnp.asarray(1.0 / math.sqrt(hd), BF16)
    queries = [qkv_ref[rq, :, h * hd : (h + 1) * hd] * scale for h in range(heads)]
    seg_q = seg_row_ref[rq]

    def step(rk, state, causal):
        allowed = seg_col_ref[rk] == seg_q
        if causal:
            k_pos = lax.broadcasted_iota(jnp.int32, (block, block), 0)
            q_pos = lax.broadcasted_iota(jnp.int32, (block, block), 1)
            allowed = allowed & (k_pos <= q_pos)
        new = []
        for h in range(heads):
            top, total, mixed = state[h]
            key = qkv_ref[rk, :, width + h * hd : width + (h + 1) * hd]
            value = qkv_ref[rk, :, 2 * width + h * hd : 2 * width + (h + 1) * hd]
            scores = jnp.where(allowed, dot_nt(key, queries[h]), MASKED)
            higher = jnp.maximum(top, jnp.max(scores, 0, keepdims=True))
            weights = jnp.exp(scores - higher)
            fade = jnp.exp(top - higher)
            total = total * fade + jnp.sum(weights, 0, keepdims=True)
            mixed = mixed * fade + dot_tn(value, weights.astype(BF16))
            new.append((higher, total, mixed))
        return tuple(new)

    start = tuple(
        (jnp.full((1, block), MASKED, F32), jnp.zeros((1, block), F32), jnp.zeros((hd, block), F32))
        for _ in range(heads)
    )
    state = lax.fori_loop(0, qi, lambda kj, c: step(kj ^ me, c, False), start)
    state = step(rq, state, True)
    rows = []
    for h in range(heads):
        top, total, mixed = state[h]
        rows.append(mixed / total)
        lse_ref[0, h : h + 1, :] = top + jnp.log(total)
    full = jnp.concatenate(rows, 0)
    full_ref[0] = full
    low_ref[0] = full.astype(BF16)


def attend(me, qkv, seg_row, seg_col, heads, hd):
    n, block, _ = qkv.shape
    width = heads * hd

    def whole(shape):
        return pl.BlockSpec(shape, lambda i, me: (0,) * len(shape))

    def own(shape):
        return pl.BlockSpec(shape, lambda i, me: (i ^ me[0], 0, 0))

    return pl.pallas_call(
        functools.partial(attend_kernel, heads=heads, hd=hd),
        grid_spec=pltpu.PrefetchScalarGridSpec(
            num_scalar_prefetch=1,
            grid=(n,),
            in_specs=[whole(qkv.shape), whole(seg_row.shape), whole(seg_col.shape)],
            out_specs=[own((1, width, block)), own((1, width, block)), own((1, 8, block))],
        ),
        out_shape=[
            jax.ShapeDtypeStruct((n, width, block), BF16),
            jax.ShapeDtypeStruct((n, width, block), F32),
            jax.ShapeDtypeStruct((n, 8, block), F32),
        ],
        compiler_params=pltpu.CompilerParams(vmem_limit_bytes=40 * 1024 * 1024),
        cost_estimate=pl.CostEstimate(
            flops=20 * 1000**3, bytes_accessed=8 * 1000**2, transcendentals=8 * 1000**2
        ),
        name="attend",
    )(me, qkv, seg_row, seg_col)


def attend_back_kernel(
    me_ref, qkv_ref, go_ref, full_ref, lse_ref, seg_row_ref, seg_col_ref, grad_ref, gq_ref, dot_ref, *, heads, hd
):
    me = me_ref[0]
    kj = pl.program_id(0)
    rk = kj ^ me
    n, block, _ = qkv_ref.shape
    width = heads * hd
    scale = 1.0 / math.sqrt(hd)
    low_scale = jnp.asarray(scale, BF16)

    @pl.when(kj == 0)
    def _():
        gq_ref[...] = jnp.zeros_like(gq_ref)
        for b in range(n):
            prod = go_ref[b].astype(F32) * full_ref[b]
            for h in range(heads):
                dot_ref[b, h : h + 1, :] = jnp.sum(prod[h * hd : (h + 1) * hd], 0, keepdims=True)

    keys = [qkv_ref[rk, :, width + h * hd : width + (h + 1) * hd] for h in range(heads)]
    values = [qkv_ref[rk, :, 2 * width + h * hd : 2 * width + (h + 1) * hd] for h in range(heads)]
    seg_k = seg_col_ref[rk]

    def step(rq, state, causal):
        allowed = seg_k == seg_row_ref[rq]
        if causal:
            k_pos = lax.broadcasted_iota(jnp.int32, (block, block), 0)
            q_pos = lax.broadcasted_iota(jnp.int32, (block, block), 1)
            allowed = allowed & (k_pos <= q_pos)
        new = []
        for h in range(heads):
            gk, gv = state[h]
            query = qkv_ref[rq, :, h * hd : (h + 1) * hd] * low_scale
            go = go_ref[rq, h * hd : (h + 1) * hd, :]
            scores = jnp.where(allowed, dot_nt(keys[h], query), MASKED)
            weights = jnp.exp(scores - lse_ref[rq, h : h + 1, :])
            gw = dot_nn(values[h], go)
            ds = (weights * (gw - dot_ref[rq, h : h + 1, :])).astype(BF16)
            gv = gv + dot_nt(weights.astype(BF16), go)
            gk = gk + dot_nn(ds, query)
            gq_ref[rq, h * hd : (h + 1) * hd, :] += dot_tn(keys[h], ds)
            new.append((gk, gv))
        return tuple(new)

    zero = jnp.zeros((block, hd), F32)
    state = step(rk, tuple((zero, zero) for _ in range(heads)), True)
    state = lax.fori_loop(kj + 1, n, lambda qi, c: step(qi ^ me, c, False), state)
    grad_ref[0, :, :width] = (gq_ref[rk] * scale).T.astype(BF16)
    for h in range(heads):
        gk, gv = state[h]
        grad_ref[0, :, width + h * hd : width + (h + 1) * hd] = gk.astype(BF16)
        grad_ref[0, :, 2 * width + h * hd : 2 * width + (h + 1) * hd] = gv.astype(BF16)


def attend_back(me, qkv, go, full, lse, seg_row, seg_col, heads, hd):
    n, block, wide = qkv.shape
    width = heads * hd

    def whole(shape):
        return pl.BlockSpec(shape, lambda i, me: (0,) * len(shape))

    return pl.pallas_call(
        functools.partial(attend_back_kernel, heads=heads, hd=hd),
        grid_spec=pltpu.PrefetchScalarGridSpec(
            num_scalar_prefetch=1,
            grid=(n,),
            in_specs=[whole(a.shape) for a in (qkv, go, full, lse, seg_row, seg_col)],
            out_specs=pl.BlockSpec((1, block, wide), lambda i, me: (i ^ me[0], 0, 0)),
            scratch_shapes=[pltpu.VMEM((n, width, block), F32), pltpu.VMEM((n, 8, block), F32)],
        ),
        out_shape=jax.ShapeDtypeStruct((n, block, wide), BF16),
        compiler_params=pltpu.CompilerParams(vmem_limit_bytes=40 * 1024 * 1024),
        cost_estimate=pl.CostEstimate(
            flops=40 * 1000**3, bytes_accessed=12 * 1000**2, transcendentals=8 * 1000**2
        ),
        name="attend_back",
    )(me, qkv, go, full, lse, seg_row, seg_col)


def normed_parts(value):
    mean = jnp.mean(value, -1, keepdims=True)
    centred = value - mean
    inv_std = lax.rsqrt(jnp.mean(centred * centred, -1, keepdims=True) + EPSILON)
    return centred * inv_std, inv_std


def normalize_back(grad_in, normed, inv_std, gain):
    scaled = grad_in * gain
    return inv_std * (
        scaled
        - jnp.mean(scaled, -1, keepdims=True)
        - normed * jnp.mean(scaled * normed, -1, keepdims=True)
    )


def gelu_and_slope(value):
    cumul = 0.5 * (1.0 + lax.erf(value * (1.0 / math.sqrt(2.0))))
    slope = cumul + value * jnp.exp(-0.5 * value * value) * (1.0 / math.sqrt(2.0 * math.pi))
    return value * cumul, slope


def tie(value, *others):
    return lax.optimization_barrier((value,) + others)[0] if others else value


def swap(value, axis, size, mask):
    return lax.ppermute(value, axis, [(i, i ^ mask) for i in range(size)])


def bits_of(size):
    count = size.bit_length() - 1
    return [1 << b for b in range(count)]


def ordered(parts, index):
    parts = [part[None] for part in parts]
    bit = 1
    while len(parts) > 1:
        on = (index & bit) != 0
        parts = [
            jnp.where(on, jnp.concatenate([b, a], 0), jnp.concatenate([a, b], 0))
            for a, b in zip(parts[::2], parts[1::2])
        ]
        bit *= 2
    return parts[0]


def gathered_ids(masks):
    held, lists = [0], [[0]]
    for mask in masks:
        new = [r ^ mask for r in held]
        lists.append(new)
        held = held + new
    return lists


def settle(parts, index, size, masks, count):
    ids = gathered_ids(masks)
    rows = parts[0].shape[1] // count
    if rows % 16 == 0:
        return parts, ids
    held = sum(ids, [])
    at = jnp.asarray([held.index(r) for r in range(size)])
    whole = jnp.concatenate(parts, 0)[at[jnp.arange(size) ^ index]]
    whole = whole.reshape(size, count, rows, -1).transpose(1, 0, 2, 3)
    return [whole.reshape(1, size * count * rows, -1)], [[None]]


def place(refs, ids, index, count, put):
    for ref, held in zip(refs, ids):
        rows = ref.shape[1] // count
        for j, r in enumerate(held):
            where = slice(None) if r is None else pl.ds(pl.multiple_of((index ^ r) * rows, rows), rows)
            for k in range(count):
                put(k, where, ref[j, k * rows : (k + 1) * rows, :])


def halves(value, index, size, mask):
    value = value.reshape((-1, 2, mask) + value.shape[1:])
    on = ((index & mask) != 0).astype(jnp.int32)
    shape = (-1,) + value.shape[3:]
    keep = lax.dynamic_index_in_dim(value, on, 1, False).reshape(shape)
    return keep, lax.dynamic_index_in_dim(value, 1 - on, 1, False).reshape(shape)


def add_low(a, b, kind=BF16):
    return (a.astype(F32) + b.astype(F32)).astype(kind)


def collect_dp(value, index, size, last=F32, shift=0):
    masks = bits_of(size)
    shape = value.shape[1:]
    value = value.reshape((2,) * len(masks) + shape)
    for step, mask in enumerate(masks):
        axis = len(masks) - 1 - step
        on = ((index & mask) != 0).astype(jnp.int32)
        keep = lax.dynamic_index_in_dim(value, on, axis, False)
        send = lax.dynamic_index_in_dim(value, 1 - on, axis, False)
        got = swap(send, "dp", size << shift, mask << shift)
        value = keep.astype(F32) + got.astype(F32)
        value = value.astype(BF16 if step < len(masks) - 1 else last)
    return value


def collect_pairs(even, odd, size, tied=()):
    got = swap(odd, "seq", size, 1)
    sums = [(even[i].astype(F32) + got[i].astype(F32)).astype(BF16) for i in range(size // 2)]
    mask = 2
    while len(sums) > 2:
        sent = [swap(b, "seq", size, mask) for b in sums[1::2]]
        sums = [(a.astype(F32) + b.astype(F32)).astype(BF16) for a, b in zip(sums[::2], sent)]
        mask *= 2
    return sums[0], sums[1], swap(tie(sums[1], *tied), "seq", size, mask)


def spread_seq(value, size, gate=()):
    got = {0: value}
    for mask in bits_of(size)[::-1]:
        for p in list(got):
            got[p | mask] = swap(tie(got[p], *gate) if p else got[p], "seq", size, mask)
    return [got[p] for p in range(size)]


def trade_seq(pieces, index, size):
    return [
        swap(lax.dynamic_index_in_dim(pieces, index ^ p, 0, False), "seq", size, p)
        if p
        else lax.dynamic_index_in_dim(pieces, index, 0, False)
        for p in range(size)
    ]


def enter_kernel(me_ref, *refs, ids, n, width):
    count = len(ids)
    pieces, (x_ref, qkv_ref, w_ref, vec_ref, tile_ref, add_ref) = refs[:count], refs[count:]
    me = me_ref[0]

    @pl.when(pl.program_id(0) == 0)
    def _():
        def put(k, where, rows):
            w_ref[where, :] = rows[:, : 3 * width]
            tile_ref[where, :] = rows[:, 3 * width :].astype(F32)

        place(pieces, ids, me_ref[1], 1, put)
        vecs = tile_ref[...].T[:16]
        vec_ref[...] = vecs
        for i, row in ((0, 6), (2, 7)):
            add = vecs[row : row + 1, :width]
            for t in range(1, n):
                add = jnp.where(me == t, vecs[row : row + 1, t * width : (t + 1) * width], add)
            add_ref[0:1, i * width : (i + 1) * width] = add
        add_ref[0:1, width : 2 * width] = jnp.zeros((1, width), F32)

    normed, _ = normed_parts(x_ref[0].astype(F32))
    h = (normed * vec_ref[0:1, :] + vec_ref[1:2, :]).astype(BF16)
    qkv_ref[0] = (dot_nn(h, w_ref[...]) + add_ref[0:1, :]).astype(BF16)


def enter(me, pieces, ids, x_all, width):
    n, block, dm = x_all.shape

    def whole(shape):
        return pl.BlockSpec(shape, lambda i, me: (0,) * len(shape))

    def one(width):
        return pl.BlockSpec((1, block, width), lambda i, me: (i, 0, 0))

    return pl.pallas_call(
        functools.partial(enter_kernel, ids=ids, n=n, width=width),
        grid_spec=pltpu.PrefetchScalarGridSpec(
            num_scalar_prefetch=1,
            grid=(n,),
            in_specs=[whole(a.shape) for a in pieces] + [one(dm)],
            out_specs=[one(3 * width), whole((dm, 3 * width)), whole((16, dm))],
            scratch_shapes=[pltpu.VMEM((dm, LANES), F32), pltpu.VMEM((8, 3 * width), F32)],
        ),
        out_shape=[
            jax.ShapeDtypeStruct((n, block, 3 * width), BF16),
            jax.ShapeDtypeStruct((dm, 3 * width), BF16),
            jax.ShapeDtypeStruct((16, dm), F32),
        ],
        compiler_params=pltpu.CompilerParams(vmem_limit_bytes=40 * 1024 * 1024),
        cost_estimate=pl.CostEstimate(flops=5 * 1000**3, bytes_accessed=8 * 1000**2, transcendentals=0),
        name="enter",
    )(me, *pieces, x_all)


def feed_kernel(
    me_ref, *refs, n, tile, ids
):
    count = len(ids[0])
    got, left, right, refs = refs[:n], refs[n : n + count], refs[n + count : n + 2 * count], refs[n + 2 * count :]
    x_ref, g_ref, vec_ref = refs[:3]
    h_ref, act_ref, gu_ref, even_ref, odd_ref, x_two_ref, sum_ref, out_w_ref, down_ref, up_ref = refs[3:]
    me = me_ref[0]
    i = pl.program_id(0)
    part = up_ref.shape[1]
    width = got[0].shape[1]

    @pl.when(i == 0)
    def _():
        sum_ref[...] = jnp.zeros_like(sum_ref)
        for first, pieces, held in ((0, left, ids[0]), (part // 2, right, ids[1])):

            def put(k, where, rows, first=first):
                (out_w_ref, up_ref, down_ref)[k][where, first : first + part // 2] = rows

            place(pieces, held, me_ref[1], 3, put)

    x_two = x_ref[0].astype(F32) + vec_ref[4:5, :]
    for p in range(n):
        own = pl.ds(pl.multiple_of((me ^ p) * width, width), width)
        x_two = x_two + dot_tn(got[p][0], out_w_ref[own, :])

    @pl.when(i == 0)
    def _():
        x_two_ref[...] = x_two

    normed, _ = normed_parts(x_two)
    h = (normed * vec_ref[2:3, :] + vec_ref[3:4, :]).astype(BF16)
    h_ref[0] = h
    g = g_ref[0]
    total = None
    for t in range(0, part, tile):
        cols = slice(t, t + tile)
        u = dot_nn(h, up_ref[:, cols]) + vec_ref[8:9, cols]
        act, slope = gelu_and_slope(u)
        act_ref[0, :, cols] = act.astype(BF16)
        gu = (dot_nt(g, down_ref[cols, :]) * slope).astype(BF16)
        gu_ref[0, :, cols] = gu
        sum_ref[0:1, cols] += jnp.sum(gu.astype(F32), 0, keepdims=True)
        term = dot_nt(gu, up_ref[:, cols])
        total = term if total is None else total + term
    total = total.astype(BF16)

    @pl.when(i % 2 == 0)
    def _():
        even_ref[0] = total

    @pl.when(i % 2 == 1)
    def _():
        odd_ref[0] = total


def feed(me, got, left, right, ids, x_all, g_all, vecs):
    n, _, dm = x_all.shape
    block = g_all.shape[1]
    part = 2 * left[0].shape[2]
    width = got[0].shape[1]

    def whole(shape):
        return pl.BlockSpec(shape, lambda i, me: (0,) * len(shape))

    def one(width):
        return pl.BlockSpec((1, block, width), lambda i, me: (i, 0, 0))

    def half(width):
        return pl.BlockSpec((1, block, width), lambda i, me: (i // 2, 0, 0))

    def piece(p):
        return pl.BlockSpec((1, width, block), lambda i, me: (i ^ p, 0, 0))

    wide = jax.ShapeDtypeStruct((n, block, dm), BF16)
    pair = jax.ShapeDtypeStruct((n // 2, block, dm), BF16)
    hidden = jax.ShapeDtypeStruct((n, block, part), BF16)
    return pl.pallas_call(
        functools.partial(feed_kernel, n=n, tile=256 if part % 256 == 0 else part, ids=ids),
        grid_spec=pltpu.PrefetchScalarGridSpec(
            num_scalar_prefetch=1,
            grid=(n,),
            in_specs=[piece(p) for p in range(n)]
            + [whole(a.shape) for a in (*left, *right)]
            + [one(dm), one(dm), whole(vecs.shape)],
            out_specs=[
                one(dm),
                one(part),
                one(part),
                half(dm),
                half(dm),
                whole((block, dm)),
                whole((8, part)),
                whole((dm, dm)),
                whole((part, dm)),
            ],
            scratch_shapes=[pltpu.VMEM((dm, part), BF16)],
        ),
        out_shape=[
            wide,
            hidden,
            hidden,
            pair,
            pair,
            jax.ShapeDtypeStruct((block, dm), F32),
            jax.ShapeDtypeStruct((8, part), F32),
            jax.ShapeDtypeStruct((dm, dm), BF16),
            jax.ShapeDtypeStruct((part, dm), BF16),
        ],
        compiler_params=pltpu.CompilerParams(vmem_limit_bytes=48 * 1024 * 1024),
        cost_estimate=pl.CostEstimate(
            flops=15 * 1000**3, bytes_accessed=16 * 1000**2, transcendentals=3 * 1000**2
        ),
        name="feed",
    )(me, *got, *left, *right, x_all, g_all, vecs)


def turn_kernel(me_ref, *refs, n):
    got, refs = refs[:n], refs[n:]
    keep_ref, far_ref, x_two_ref, g_ref, out_w_ref, vec_ref = refs[:6]
    gos, (gx_ref, d_out_ref, sum_ref) = refs[6 : 6 + n], refs[6 + n :]
    me = me_ref[0]
    width = got[0].shape[1]
    gh = keep_ref[...].astype(F32) + far_ref[...].astype(F32)
    normed, inv_std = normed_parts(x_two_ref[...])
    g = g_ref[...].astype(F32)
    gx = g + normalize_back(gh, normed, inv_std, vec_ref[2:3, :])
    gx_ref[...] = gx
    gb = gx.astype(BF16)
    for p in range(n):
        own = pl.ds(pl.multiple_of((me ^ p) * width, width), width)
        gos[p][...] = dot_nt(out_w_ref[own, :], gb).astype(BF16)
        d_out_ref[own, :] = dot_nn(got[p][0], gb).astype(BF16)
    sum_ref[0:1, :] = jnp.sum(gh * normed, 0, keepdims=True)
    sum_ref[1:2, :] = jnp.sum(gh, 0, keepdims=True)
    sum_ref[2:3, :] = jnp.sum(gb.astype(F32), 0, keepdims=True)
    sum_ref[3:4, :] = jnp.sum(g, 0, keepdims=True)


def turn(me, got, keep, far, x_two, g, out_w, vecs):
    n = len(got)
    _, width, block = got[0].shape
    dm = out_w.shape[1]

    def whole(shape):
        return pl.BlockSpec(shape, lambda i, me: (0,) * len(shape))

    def piece(p):
        return pl.BlockSpec((1, width, block), lambda i, me: (p, 0, 0))

    outs = [jax.ShapeDtypeStruct((width, block), BF16)] * n + [
        jax.ShapeDtypeStruct((block, dm), F32),
        jax.ShapeDtypeStruct(out_w.shape, BF16),
        jax.ShapeDtypeStruct((8, dm), F32),
    ]
    return pl.pallas_call(
        functools.partial(turn_kernel, n=n),
        grid_spec=pltpu.PrefetchScalarGridSpec(
            num_scalar_prefetch=1,
            grid=(1,),
            in_specs=[piece(p) for p in range(n)]
            + [whole(a.shape) for a in (keep, far, x_two, g, out_w, vecs)],
            out_specs=[whole(o.shape) for o in outs],
        ),
        out_shape=outs,
        compiler_params=pltpu.CompilerParams(vmem_limit_bytes=48 * 1024 * 1024),
        cost_estimate=pl.CostEstimate(flops=3 * 1000**3, bytes_accessed=8 * 1000**2, transcendentals=0),
        name="turn",
    )(me, *got, keep, far, x_two, g, out_w, vecs)


def leave_kernel(
    me_ref, x_ref, grad_ref, w_ref, vec_ref, two_ref, up_ref, even_ref, odd_ref, d_w_ref, sum_ref, add_ref, total_ref, tile_ref
):
    i = pl.program_id(0)

    @pl.when(i == 0)
    def _():
        sum_ref[...] = jnp.zeros_like(sum_ref)
        add_ref[...] = jnp.zeros_like(add_ref)
        total_ref[...] = jnp.zeros_like(total_ref)

    grads = grad_ref[0]
    gh = dot_nt(grads, w_ref[...])
    normed, _ = normed_parts(x_ref[0].astype(F32))
    h = (normed * vec_ref[0:1, :] + vec_ref[1:2, :]).astype(BF16)
    low = gh.astype(BF16)

    @pl.when(i % 2 == 0)
    def _():
        even_ref[0] = low

    @pl.when(i % 2 == 1)
    def _():
        odd_ref[0] = low

    sum_ref[0:1, :] += jnp.sum(gh * normed, 0, keepdims=True)
    sum_ref[1:2, :] += jnp.sum(gh, 0, keepdims=True)
    add_ref[0:1, :] += jnp.sum(grads.astype(F32), 0, keepdims=True)
    total_ref[...] += dot_tn(h, grads)

    @pl.when(i == pl.num_programs(0) - 1)
    def _():
        wide = total_ref.shape[1]
        width = wide // 3
        d_w_ref[:, :wide] = total_ref[...].astype(BF16)
        dm = w_ref.shape[0]
        rows = [sum_ref[0:2, :], two_ref[0:4, :], jnp.zeros((2, dm), F32), up_ref[0:1, :]]
        rows = jnp.concatenate(rows + [jnp.zeros((LANES - 9, dm), F32)], 0)
        tile_ref[...] = rows.T
        add = jnp.concatenate(
            [
                jnp.zeros((6, width), F32),
                add_ref[0:1, :width],
                add_ref[0:1, 2 * width :],
                jnp.zeros((LANES - 8, width), F32),
            ],
            0,
        )
        own = pl.ds(pl.multiple_of(me_ref[0] * width, width), width)
        tile_ref[own, :] += add.T
        d_w_ref[:, wide:] = tile_ref[...].astype(BF16)


def leave(me, x_all, grads, w, vecs, sums_two, sums_up):
    n, block, wide = grads.shape
    dm = w.shape[0]

    def whole(shape):
        return pl.BlockSpec(shape, lambda i, me: (0,) * len(shape))

    def one(width):
        return pl.BlockSpec((1, block, width), lambda i, me: (i, 0, 0))

    def half(width):
        return pl.BlockSpec((1, block, width), lambda i, me: (i // 2, 0, 0))

    pair = jax.ShapeDtypeStruct((n // 2, block, dm), BF16)
    return pl.pallas_call(
        leave_kernel,
        grid_spec=pltpu.PrefetchScalarGridSpec(
            num_scalar_prefetch=1,
            grid=(n,),
            in_specs=[one(dm), one(wide)] + [whole(a.shape) for a in (w, vecs, sums_two, sums_up)],
            out_specs=[half(dm), half(dm), whole((dm, wide + LANES))],
            scratch_shapes=[
                pltpu.VMEM((8, dm), F32),
                pltpu.VMEM((8, wide), F32),
                pltpu.VMEM(w.shape, F32),
                pltpu.VMEM((dm, LANES), F32),
            ],
        ),
        out_shape=[
            pair,
            pair,
            jax.ShapeDtypeStruct((dm, wide + LANES), BF16),
        ],
        compiler_params=pltpu.CompilerParams(vmem_limit_bytes=48 * 1024 * 1024),
        cost_estimate=pl.CostEstimate(flops=6 * 1000**3, bytes_accessed=10 * 1000**2, transcendentals=0),
        name="leave",
    )(me, x_all, grads, w, vecs, sums_two, sums_up)


def finish_kernel(me_ref, *refs, n, width):
    pieces, (q_ref, k_ref, v_ref, vec_ref) = refs[:n], refs[n:]
    vec_ref[...] = sum(p[:, 3 * width :] for p in pieces)
    parts = [p[:, : 3 * width] for p in pieces]
    bit = 1
    while bit < n:
        on = (me_ref[0] & bit) != 0
        for p in range(n):
            if not p & bit:
                a, b = parts[p], parts[p | bit]
                parts[p] = jnp.where(on, b, a)
                parts[p | bit] = jnp.where(on, a, b)
        bit *= 2
    for t in range(n):
        for i, ref in enumerate((q_ref, k_ref, v_ref)):
            ref[:, t * width : (t + 1) * width] = parts[t][:, i * width : (i + 1) * width]


def finish(me, pieces, width):
    n = len(pieces)
    rows = pieces[0].shape[0]
    weight = jax.ShapeDtypeStruct((rows, n * width), F32)
    return pl.pallas_call(
        functools.partial(finish_kernel, n=n, width=width),
        in_specs=[pl.BlockSpec(memory_space=pltpu.SMEM)] + [pl.BlockSpec(memory_space=pltpu.VMEM)] * n,
        out_specs=[pl.BlockSpec(memory_space=pltpu.VMEM)] * 4,
        out_shape=[weight] * 3 + [jax.ShapeDtypeStruct((rows, LANES), F32)],
        name="finish",
    )(me, *pieces)


def body(
    nd,
    ns,
    tokens,
    cotangent,
    segments,
    w_query,
    w_key,
    w_value,
    w_out,
    w_up,
    w_down,
    ln1_gain,
    ln1_shift,
    query_bias,
    value_bias,
    out_bias,
    ln2_gain,
    ln2_shift,
    up_bias,
    down_bias,
):
    d = lax.axis_index("dp")
    s = lax.axis_index("seq")
    me = s.astype(jnp.int32).reshape(1)
    _, block, dm = tokens.shape
    hd = dm // H
    heads = H // ns
    width = heads * hd
    rows = w_query.shape[0]
    ff_rows, ff = w_down.shape[0], w_up.shape[1]
    ratio = ff_rows // rows
    part = ff // ns
    pad = 16

    me = jnp.stack([s, d]).astype(jnp.int32)
    masks = bits_of(nd)[::-1]
    far = bits_of(ns)[-1]
    x_own = tokens.reshape(block, dm)
    g = cotangent.reshape(block, dm)
    x_far = swap(x_own, "seq", ns, far)

    cols = [w.reshape(rows, ns, width) for w in (w_query, w_key, w_value)]
    vec = jnp.stack([ln1_gain, ln1_shift, ln2_gain, ln2_shift, out_bias, down_bias, query_bias, value_bias], 1)
    vec = jnp.pad(vec, ((0, 0), (0, LANES - vec.shape[1])))
    up_cols = w_up.reshape(rows, nd, ns, ff_rows).transpose(0, 2, 1, 3).reshape(rows, ns, part)
    lanes = LANES * -(-block // (rows * LANES))
    seg = jnp.pad(segments.reshape(block).astype(BF16), (0, rows * lanes - block)).reshape(rows, lanes)
    same = jnp.concatenate([vec, w_out, seg], 1)
    same = jnp.broadcast_to(same[:, None], (rows, ns, same.shape[1]))
    pieces = jnp.concatenate(cols + [same, up_cols], 2).transpose(1, 0, 2)
    first = 3 * width + LANES
    size = ns * rows
    pieces = trade_seq(pieces, s, ns)
    start = first + dm
    segs = jnp.stack([p[:, start : start + lanes].reshape(-1)[:block] for p in pieces]).astype(jnp.int32)
    seg_row = segs.reshape(ns, 1, block)
    seg_col = segs.reshape(ns, block, 1)
    pieces = ordered(pieces, s).reshape(size, -1)
    lane = lax.broadcasted_iota(jnp.int32, (size, first), 1)
    one = jnp.where(lane == 3 * width + 8, jnp.pad(up_bias, (0, size - ff_rows))[:, None], pieces[:, :first])
    two = jnp.concatenate([pieces[:, first:start], pieces[:, start + lanes :], w_down], 0)
    left, right = two[:, : dm // 2], two[:, dm // 2 :]

    ones, lefts = [one[None]], [left[None]]
    g_far = None
    for step, mask in enumerate(masks):
        got = swap(jnp.concatenate(ones, 0), "dp", nd, mask)
        if step == 1:
            got, x_far = lax.optimization_barrier((got, x_far))
            g_far = swap(tie(g, x_far), "seq", ns, far)
        if step > 0:
            lefts.append(swap(tie(jnp.concatenate(lefts, 0), got), "dp", nd, masks[step - 1]))
        ones.append(got)
    lefts.append(swap(tie(jnp.concatenate(lefts, 0), ones[-1]), "dp", nd, masks[-1]))
    rights = [right[None]]
    turned = masks[:-2] + masks[:-3:-1]
    for step, mask in enumerate(turned):
        rights.append(swap(tie(jnp.concatenate(rights, 0), lefts[min(step + 1, len(masks) - 1)]), "dp", nd, mask))
    parts = {0: x_own, far: x_far}
    g_parts = {0: g, far: g_far}
    for mask in bits_of(ns)[-2::-1]:
        for p in list(parts):
            parts[p | mask] = swap(parts[p], "seq", ns, mask)
            g_parts[p | mask] = swap(g_parts[p], "seq", ns, mask)
    x_all = jnp.stack([parts[p] for p in range(ns)])
    g_all = jnp.stack([g_parts[p] for p in range(ns)])

    ones, ids = settle(ones, d, nd, masks, 1)
    ones[-1], x_all, g_all = lax.optimization_barrier((ones[-1], x_all, g_all))
    qkv, w_qkv, vecs = enter(me, ones, ids, x_all, width)
    qkv, *rights[1:-1] = lax.optimization_barrier((qkv, *rights[1:-1]))
    o_low, o_full, lse = attend(me, qkv, seg_row, seg_col, heads, hd)
    o_got = spread_seq(o_low, ns)
    lefts, left_ids = settle(lefts, d, nd, masks, 3)
    rights, right_ids = settle(rights, d, nd, turned, 3)
    ids = (left_ids, right_ids)
    h_two, act, gu, even, odd, x_two, sums_up, w_out_all, w_down_own = feed(
        me, o_got, lefts, rights, ids, x_all, g_all, vecs
    )
    keep, sent, got = collect_pairs(even, odd, ns)
    act, gu, h_two = lax.optimization_barrier((act, gu, h_two, sent))[:3]
    d_down = jnp.einsum("nbk,nbc->kc", act, g_all, preferred_element_type=F32).astype(BF16)
    d_up = jnp.einsum("nbk,nbc->kc", h_two, gu, preferred_element_type=F32).astype(BF16)
    feeds = jnp.concatenate([d_up.reshape(nd, size, part), d_down.reshape(nd, ff_rows, dm)], 1)
    feed_keep, feed_sent = halves(feeds, d, nd, 1)
    feed_got = swap(feed_sent, "dp", nd, 1)
    got, feed_sent = lax.optimization_barrier((got, feed_sent))
    out_part = jnp.einsum("nbk,kc->nbc", act, w_down_own, preferred_element_type=F32).astype(BF16)
    *gos, gx_two, d_out, sums_two = turn(me, o_got, keep, got, x_two, g, w_out_all, vecs)
    go_got = [gos[0]] + [swap(gos[p], "seq", ns, p) for p in range(1, ns)]
    outs_keep, outs_sent = halves(d_out.reshape(nd, size, dm), d, nd, 1)
    outs_got = swap(outs_sent, "dp", nd, 1)
    out_keep, _, out_got = collect_pairs(out_part[::2], out_part[1::2], ns, (go_got[-1],))

    go_all = jnp.stack(go_got)
    go_all, feed_got = lax.optimization_barrier((go_all, feed_got))
    feeds = add_low(feed_keep, feed_got)
    feed_keep, feed_sent = halves(feeds, d >> 1, nd // 2, 1)
    feed_got = swap(feed_sent, "dp", nd, 2)
    grads = attend_back(me, qkv, go_all, o_full, lse, seg_row, seg_col, heads, hd)
    grads, out_got, outs_got, feed_got = lax.optimization_barrier((grads, out_got, outs_got, feed_got))
    feeds = add_low(feed_keep, feed_got)
    outs = add_low(outs_keep, outs_got)
    out = out_keep.astype(F32) + out_got.astype(F32) + x_two + vecs[5:6]
    even, odd, blob = leave(me, x_all, grads, w_qkv, vecs, sums_two, sums_up)
    keep, sent, got = collect_pairs(even, odd, ns)
    blob_keep, blob_sent = halves(blob.reshape(nd, size, first), d, nd, 1)
    blob_got = swap(tie(blob_sent, sent), "dp", nd, 1)
    blob = add_low(blob_keep, blob_got)
    blob_keep, blob_sent = halves(blob, d >> 1, nd // 2, 1)
    blob_got = swap(blob_sent, "dp", nd, 2)
    blob_got, got, feeds, outs = lax.optimization_barrier((blob_got, got, feeds, outs))
    blob = add_low(blob_keep, blob_got)
    blob = collect_dp(blob, d >> 2, nd // 4, shift=2)
    trades = trade_seq(blob.reshape(ns, rows, first), s, ns)
    sum_up_bias = blob[:ff_rows, 3 * width + 8]
    gh_one = keep.astype(F32) + got.astype(F32)
    n_own, inv_own = normed_parts(x_own.astype(F32))
    grad_x = gx_two + normalize_back(gh_one, n_own, inv_own, vecs[0:1])
    sum_q, sum_k, sum_v, vec_sum = finish(me, trades, width)
    vec_sum = vec_sum.T
    outs = collect_dp(outs, d >> 1, nd // 2, shift=1)
    feeds = collect_dp(feeds, d >> 2, nd // 4, shift=2)
    sum_down = feeds[size:]
    both = jnp.concatenate([outs, feeds[:size]], 1).reshape(ns, rows, dm + part)
    both = trade_seq(both, s, ns)
    sum_out = sum(b[:, :dm] for b in both)
    sum_up = ordered([b[:, dm:] for b in both], s)
    sum_up = sum_up.reshape(ns, rows, nd, ff_rows).transpose(1, 2, 0, 3).reshape(rows, ff)
    v = [vec_sum[i] for i in range(8)]
    return (
        out.reshape(1, block, dm),
        grad_x.reshape(1, block, dm),
        sum_q,
        sum_k,
        sum_v,
        sum_out,
        sum_up,
        sum_down,
        v[0],
        v[1],
        v[6],
        v[7],
        v[4],
        v[2],
        v[3],
        sum_up_bias,
        v[5],
    )


def solution(mesh):
    act = P("dp", "seq", None)
    weight = P(("dp", "seq"), None)
    vector = P(("dp", "seq"))
    return jax.shard_map(
        functools.partial(body, mesh.shape["dp"], mesh.shape["seq"]),
        mesh=mesh,
        in_specs=(act, act, P("dp", "seq")) + (weight,) * 6 + (vector,) * 9,
        out_specs=(act, act) + (weight,) * 6 + (vector,) * 9,
        check_vma=False,
    )
```

time: 459 us -> 336 us (0.73)
  matrix products: 72.9 us -> 10.3 us
  waiting for transfers between devices: 185 us -> 125 us
  Pallas kernels: 44.3 us -> 95.2 us
  local copies, waits for them, and re-layouts: 47.3 us -> 24.7 us
  other arithmetic: 47 us -> 31.7 us
  starting transfers between devices: 51.4 us -> 42.4 us
    dot_general x30 -> x3, matrix products: 72.9 us -> 10.3 us  [the longest x1 4.74 us: body(): jnp.einsum('nbk,nbc->kc', act, g_all, preferred_element_type=F32)]
    ppermute x57 -> x45, waiting for transfers between devices: 185 us -> 125 us  [swap(): return lax.ppermute(value, axis, [(i, i ^ mask) for i in range(size)])]
    pallas_call x0 -> x5, Pallas kernels: none -> 50.5 us  [the longest x1 23.2 us: feed(): pl.pallas_call(functools.partial(feed_kernel, n=n, tile=256 if part % 256...]
    select_n x9 -> x0, other arithmetic: 13.7 us -> none  [spread_dp(): jnp.where(on, jnp.concatenate([other, value], axis), jnp.concatenate([val...]
    slice x20 -> x9, local copies, waits for them, and re-layouts: 16.7 us -> 5.83 us  [the longest x4 2.35 us: body(): p[:, start:start + lanes].reshape(-1)[:block]]
    ppermute x57 -> x45, starting transfers between devices: 51.4 us -> 42.4 us  [swap(): return lax.ppermute(value, axis, [(i, i ^ mask) for i in range(size)])]
    squeeze x7 -> x2, local copies, waits for them, and re-layouts: 7.1 us -> 0.76 us  [trade_seq(): lax.dynamic_index_in_dim(pieces, index, 0, False)]
    concatenate x12 -> x4, local copies, waits for them, and re-layouts: 5.94 us -> 0.39 us  [ordered(): jnp.concatenate([b, a], 0)]
  transfers between devices with their start and end apart: 57 -> 45, of which waited for: 22 -> 24; matrix products, arithmetic and copies ran while one was open for 31% -> 14% of each run, Pallas kernels for 10% -> 12%
where the time goes in v2:
time: 336 us; the launch traced here: 332 us
  waiting for transfers between devices  125 us (37%)
  Pallas kernels  95.2 us (28%)
  starting transfers between devices  42.4 us (13%)
  other arithmetic  31.7 us (9%)
  local copies, waits for them, and re-layouts  24.7 us (7%)
  matrix products  10.3 us (3%)
    ppermute x45, waiting for transfers between devices, swap(): return lax.ppermute(value, axis, [(i, i ^ mask) for i in range(size)])  125 us
    ppermute x45, starting transfers between devices, swap(): return lax.ppermute(value, axis, [(i, i ^ mask) for i in range(size)])  42.4 us
    pallas_call x1, Pallas kernels, attend_back(): pl.pallas_call(functools.partial(attend_back_kernel, heads=heads, hd=hd),...  26.7 us
    pallas_call x1, Pallas kernels, feed(): pl.pallas_call(functools.partial(feed_kernel, n=n, tile=256 if part % 256...  23.2 us
    pallas_call x1, Pallas kernels, attend(): pl.pallas_call(functools.partial(attend_kernel, heads=heads, hd=hd), grid...  18 us
    pallas_call x1, Pallas kernels, leave(): pl.pallas_call(leave_kernel, grid_spec=pltpu.PrefetchScalarGridSpec(num_s...  12.6 us
    pallas_call x1, Pallas kernels, turn(): pl.pallas_call(functools.partial(turn_kernel, n=n), grid_spec=pltpu.Prefe...  7.06 us
  transfers between devices with their start and end apart: 45, of which 24 were waited for; matrix products, arithmetic and copies ran while one was open for 14% of the time, Pallas kernels for 12%

profile of v2, /device:TPU:0, one launch (start us, length us, event | category | flops | bytes accessed | tf_op | source)
XLA Modules:
  0.0 331.8 jit_solution(12634715710220399296)
XLA Ops:
  7.4 2.4 collective-permute-start
  10.5 1.7 collective-permute-start.5
  13.4 3.1 collective-permute-done.1
  16.9 3.0 collective-permute-start.3
  19.9 7.2 %collective-permute-done.3.refs_1_ = bf16[1,96,704]{2,1,0:T(8,128)(2,1)S(1)} collective-permute-done((bf16[1,96,704]{2,1,0:T(8,128)(2,1)S(1)}, bf16[1,96,704]{2,1,0:T(8,128)(2,1)S(1)}, u32[]{:S(2)}, u32[]{:S(2)}) %collective-permute-start.3) | collective-permute-done | bytes 135200 | tf_op jit(solution)/shard_map/ppermute | solution.py:214
  28.0 7.7 %collective-permute-done.4.refs_2_ = bf16[2,96,704]{2,1,0:T(8,128)(2,1)S(1)} collective-permute-done((bf16[2,96,704]{2,1,0:T(8,128)(2,1)S(1)}, bf16[2,96,704]{2,1,0:T(8,128)(2,1)S(1)}, u32[]{:S(2)}, u32[]{:S(2)}) %collective-permute-start.4) | collective-permute-done | bytes 270368 | tf_op jit(solution)/shard_map/ppermute | solution.py:214
  39.7 3.2 collective-permute-start.12
  43.3 8.8 %collective-permute-done.12.refs_5_ = bf16[1,288,384]{2,1,0:T(8,128)(2,1)S(1)} collective-permute-done((bf16[1,288,384]{2,1,0:T(8,128)(2,1)S(1)}, bf16[1,288,384]{2,1,0:T(8,128)(2,1)S(1)}, u32[]{:S(2)}, u32[]{:S(2)}) %collective-permute-start.12) | collective-permute-done | bytes 221216 | tf_op jit(solution)/shard_map/ppermute | solution.py:214
  52.1 2.0 collective-permute-done.10
  57.7 3.8 %collective-permute-start.13 = (bf16[1,288,384]{2,1,0:T(8,128)(2,1)S(1)}, bf16[1,288,384]{2,1,0:T(8,128)(2,1)S(1)}, u32[]{:S(2)}, u32[]{:S(2)}) collective-permute-start(bf16[1,288,384]{2,1,0:T(8,128)(2,1)S(1)} %get-tuple-element.84.refs_8_), channel_id=1, source_target_pairs={{0,16},{4,20},{8,24},{12,28},{16,0},{20,4},{24,8},{28,12},{1,17},{... | collective-permute-start | bytes 663560 | tf_op jit(solution)/shard_map/ppermute | solution.py:214
  61.8 10.5 %collective-permute-done.13.refs_9_ = bf16[1,288,384]{2,1,0:T(8,128)(2,1)S(1)} collective-permute-done((bf16[1,288,384]{2,1,0:T(8,128)(2,1)S(1)}, bf16[1,288,384]{2,1,0:T(8,128)(2,1)S(1)}, u32[]{:S(2)}, u32[]{:S(2)}) %collective-permute-start.13) | collective-permute-done | bytes 221216 | tf_op jit(solution)/shard_map/ppermute | solution.py:214
  73.1 2.3 pad_maximum_fusion.refs_4_.refs_12_.x_ref
  75.5 8.9 %collective-permute-done.14.refs_6_ = bf16[2,288,384]{2,1,0:T(8,128)(2,1)S(1)} collective-permute-done((bf16[2,288,384]{2,1,0:T(8,128)(2,1)S(1)}, bf16[2,288,384]{2,1,0:T(8,128)(2,1)S(1)}, u32[]{:S(2)}, u32[]{:S(2)}) %collective-permute-start.14) | collective-permute-done | bytes 442400 | tf_op jit(solution)/shard_map/ppermute | solution.py:214
  85.9 3.2 pad_maximum_fusion.1.refs_13_
  89.1 5.9 %enter.1 = (bf16[4,512,576]{2,1,0:T(8,128)(2,1)S(1)}, bf16[768,576]{1,0:T(8,128)(2,1)S(1)}, f32[16,768]{1,0:T(8,128)S(1)}) custom-call(s32[2]{0:T(128)S(1)} %pad_add_fusion.me_ref, bf16[1,96,704]{2,1,0:T(8,128)(2,1)S(1)} %fusion.33.refs_0_, bf16[1,96,704]{2,1,0:T(8,128)(2,1)S(1)} %collective-permute-done.3.refs_1_, ...), custom_call_target="tpu_custom_call" | custom-call | flops 5000000000 | bytes 8000000 | tf_op jit(solution)/shard_map/enter/pallas_call | solution.py:355
  95.5 18.0 %attend.1 = (bf16[4,192,512]{2,1,0:T(8,128)(2,1)S(1)}, f32[4,192,512]{2,1,0:T(8,128)S(1)}, f32[4,8,512]{2,1,0:T(8,128)S(1)}) custom-call(s32[2]{0:T(128)S(1)} %pad_add_fusion.me_ref, bf16[4,512,576]{2,1,0:T(8,128)(2,1)S(1)} %get-tuple-element.87.qkv_ref, s32[4,1,512]{2,1,0:T(1,128)S(1)} %maximum_convert_fusion.1.seg_row_ref, ...), custom_call_target="tpu_custom_call" | custom-call | flops 20000000000 | bytes 8000000 | tf_op jit(solution)/shard_map/attend/pallas_call | solution.py:87
  113.5 1.6 collective-permute-start.17
  115.2 1.6 collective-permute-start.19
  117.7 13.6 %collective-permute-done.17.refs_2_ = bf16[4,192,512]{2,1,0:T(8,128)(2,1)S(1)} collective-permute-done((bf16[4,192,512]{2,1,0:T(8,128)(2,1)S(1)}, bf16[4,192,512]{2,1,0:T(8,128)(2,1)S(1)}, u32[]{:S(2)}, u32[]{:S(2)}) %collective-permute-start.17) | collective-permute-done | bytes 786464 | tf_op jit(solution)/shard_map/ppermute | solution.py:214
  131.4 3.5 %collective-permute-done.19.refs_7_ = bf16[4,288,384]{2,1,0:T(8,128)(2,1)S(1)} collective-permute-done((bf16[4,288,384]{2,1,0:T(8,128)(2,1)S(1)}, bf16[4,288,384]{2,1,0:T(8,128)(2,1)S(1)}, u32[]{:S(2)}, u32[]{:S(2)}) %collective-permute-start.19) | collective-permute-done | bytes 884768 | tf_op jit(solution)/shard_map/ppermute | solution.py:214
  137.0 23.2 %feed.1 = (bf16[4,512,768]{2,1,0:T(8,128)(2,1)}, bf16[4,512,768]{2,1,0:T(8,128)(2,1)}, bf16[4,512,768]{2,1,0:T(8,128)(2,1)}, bf16[2,512,768]{2,1,0:T(8,128)(2,1)...) custom-call(s32[2]{0:T(128)S(1)} %pad_add_fusion.me_ref, ...), custom_call_target="tpu_custom_call" | custom-call | flops 15000000512 | bytes 16000000 | tf_op jit(solution)/shard_map/feed/pallas_call | solution.py:453
  160.4 3.7 %collective-permute-done.21 = bf16[2,512,768]{2,1,0:T(8,128)(2,1)} collective-permute-done((bf16[2,512,768]{2,1,0:T(8,128)(2,1)}, bf16[2,512,768]{2,1,0:T(8,128)(2,1)}, u32[]{:S(2)}, u32[]{:S(2)}) %collective-permute-start.21) | collective-permute-done | bytes 1572896 | tf_op jit(solution)/shard_map/ppermute | solution.py:214
  164.1 2.4 fusion.24
  167.1 4.7 %bitcast_convert_fusion = bf16[768,768]{1,0:T(8,128)(2,1)S(1)} fusion(bf16[4,512,768]{2,1,0:T(8,128)(2,1)} %get-tuple-element.100, bf16[4,512,768]{2,1,0:T(8,128)(2,1)S(1)} %copy-done.24), kind=kOutput, calls=%fused_computation.8 | convolution fusion | flops 2416508928 | bytes 7471104 | tf_op jit(solution)/shard_map/nbk,nbc->kc/dot_general | solution.py:772
  171.8 2.8 bitcast_convert_fusion.1
  177.4 2.8 convolution_convert_fusion
  180.3 1.9 fusion.37
  182.2 4.0 %collective-permute-done.23.refs_5_ = bf16[512,768]{1,0:T(8,128)(2,1)S(1)} collective-permute-done((bf16[512,768]{1,0:T(8,128)(2,1)S(1)}, bf16[512,768]{1,0:T(8,128)(2,1)S(1)}, u32[]{:S(2)}, u32[]{:S(2)}) %collective-permute-start.23) | collective-permute-done | bytes 786464 | tf_op jit(solution)/shard_map/ppermute | solution.py:214
  186.2 7.1 %turn.1 = (bf16[192,512]{1,0:T(8,128)(2,1)S(1)}, bf16[192,512]{1,0:T(8,128)(2,1)S(1)}, bf16[192,512]{1,0:T(8,128)(2,1)S(1)}, bf16[192,512]{1,0:T(8,128)(2,1)S(1)...) custom-call(s32[2]{0:T(128)S(1)} %pad_add_fusion.me_ref, ...), custom_call_target="tpu_custom_call" | custom-call | flops 3000000000 | bytes 8000000 | tf_op jit(solution)/shard_map/turn/pallas_call | solution.py:531
  196.9 4.0 %collective-permute-done.25 = bf16[192,512]{1,0:T(8,128)(2,1)S(1)} collective-permute-done((bf16[192,512]{1,0:T(8,128)(2,1)S(1)}, bf16[192,512]{1,0:T(8,128)(2,1)S(1)}, u32[]{:S(2)}, u32[]{:S(2)}) %collective-permute-start.25) | collective-permute-done | bytes 196640 | tf_op jit(solution)/shard_map/ppermute | solution.py:214
  200.9 3.4 %collective-permute-done.26 = bf16[192,512]{1,0:T(8,128)(2,1)S(1)} collective-permute-done((bf16[192,512]{1,0:T(8,128)(2,1)S(1)}, bf16[192,512]{1,0:T(8,128)(2,1)S(1)}, u32[]{:S(2)}, u32[]{:S(2)}) %collective-permute-start.26) | collective-permute-done | bytes 196640 | tf_op jit(solution)/shard_map/ppermute | solution.py:214
  204.9 2.0 fusion
  207.9 1.6 fusion.27
  209.5 1.6 collective-permute-start.28
  211.1 26.7 %attend_back.1.grad_ref = bf16[4,512,576]{2,1,0:T(8,128)(2,1)S(1)} custom-call(s32[2]{0:T(128)S(1)} %pad_add_fusion.me_ref, bf16[4,512,576]{2,1,0:T(8,128)(2,1)S(1)} %copy-done.11, bf16[4,192,512]{2,1,0:T(8,128)(2,1)S(1)} %pad_maximum_fusion.4.go_ref, f32[4,192,512]{2,1,0:T(8,128)S(1)} %copy-done.16, f32[4,8,512]{2,1,0:T(8,128)S(1)} %get-tuple-element.113.lse_ref, ...), custom_call_target="tpu_custom_call" | custom-call | flops 40000000000 | bytes 12000000 | tf_op jit(solution)/shard_map/attend_back/pallas_call | solution.py:169
  237.8 1.5 copy-done.12
  240.4 12.6 %leave.1 = (bf16[2,512,768]{2,1,0:T(8,128)(2,1)S(1)}, bf16[2,512,768]{2,1,0:T(8,128)(2,1)S(1)}, bf16[768,704]{1,0:T(8,128)(2,1)S(1)}) custom-call(s32[2]{0:T(128)S(1)} %pad_add_fusion.me_ref, bf16[4,512,768]{2,1,0:T(8,128)(2,1)} %copy-done, bf16[4,512,576]{2,1,0:T(8,128)(2,1)} %copy-done.12, bf16[768,576]{1,0:T(8,128)(2,1)S(1)} %copy-done.14, ...), custom_call_target="tpu_custom_call" | custom-call | flops 6000000000 | bytes 10000000 | tf_op jit(solution)/shard_map/leave/pallas_call | solution.py:614
  259.5 3.7 %fusion.14 = f32[1,512,768]{2,1,0:T(8,128)} fusion(f32[512,768]{1,0:T(8,128)} %get-tuple-element.105.refs_6_, bf16[512,768]{1,0:T(8,128)(2,1)} %copy-done.29, bf16[2,512,768]{2,1,0:T(8,128)(2,1)} %collective-permute-done.22, bf16[2,512,768]{2,1,0:T(8,128)(2,1)} %get-tuple-element.149, f32[768]{0:T(1024)S(1)} %get-tuple-element.140), kind=kLoop, calls=%fused_computation.28 | loop fusion | flops 3538944 | bytes 5508096 | tf_op jit(solution)/shard_map/reshape | solution.py:822
  263.9 10.4 %collective-permute-done.32 = bf16[4,96,704]{2,1,0:T(8,128)(2,1)} collective-permute-done((bf16[4,96,704]{2,1,0:T(8,128)(2,1)S(1)}, bf16[4,96,704]{2,1,0:T(8,128)(2,1)}, u32[]{:S(2)}, u32[]{:S(2)}) %collective-permute-start.32) | collective-permute-done | bytes 540704 | tf_op jit(solution)/shard_map/ppermute | solution.py:214
  277.1 5.5 %collective-permute-done.34 = bf16[512,768]{1,0:T(8,128)(2,1)S(1)} collective-permute-done((bf16[512,768]{1,0:T(8,128)(2,1)S(1)}, bf16[512,768]{1,0:T(8,128)(2,1)S(1)}, u32[]{:S(2)}, u32[]{:S(2)}) %collective-permute-start.34) | collective-permute-done | bytes 786464 | tf_op jit(solution)/shard_map/ppermute | solution.py:214
  284.9 3.3 collective-permute-start.41
  288.4 2.0 fusion.15
  290.5 3.0 fusion.9
  293.5 12.7 %collective-permute-done.35 = bf16[96,704]{1,0:T(8,128)(2,1)S(1)} collective-permute-done((bf16[96,704]{1,0:T(8,128)(2,1)S(1)}, bf16[96,704]{1,0:T(8,128)(2,1)S(1)}, u32[]{:S(2)}, u32[]{:S(2)}) %collective-permute-start.35) | collective-permute-done | bytes 135200 | tf_op jit(solution)/shard_map/ppermute | solution.py:214
  309.8 9.2 %collective-permute-done.40 = bf16[96,768]{1,0:T(8,128)(2,1)S(1)} collective-permute-done((bf16[96,768]{1,0:T(8,128)(2,1)S(1)}, bf16[96,768]{1,0:T(8,128)(2,1)S(1)}, u32[]{:S(2)}, u32[]{:S(2)}) %collective-permute-start.40) | collective-permute-done | bytes 147488 | tf_op jit(solution)/shard_map/ppermute | solution.py:214
  322.5 1.8 finish.1
  324.3 1.8 slice_reduce_fusion.1
  326.1 2.1 collective-permute-done.44
  (242 shorter events, 56.3 us)
Async XLA Ops:
  7.4 6.0 %collective-permute-start = (bf16[24,2368]{1,0:T(8,128)(2,1)S(1)}, bf16[24,2368]{1,0:T(8,128)(2,1)S(1)}, u32[]{:S(2)}, u32[]{:S(2)}) collective-permute-start(bf16[24,2368]{1,0:T(8,128)(2,1)S(1)} %get-tuple-element.163), channel_id=1, source_target_pairs={{0,3},{1,2},{2,1},{3,0},{4,7},{5,6},{6,5},{7,4},{8,11},{9,10},{10,... | collective-permute-start | bytes 341000 | tf_op jit(solution)/shard_map/ppermute | solution.py:214
  9.8 6.7 %collective-permute-start.1 = (bf16[24,2368]{1,0:T(8,128)(2,1)S(1)}, bf16[24,2368]{1,0:T(8,128)(2,1)S(1)}, u32[]{:S(2)}, u32[]{:S(2)}) collective-permute-start(bf16[24,2368]{1,0:T(8,128)(2,1)S(1)} %get-tuple-element.162), channel_id=1, source_target_pairs={{0,2},{1,3},{2,0},{3,1},{4,6},{5,7},{6,4},{7,5},{8,10},{9,11},{10,... | collective-permute-start | bytes 341000 | tf_op jit(solution)/shard_map/ppermute | solution.py:214
  10.4 6.2 %collective-permute-start.2 = (bf16[24,2368]{1,0:T(8,128)(2,1)S(1)}, bf16[24,2368]{1,0:T(8,128)(2,1)S(1)}, u32[]{:S(2)}, u32[]{:S(2)}) collective-permute-start(bf16[24,2368]{1,0:T(8,128)(2,1)S(1)} %get-tuple-element.161), channel_id=1, source_target_pairs={{0,1},{1,0},{2,3},{3,2},{4,5},{5,4},{6,7},{7,6},{8,9},{9,8},{10,11... | collective-permute-start | bytes 341000 | tf_op jit(solution)/shard_map/ppermute | solution.py:214
  10.5 25.2 %collective-permute-start.5 = (bf16[512,768]{1,0:T(8,128)(2,1)}, bf16[512,768]{1,0:T(8,128)(2,1)S(1)}, u32[]{:S(2)}, u32[]{:S(2)}) collective-permute-start(bf16[512,768]{1,0:T(8,128)(2,1)} %bitcast.21), channel_id=1, source_target_pairs={{0,2},{1,3},{2,0},{3,1},{4,6},{5,7},{6,4},{7,5},{8,10},{9,11},{10,... | collective-permute-start | bytes 2359304 | tf_op jit(solution)/shard_map/ppermute | solution.py:214
  16.9 10.3 %collective-permute-start.3 = (bf16[1,96,704]{2,1,0:T(8,128)(2,1)S(1)}, bf16[1,96,704]{2,1,0:T(8,128)(2,1)S(1)}, u32[]{:S(2)}, u32[]{:S(2)}) collective-permute-start(bf16[1,96,704]{2,1,0:T(8,128)(2,1)S(1)} %fusion.33.refs_0_), channel_id=1, source_target_pairs={{0,16},{4,20},{8,24},{12,28},{16,0},{20,4},{24,8},{28,12},{1,17},{... | collective-permute-start | bytes 405512 | tf_op jit(solution)/shard_map/ppermute | solution.py:214
  27.2 8.5 %collective-permute-start.4 = (bf16[2,96,704]{2,1,0:T(8,128)(2,1)S(1)}, bf16[2,96,704]{2,1,0:T(8,128)(2,1)S(1)}, u32[]{:S(2)}, u32[]{:S(2)}) collective-permute-start(bf16[2,96,704]{2,1,0:T(8,128)(2,1)S(1)} %pad_maximum_fusion.10), channel_id=1, source_target_pairs={{0,8},{4,12},{8,0},{12,4},{16,24},{20,28},{24,16},{28,20},{1,9},{5... | collective-permute-start | bytes 811016 | tf_op jit(solution)/shard_map/ppermute | solution.py:214
  35.7 18.4 %collective-permute-start.10 = (bf16[512,768]{1,0:T(8,128)(2,1)}, bf16[512,768]{1,0:T(8,128)(2,1)}, u32[]{:S(2)}, u32[]{:S(2)}) collective-permute-start(bf16[512,768]{1,0:T(8,128)(2,1)} %bitcast.25.refs_7_), channel_id=1, source_target_pairs={{0,2},{1,3},{2,0},{3,1},{4,6},{5,7},{6,4},{7,5},{8,10},{9,11},{10,... | collective-permute-start | bytes 2359304 | tf_op jit(solution)/shard_map/ppermute | solution.py:214
  38.1 19.6 %collective-permute-start.6 = (bf16[4,96,704]{2,1,0:T(8,128)(2,1)}, bf16[4,96,704]{2,1,0:T(8,128)(2,1)S(1)}, u32[]{:S(2)}, u32[]{:S(2)}) collective-permute-start(bf16[4,96,704]{2,1,0:T(8,128)(2,1)} %pad_maximum_fusion.5), channel_id=1, source_target_pairs={{0,4},{4,0},{8,12},{12,8},{16,20},{20,16},{24,28},{28,24},{1,5},{5... | collective-permute-start | bytes 1622024 | tf_op jit(solution)/shard_map/ppermute | solution.py:214
  39.7 12.4 %collective-permute-start.12 = (bf16[1,288,384]{2,1,0:T(8,128)(2,1)S(1)}, bf16[1,288,384]{2,1,0:T(8,128)(2,1)S(1)}, u32[]{:S(2)}, u32[]{:S(2)}) collective-permute-start(bf16[1,288,384]{2,1,0:T(8,128)(2,1)S(1)} %get-tuple-element.83.refs_4_), channel_id=1, source_target_pairs={{0,16},{4,20},{8,24},{12,28},{16,0},{20,4},{24,8},{28,12},{1,17},{... | collective-permute-start | bytes 663560 | tf_op jit(solution)/shard_map/ppermute | solution.py:214
  42.8 30.3 %collective-permute-start.7 = (bf16[512,768]{1,0:T(8,128)(2,1)}, bf16[512,768]{1,0:T(8,128)(2,1)}, u32[]{:S(2)}, u32[]{:S(2)}) collective-permute-start(bf16[512,768]{1,0:T(8,128)(2,1)} %bitcast.21), channel_id=1, source_target_pairs={{0,1},{1,0},{2,3},{3,2},{4,5},{5,4},{6,7},{7,6},{8,9},{9,8},{10,11... | collective-permute-start | bytes 2359304 | tf_op jit(solution)/shard_map/ppermute | solution.py:214
  42.8 30.3 %collective-permute-start.8 = (bf16[512,768]{1,0:T(8,128)(2,1)}, bf16[512,768]{1,0:T(8,128)(2,1)}, u32[]{:S(2)}, u32[]{:S(2)}) collective-permute-start(bf16[512,768]{1,0:T(8,128)(2,1)} %copy-done.27), channel_id=1, source_target_pairs={{0,1},{1,0},{2,3},{3,2},{4,5},{5,4},{6,7},{7,6},{8,9},{9,8},{10,11... | collective-permute-start | bytes 2359304 | tf_op jit(solution)/shard_map/ppermute | solution.py:214
  52.1 33.8 %collective-permute-start.9 = (bf16[512,768]{1,0:T(8,128)(2,1)}, bf16[512,768]{1,0:T(8,128)(2,1)}, u32[]{:S(2)}, u32[]{:S(2)}) collective-permute-start(bf16[512,768]{1,0:T(8,128)(2,1)} %bitcast.25.refs_7_), channel_id=1, source_target_pairs={{0,1},{1,0},{2,3},{3,2},{4,5},{5,4},{6,7},{7,6},{8,9},{9,8},{10,11... | collective-permute-start | bytes 2359304 | tf_op jit(solution)/shard_map/ppermute | solution.py:214
  54.1 31.8 %collective-permute-start.11 = (bf16[512,768]{1,0:T(8,128)(2,1)}, bf16[512,768]{1,0:T(8,128)(2,1)}, u32[]{:S(2)}, u32[]{:S(2)}) collective-permute-start(bf16[512,768]{1,0:T(8,128)(2,1)} %collective-permute-done.10), channel_id=1, source_target_pairs={{0,1},{1,0},{2,3},{3,2},{4,5},{5,4},{6,7},{7,6},{8,9},{9,8},{10,11... | collective-permute-start | bytes 2359304 | tf_op jit(solution)/shard_map/ppermute | solution.py:214
  54.1 186.3 %copy-start.1 = (s32[2]{0:T(128)}, s32[2]{0:T(128)S(1)}, u32[]{:S(2)}) copy-start(s32[2]{0:T(128)S(1)} %pad_add_fusion.me_ref) | copy-start | bytes 28
  57.7 14.7 %collective-permute-start.13 = (bf16[1,288,384]{2,1,0:T(8,128)(2,1)S(1)}, bf16[1,288,384]{2,1,0:T(8,128)(2,1)S(1)}, u32[]{:S(2)}, u32[]{:S(2)}) collective-permute-start(bf16[1,288,384]{2,1,0:T(8,128)(2,1)S(1)} %get-tuple-element.84.refs_8_), channel_id=1, source_target_pairs={{0,16},{4,20},{8,24},{12,28},{16,0},{20,4},{24,8},{28,12},{1,17},{... | collective-permute-start | bytes 663560 | tf_op jit(solution)/shard_map/ppermute | solution.py:214
  72.3 12.0 %collective-permute-start.14 = (bf16[2,288,384]{2,1,0:T(8,128)(2,1)S(1)}, bf16[2,288,384]{2,1,0:T(8,128)(2,1)S(1)}, u32[]{:S(2)}, u32[]{:S(2)}) collective-permute-start(bf16[2,288,384]{2,1,0:T(8,128)(2,1)S(1)} %pad_maximum_fusion.9), channel_id=1, source_target_pairs={{0,8},{4,12},{8,0},{12,4},{16,24},{20,28},{24,16},{28,20},{1,9},{5... | collective-permute-start | bytes 1327112 | tf_op jit(solution)/shard_map/ppermute | solution.py:214
  84.3 11.1 %collective-permute-start.15 = (bf16[2,288,384]{2,1,0:T(8,128)(2,1)S(1)}, bf16[2,288,384]{2,1,0:T(8,128)(2,1)S(1)}, u32[]{:S(2)}, u32[]{:S(2)}) collective-permute-start(bf16[2,288,384]{2,1,0:T(8,128)(2,1)S(1)} %pad_maximum_fusion.8), channel_id=1, source_target_pairs={{0,4},{4,0},{8,12},{12,8},{16,20},{20,16},{24,28},{28,24},{1,5},{5... | collective-permute-start | bytes 1327112 | tf_op jit(solution)/shard_map/ppermute | solution.py:214
  113.5 17.9 %collective-permute-start.17 = (bf16[4,192,512]{2,1,0:T(8,128)(2,1)S(1)}, bf16[4,192,512]{2,1,0:T(8,128)(2,1)S(1)}, u32[]{:S(2)}, u32[]{:S(2)}) collective-permute-start(bf16[4,192,512]{2,1,0:T(8,128)(2,1)S(1)} %get-tuple-element.88.refs_0_), channel_id=1, source_target_pairs={{0,2},{1,3},{2,0},{3,1},{4,6},{5,7},{6,4},{7,5},{8,10},{9,11},{10,... | collective-permute-start | bytes 2359304 | tf_op jit(solution)/shard_map/ppermute | solution.py:214
  115.2 19.7 %collective-permute-start.19 = (bf16[4,288,384]{2,1,0:T(8,128)(2,1)S(1)}, bf16[4,288,384]{2,1,0:T(8,128)(2,1)S(1)}, u32[]{:S(2)}, u32[]{:S(2)}) collective-permute-start(bf16[4,288,384]{2,1,0:T(8,128)(2,1)S(1)} %pad_maximum_fusion.2), channel_id=1, source_target_pairs={{0,4},{4,0},{8,12},{12,8},{16,20},{20,16},{24,28},{28,24},{1,5},{5... | collective-permute-start | bytes 2654216 | tf_op jit(solution)/shard_map/ppermute | solution.py:214
  116.9 19.2 %collective-permute-start.20 = (bf16[4,288,384]{2,1,0:T(8,128)(2,1)S(1)}, bf16[4,288,384]{2,1,0:T(8,128)(2,1)S(1)}, u32[]{:S(2)}, u32[]{:S(2)}) collective-permute-start(bf16[4,288,384]{2,1,0:T(8,128)(2,1)S(1)} %pad_maximum_fusion.3), channel_id=1, source_target_pairs={{0,8},{4,12},{8,0},{12,4},{16,24},{20,28},{24,16},{28,20},{1,9},{5... | collective-permute-start | bytes 2654216 | tf_op jit(solution)/shard_map/ppermute | solution.py:214
  117.7 18.4 %collective-permute-start.16 = (bf16[4,192,512]{2,1,0:T(8,128)(2,1)S(1)}, bf16[4,192,512]{2,1,0:T(8,128)(2,1)S(1)}, u32[]{:S(2)}, u32[]{:S(2)}) collective-permute-start(bf16[4,192,512]{2,1,0:T(8,128)(2,1)S(1)} %get-tuple-element.88.refs_0_), channel_id=1, source_target_pairs={{0,1},{1,0},{2,3},{3,2},{4,5},{5,4},{6,7},{7,6},{8,9},{9,8},{10,11... | collective-permute-start | bytes 2359304 | tf_op jit(solution)/shard_map/ppermute | solution.py:214
  131.4 28.9 %copy-start.4 = (bf16[4,192,512]{2,1,0:T(8,128)(2,1)}, bf16[4,192,512]{2,1,0:T(8,128)(2,1)S(1)}, u32[]{:S(2)}) copy-start(bf16[4,192,512]{2,1,0:T(8,128)(2,1)S(1)} %collective-permute-done.17.refs_2_) | copy-start | bytes 2359300
  131.4 4.8 %collective-permute-start.18 = (bf16[4,192,512]{2,1,0:T(8,128)(2,1)S(1)}, bf16[4,192,512]{2,1,0:T(8,128)(2,1)S(1)}, u32[]{:S(2)}, u32[]{:S(2)}) collective-permute-start(bf16[4,192,512]{2,1,0:T(8,128)(2,1)S(1)} %collective-permute-done.17.refs_2_), channel_id=1, source_target_pairs={{0,1},{1,0},{2,3},{3,2},{4,5},{5,4},{6,7},{7,6},{8,9},{9,8},{10,11... | collective-permute-start | bytes 2359304 | tf_op jit(solution)/shard_map/ppermute | solution.py:214
  160.3 3.8 %collective-permute-start.21 = (bf16[2,512,768]{2,1,0:T(8,128)(2,1)}, bf16[2,512,768]{2,1,0:T(8,128)(2,1)}, u32[]{:S(2)}, u32[]{:S(2)}) collective-permute-start(bf16[2,512,768]{2,1,0:T(8,128)(2,1)} %get-tuple-element.99), channel_id=1, source_target_pairs={{0,1},{1,0},{2,3},{3,2},{4,5},{5,4},{6,7},{7,6},{8,9},{9,8},{10,11... | collective-permute-start | bytes 4718600 | tf_op jit(solution)/shard_map/ppermute | solution.py:214
  166.5 19.6 %collective-permute-start.23 = (bf16[512,768]{1,0:T(8,128)(2,1)S(1)}, bf16[512,768]{1,0:T(8,128)(2,1)S(1)}, u32[]{:S(2)}, u32[]{:S(2)}) collective-permute-start(bf16[512,768]{1,0:T(8,128)(2,1)S(1)} %get-tuple-element.151), channel_id=1, source_target_pairs={{0,2},{1,3},{2,0},{3,1},{4,6},{5,7},{6,4},{7,5},{8,10},{9,11},{10,... | collective-permute-start | bytes 2359304 | tf_op jit(solution)/shard_map/ppermute | solution.py:214
  175.8 29.1 %collective-permute-start.27 = (bf16[4,192,768]{2,1,0:T(8,128)(2,1)}, bf16[4,192,768]{2,1,0:T(8,128)(2,1)}, u32[]{:S(2)}, u32[]{:S(2)}) collective-permute-start(bf16[4,192,768]{2,1,0:T(8,128)(2,1)} %fusion.19), channel_id=1, source_target_pairs={{0,4},{4,0},{8,12},{12,8},{16,20},{20,16},{24,28},{28,24},{1,5},{5... | collective-permute-start | bytes 3538952 | tf_op jit(solution)/shard_map/ppermute | solution.py:214
  182.1 25.8 %collective-permute-start.22 = (bf16[2,512,768]{2,1,0:T(8,128)(2,1)}, bf16[2,512,768]{2,1,0:T(8,128)(2,1)}, u32[]{:S(2)}, u32[]{:S(2)}) collective-permute-start(bf16[2,512,768]{2,1,0:T(8,128)(2,1)} %get-tuple-element.150), channel_id=1, source_target_pairs={{0,1},{1,0},{2,3},{3,2},{4,5},{5,4},{6,7},{7,6},{8,9},{9,8},{10,11... | collective-permute-start | bytes 4718600 | tf_op jit(solution)/shard_map/ppermute | solution.py:214
  193.2 3.0 collective-permute-start.24
  193.2 7.7 %collective-permute-start.25 = (bf16[192,512]{1,0:T(8,128)(2,1)S(1)}, bf16[192,512]{1,0:T(8,128)(2,1)S(1)}, u32[]{:S(2)}, u32[]{:S(2)}) collective-permute-start(bf16[192,512]{1,0:T(8,128)(2,1)S(1)} %get-tuple-element.109), channel_id=1, source_target_pairs={{0,2},{1,3},{2,0},{3,1},{4,6},{5,7},{6,4},{7,5},{8,10},{9,11},{10,... | collective-permute-start | bytes 589832 | tf_op jit(solution)/shard_map/ppermute | solution.py:214
  193.7 10.6 %collective-permute-start.26 = (bf16[192,512]{1,0:T(8,128)(2,1)S(1)}, bf16[192,512]{1,0:T(8,128)(2,1)S(1)}, u32[]{:S(2)}, u32[]{:S(2)}) collective-permute-start(bf16[192,512]{1,0:T(8,128)(2,1)S(1)} %get-tuple-element.110), channel_id=1, source_target_pairs={{0,3},{1,2},{2,1},{3,0},{4,7},{5,6},{6,5},{7,4},{8,11},{9,10},{10,... | collective-permute-start | bytes 589832 | tf_op jit(solution)/shard_map/ppermute | solution.py:214
  196.2 43.2 %collective-permute-start.29 = (bf16[4,96,768]{2,1,0:T(8,128)(2,1)S(1)}, bf16[4,96,768]{2,1,0:T(8,128)(2,1)S(1)}, u32[]{:S(2)}, u32[]{:S(2)}) collective-permute-start(bf16[4,96,768]{2,1,0:T(8,128)(2,1)S(1)} %dynamic-slice_bitcast_fusion.2), channel_id=1, source_target_pairs={{0,4},{4,0},{8,12},{12,8},{16,20},{20,16},{24,28},{28,24},{1,5},{5... | collective-permute-start | bytes 1769480 | tf_op jit(solution)/shard_map/ppermute | solution.py:214
  207.0 32.4 %collective-permute-start.30 = (bf16[2,192,768]{2,1,0:T(8,128)(2,1)S(1)}, bf16[2,192,768]{2,1,0:T(8,128)(2,1)S(1)}, u32[]{:S(2)}, u32[]{:S(2)}) collective-permute-start(bf16[2,192,768]{2,1,0:T(8,128)(2,1)S(1)} %dynamic-slice_bitcast_fusion.1), channel_id=1, source_target_pairs={{0,8},{4,12},{8,0},{12,4},{16,24},{20,28},{24,16},{28,20},{1,9},{5... | collective-permute-start | bytes 1769480 | tf_op jit(solution)/shard_map/ppermute | solution.py:214
  209.5 29.9 %collective-permute-start.28 = (bf16[512,768]{1,0:T(8,128)(2,1)S(1)}, bf16[512,768]{1,0:T(8,128)(2,1)S(1)}, u32[]{:S(2)}, u32[]{:S(2)}) collective-permute-start(bf16[512,768]{1,0:T(8,128)(2,1)S(1)} %fusion.27), channel_id=1, source_target_pairs={{0,2},{1,3},{2,0},{3,1},{4,6},{5,7},{6,4},{7,5},{8,10},{9,11},{10,... | collective-permute-start | bytes 2359304 | tf_op jit(solution)/shard_map/ppermute | solution.py:214
  211.1 29.3 %copy-start.14 = (bf16[768,576]{1,0:T(8,128)(2,1)S(1)}, bf16[768,576]{1,0:T(8,128)(2,1)}, u32[]{:S(2)}) copy-start(bf16[768,576]{1,0:T(8,128)(2,1)} %copy-done.13) | copy-start | bytes 2654212
  253.0 3.5 %collective-permute-start.31 = (bf16[2,512,768]{2,1,0:T(8,128)(2,1)S(1)}, bf16[2,512,768]{2,1,0:T(8,128)(2,1)S(1)}, u32[]{:S(2)}, u32[]{:S(2)}) collective-permute-start(bf16[2,512,768]{2,1,0:T(8,128)(2,1)S(1)} %get-tuple-element.124), channel_id=1, source_target_pairs={{0,1},{1,0},{2,3},{3,2},{4,5},{5,4},{6,7},{7,6},{8,9},{9,8},{10,11... | collective-permute-start | bytes 4718600 | tf_op jit(solution)/shard_map/ppermute | solution.py:214
  258.8 15.5 %collective-permute-start.32 = (bf16[4,96,704]{2,1,0:T(8,128)(2,1)S(1)}, bf16[4,96,704]{2,1,0:T(8,128)(2,1)}, u32[]{:S(2)}, u32[]{:S(2)}) collective-permute-start(bf16[4,96,704]{2,1,0:T(8,128)(2,1)S(1)} %dynamic-slice_bitcast_fusion), channel_id=1, source_target_pairs={{0,4},{4,0},{8,12},{12,8},{16,20},{20,16},{24,28},{28,24},{1,5},{5... | collective-permute-start | bytes 1622024 | tf_op jit(solution)/shard_map/ppermute | solution.py:214
  263.2 19.4 %collective-permute-start.34 = (bf16[512,768]{1,0:T(8,128)(2,1)S(1)}, bf16[512,768]{1,0:T(8,128)(2,1)S(1)}, u32[]{:S(2)}, u32[]{:S(2)}) collective-permute-start(bf16[512,768]{1,0:T(8,128)(2,1)S(1)} %copy-done.30), channel_id=1, source_target_pairs={{0,2},{1,3},{2,0},{3,1},{4,6},{5,7},{6,4},{7,5},{8,10},{9,11},{10,... | collective-permute-start | bytes 2359304 | tf_op jit(solution)/shard_map/ppermute | solution.py:214
  275.5 8.3 %collective-permute-start.33 = (bf16[2,96,704]{2,1,0:T(8,128)(2,1)S(1)}, bf16[2,96,704]{2,1,0:T(8,128)(2,1)S(1)}, u32[]{:S(2)}, u32[]{:S(2)}) collective-permute-start(bf16[2,96,704]{2,1,0:T(8,128)(2,1)S(1)} %dynamic-slice_bitcast_fusion.5), channel_id=1, source_target_pairs={{0,8},{4,12},{8,0},{12,4},{16,24},{20,28},{24,16},{28,20},{1,9},{5... | collective-permute-start | bytes 811016 | tf_op jit(solution)/shard_map/ppermute | solution.py:214
  283.8 24.9 %collective-permute-start.39 = (bf16[2,96,768]{2,1,0:T(8,128)(2,1)S(1)}, bf16[2,96,768]{2,1,0:T(8,128)(2,1)S(1)}, u32[]{:S(2)}, u32[]{:S(2)}) collective-permute-start(bf16[2,96,768]{2,1,0:T(8,128)(2,1)S(1)} %dynamic-slice_bitcast_fusion.4), channel_id=1, source_target_pairs={{0,8},{4,12},{8,0},{12,4},{16,24},{20,28},{24,16},{28,20},{1,9},{5... | collective-permute-start | bytes 884744 | tf_op jit(solution)/shard_map/ppermute | solution.py:214
  284.9 24.0 %collective-permute-start.41 = (bf16[192,768]{1,0:T(8,128)(2,1)S(1)}, bf16[192,768]{1,0:T(8,128)(2,1)S(1)}, u32[]{:S(2)}, u32[]{:S(2)}) collective-permute-start(bf16[192,768]{1,0:T(8,128)(2,1)S(1)} %dynamic-slice_bitcast_fusion.3), channel_id=1, source_target_pairs={{0,16},{4,20},{8,24},{12,28},{16,0},{20,4},{24,8},{28,12},{1,17},{... | collective-permute-start | bytes 884744 | tf_op jit(solution)/shard_map/ppermute | solution.py:214
  288.3 17.9 %collective-permute-start.35 = (bf16[96,704]{1,0:T(8,128)(2,1)S(1)}, bf16[96,704]{1,0:T(8,128)(2,1)S(1)}, u32[]{:S(2)}, u32[]{:S(2)}) collective-permute-start(bf16[96,704]{1,0:T(8,128)(2,1)S(1)} %dynamic-slice_bitcast_fusion.11), channel_id=1, source_target_pairs={{0,16},{4,20},{8,24},{12,28},{16,0},{20,4},{24,8},{28,12},{1,17},{... | collective-permute-start | bytes 405512 | tf_op jit(solution)/shard_map/ppermute | solution.py:214
  306.9 12.9 %collective-permute-start.36 = (f32[24,704]{1,0:T(8,128)S(1)}, f32[24,704]{1,0:T(8,128)S(1)}, u32[]{:S(2)}, u32[]{:S(2)}) collective-permute-start(f32[24,704]{1,0:T(8,128)S(1)} %get-tuple-element.170), channel_id=1, source_target_pairs={{0,1},{1,0},{2,3},{3,2},{4,5},{5,4},{6,7},{7,6},{8,9},{9,8},{10,11... | collective-permute-start | bytes 202760 | tf_op jit(solution)/shard_map/ppermute | solution.py:214
  306.9 14.9 %collective-permute-start.37 = (f32[24,704]{1,0:T(8,128)S(1)}, f32[24,704]{1,0:T(8,128)S(1)}, u32[]{:S(2)}, u32[]{:S(2)}) collective-permute-start(f32[24,704]{1,0:T(8,128)S(1)} %get-tuple-element.169), channel_id=1, source_target_pairs={{0,2},{1,3},{2,0},{3,1},{4,6},{5,7},{6,4},{7,5},{8,10},{9,11},{10,... | collective-permute-start | bytes 202760 | tf_op jit(solution)/shard_map/ppermute | solution.py:214
  307.4 14.4 %collective-permute-start.38 = (f32[24,704]{1,0:T(8,128)S(1)}, f32[24,704]{1,0:T(8,128)S(1)}, u32[]{:S(2)}, u32[]{:S(2)}) collective-permute-start(f32[24,704]{1,0:T(8,128)S(1)} %get-tuple-element.168), channel_id=1, source_target_pairs={{0,3},{1,2},{2,1},{3,0},{4,7},{5,6},{6,5},{7,4},{8,11},{9,10},{10,... | collective-permute-start | bytes 202760 | tf_op jit(solution)/shard_map/ppermute | solution.py:214
  308.9 10.2 %collective-permute-start.40 = (bf16[96,768]{1,0:T(8,128)(2,1)S(1)}, bf16[96,768]{1,0:T(8,128)(2,1)S(1)}, u32[]{:S(2)}, u32[]{:S(2)}) collective-permute-start(bf16[96,768]{1,0:T(8,128)(2,1)S(1)} %dynamic-slice_bitcast_fusion.10), channel_id=1, source_target_pairs={{0,16},{4,20},{8,24},{12,28},{16,0},{20,4},{24,8},{28,12},{1,17},{... | collective-permute-start | bytes 442376 | tf_op jit(solution)/shard_map/ppermute | solution.py:214
  319.2 6.9 %collective-permute-start.42 = (f32[24,1536]{1,0:T(8,128)S(1)}, f32[24,1536]{1,0:T(8,128)S(1)}, u32[]{:S(2)}, u32[]{:S(2)}) collective-permute-start(f32[24,1536]{1,0:T(8,128)S(1)} %get-tuple-element.158), channel_id=1, source_target_pairs={{0,1},{1,0},{2,3},{3,2},{4,5},{5,4},{6,7},{7,6},{8,9},{9,8},{10,11... | collective-permute-start | bytes 442376 | tf_op jit(solution)/shard_map/ppermute | solution.py:214
  319.2 6.8 %collective-permute-start.43 = (f32[24,1536]{1,0:T(8,128)S(1)}, f32[24,1536]{1,0:T(8,128)S(1)}, u32[]{:S(2)}, u32[]{:S(2)}) collective-permute-start(f32[24,1536]{1,0:T(8,128)S(1)} %get-tuple-element.157), channel_id=1, source_target_pairs={{0,2},{1,3},{2,0},{3,1},{4,6},{5,7},{6,4},{7,5},{8,10},{9,11},{10,... | collective-permute-start | bytes 442376 | tf_op jit(solution)/shard_map/ppermute | solution.py:214
  319.8 8.4 %collective-permute-start.44 = (f32[24,1536]{1,0:T(8,128)S(1)}, f32[24,1536]{1,0:T(8,128)S(1)}, u32[]{:S(2)}, u32[]{:S(2)}) collective-permute-start(f32[24,1536]{1,0:T(8,128)S(1)} %get-tuple-element.156), channel_id=1, source_target_pairs={{0,3},{1,2},{2,1},{3,0},{4,7},{5,6},{6,5},{7,4},{8,11},{9,10},{10,... | collective-permute-start | bytes 442376 | tf_op jit(solution)/shard_map/ppermute | solution.py:214
  (45 other events, 359.8 us)

commit v3 on v2

--- a/solution.py
+++ b/solution.py
@@ -372,36 +372,43 @@
     )(me, *pieces, x_all)
 
 
-def feed_kernel(
-    me_ref, *refs, n, tile, ids
-):
-    count = len(ids[0])
-    got, left, right, refs = refs[:n], refs[n : n + count], refs[n + count : n + 2 * count], refs[n + 2 * count :]
-    x_ref, g_ref, vec_ref = refs[:3]
-    h_ref, act_ref, gu_ref, even_ref, odd_ref, x_two_ref, sum_ref, out_w_ref, down_ref, up_ref = refs[3:]
+def feed_kernel(me_ref, *refs, n, base, tile, ids):
+    got, refs = refs[:n], refs[n:]
     me = me_ref[0]
     i = pl.program_id(0)
+    if base:
+        count = len(ids[0])
+        left, right, refs = refs[:count], refs[count : 2 * count], refs[2 * count :]
+        x_ref, g_ref, vec_ref = refs[:3]
+        h_ref, act_ref, gu_ref, low_ref, high_ref, sum_ref, out_w_ref, up_ref, down_ref = refs[3:]
+    else:
+        x_ref, g_ref, vec_ref, out_w_ref, up_ref, down_ref, sum_in_ref = refs[:7]
+        h_ref, act_ref, gu_ref, low_ref, high_ref, sum_ref, x_two_ref = refs[10:]
     part = up_ref.shape[1]
     width = got[0].shape[1]
 
     @pl.when(i == 0)
     def _():
-        sum_ref[...] = jnp.zeros_like(sum_ref)
-        for first, pieces, held in ((0, left, ids[0]), (part // 2, right, ids[1])):
-
-            def put(k, where, rows, first=first):
-                (out_w_ref, up_ref, down_ref)[k][where, first : first + part // 2] = rows
-
-            place(pieces, held, me_ref[1], 3, put)
+        if base:
+            sum_ref[...] = jnp.zeros_like(sum_ref)
+            for first, pieces, held in ((0, left, ids[0]), (part // 2, right, ids[1])):
+
+                def put(k, where, rows, first=first):
+                    (out_w_ref, up_ref, down_ref)[k][where, first : first + part // 2] = rows
+
+                place(pieces, held, me_ref[1], 3, put)
+        else:
+            sum_ref[...] = sum_in_ref[...]
 
     x_two = x_ref[0].astype(F32) + vec_ref[4:5, :]
     for p in range(n):
         own = pl.ds(pl.multiple_of((me ^ p) * width, width), width)
         x_two = x_two + dot_tn(got[p][0], out_w_ref[own, :])
-
-    @pl.when(i == 0)
-    def _():
-        x_two_ref[...] = x_two
+    if not base:
+
+        @pl.when(i == 0)
+        def _():
+            x_two_ref[...] = x_two
 
     normed, _ = normed_parts(x_two)
     h = (normed * vec_ref[2:3, :] + vec_ref[3:4, :]).astype(BF16)
@@ -420,83 +427,71 @@
         total = term if total is None else total + term
     total = total.astype(BF16)
 
-    @pl.when(i % 2 == 0)
+    @pl.when(i == 0)
     def _():
-        even_ref[0] = total
-
-    @pl.when(i % 2 == 1)
+        low_ref[...] = total
+
+    @pl.when(i == 1)
     def _():
-        odd_ref[0] = total
-
-
-def feed(me, got, left, right, ids, x_all, g_all, vecs):
-    n, _, dm = x_all.shape
-    block = g_all.shape[1]
-    part = 2 * left[0].shape[2]
+        high_ref[...] = total
+
+
+def feed(me, got, x_all, g_all, vecs, base, weights, ids=None, held=()):
+    n, block, dm = x_all.shape
+    part = dm if base else weights[1].shape[1]
     width = got[0].shape[1]
 
     def whole(shape):
         return pl.BlockSpec(shape, lambda i, me: (0,) * len(shape))
 
     def one(width):
-        return pl.BlockSpec((1, block, width), lambda i, me: (i, 0, 0))
-
-    def half(width):
-        return pl.BlockSpec((1, block, width), lambda i, me: (i // 2, 0, 0))
+        return pl.BlockSpec((1, block, width), lambda i, me: (i + base, 0, 0))
 
     def piece(p):
-        return pl.BlockSpec((1, width, block), lambda i, me: (i ^ p, 0, 0))
-
+        return pl.BlockSpec((1, width, block), lambda i, me: ((i + base) ^ p, 0, 0))
+
+    if base:
+        part = 2 * weights[0][0].shape[2]
+        weights = [*weights[0], *weights[1]]
     wide = jax.ShapeDtypeStruct((n, block, dm), BF16)
-    pair = jax.ShapeDtypeStruct((n // 2, block, dm), BF16)
     hidden = jax.ShapeDtypeStruct((n, block, part), BF16)
+    low = jax.ShapeDtypeStruct((block, dm), BF16)
+    outs = [wide, hidden, hidden, low, low, jax.ShapeDtypeStruct((8, part), F32)]
+    specs = [one(dm), one(part), one(part)] + [whole(o.shape) for o in outs[3:]]
+    more = [(dm, dm), (dm, part), (part, dm)] if base else []
+    outs += [jax.ShapeDtypeStruct(m, BF16) for m in more] or [jax.ShapeDtypeStruct((block, dm), F32)]
+    specs += [whole(o.shape) for o in outs[6:]]
+    args = [*got]
+    ins = [piece(p) for p in range(n)]
+    if base:
+        args += [*weights, x_all, g_all, vecs]
+        ins += [whole(a.shape) for a in weights] + [one(dm), one(dm), whole(vecs.shape)]
+        alias = {}
+    else:
+        args += [x_all, g_all, vecs, *weights, *held]
+        ins += [one(dm), one(dm)] + [whole(a.shape) for a in (vecs, *weights, held[0])]
+        ins += [pl.BlockSpec(memory_space=pl.ANY)] * 3
+        alias = {len(args) - 3 + k + 1: k for k in range(3)}
     return pl.pallas_call(
-        functools.partial(feed_kernel, n=n, tile=256 if part % 256 == 0 else part, ids=ids),
-        grid_spec=pltpu.PrefetchScalarGridSpec(
-            num_scalar_prefetch=1,
-            grid=(n,),
-            in_specs=[piece(p) for p in range(n)]
-            + [whole(a.shape) for a in (*left, *right)]
-            + [one(dm), one(dm), whole(vecs.shape)],
-            out_specs=[
-                one(dm),
-                one(part),
-                one(part),
-                half(dm),
-                half(dm),
-                whole((block, dm)),
-                whole((8, part)),
-                whole((dm, dm)),
-                whole((part, dm)),
-            ],
-            scratch_shapes=[pltpu.VMEM((dm, part), BF16)],
-        ),
-        out_shape=[
-            wide,
-            hidden,
-            hidden,
-            pair,
-            pair,
-            jax.ShapeDtypeStruct((block, dm), F32),
-            jax.ShapeDtypeStruct((8, part), F32),
-            jax.ShapeDtypeStruct((dm, dm), BF16),
-            jax.ShapeDtypeStruct((part, dm), BF16),
-        ],
+        functools.partial(feed_kernel, n=n, base=base, tile=256 if part % 256 == 0 else part, ids=ids),
+        grid_spec=pltpu.PrefetchScalarGridSpec(num_scalar_prefetch=1, grid=(2,), in_specs=ins, out_specs=specs),
+        out_shape=outs,
+        input_output_aliases=alias,
         compiler_params=pltpu.CompilerParams(vmem_limit_bytes=48 * 1024 * 1024),
         cost_estimate=pl.CostEstimate(
-            flops=15 * 1000**3, bytes_accessed=16 * 1000**2, transcendentals=3 * 1000**2
+            flops=9 * 1000**3, bytes_accessed=16 * 1000**2, transcendentals=3 * 1000**2
         ),
-        name="feed",
-    )(me, *got, *left, *right, x_all, g_all, vecs)
+        name="feed_far" if base else "feed_near",
+    )(me, *args)
 
 
 def turn_kernel(me_ref, *refs, n):
     got, refs = refs[:n], refs[n:]
-    keep_ref, far_ref, x_two_ref, g_ref, out_w_ref, vec_ref = refs[:6]
-    gos, (gx_ref, d_out_ref, sum_ref) = refs[6 : 6 + n], refs[6 + n :]
+    keep_ref, near_ref, far_ref, x_two_ref, g_ref, out_w_ref, vec_ref = refs[:7]
+    gos, (gx_ref, d_out_ref, sum_ref) = refs[7 : 7 + n], refs[7 + n :]
     me = me_ref[0]
     width = got[0].shape[1]
-    gh = keep_ref[...].astype(F32) + far_ref[...].astype(F32)
+    gh = keep_ref[...].astype(F32) + near_ref[...].astype(F32) + far_ref[...].astype(F32)
     normed, inv_std = normed_parts(x_two_ref[...])
     g = g_ref[...].astype(F32)
     gx = g + normalize_back(gh, normed, inv_std, vec_ref[2:3, :])
@@ -512,7 +507,7 @@
     sum_ref[3:4, :] = jnp.sum(g, 0, keepdims=True)
 
 
-def turn(me, got, keep, far, x_two, g, out_w, vecs):
+def turn(me, got, keep, near, far, x_two, g, out_w, vecs):
     n = len(got)
     _, width, block = got[0].shape
     dm = out_w.shape[1]
@@ -534,14 +529,14 @@
             num_scalar_prefetch=1,
             grid=(1,),
             in_specs=[piece(p) for p in range(n)]
-            + [whole(a.shape) for a in (keep, far, x_two, g, out_w, vecs)],
+            + [whole(a.shape) for a in (keep, near, far, x_two, g, out_w, vecs)],
             out_specs=[whole(o.shape) for o in outs],
         ),
         out_shape=outs,
         compiler_params=pltpu.CompilerParams(vmem_limit_bytes=48 * 1024 * 1024),
         cost_estimate=pl.CostEstimate(flops=3 * 1000**3, bytes_accessed=8 * 1000**2, transcendentals=0),
         name="turn",
-    )(me, *got, keep, far, x_two, g, out_w, vecs)
+    )(me, *got, keep, near, far, x_two, g, out_w, vecs)
 
 
 def leave_kernel(
@@ -731,56 +726,71 @@
     two = jnp.concatenate([pieces[:, first:start], pieces[:, start + lanes :], w_down], 0)
     left, right = two[:, : dm // 2], two[:, dm // 2 :]
 
-    ones, lefts = [one[None]], [left[None]]
-    g_far = None
+    turned = masks[:-2] + masks[:-3:-1]
+    ones, lefts, rights = [one[None]], [left[None]], [right[None]]
     for step, mask in enumerate(masks):
         got = swap(jnp.concatenate(ones, 0), "dp", nd, mask)
-        if step == 1:
+        if step == len(masks) - 2:
             got, x_far = lax.optimization_barrier((got, x_far))
             g_far = swap(tie(g, x_far), "seq", ns, far)
-        if step > 0:
-            lefts.append(swap(tie(jnp.concatenate(lefts, 0), got), "dp", nd, masks[step - 1]))
+            lefts[0], rights[0] = tie(lefts[0], got), tie(rights[0], got)
         ones.append(got)
-    lefts.append(swap(tie(jnp.concatenate(lefts, 0), ones[-1]), "dp", nd, masks[-1]))
-    rights = [right[None]]
-    turned = masks[:-2] + masks[:-3:-1]
-    for step, mask in enumerate(turned):
-        rights.append(swap(tie(jnp.concatenate(rights, 0), lefts[min(step + 1, len(masks) - 1)]), "dp", nd, mask))
+
+    def onward(step):
+        for parts, order in ((lefts, masks), (rights, turned)):
+            parts.append(swap(jnp.concatenate(parts, 0), "dp", nd, order[step]))
+
+    for step in range(len(masks) - 2):
+        onward(step)
     parts = {0: x_own, far: x_far}
-    g_parts = {0: g, far: g_far}
     for mask in bits_of(ns)[-2::-1]:
         for p in list(parts):
             parts[p | mask] = swap(parts[p], "seq", ns, mask)
+    x_all = jnp.stack([parts[p] for p in range(ns)])
+
+    ones, ids = settle(ones, d, nd, masks, 1)
+    ones[-1], x_all = lax.optimization_barrier((ones[-1], x_all))
+    qkv, w_qkv, vecs = enter(me, ones, ids, x_all, width)
+    qkv, g_far, lefts[-1], rights[-1] = lax.optimization_barrier((qkv, g_far, lefts[-1], rights[-1]))
+    onward(len(masks) - 2)
+    g_parts = {0: g, far: g_far}
+    for mask in bits_of(ns)[-2::-1]:
+        for p in list(g_parts):
             g_parts[p | mask] = swap(g_parts[p], "seq", ns, mask)
-    x_all = jnp.stack([parts[p] for p in range(ns)])
-    g_all = jnp.stack([g_parts[p] for p in range(ns)])
-
-    ones, ids = settle(ones, d, nd, masks, 1)
-    ones[-1], x_all, g_all = lax.optimization_barrier((ones[-1], x_all, g_all))
-    qkv, w_qkv, vecs = enter(me, ones, ids, x_all, width)
-    qkv, *rights[1:-1] = lax.optimization_barrier((qkv, *rights[1:-1]))
     o_low, o_full, lse = attend(me, qkv, seg_row, seg_col, heads, hd)
     o_got = spread_seq(o_low, ns)
+    lefts[-1], rights[-1], g_parts[ns - 1] = lax.optimization_barrier((lefts[-1], rights[-1], g_parts[ns - 1], o_low))[:3]
+    onward(len(masks) - 1)
+    g_all = jnp.stack([g_parts[p] for p in range(ns)])
     lefts, left_ids = settle(lefts, d, nd, masks, 3)
     rights, right_ids = settle(rights, d, nd, turned, 3)
     ids = (left_ids, right_ids)
-    h_two, act, gu, even, odd, x_two, sums_up, w_out_all, w_down_own = feed(
-        me, o_got, lefts, rights, ids, x_all, g_all, vecs
+    h_two, act, gu, gh_two, gh_three, sums_up, *weights = feed(
+        me, o_got, x_all, g_all, vecs, 2, (lefts, rights), ids
     )
-    keep, sent, got = collect_pairs(even, odd, ns)
-    act, gu, h_two = lax.optimization_barrier((act, gu, h_two, sent))[:3]
+    w_out_all, _, w_down_own = weights
+    sent = add_low(gh_two, swap(gh_three, "seq", ns, 1))
+    far_got = swap(sent, "seq", ns, 2)
+    h_two, act, gu, sums_up = lax.optimization_barrier((h_two, act, gu, sums_up, sent))[:4]
+    h_two, act, gu, gh_zero, gh_one, sums_up, x_two = feed(
+        me, o_got, x_all, g_all, vecs, 0, weights, None, (sums_up, h_two, act, gu)
+    )
+    near_got = swap(gh_one, "seq", ns, 1)
     d_down = jnp.einsum("nbk,nbc->kc", act, g_all, preferred_element_type=F32).astype(BF16)
     d_up = jnp.einsum("nbk,nbc->kc", h_two, gu, preferred_element_type=F32).astype(BF16)
     feeds = jnp.concatenate([d_up.reshape(nd, size, part), d_down.reshape(nd, ff_rows, dm)], 1)
     feed_keep, feed_sent = halves(feeds, d, nd, 1)
     feed_got = swap(feed_sent, "dp", nd, 1)
-    got, feed_sent = lax.optimization_barrier((got, feed_sent))
-    out_part = jnp.einsum("nbk,kc->nbc", act, w_down_own, preferred_element_type=F32).astype(BF16)
-    *gos, gx_two, d_out, sums_two = turn(me, o_got, keep, got, x_two, g, w_out_all, vecs)
+    far_got, feed_sent = lax.optimization_barrier((far_got, feed_sent))
+    *gos, gx_two, d_out, sums_two = turn(me, o_got, gh_zero, near_got, far_got, x_two, g, w_out_all, vecs)
     go_got = [gos[0]] + [swap(gos[p], "seq", ns, p) for p in range(1, ns)]
     outs_keep, outs_sent = halves(d_out.reshape(nd, size, dm), d, nd, 1)
     outs_got = swap(outs_sent, "dp", nd, 1)
-    out_keep, _, out_got = collect_pairs(out_part[::2], out_part[1::2], ns, (go_got[-1],))
+    act = tie(act, gos[0])
+    out_parts = [dot_nn(act[p], w_down_own).astype(BF16) for p in range(ns)]
+    out_sent = add_low(out_parts[2], swap(out_parts[3], "seq", ns, 1))
+    out_near = swap(out_parts[1], "seq", ns, 1)
+    out_far = swap(tie(out_sent, go_got[-1]), "seq", ns, 2)
 
     go_all = jnp.stack(go_got)
     go_all, feed_got = lax.optimization_barrier((go_all, feed_got))
@@ -788,20 +798,28 @@
     feed_keep, feed_sent = halves(feeds, d >> 1, nd // 2, 1)
     feed_got = swap(feed_sent, "dp", nd, 2)
     grads = attend_back(me, qkv, go_all, o_full, lse, seg_row, seg_col, heads, hd)
-    grads, out_got, outs_got, feed_got = lax.optimization_barrier((grads, out_got, outs_got, feed_got))
-    feeds = add_low(feed_keep, feed_got)
-    outs = add_low(outs_keep, outs_got)
-    out = out_keep.astype(F32) + out_got.astype(F32) + x_two + vecs[5:6]
+    grads, out_far, outs_got, feed_got = lax.optimization_barrier((grads, out_far, outs_got, feed_got))
+    feed_keep, feed_sent = halves(add_low(feed_keep, feed_got), d >> 2, nd // 4, 1)
+    feed_got = swap(feed_sent, "dp", nd, 4)
+    outs_keep, outs_sent = halves(add_low(outs_keep, outs_got), d >> 1, nd // 2, 1)
+    outs_got = swap(outs_sent, "dp", nd, 2)
     even, odd, blob = leave(me, x_all, grads, w_qkv, vecs, sums_two, sums_up)
     keep, sent, got = collect_pairs(even, odd, ns)
     blob_keep, blob_sent = halves(blob.reshape(nd, size, first), d, nd, 1)
     blob_got = swap(tie(blob_sent, sent), "dp", nd, 1)
+    blob_got, feed_got, outs_got = lax.optimization_barrier((blob_got, feed_got, outs_got))
     blob = add_low(blob_keep, blob_got)
     blob_keep, blob_sent = halves(blob, d >> 1, nd // 2, 1)
     blob_got = swap(blob_sent, "dp", nd, 2)
-    blob_got, got, feeds, outs = lax.optimization_barrier((blob_got, got, feeds, outs))
+    feeds = add_low(feed_keep, feed_got, F32 if nd == 8 else BF16)
+    outs = add_low(outs_keep, outs_got)
+    if nd > 8:
+        feeds = collect_dp(feeds, d >> 3, nd // 8, shift=3)
+    outs = collect_dp(outs, d >> 2, nd // 4, shift=2)
+    blob_got, got = lax.optimization_barrier((blob_got, got))
     blob = add_low(blob_keep, blob_got)
     blob = collect_dp(blob, d >> 2, nd // 4, shift=2)
+    out = out_parts[0].astype(F32) + out_near.astype(F32) + out_far.astype(F32) + x_two + vecs[5:6]
     trades = trade_seq(blob.reshape(ns, rows, first), s, ns)
     sum_up_bias = blob[:ff_rows, 3 * width + 8]
     gh_one = keep.astype(F32) + got.astype(F32)
@@ -809,8 +827,7 @@
     grad_x = gx_two + normalize_back(gh_one, n_own, inv_own, vecs[0:1])
     sum_q, sum_k, sum_v, vec_sum = finish(me, trades, width)
     vec_sum = vec_sum.T
-    outs = collect_dp(outs, d >> 1, nd // 2, shift=1)
-    feeds = collect_dp(feeds, d >> 2, nd // 4, shift=2)
+    feeds = feeds.reshape(size + ff_rows, dm)
     sum_down = feeds[size:]
     both = jnp.concatenate([outs, feeds[:size]], 1).reshape(ns, rows, dm + part)
     both = trade_seq(both, s, ns)

time: 336 us -> 291 us (0.87)
  waiting for transfers between devices: 125 us -> 82.2 us
  other arithmetic: 31.7 us -> 22.5 us
  Pallas kernels: 95.2 us -> 103 us
    ppermute x45 -> x47, waiting for transfers between devices: 125 us -> 82.2 us  [swap(): return lax.ppermute(value, axis, [(i, i ^ mask) for i in range(size)])]
    pallas_call x1 -> x2, Pallas kernels: 23.2 us -> 28.1 us  [feed(): pl.pallas_call(functools.partial(feed_kernel, n=n, base=base, tile=256 if...]
    convert_element_type x3 -> x1, other arithmetic: 5.04 us -> 0.22 us  [collect_pairs(): (even[i].astype(F32) + got[i].astype(F32)).astype(BF16)]
    ppermute x45 -> x47, starting transfers between devices: 42.4 us -> 43.7 us  [swap(): return lax.ppermute(value, axis, [(i, i ^ mask) for i in range(size)])]
    unnamed x97 -> x123, local copies, waits for them, and re-layouts: 6.57 us -> 7.79 us
  transfers between devices with their start and end apart: 45 -> 47, of which waited for: 24 -> 22; matrix products, arithmetic and copies ran while one was open for 14% -> 13% of each run, Pallas kernels for 12% -> 26%
where the time goes in v3:
time: 291 us; the launch traced here: 287 us
  Pallas kernels  103 us (35%)
  waiting for transfers between devices  82.2 us (28%)
  starting transfers between devices  43.7 us (15%)
  local copies, waits for them, and re-layouts  23 us (8%)
  other arithmetic  22.5 us (8%)
  matrix products  10.6 us (4%)
    ppermute x47, waiting for transfers between devices, swap(): return lax.ppermute(value, axis, [(i, i ^ mask) for i in range(size)])  82.2 us
    ppermute x47, starting transfers between devices, swap(): return lax.ppermute(value, axis, [(i, i ^ mask) for i in range(size)])  43.7 us
    pallas_call x2, Pallas kernels, feed(): pl.pallas_call(functools.partial(feed_kernel, n=n, base=base, tile=256 if...  28.1 us
    pallas_call x1, Pallas kernels, attend_back(): pl.pallas_call(functools.partial(attend_back_kernel, heads=heads, hd=hd),...  27.1 us
    pallas_call x1, Pallas kernels, attend(): pl.pallas_call(functools.partial(attend_kernel, heads=heads, hd=hd), grid...  17.9 us
    pallas_call x1, Pallas kernels, leave(): pl.pallas_call(leave_kernel, grid_spec=pltpu.PrefetchScalarGridSpec(num_s...  12.8 us
    pallas_call x1, Pallas kernels, turn(): pl.pallas_call(functools.partial(turn_kernel, n=n), grid_spec=pltpu.Prefe...  7.96 us
    unnamed x123, local copies, waits for them, and re-layouts  7.79 us
  transfers between devices with their start and end apart: 47, of which 22 were waited for; matrix products, arithmetic and copies ran while one was open for 13% of the time, Pallas kernels for 26%

profile of v3, /device:TPU:0, one launch (start us, length us, event | category | flops | bytes accessed | tf_op | source)
XLA Modules:
  0.0 286.6 jit_solution(10893950326334991173)
XLA Ops:
  6.8 2.4 collective-permute-start
  10.0 1.7 collective-permute-start.5
  12.9 3.1 %collective-permute-done.1 = bf16[24,2368]{1,0:T(8,128)(2,1)S(1)} collective-permute-done((bf16[24,2368]{1,0:T(8,128)(2,1)S(1)}, bf16[24,2368]{1,0:T(8,128)(2,1)S(1)}, u32[]{:S(2)}, u32[]{:S(2)}) %collective-permute-start.1) | collective-permute-done | bytes 113696 | tf_op jit(solution)/shard_map/ppermute | solution.py:214
  17.7 3.0 %collective-permute-start.3 = (bf16[1,96,704]{2,1,0:T(8,128)(2,1)S(1)}, bf16[1,96,704]{2,1,0:T(8,128)(2,1)S(1)}, u32[]{:S(2)}, u32[]{:S(2)}) collective-permute-start(bf16[1,96,704]{2,1,0:T(8,128)(2,1)S(1)} %fusion.41.refs_0_), channel_id=1, source_target_pairs={{0,16},{4,20},{8,24},{12,28},{16,0},{20,4},{24,8},{28,12},{1,17},{... | collective-permute-start | bytes 405512 | tf_op jit(solution)/shard_map/ppermute | solution.py:214
  20.7 7.2 %collective-permute-done.3.refs_1_ = bf16[1,96,704]{2,1,0:T(8,128)(2,1)S(1)} collective-permute-done((bf16[1,96,704]{2,1,0:T(8,128)(2,1)S(1)}, bf16[1,96,704]{2,1,0:T(8,128)(2,1)S(1)}, u32[]{:S(2)}, u32[]{:S(2)}) %collective-permute-start.3) | collective-permute-done | bytes 135200 | tf_op jit(solution)/shard_map/ppermute | solution.py:214
  29.8 6.6 %collective-permute-done.4.refs_2_ = bf16[2,96,704]{2,1,0:T(8,128)(2,1)S(1)} collective-permute-done((bf16[2,96,704]{2,1,0:T(8,128)(2,1)S(1)}, bf16[2,96,704]{2,1,0:T(8,128)(2,1)S(1)}, u32[]{:S(2)}, u32[]{:S(2)}) %collective-permute-start.4) | collective-permute-done | bytes 270368 | tf_op jit(solution)/shard_map/ppermute | solution.py:214
  42.3 1.6 collective-permute-start.9
  43.9 3.2 %collective-permute-start.10 = (bf16[1,288,384]{2,1,0:T(8,128)(2,1)}, bf16[1,288,384]{2,1,0:T(8,128)(2,1)S(1)}, u32[]{:S(2)}, u32[]{:S(2)}) collective-permute-start(bf16[1,288,384]{2,1,0:T(8,128)(2,1)} %get-tuple-element.92.refs_4_), channel_id=1, source_target_pairs={{0,16},{4,20},{8,24},{12,28},{16,0},{20,4},{24,8},{28,12},{1,17},{... | collective-permute-start | bytes 663560 | tf_op jit(solution)/shard_map/ppermute | solution.py:214
  47.2 1.7 pad_maximum_fusion.refs_4_.refs_12_.x_ref
  48.9 4.7 %collective-permute-done.6.refs_3_ = bf16[4,96,704]{2,1,0:T(8,128)(2,1)} collective-permute-done((bf16[4,96,704]{2,1,0:T(8,128)(2,1)}, bf16[4,96,704]{2,1,0:T(8,128)(2,1)}, u32[]{:S(2)}, u32[]{:S(2)}) %collective-permute-start.6) | collective-permute-done | bytes 540704 | tf_op jit(solution)/shard_map/ppermute | solution.py:214
  53.6 7.0 %enter.1 = (bf16[4,512,576]{2,1,0:T(8,128)(2,1)S(1)}, bf16[768,576]{1,0:T(8,128)(2,1)S(1)}, f32[16,768]{1,0:T(8,128)S(1)}) custom-call(s32[2]{0:T(128)S(1)} %pad_add_fusion.me_ref, bf16[1,96,704]{2,1,0:T(8,128)(2,1)S(1)} %fusion.41.refs_0_, bf16[1,96,704]{2,1,0:T(8,128)(2,1)S(1)} %copy-done.4, bf16[2,96,704]{2,1,0:T(8,128)(2,1)S(1)} %copy-done.6, ...), custom_call_target="tpu_custom_call" | custom-call | flops 5000000000 | bytes 8000000 | tf_op jit(solution)/shard_map/enter/pallas_call | solution.py:355
  63.0 4.0 %collective-permute-done.11.refs_9_ = bf16[1,288,384]{2,1,0:T(8,128)(2,1)S(1)} collective-permute-done((bf16[1,288,384]{2,1,0:T(8,128)(2,1)S(1)}, bf16[1,288,384]{2,1,0:T(8,128)(2,1)S(1)}, u32[]{:S(2)}, u32[]{:S(2)}) %collective-permute-start.11) | collective-permute-done | bytes 221216 | tf_op jit(solution)/shard_map/ppermute | solution.py:214
  69.5 17.9 %attend.1 = (bf16[4,192,512]{2,1,0:T(8,128)(2,1)S(1)}, f32[4,192,512]{2,1,0:T(8,128)S(1)}, f32[4,8,512]{2,1,0:T(8,128)S(1)}) custom-call(s32[2]{0:T(128)S(1)} %pad_add_fusion.me_ref, bf16[4,512,576]{2,1,0:T(8,128)(2,1)S(1)} %get-tuple-element.94.qkv_ref, s32[4,1,512]{2,1,0:T(1,128)S(1)} %maximum_convert_fusion.1.seg_row_ref, ...), custom_call_target="tpu_custom_call" | custom-call | flops 20000000000 | bytes 8000000 | tf_op jit(solution)/shard_map/attend/pallas_call | solution.py:87
  90.8 1.6 collective-permute-start.19
  92.4 15.1 %collective-permute-done.13.refs_2_ = bf16[4,192,512]{2,1,0:T(8,128)(2,1)S(1)} collective-permute-done((bf16[4,192,512]{2,1,0:T(8,128)(2,1)S(1)}, bf16[4,192,512]{2,1,0:T(8,128)(2,1)S(1)}, u32[]{:S(2)}, u32[]{:S(2)}) %collective-permute-start.13) | collective-permute-done | bytes 786464 | tf_op jit(solution)/shard_map/ppermute | solution.py:214
  107.5 1.9 pad_maximum_fusion.1.refs_13_.refs_5_
  110.3 2.2 collective-permute-done.19.refs_7_
  113.4 14.3 %feed_far.1 = (bf16[4,512,768]{2,1,0:T(8,128)(2,1)}, bf16[4,512,768]{2,1,0:T(8,128)(2,1)}, bf16[4,512,768]{2,1,0:T(8,128)(2,1)}, bf16[512,768]{1,0:T(8,128)(2,1)...) custom-call(s32[2]{0:T(128)S(1)} %pad_add_fusion.me_ref, ...), custom_call_target="tpu_custom_call" | custom-call | flops 8999999488 | bytes 16000000 | tf_op jit(solution)/shard_map/feed_far/pallas_call | solution.py:475
  130.4 2.2 add_convert_fusion.3
  132.6 1.5 collective-permute-start.23
  134.2 13.8 %feed_near.1 = (bf16[4,512,768]{2,1,0:T(8,128)(2,1)}, bf16[4,512,768]{2,1,0:T(8,128)(2,1)}, bf16[4,512,768]{2,1,0:T(8,128)(2,1)}, bf16[512,768]{1,0:T(8,128)(2,1...) custom-call(s32[2]{0:T(128)S(1)} %pad_add_fusion.me_ref, ...), custom_call_target="tpu_custom_call", output_to_operand_aliasing={{0}: (12, {}), {1}: (13, {}), {2}: (14, {})} | custom-call | flops 8999999488 | bytes 16000000 | tf_op jit(solution)/shard_map/feed_near/pallas_call | solution.py:475
  148.1 4.9 %bitcast_convert_fusion = bf16[768,768]{1,0:T(8,128)(2,1)S(1)} fusion(bf16[4,512,768]{2,1,0:T(8,128)(2,1)} %get-tuple-element.124, bf16[1,512,768]{2,1,0:T(8,128)(2,1)S(1)} %bitcast.209, bf16[1,512,768]{2,1,0:T(8,128)(2,1)S(1)} %bitcast.206, bf16[1,512,768]{2,1,0:T(8,128)(2,1)S(1)} %bitcast.211, bf16[1,512,768]{2,1,0:T(8,128)(2,1)S(1)} %copy-done.37), kind=kOutput, calls=%fused_computation.8 | convolution fusion | flops 2421227520 | bytes 7471104 | tf_op jit(solution)/shard_map/nbk,nbc->kc/dot_general | solution.py:779
  153.1 2.7 bitcast_convert_fusion.1
  157.2 1.5 collective-permute-start.28
  159.9 8.0 %turn.1 = (bf16[192,512]{1,0:T(8,128)(2,1)S(1)}, bf16[192,512]{1,0:T(8,128)(2,1)S(1)}, bf16[192,512]{1,0:T(8,128)(2,1)S(1)}, bf16[192,512]{1,0:T(8,128)(2,1)S(1)...) custom-call(s32[2]{0:T(128)S(1)} %pad_add_fusion.me_ref, ...), custom_call_target="tpu_custom_call" | custom-call | flops 3000000000 | bytes 8000000 | tf_op jit(solution)/shard_map/turn/pallas_call | solution.py:526
  172.6 3.2 %collective-permute-done.26 = bf16[192,512]{1,0:T(8,128)(2,1)S(1)} collective-permute-done((bf16[192,512]{1,0:T(8,128)(2,1)S(1)}, bf16[192,512]{1,0:T(8,128)(2,1)S(1)}, u32[]{:S(2)}, u32[]{:S(2)}) %collective-permute-start.26) | collective-permute-done | bytes 196640 | tf_op jit(solution)/shard_map/ppermute | solution.py:214
  175.8 3.0 %collective-permute-done.27 = bf16[192,512]{1,0:T(8,128)(2,1)S(1)} collective-permute-done((bf16[192,512]{1,0:T(8,128)(2,1)S(1)}, bf16[192,512]{1,0:T(8,128)(2,1)S(1)}, u32[]{:S(2)}, u32[]{:S(2)}) %collective-permute-start.27) | collective-permute-done | bytes 196640 | tf_op jit(solution)/shard_map/ppermute | solution.py:214
  178.9 7.4 %collective-permute-done.28 = bf16[4,192,768]{2,1,0:T(8,128)(2,1)} collective-permute-done((bf16[4,192,768]{2,1,0:T(8,128)(2,1)}, bf16[4,192,768]{2,1,0:T(8,128)(2,1)}, u32[]{:S(2)}, u32[]{:S(2)}) %collective-permute-start.28) | collective-permute-done | bytes 1179680 | tf_op jit(solution)/shard_map/ppermute | solution.py:214
  186.3 1.7 fusion
  189.8 27.1 %attend_back.1.grad_ref = bf16[4,512,576]{2,1,0:T(8,128)(2,1)S(1)} custom-call(s32[2]{0:T(128)S(1)} %pad_add_fusion.me_ref, bf16[4,512,576]{2,1,0:T(8,128)(2,1)S(1)} %copy-done.19, bf16[4,192,512]{2,1,0:T(8,128)(2,1)S(1)} %pad_maximum_fusion.4.go_ref, f32[4,192,512]{2,1,0:T(8,128)S(1)} %copy-done.24, f32[4,8,512]{2,1,0:T(8,128)S(1)} %copy-done.26, ...), custom_call_target="tpu_custom_call" | custom-call | flops 40000000000 | bytes 12000000 | tf_op jit(solution)/shard_map/attend_back/pallas_call | solution.py:169
  216.9 1.5 copy-done.20
  218.5 12.8 %leave.1 = (bf16[2,512,768]{2,1,0:T(8,128)(2,1)S(1)}, bf16[2,512,768]{2,1,0:T(8,128)(2,1)S(1)}, bf16[768,704]{1,0:T(8,128)(2,1)S(1)}) custom-call(s32[2]{0:T(128)S(1)} %pad_add_fusion.me_ref, bf16[4,512,768]{2,1,0:T(8,128)(2,1)} %copy-done, bf16[4,512,576]{2,1,0:T(8,128)(2,1)} %copy-done.20, bf16[768,576]{1,0:T(8,128)(2,1)S(1)} %copy-done.22, ...), custom_call_target="tpu_custom_call" | custom-call | flops 6000000000 | bytes 10000000 | tf_op jit(solution)/shard_map/leave/pallas_call | solution.py:609
  235.7 1.6 collective-permute-start.34
  237.4 3.0 %collective-permute-start.35 = (bf16[1,192,768]{2,1,0:T(8,128)(2,1)S(1)}, bf16[1,192,768]{2,1,0:T(8,128)(2,1)S(1)}, u32[]{:S(2)}, u32[]{:S(2)}) collective-permute-start(bf16[1,192,768]{2,1,0:T(8,128)(2,1)S(1)} %constant_dynamic-slice_fusion), channel_id=1, source_target_pairs={{0,16},{4,20},{8,24},{12,28},{16,0},{20,4},{24,8},{28,12},{1,17},{... | collective-permute-start | bytes 884744 | tf_op jit(solution)/shard_map/ppermute | solution.py:214
  240.4 1.6 add_bitcast_fusion
  243.2 5.0 %collective-permute-done.36 = bf16[2,96,768]{2,1,0:T(8,128)(2,1)S(1)} collective-permute-done((bf16[2,96,768]{2,1,0:T(8,128)(2,1)S(1)}, bf16[2,96,768]{2,1,0:T(8,128)(2,1)S(1)}, u32[]{:S(2)}, u32[]{:S(2)}) %collective-permute-start.36) | collective-permute-done | bytes 294944 | tf_op jit(solution)/shard_map/ppermute | solution.py:214
  248.2 5.3 %collective-permute-done.35 = bf16[1,192,768]{2,1,0:T(8,128)(2,1)S(1)} collective-permute-done((bf16[1,192,768]{2,1,0:T(8,128)(2,1)S(1)}, bf16[1,192,768]{2,1,0:T(8,128)(2,1)S(1)}, u32[]{:S(2)}, u32[]{:S(2)}) %collective-permute-start.35) | collective-permute-done | bytes 294944 | tf_op jit(solution)/shard_map/ppermute | solution.py:214
  254.0 3.6 %collective-permute-start.37 = (bf16[2,96,704]{2,1,0:T(8,128)(2,1)S(1)}, bf16[2,96,704]{2,1,0:T(8,128)(2,1)S(1)}, u32[]{:S(2)}, u32[]{:S(2)}) collective-permute-start(bf16[2,96,704]{2,1,0:T(8,128)(2,1)S(1)} %dynamic-slice_bitcast_fusion.3), channel_id=1, source_target_pairs={{0,8},{4,12},{8,0},{12,4},{16,24},{20,28},{24,16},{28,20},{1,9},{5... | collective-permute-start | bytes 811016 | tf_op jit(solution)/shard_map/ppermute | solution.py:214
  258.5 4.0 %collective-permute-done.43 = bf16[96,768]{1,0:T(8,128)(2,1)S(1)} collective-permute-done((bf16[96,768]{1,0:T(8,128)(2,1)S(1)}, bf16[96,768]{1,0:T(8,128)(2,1)S(1)}, u32[]{:S(2)}, u32[]{:S(2)}) %collective-permute-start.43) | collective-permute-done | bytes 147488 | tf_op jit(solution)/shard_map/ppermute | solution.py:214
  262.7 1.6 collective-permute-start.45
  264.5 1.5 collective-permute-done.37
  268.1 1.9 fusion.9
  270.0 1.6 collective-permute-done.46
  276.2 1.5 collective-permute-start.41
  278.5 2.1 collective-permute-done.41.refs_2_
  280.6 1.7 collective-permute-done.42.refs_3_
  282.9 1.8 finish.1
  284.6 1.8 slice_reduce_fusion.1
  (274 shorter events, 54.5 us)
Async XLA Ops:
  6.8 6.0 %collective-permute-start = (bf16[24,2368]{1,0:T(8,128)(2,1)S(1)}, bf16[24,2368]{1,0:T(8,128)(2,1)S(1)}, u32[]{:S(2)}, u32[]{:S(2)}) collective-permute-start(bf16[24,2368]{1,0:T(8,128)(2,1)S(1)} %get-tuple-element.177), channel_id=1, source_target_pairs={{0,3},{1,2},{2,1},{3,0},{4,7},{5,6},{6,5},{7,4},{8,11},{9,10},{10,... | collective-permute-start | bytes 341000 | tf_op jit(solution)/shard_map/ppermute | solution.py:214
  9.3 6.7 %collective-permute-start.1 = (bf16[24,2368]{1,0:T(8,128)(2,1)S(1)}, bf16[24,2368]{1,0:T(8,128)(2,1)S(1)}, u32[]{:S(2)}, u32[]{:S(2)}) collective-permute-start(bf16[24,2368]{1,0:T(8,128)(2,1)S(1)} %get-tuple-element.176), channel_id=1, source_target_pairs={{0,2},{1,3},{2,0},{3,1},{4,6},{5,7},{6,4},{7,5},{8,10},{9,11},{10,... | collective-permute-start | bytes 341000 | tf_op jit(solution)/shard_map/ppermute | solution.py:214
  9.9 6.8 %collective-permute-start.2 = (bf16[24,2368]{1,0:T(8,128)(2,1)S(1)}, bf16[24,2368]{1,0:T(8,128)(2,1)S(1)}, u32[]{:S(2)}, u32[]{:S(2)}) collective-permute-start(bf16[24,2368]{1,0:T(8,128)(2,1)S(1)} %get-tuple-element.175), channel_id=1, source_target_pairs={{0,1},{1,0},{2,3},{3,2},{4,5},{5,4},{6,7},{7,6},{8,9},{9,8},{10,11... | collective-permute-start | bytes 341000 | tf_op jit(solution)/shard_map/ppermute | solution.py:214
  10.0 26.5 %collective-permute-start.5 = (bf16[512,768]{1,0:T(8,128)(2,1)S(1)}, bf16[512,768]{1,0:T(8,128)(2,1)S(1)}, u32[]{:S(2)}, u32[]{:S(2)}) collective-permute-start(bf16[512,768]{1,0:T(8,128)(2,1)S(1)} %bitcast.183), channel_id=1, source_target_pairs={{0,2},{1,3},{2,0},{3,1},{4,6},{5,7},{6,4},{7,5},{8,10},{9,11},{10,... | collective-permute-start | bytes 2359304 | tf_op jit(solution)/shard_map/ppermute | solution.py:214
  17.7 10.3 %collective-permute-start.3 = (bf16[1,96,704]{2,1,0:T(8,128)(2,1)S(1)}, bf16[1,96,704]{2,1,0:T(8,128)(2,1)S(1)}, u32[]{:S(2)}, u32[]{:S(2)}) collective-permute-start(bf16[1,96,704]{2,1,0:T(8,128)(2,1)S(1)} %fusion.41.refs_0_), channel_id=1, source_target_pairs={{0,16},{4,20},{8,24},{12,28},{16,0},{20,4},{24,8},{28,12},{1,17},{... | collective-permute-start | bytes 405512 | tf_op jit(solution)/shard_map/ppermute | solution.py:214
  28.0 8.5 %collective-permute-start.4 = (bf16[2,96,704]{2,1,0:T(8,128)(2,1)S(1)}, bf16[2,96,704]{2,1,0:T(8,128)(2,1)S(1)}, u32[]{:S(2)}, u32[]{:S(2)}) collective-permute-start(bf16[2,96,704]{2,1,0:T(8,128)(2,1)S(1)} %pad_maximum_fusion.9), channel_id=1, source_target_pairs={{0,8},{4,12},{8,0},{12,4},{16,24},{20,28},{24,16},{28,20},{1,9},{5... | collective-permute-start | bytes 811016 | tf_op jit(solution)/shard_map/ppermute | solution.py:214
  28.7 18.4 %collective-permute-start.7 = (bf16[512,768]{1,0:T(8,128)(2,1)S(1)}, bf16[512,768]{1,0:T(8,128)(2,1)}, u32[]{:S(2)}, u32[]{:S(2)}) collective-permute-start(bf16[512,768]{1,0:T(8,128)(2,1)S(1)} %bitcast.184), channel_id=1, source_target_pairs={{0,1},{1,0},{2,3},{3,2},{4,5},{5,4},{6,7},{7,6},{8,9},{9,8},{10,11... | collective-permute-start | bytes 2359304 | tf_op jit(solution)/shard_map/ppermute | solution.py:214
  29.8 188.6 %copy-start.9 = (s32[2]{0:T(128)}, s32[2]{0:T(128)S(1)}, u32[]{:S(2)}) copy-start(s32[2]{0:T(128)S(1)} %pad_add_fusion.me_ref) | copy-start | bytes 28
  36.4 10.7 %collective-permute-start.8 = (bf16[512,768]{1,0:T(8,128)(2,1)S(1)}, bf16[512,768]{1,0:T(8,128)(2,1)}, u32[]{:S(2)}, u32[]{:S(2)}) collective-permute-start(bf16[512,768]{1,0:T(8,128)(2,1)S(1)} %collective-permute-done.5), channel_id=1, source_target_pairs={{0,1},{1,0},{2,3},{3,2},{4,5},{5,4},{6,7},{7,6},{8,9},{9,8},{10,11... | collective-permute-start | bytes 2359304 | tf_op jit(solution)/shard_map/ppermute | solution.py:214
  37.6 16.1 %collective-permute-start.6 = (bf16[4,96,704]{2,1,0:T(8,128)(2,1)}, bf16[4,96,704]{2,1,0:T(8,128)(2,1)}, u32[]{:S(2)}, u32[]{:S(2)}) collective-permute-start(bf16[4,96,704]{2,1,0:T(8,128)(2,1)} %pad_maximum_fusion.5), channel_id=1, source_target_pairs={{0,4},{4,0},{8,12},{12,8},{16,20},{20,16},{24,28},{28,24},{1,5},{5... | collective-permute-start | bytes 1622024 | tf_op jit(solution)/shard_map/ppermute | solution.py:214
  42.3 24.8 %collective-permute-start.9 = (bf16[512,768]{1,0:T(8,128)(2,1)S(1)}, bf16[512,768]{1,0:T(8,128)(2,1)S(1)}, u32[]{:S(2)}, u32[]{:S(2)}) collective-permute-start(bf16[512,768]{1,0:T(8,128)(2,1)S(1)} %bitcast.203), channel_id=1, source_target_pairs={{0,2},{1,3},{2,0},{3,1},{4,6},{5,7},{6,4},{7,5},{8,10},{9,11},{10,... | collective-permute-start | bytes 2359304 | tf_op jit(solution)/shard_map/ppermute | solution.py:214
  43.9 19.1 %collective-permute-start.10 = (bf16[1,288,384]{2,1,0:T(8,128)(2,1)}, bf16[1,288,384]{2,1,0:T(8,128)(2,1)S(1)}, u32[]{:S(2)}, u32[]{:S(2)}) collective-permute-start(bf16[1,288,384]{2,1,0:T(8,128)(2,1)} %get-tuple-element.92.refs_4_), channel_id=1, source_target_pairs={{0,16},{4,20},{8,24},{12,28},{16,0},{20,4},{24,8},{28,12},{1,17},{... | collective-permute-start | bytes 663560 | tf_op jit(solution)/shard_map/ppermute | solution.py:214
  47.1 20.0 %collective-permute-start.11 = (bf16[1,288,384]{2,1,0:T(8,128)(2,1)S(1)}, bf16[1,288,384]{2,1,0:T(8,128)(2,1)S(1)}, u32[]{:S(2)}, u32[]{:S(2)}) collective-permute-start(bf16[1,288,384]{2,1,0:T(8,128)(2,1)S(1)} %get-tuple-element.93.refs_8_), channel_id=1, source_target_pairs={{0,16},{4,20},{8,24},{12,28},{16,0},{20,4},{24,8},{28,12},{1,17},{... | collective-permute-start | bytes 663560 | tf_op jit(solution)/shard_map/ppermute | solution.py:214
  67.1 21.1 %collective-permute-start.17 = (bf16[2,288,384]{2,1,0:T(8,128)(2,1)S(1)}, bf16[2,288,384]{2,1,0:T(8,128)(2,1)S(1)}, u32[]{:S(2)}, u32[]{:S(2)}) collective-permute-start(bf16[2,288,384]{2,1,0:T(8,128)(2,1)S(1)} %pad_maximum_fusion.8), channel_id=1, source_target_pairs={{0,4},{4,0},{8,12},{12,8},{16,20},{20,16},{24,28},{28,24},{1,5},{5... | collective-permute-start | bytes 1327112 | tf_op jit(solution)/shard_map/ppermute | solution.py:214
  68.7 19.6 %collective-permute-start.16 = (bf16[2,288,384]{2,1,0:T(8,128)(2,1)S(1)}, bf16[2,288,384]{2,1,0:T(8,128)(2,1)S(1)}, u32[]{:S(2)}, u32[]{:S(2)}) collective-permute-start(bf16[2,288,384]{2,1,0:T(8,128)(2,1)S(1)} %pad_maximum_fusion.7), channel_id=1, source_target_pairs={{0,8},{4,12},{8,0},{12,4},{16,24},{20,28},{24,16},{28,20},{1,9},{5... | collective-permute-start | bytes 1327112 | tf_op jit(solution)/shard_map/ppermute | solution.py:214
  69.5 18.8 %collective-permute-start.18 = (bf16[512,768]{1,0:T(8,128)(2,1)S(1)}, bf16[512,768]{1,0:T(8,128)(2,1)S(1)}, u32[]{:S(2)}, u32[]{:S(2)}) collective-permute-start(bf16[512,768]{1,0:T(8,128)(2,1)S(1)} %collective-permute-done.9), channel_id=1, source_target_pairs={{0,1},{1,0},{2,3},{3,2},{4,5},{5,4},{6,7},{7,6},{8,9},{9,8},{10,11... | collective-permute-start | bytes 2359304 | tf_op jit(solution)/shard_map/ppermute | solution.py:214
  87.5 20.0 %collective-permute-start.13 = (bf16[4,192,512]{2,1,0:T(8,128)(2,1)S(1)}, bf16[4,192,512]{2,1,0:T(8,128)(2,1)S(1)}, u32[]{:S(2)}, u32[]{:S(2)}) collective-permute-start(bf16[4,192,512]{2,1,0:T(8,128)(2,1)S(1)} %get-tuple-element.95.refs_0_), channel_id=1, source_target_pairs={{0,2},{1,3},{2,0},{3,1},{4,6},{5,7},{6,4},{7,5},{8,10},{9,11},{10,... | collective-permute-start | bytes 2359304 | tf_op jit(solution)/shard_map/ppermute | solution.py:214
  88.0 19.5 %collective-permute-start.15 = (bf16[512,768]{1,0:T(8,128)(2,1)S(1)}, bf16[512,768]{1,0:T(8,128)(2,1)S(1)}, u32[]{:S(2)}, u32[]{:S(2)}) collective-permute-start(bf16[512,768]{1,0:T(8,128)(2,1)S(1)} %bitcast.204), channel_id=1, source_target_pairs={{0,1},{1,0},{2,3},{3,2},{4,5},{5,4},{6,7},{7,6},{8,9},{9,8},{10,11... | collective-permute-start | bytes 2359304 | tf_op jit(solution)/shard_map/ppermute | solution.py:214
  88.4 21.9 %collective-permute-start.20 = (bf16[4,288,384]{2,1,0:T(8,128)(2,1)S(1)}, bf16[4,288,384]{2,1,0:T(8,128)(2,1)S(1)}, u32[]{:S(2)}, u32[]{:S(2)}) collective-permute-start(bf16[4,288,384]{2,1,0:T(8,128)(2,1)S(1)} %pad_maximum_fusion.3), channel_id=1, source_target_pairs={{0,8},{4,12},{8,0},{12,4},{16,24},{20,28},{24,16},{28,20},{1,9},{5... | collective-permute-start | bytes 2654216 | tf_op jit(solution)/shard_map/ppermute | solution.py:214
  90.8 21.6 %collective-permute-start.19 = (bf16[4,288,384]{2,1,0:T(8,128)(2,1)S(1)}, bf16[4,288,384]{2,1,0:T(8,128)(2,1)S(1)}, u32[]{:S(2)}, u32[]{:S(2)}) collective-permute-start(bf16[4,288,384]{2,1,0:T(8,128)(2,1)S(1)} %pad_maximum_fusion.2), channel_id=1, source_target_pairs={{0,4},{4,0},{8,12},{12,8},{16,20},{20,16},{24,28},{28,24},{1,5},{5... | collective-permute-start | bytes 2654216 | tf_op jit(solution)/shard_map/ppermute | solution.py:214
  92.4 17.0 %collective-permute-start.12 = (bf16[4,192,512]{2,1,0:T(8,128)(2,1)S(1)}, bf16[4,192,512]{2,1,0:T(8,128)(2,1)S(1)}, u32[]{:S(2)}, u32[]{:S(2)}) collective-permute-start(bf16[4,192,512]{2,1,0:T(8,128)(2,1)S(1)} %get-tuple-element.95.refs_0_), channel_id=1, source_target_pairs={{0,1},{1,0},{2,3},{3,2},{4,5},{5,4},{6,7},{7,6},{8,9},{9,8},{10,11... | collective-permute-start | bytes 2359304 | tf_op jit(solution)/shard_map/ppermute | solution.py:214
  107.5 2.3 collective-permute-start.14
  127.7 2.7 collective-permute-start.21
  132.6 26.1 %collective-permute-start.23 = (bf16[512,768]{1,0:T(8,128)(2,1)}, bf16[512,768]{1,0:T(8,128)(2,1)}, u32[]{:S(2)}, u32[]{:S(2)}) collective-permute-start(bf16[512,768]{1,0:T(8,128)(2,1)} %add_convert_fusion.3), channel_id=1, source_target_pairs={{0,2},{1,3},{2,0},{3,1},{4,6},{5,7},{6,4},{7,5},{8,10},{9,11},{10,... | collective-permute-start | bytes 2359304 | tf_op jit(solution)/shard_map/ppermute | solution.py:214
  153.0 5.7 %collective-permute-start.22 = (bf16[512,768]{1,0:T(8,128)(2,1)}, bf16[512,768]{1,0:T(8,128)(2,1)}, u32[]{:S(2)}, u32[]{:S(2)}) collective-permute-start(bf16[512,768]{1,0:T(8,128)(2,1)} %get-tuple-element.118), channel_id=1, source_target_pairs={{0,1},{1,0},{2,3},{3,2},{4,5},{5,4},{6,7},{7,6},{8,9},{9,8},{10,11... | collective-permute-start | bytes 2359304 | tf_op jit(solution)/shard_map/ppermute | solution.py:214
  157.2 29.1 %collective-permute-start.28 = (bf16[4,192,768]{2,1,0:T(8,128)(2,1)}, bf16[4,192,768]{2,1,0:T(8,128)(2,1)}, u32[]{:S(2)}, u32[]{:S(2)}) collective-permute-start(bf16[4,192,768]{2,1,0:T(8,128)(2,1)} %fusion.16), channel_id=1, source_target_pairs={{0,4},{4,0},{8,12},{12,8},{16,20},{20,16},{24,28},{28,24},{1,5},{5... | collective-permute-start | bytes 3538952 | tf_op jit(solution)/shard_map/ppermute | solution.py:214
  167.8 4.1 %collective-permute-start.25 = (bf16[192,512]{1,0:T(8,128)(2,1)S(1)}, bf16[192,512]{1,0:T(8,128)(2,1)S(1)}, u32[]{:S(2)}, u32[]{:S(2)}) collective-permute-start(bf16[192,512]{1,0:T(8,128)(2,1)S(1)} %get-tuple-element.125), channel_id=1, source_target_pairs={{0,1},{1,0},{2,3},{3,2},{4,5},{5,4},{6,7},{7,6},{8,9},{9,8},{10,11... | collective-permute-start | bytes 589832 | tf_op jit(solution)/shard_map/ppermute | solution.py:214
  168.0 7.7 %collective-permute-start.26 = (bf16[192,512]{1,0:T(8,128)(2,1)S(1)}, bf16[192,512]{1,0:T(8,128)(2,1)S(1)}, u32[]{:S(2)}, u32[]{:S(2)}) collective-permute-start(bf16[192,512]{1,0:T(8,128)(2,1)S(1)} %get-tuple-element.126), channel_id=1, source_target_pairs={{0,2},{1,3},{2,0},{3,1},{4,6},{5,7},{6,4},{7,5},{8,10},{9,11},{10,... | collective-permute-start | bytes 589832 | tf_op jit(solution)/shard_map/ppermute | solution.py:214
  168.5 10.2 %collective-permute-start.27 = (bf16[192,512]{1,0:T(8,128)(2,1)S(1)}, bf16[192,512]{1,0:T(8,128)(2,1)S(1)}, u32[]{:S(2)}, u32[]{:S(2)}) collective-permute-start(bf16[192,512]{1,0:T(8,128)(2,1)S(1)} %get-tuple-element.127), channel_id=1, source_target_pairs={{0,3},{1,2},{2,1},{3,0},{4,7},{5,6},{6,5},{7,4},{8,11},{9,10},{10,... | collective-permute-start | bytes 589832 | tf_op jit(solution)/shard_map/ppermute | solution.py:214
  170.5 18.4 %collective-permute-start.29 = (bf16[512,768]{1,0:T(8,128)(2,1)S(1)}, bf16[512,768]{1,0:T(8,128)(2,1)S(1)}, u32[]{:S(2)}, u32[]{:S(2)}) collective-permute-start(bf16[512,768]{1,0:T(8,128)(2,1)S(1)} %convolution_convert_fusion), channel_id=1, source_target_pairs={{0,1},{1,0},{2,3},{3,2},{4,5},{5,4},{6,7},{7,6},{8,9},{9,8},{10,11... | collective-permute-start | bytes 2359304 | tf_op jit(solution)/shard_map/ppermute | solution.py:214
  171.9 46.5 %collective-permute-start.31 = (bf16[4,96,768]{2,1,0:T(8,128)(2,1)S(1)}, bf16[4,96,768]{2,1,0:T(8,128)(2,1)S(1)}, u32[]{:S(2)}, u32[]{:S(2)}) collective-permute-start(bf16[4,96,768]{2,1,0:T(8,128)(2,1)S(1)} %dynamic-slice_bitcast_fusion.2), channel_id=1, source_target_pairs={{0,4},{4,0},{8,12},{12,8},{16,20},{20,16},{24,28},{28,24},{1,5},{5... | collective-permute-start | bytes 1769480 | tf_op jit(solution)/shard_map/ppermute | solution.py:214
  188.1 30.3 %collective-permute-start.32 = (bf16[2,192,768]{2,1,0:T(8,128)(2,1)S(1)}, bf16[2,192,768]{2,1,0:T(8,128)(2,1)S(1)}, u32[]{:S(2)}, u32[]{:S(2)}) collective-permute-start(bf16[2,192,768]{2,1,0:T(8,128)(2,1)S(1)} %dynamic-slice_bitcast_fusion.1), channel_id=1, source_target_pairs={{0,8},{4,12},{8,0},{12,4},{16,24},{20,28},{24,16},{28,20},{1,9},{5... | collective-permute-start | bytes 1769480 | tf_op jit(solution)/shard_map/ppermute | solution.py:214
  189.1 29.4 %collective-permute-start.30 = (bf16[512,768]{1,0:T(8,128)(2,1)S(1)}, bf16[512,768]{1,0:T(8,128)(2,1)S(1)}, u32[]{:S(2)}, u32[]{:S(2)}) collective-permute-start(bf16[512,768]{1,0:T(8,128)(2,1)S(1)} %add_convert_fusion.2), channel_id=1, source_target_pairs={{0,2},{1,3},{2,0},{3,1},{4,6},{5,7},{6,4},{7,5},{8,10},{9,11},{10,... | collective-permute-start | bytes 2359304 | tf_op jit(solution)/shard_map/ppermute | solution.py:214
  231.3 4.1 %collective-permute-start.33 = (bf16[2,512,768]{2,1,0:T(8,128)(2,1)S(1)}, bf16[2,512,768]{2,1,0:T(8,128)(2,1)S(1)}, u32[]{:S(2)}, u32[]{:S(2)}) collective-permute-start(bf16[2,512,768]{2,1,0:T(8,128)(2,1)S(1)} %get-tuple-element.141), channel_id=1, source_target_pairs={{0,1},{1,0},{2,3},{3,2},{4,5},{5,4},{6,7},{7,6},{8,9},{9,8},{10,11... | collective-permute-start | bytes 4718600 | tf_op jit(solution)/shard_map/ppermute | solution.py:214
  232.6 7.8 %collective-permute-start.24 = (bf16[512,768]{1,0:T(8,128)(2,1)S(1)}, bf16[512,768]{1,0:T(8,128)(2,1)S(1)}, u32[]{:S(2)}, u32[]{:S(2)}) collective-permute-start(bf16[512,768]{1,0:T(8,128)(2,1)S(1)} %convolution_convert_fusion.2), channel_id=1, source_target_pairs={{0,1},{1,0},{2,3},{3,2},{4,5},{5,4},{6,7},{7,6},{8,9},{9,8},{10,11... | collective-permute-start | bytes 2359304 | tf_op jit(solution)/shard_map/ppermute | solution.py:214
  234.1 14.1 %collective-permute-start.36 = (bf16[2,96,768]{2,1,0:T(8,128)(2,1)S(1)}, bf16[2,96,768]{2,1,0:T(8,128)(2,1)S(1)}, u32[]{:S(2)}, u32[]{:S(2)}) collective-permute-start(bf16[2,96,768]{2,1,0:T(8,128)(2,1)S(1)} %dynamic-slice_bitcast_fusion.4), channel_id=1, source_target_pairs={{0,8},{4,12},{8,0},{12,4},{16,24},{20,28},{24,16},{28,20},{1,9},{5... | collective-permute-start | bytes 884744 | tf_op jit(solution)/shard_map/ppermute | solution.py:214
  235.7 17.8 %collective-permute-start.34 = (bf16[4,96,704]{2,1,0:T(8,128)(2,1)S(1)}, bf16[4,96,704]{2,1,0:T(8,128)(2,1)S(1)}, u32[]{:S(2)}, u32[]{:S(2)}) collective-permute-start(bf16[4,96,704]{2,1,0:T(8,128)(2,1)S(1)} %dynamic-slice_bitcast_fusion), channel_id=1, source_target_pairs={{0,4},{4,0},{8,12},{12,8},{16,20},{20,16},{24,28},{28,24},{1,5},{5... | collective-permute-start | bytes 1622024 | tf_op jit(solution)/shard_map/ppermute | solution.py:214
  237.4 16.0 %collective-permute-start.35 = (bf16[1,192,768]{2,1,0:T(8,128)(2,1)S(1)}, bf16[1,192,768]{2,1,0:T(8,128)(2,1)S(1)}, u32[]{:S(2)}, u32[]{:S(2)}) collective-permute-start(bf16[1,192,768]{2,1,0:T(8,128)(2,1)S(1)} %constant_dynamic-slice_fusion), channel_id=1, source_target_pairs={{0,16},{4,20},{8,24},{12,28},{16,0},{20,4},{24,8},{28,12},{1,17},{... | collective-permute-start | bytes 884744 | tf_op jit(solution)/shard_map/ppermute | solution.py:214
  242.0 22.5 %collective-permute-start.38 = (bf16[512,768]{1,0:T(8,128)(2,1)S(1)}, bf16[512,768]{1,0:T(8,128)(2,1)S(1)}, u32[]{:S(2)}, u32[]{:S(2)}) collective-permute-start(bf16[512,768]{1,0:T(8,128)(2,1)S(1)} %fusion.21), channel_id=1, source_target_pairs={{0,2},{1,3},{2,0},{3,1},{4,6},{5,7},{6,4},{7,5},{8,10},{9,11},{10,... | collective-permute-start | bytes 2359304 | tf_op jit(solution)/shard_map/ppermute | solution.py:214
  253.6 8.9 %collective-permute-start.43 = (bf16[96,768]{1,0:T(8,128)(2,1)S(1)}, bf16[96,768]{1,0:T(8,128)(2,1)S(1)}, u32[]{:S(2)}, u32[]{:S(2)}) collective-permute-start(bf16[96,768]{1,0:T(8,128)(2,1)S(1)} %dynamic-slice_bitcast_fusion.5), channel_id=1, source_target_pairs={{0,16},{4,20},{8,24},{12,28},{16,0},{20,4},{24,8},{28,12},{1,17},{... | collective-permute-start | bytes 442376 | tf_op jit(solution)/shard_map/ppermute | solution.py:214
  254.0 12.0 %collective-permute-start.37 = (bf16[2,96,704]{2,1,0:T(8,128)(2,1)S(1)}, bf16[2,96,704]{2,1,0:T(8,128)(2,1)S(1)}, u32[]{:S(2)}, u32[]{:S(2)}) collective-permute-start(bf16[2,96,704]{2,1,0:T(8,128)(2,1)S(1)} %dynamic-slice_bitcast_fusion.3), channel_id=1, source_target_pairs={{0,8},{4,12},{8,0},{12,4},{16,24},{20,28},{24,16},{28,20},{1,9},{5... | collective-permute-start | bytes 811016 | tf_op jit(solution)/shard_map/ppermute | solution.py:214
  262.6 7.4 %collective-permute-start.44 = (f32[24,1536]{1,0:T(8,128)S(1)}, f32[24,1536]{1,0:T(8,128)S(1)}, u32[]{:S(2)}, u32[]{:S(2)}) collective-permute-start(f32[24,1536]{1,0:T(8,128)S(1)} %get-tuple-element.170), channel_id=1, source_target_pairs={{0,1},{1,0},{2,3},{3,2},{4,5},{5,4},{6,7},{7,6},{8,9},{9,8},{10,11... | collective-permute-start | bytes 442376 | tf_op jit(solution)/shard_map/ppermute | solution.py:214
  262.7 7.4 %collective-permute-start.45 = (f32[24,1536]{1,0:T(8,128)S(1)}, f32[24,1536]{1,0:T(8,128)S(1)}, u32[]{:S(2)}, u32[]{:S(2)}) collective-permute-start(f32[24,1536]{1,0:T(8,128)S(1)} %get-tuple-element.171), channel_id=1, source_target_pairs={{0,2},{1,3},{2,0},{3,1},{4,6},{5,7},{6,4},{7,5},{8,10},{9,11},{10,... | collective-permute-start | bytes 442376 | tf_op jit(solution)/shard_map/ppermute | solution.py:214
  264.3 7.4 %collective-permute-start.46 = (f32[24,1536]{1,0:T(8,128)S(1)}, f32[24,1536]{1,0:T(8,128)S(1)}, u32[]{:S(2)}, u32[]{:S(2)}) collective-permute-start(f32[24,1536]{1,0:T(8,128)S(1)} %get-tuple-element.172), channel_id=1, source_target_pairs={{0,3},{1,2},{2,1},{3,0},{4,7},{5,6},{6,5},{7,4},{8,11},{9,10},{10,... | collective-permute-start | bytes 442376 | tf_op jit(solution)/shard_map/ppermute | solution.py:214
  266.1 8.8 %collective-permute-start.39 = (bf16[96,704]{1,0:T(8,128)(2,1)S(1)}, bf16[96,704]{1,0:T(8,128)(2,1)S(1)}, u32[]{:S(2)}, u32[]{:S(2)}) collective-permute-start(bf16[96,704]{1,0:T(8,128)(2,1)S(1)} %dynamic-slice_bitcast_fusion.6), channel_id=1, source_target_pairs={{0,16},{4,20},{8,24},{12,28},{16,0},{20,4},{24,8},{28,12},{1,17},{... | collective-permute-start | bytes 405512 | tf_op jit(solution)/shard_map/ppermute | solution.py:214
  275.7 2.8 collective-permute-start.40
  276.2 4.4 %collective-permute-start.41 = (f32[24,704]{1,0:T(8,128)S(1)}, f32[24,704]{1,0:T(8,128)S(1)}, u32[]{:S(2)}, u32[]{:S(2)}) collective-permute-start(f32[24,704]{1,0:T(8,128)S(1)} %get-tuple-element.183), channel_id=1, source_target_pairs={{0,2},{1,3},{2,0},{3,1},{4,6},{5,7},{6,4},{7,5},{8,10},{9,11},{10,... | collective-permute-start | bytes 202760 | tf_op jit(solution)/shard_map/ppermute | solution.py:214
  277.8 4.5 %collective-permute-start.42 = (f32[24,704]{1,0:T(8,128)S(1)}, f32[24,704]{1,0:T(8,128)S(1)}, u32[]{:S(2)}, u32[]{:S(2)}) collective-permute-start(f32[24,704]{1,0:T(8,128)S(1)} %get-tuple-element.182), channel_id=1, source_target_pairs={{0,3},{1,2},{2,1},{3,0},{4,7},{5,6},{6,5},{7,4},{8,11},{9,10},{10,... | collective-permute-start | bytes 202760 | tf_op jit(solution)/shard_map/ppermute | solution.py:214
  (60 other events, 535.2 us)

commit v4 on v3

--- a/solution.py
+++ b/solution.py
@@ -106,7 +106,8 @@
 
 
 def attend_back_kernel(
-    me_ref, qkv_ref, go_ref, full_ref, lse_ref, seg_row_ref, seg_col_ref, grad_ref, gq_ref, dot_ref, *, heads, hd
+    me_ref, qkv_ref, go_ref, full_ref, lse_ref, seg_row_ref, seg_col_ref, h_ref, grad_ref, d_w_ref,
+    gq_ref, dot_ref, total_ref, *, heads, hd
 ):
     me = me_ref[0]
     kj = pl.program_id(0)
@@ -119,6 +120,7 @@
     @pl.when(kj == 0)
     def _():
         gq_ref[...] = jnp.zeros_like(gq_ref)
+        total_ref[...] = jnp.zeros_like(total_ref)
         for b in range(n):
             prod = go_ref[b].astype(F32) * full_ref[b]
             for h in range(heads):
@@ -157,10 +159,16 @@
         gk, gv = state[h]
         grad_ref[0, :, width + h * hd : width + (h + 1) * hd] = gk.astype(BF16)
         grad_ref[0, :, 2 * width + h * hd : 2 * width + (h + 1) * hd] = gv.astype(BF16)
-
-
-def attend_back(me, qkv, go, full, lse, seg_row, seg_col, heads, hd):
+    total_ref[...] += dot_tn(h_ref[0], grad_ref[0])
+
+    @pl.when(kj == n - 1)
+    def _():
+        d_w_ref[...] = total_ref[...].astype(BF16)
+
+
+def attend_back(me, qkv, go, full, lse, seg_row, seg_col, h_one, heads, hd):
     n, block, wide = qkv.shape
+    dm = h_one.shape[2]
     width = heads * hd
 
     def whole(shape):
@@ -171,17 +179,25 @@
         grid_spec=pltpu.PrefetchScalarGridSpec(
             num_scalar_prefetch=1,
             grid=(n,),
-            in_specs=[whole(a.shape) for a in (qkv, go, full, lse, seg_row, seg_col)],
-            out_specs=pl.BlockSpec((1, block, wide), lambda i, me: (i ^ me[0], 0, 0)),
-            scratch_shapes=[pltpu.VMEM((n, width, block), F32), pltpu.VMEM((n, 8, block), F32)],
+            in_specs=[whole(a.shape) for a in (qkv, go, full, lse, seg_row, seg_col)]
+            + [pl.BlockSpec((1, block, dm), lambda i, me: (i ^ me[0], 0, 0))],
+            out_specs=[pl.BlockSpec((1, block, wide), lambda i, me: (i ^ me[0], 0, 0)), whole((dm, wide))],
+            scratch_shapes=[
+                pltpu.VMEM((n, width, block), F32),
+                pltpu.VMEM((n, 8, block), F32),
+                pltpu.VMEM((dm, wide), F32),
+            ],
         ),
-        out_shape=jax.ShapeDtypeStruct((n, block, wide), BF16),
+        out_shape=[
+            jax.ShapeDtypeStruct((n, block, wide), BF16),
+            jax.ShapeDtypeStruct((dm, wide), BF16),
+        ],
         compiler_params=pltpu.CompilerParams(vmem_limit_bytes=40 * 1024 * 1024),
         cost_estimate=pl.CostEstimate(
             flops=40 * 1000**3, bytes_accessed=12 * 1000**2, transcendentals=8 * 1000**2
         ),
         name="attend_back",
-    )(me, qkv, go, full, lse, seg_row, seg_col)
+    )(me, qkv, go, full, lse, seg_row, seg_col, h_one)
 
 
 def normed_parts(value):
@@ -319,7 +335,7 @@
 
 def enter_kernel(me_ref, *refs, ids, n, width):
     count = len(ids)
-    pieces, (x_ref, qkv_ref, w_ref, vec_ref, tile_ref, add_ref) = refs[:count], refs[count:]
+    pieces, (x_ref, qkv_ref, h_ref, w_ref, vec_ref, tile_ref, add_ref) = refs[:count], refs[count:]
     me = me_ref[0]
 
     @pl.when(pl.program_id(0) == 0)
@@ -340,6 +356,7 @@
 
     normed, _ = normed_parts(x_ref[0].astype(F32))
     h = (normed * vec_ref[0:1, :] + vec_ref[1:2, :]).astype(BF16)
+    h_ref[0] = h
     qkv_ref[0] = (dot_nn(h, w_ref[...]) + add_ref[0:1, :]).astype(BF16)
 
 
@@ -358,11 +375,12 @@
             num_scalar_prefetch=1,
             grid=(n,),
             in_specs=[whole(a.shape) for a in pieces] + [one(dm)],
-            out_specs=[one(3 * width), whole((dm, 3 * width)), whole((16, dm))],
+            out_specs=[one(3 * width), one(dm), whole((dm, 3 * width)), whole((16, dm))],
             scratch_shapes=[pltpu.VMEM((dm, LANES), F32), pltpu.VMEM((8, 3 * width), F32)],
         ),
         out_shape=[
             jax.ShapeDtypeStruct((n, block, 3 * width), BF16),
+            jax.ShapeDtypeStruct((n, block, dm), BF16),
             jax.ShapeDtypeStruct((dm, 3 * width), BF16),
             jax.ShapeDtypeStruct((16, dm), F32),
         ],
@@ -383,7 +401,7 @@
         h_ref, act_ref, gu_ref, low_ref, high_ref, sum_ref, out_w_ref, up_ref, down_ref = refs[3:]
     else:
         x_ref, g_ref, vec_ref, out_w_ref, up_ref, down_ref, sum_in_ref = refs[:7]
-        h_ref, act_ref, gu_ref, low_ref, high_ref, sum_ref, x_two_ref = refs[10:]
+        h_ref, act_ref, gu_ref, low_ref, high_ref, sum_ref, x_two_ref = refs[7:]
     part = up_ref.shape[1]
     width = got[0].shape[1]
 
@@ -447,17 +465,20 @@
     def one(width):
         return pl.BlockSpec((1, block, width), lambda i, me: (i + base, 0, 0))
 
+    def new(width):
+        return pl.BlockSpec((1, block, width), lambda i, me: (i, 0, 0))
+
     def piece(p):
         return pl.BlockSpec((1, width, block), lambda i, me: ((i + base) ^ p, 0, 0))
 
     if base:
         part = 2 * weights[0][0].shape[2]
         weights = [*weights[0], *weights[1]]
-    wide = jax.ShapeDtypeStruct((n, block, dm), BF16)
-    hidden = jax.ShapeDtypeStruct((n, block, part), BF16)
+    wide = jax.ShapeDtypeStruct((2, block, dm), BF16)
+    hidden = jax.ShapeDtypeStruct((2, block, part), BF16)
     low = jax.ShapeDtypeStruct((block, dm), BF16)
     outs = [wide, hidden, hidden, low, low, jax.ShapeDtypeStruct((8, part), F32)]
-    specs = [one(dm), one(part), one(part)] + [whole(o.shape) for o in outs[3:]]
+    specs = [new(dm), new(part), new(part)] + [whole(o.shape) for o in outs[3:]]
     more = [(dm, dm), (dm, part), (part, dm)] if base else []
     outs += [jax.ShapeDtypeStruct(m, BF16) for m in more] or [jax.ShapeDtypeStruct((block, dm), F32)]
     specs += [whole(o.shape) for o in outs[6:]]
@@ -466,17 +487,13 @@
     if base:
         args += [*weights, x_all, g_all, vecs]
         ins += [whole(a.shape) for a in weights] + [one(dm), one(dm), whole(vecs.shape)]
-        alias = {}
     else:
-        args += [x_all, g_all, vecs, *weights, *held]
-        ins += [one(dm), one(dm)] + [whole(a.shape) for a in (vecs, *weights, held[0])]
-        ins += [pl.BlockSpec(memory_space=pl.ANY)] * 3
-        alias = {len(args) - 3 + k + 1: k for k in range(3)}
+        args += [x_all, g_all, vecs, *weights, held]
+        ins += [one(dm), one(dm)] + [whole(a.shape) for a in (vecs, *weights, held)]
     return pl.pallas_call(
         functools.partial(feed_kernel, n=n, base=base, tile=256 if part % 256 == 0 else part, ids=ids),
         grid_spec=pltpu.PrefetchScalarGridSpec(num_scalar_prefetch=1, grid=(2,), in_specs=ins, out_specs=specs),
         out_shape=outs,
-        input_output_aliases=alias,
         compiler_params=pltpu.CompilerParams(vmem_limit_bytes=48 * 1024 * 1024),
         cost_estimate=pl.CostEstimate(
             flops=9 * 1000**3, bytes_accessed=16 * 1000**2, transcendentals=3 * 1000**2
@@ -540,7 +557,7 @@
 
 
 def leave_kernel(
-    me_ref, x_ref, grad_ref, w_ref, vec_ref, two_ref, up_ref, even_ref, odd_ref, d_w_ref, sum_ref, add_ref, total_ref, tile_ref
+    me_ref, x_ref, grad_ref, w_ref, vec_ref, two_ref, up_ref, even_ref, odd_ref, out_ref, sum_ref, add_ref, tile_ref
 ):
     i = pl.program_id(0)
 
@@ -548,12 +565,10 @@
     def _():
         sum_ref[...] = jnp.zeros_like(sum_ref)
         add_ref[...] = jnp.zeros_like(add_ref)
-        total_ref[...] = jnp.zeros_like(total_ref)
 
     grads = grad_ref[0]
     gh = dot_nt(grads, w_ref[...])
     normed, _ = normed_parts(x_ref[0].astype(F32))
-    h = (normed * vec_ref[0:1, :] + vec_ref[1:2, :]).astype(BF16)
     low = gh.astype(BF16)
 
     @pl.when(i % 2 == 0)
@@ -567,13 +582,10 @@
     sum_ref[0:1, :] += jnp.sum(gh * normed, 0, keepdims=True)
     sum_ref[1:2, :] += jnp.sum(gh, 0, keepdims=True)
     add_ref[0:1, :] += jnp.sum(grads.astype(F32), 0, keepdims=True)
-    total_ref[...] += dot_tn(h, grads)
 
     @pl.when(i == pl.num_programs(0) - 1)
     def _():
-        wide = total_ref.shape[1]
-        width = wide // 3
-        d_w_ref[:, :wide] = total_ref[...].astype(BF16)
+        width = grads.shape[1] // 3
         dm = w_ref.shape[0]
         rows = [sum_ref[0:2, :], two_ref[0:4, :], jnp.zeros((2, dm), F32), up_ref[0:1, :]]
         rows = jnp.concatenate(rows + [jnp.zeros((LANES - 9, dm), F32)], 0)
@@ -589,7 +601,7 @@
         )
         own = pl.ds(pl.multiple_of(me_ref[0] * width, width), width)
         tile_ref[own, :] += add.T
-        d_w_ref[:, wide:] = tile_ref[...].astype(BF16)
+        out_ref[...] = tile_ref[...].astype(BF16)
 
 
 def leave(me, x_all, grads, w, vecs, sums_two, sums_up):
@@ -612,18 +624,17 @@
             num_scalar_prefetch=1,
             grid=(n,),
             in_specs=[one(dm), one(wide)] + [whole(a.shape) for a in (w, vecs, sums_two, sums_up)],
-            out_specs=[half(dm), half(dm), whole((dm, wide + LANES))],
+            out_specs=[half(dm), half(dm), whole((dm, LANES))],
             scratch_shapes=[
                 pltpu.VMEM((8, dm), F32),
                 pltpu.VMEM((8, wide), F32),
-                pltpu.VMEM(w.shape, F32),
                 pltpu.VMEM((dm, LANES), F32),
             ],
         ),
         out_shape=[
             pair,
             pair,
-            jax.ShapeDtypeStruct((dm, wide + LANES), BF16),
+            jax.ShapeDtypeStruct((dm, LANES), BF16),
         ],
         compiler_params=pltpu.CompilerParams(vmem_limit_bytes=48 * 1024 * 1024),
         cost_estimate=pl.CostEstimate(flops=6 * 1000**3, bytes_accessed=10 * 1000**2, transcendentals=0),
@@ -631,33 +642,78 @@
     )(me, x_all, grads, w, vecs, sums_two, sums_up)
 
 
-def finish_kernel(me_ref, *refs, n, width):
-    pieces, (q_ref, k_ref, v_ref, vec_ref) = refs[:n], refs[n:]
-    vec_ref[...] = sum(p[:, 3 * width :] for p in pieces)
-    parts = [p[:, : 3 * width] for p in pieces]
+def hand_over_kernel(me_ref, *refs, n, rows):
+    blob_a, blob_b, outs_a, outs_b, feed_a, feed_b = refs[:6]
+    pieces, (out_ref, down_ref, last_ref) = refs[6 : 6 + n], refs[6 + n :]
+    size = n * rows
+    blob = blob_a[...].astype(F32) + blob_b[...].astype(F32)
+    feed = feed_a[...].astype(F32) + feed_b[...].astype(F32)
+    out_ref[...] = outs_a[...].astype(F32) + outs_b[...].astype(F32)
+    down_ref[...] = feed[size:]
+    last_ref[...] = blob[:, -LANES:]
+    both = jnp.concatenate([blob, feed[:size]], 1)
+    parts = [both[t * rows : (t + 1) * rows] for t in range(n)]
+    for p, ref in enumerate(pieces):
+        chosen = parts[0]
+        for t in range(1, n):
+            chosen = jnp.where((me_ref[0] ^ p) == t, parts[t], chosen)
+        ref[...] = chosen.astype(BF16)
+
+
+def hand_over(me, blob, outs, feeds, rows, n):
+    args = [*blob, *outs, *feeds]
+    wide = blob[0].shape[1] + feeds[0].shape[1]
+    size = blob[0].shape[0]
+    vmem = pl.BlockSpec(memory_space=pltpu.VMEM)
+    *pieces, out, down, last = pl.pallas_call(
+        functools.partial(hand_over_kernel, n=n, rows=rows),
+        in_specs=[pl.BlockSpec(memory_space=pltpu.SMEM)] + [vmem] * 6,
+        out_specs=[vmem] * (n + 3),
+        out_shape=[jax.ShapeDtypeStruct((rows, wide), BF16)] * n
+        + [
+            jax.ShapeDtypeStruct(outs[0].shape, F32),
+            jax.ShapeDtypeStruct((feeds[0].shape[0] - size, feeds[0].shape[1]), F32),
+            jax.ShapeDtypeStruct((size, LANES), F32),
+        ],
+        name="hand_over",
+    )(me, *args)
+    return pieces, out, down, last
+
+
+def finish_kernel(me_ref, *refs, n, width, nd):
+    pieces, (q_ref, k_ref, v_ref, vec_ref, up_ref) = refs[:n], refs[n:]
+    first = 3 * width + LANES
+    pieces = [p[...].astype(F32) for p in pieces]
+    vec_ref[...] = sum(p[:, 3 * width : first] for p in pieces)
     bit = 1
     while bit < n:
         on = (me_ref[0] & bit) != 0
         for p in range(n):
             if not p & bit:
-                a, b = parts[p], parts[p | bit]
-                parts[p] = jnp.where(on, b, a)
-                parts[p | bit] = jnp.where(on, a, b)
+                a, b = pieces[p], pieces[p | bit]
+                pieces[p] = jnp.where(on, b, a)
+                pieces[p | bit] = jnp.where(on, a, b)
         bit *= 2
+    step = (pieces[0].shape[1] - first) // nd
     for t in range(n):
         for i, ref in enumerate((q_ref, k_ref, v_ref)):
-            ref[:, t * width : (t + 1) * width] = parts[t][:, i * width : (i + 1) * width]
-
-
-def finish(me, pieces, width):
+            ref[:, t * width : (t + 1) * width] = pieces[t][:, i * width : (i + 1) * width]
+        for j in range(nd):
+            to = (j * n + t) * step
+            up_ref[:, to : to + step] = pieces[t][:, first + j * step : first + (j + 1) * step]
+
+
+def finish(me, pieces, width, nd):
     n = len(pieces)
-    rows = pieces[0].shape[0]
+    rows, wide = pieces[0].shape
     weight = jax.ShapeDtypeStruct((rows, n * width), F32)
+    tile = jax.ShapeDtypeStruct((rows, LANES), F32)
+    vmem = pl.BlockSpec(memory_space=pltpu.VMEM)
     return pl.pallas_call(
-        functools.partial(finish_kernel, n=n, width=width),
-        in_specs=[pl.BlockSpec(memory_space=pltpu.SMEM)] + [pl.BlockSpec(memory_space=pltpu.VMEM)] * n,
-        out_specs=[pl.BlockSpec(memory_space=pltpu.VMEM)] * 4,
-        out_shape=[weight] * 3 + [jax.ShapeDtypeStruct((rows, LANES), F32)],
+        functools.partial(finish_kernel, n=n, width=width, nd=nd),
+        in_specs=[pl.BlockSpec(memory_space=pltpu.SMEM)] + [vmem] * n,
+        out_specs=[vmem] * 5,
+        out_shape=[weight] * 3 + [tile, jax.ShapeDtypeStruct((rows, n * (wide - 3 * width - LANES)), F32)],
         name="finish",
     )(me, *pieces)
 
@@ -727,21 +783,22 @@
     left, right = two[:, : dm // 2], two[:, dm // 2 :]
 
     turned = masks[:-2] + masks[:-3:-1]
-    ones, lefts, rights = [one[None]], [left[None]], [right[None]]
+    ones, lefts, rights = [one[None]], None, None
     for step, mask in enumerate(masks):
-        got = swap(jnp.concatenate(ones, 0), "dp", nd, mask)
+        both = jnp.concatenate(ones, 0)
+        if step == len(masks) - 2:
+            both, left, right, seg_row, seg_col = lax.optimization_barrier((both, left, right, seg_row, seg_col))
+            lefts, rights = [left[None]], [right[None]]
+        got = swap(both, "dp", nd, mask)
         if step == len(masks) - 2:
             got, x_far = lax.optimization_barrier((got, x_far))
             g_far = swap(tie(g, x_far), "seq", ns, far)
             lefts[0], rights[0] = tie(lefts[0], got), tie(rights[0], got)
         ones.append(got)
 
-    def onward(step):
-        for parts, order in ((lefts, masks), (rights, turned)):
-            parts.append(swap(jnp.concatenate(parts, 0), "dp", nd, order[step]))
-
     for step in range(len(masks) - 2):
-        onward(step)
+        lefts.append(swap(jnp.concatenate(lefts, 0), "dp", nd, masks[step]))
+        rights.append(swap(jnp.concatenate(rights, 0), "dp", nd, turned[step]))
     parts = {0: x_own, far: x_far}
     for mask in bits_of(ns)[-2::-1]:
         for p in list(parts):
@@ -750,90 +807,123 @@
 
     ones, ids = settle(ones, d, nd, masks, 1)
     ones[-1], x_all = lax.optimization_barrier((ones[-1], x_all))
-    qkv, w_qkv, vecs = enter(me, ones, ids, x_all, width)
-    qkv, g_far, lefts[-1], rights[-1] = lax.optimization_barrier((qkv, g_far, lefts[-1], rights[-1]))
-    onward(len(masks) - 2)
+    qkv, h_one, w_qkv, vecs = enter(me, ones, ids, x_all, width)
+    qkv, h_one, w_qkv, vecs, g_far, lefts[-1], rights[-1] = lax.optimization_barrier(
+        (qkv, h_one, w_qkv, vecs, g_far, lefts[-1], rights[-1])
+    )
+
+    def onward(parts, mask):
+        held = jnp.concatenate(parts, 0)
+        return held, swap(held, "dp", nd, mask)
+
+    left_held, left_got = onward(lefts, masks[-2])
+    right_held, right_got = onward(rights, turned[-2])
     g_parts = {0: g, far: g_far}
     for mask in bits_of(ns)[-2::-1]:
         for p in list(g_parts):
             g_parts[p | mask] = swap(g_parts[p], "seq", ns, mask)
+    qkv, left_held, right_held = lax.optimization_barrier((qkv, left_held, right_held))
     o_low, o_full, lse = attend(me, qkv, seg_row, seg_col, heads, hd)
+    o_low, o_full, lse, left_got, right_got, *g_last = lax.optimization_barrier(
+        (o_low, o_full, lse, left_got, right_got, g_parts[1], g_parts[ns - 1])
+    )
     o_got = spread_seq(o_low, ns)
-    lefts[-1], rights[-1], g_parts[ns - 1] = lax.optimization_barrier((lefts[-1], rights[-1], g_parts[ns - 1], o_low))[:3]
-    onward(len(masks) - 1)
-    g_all = jnp.stack([g_parts[p] for p in range(ns)])
+    lefts.append(left_got)
+    rights.append(right_got)
+    lefts.append(onward(lefts, masks[-1])[1])
+    rights.append(onward(rights, turned[-1])[1])
+    g_all = jnp.stack([g, g_last[0], g_far, g_last[1]])
     lefts, left_ids = settle(lefts, d, nd, masks, 3)
     rights, right_ids = settle(rights, d, nd, turned, 3)
     ids = (left_ids, right_ids)
-    h_two, act, gu, gh_two, gh_three, sums_up, *weights = feed(
+    far_h, far_act, far_gu, gh_two, gh_three, sums_up, *weights = feed(
         me, o_got, x_all, g_all, vecs, 2, (lefts, rights), ids
     )
     w_out_all, _, w_down_own = weights
+
+    def over_rows(a, b):
+        return jnp.einsum("nbk,nbc->kc", a, b, preferred_element_type=F32)
+
+    d_down = over_rows(far_act, g_all[2:])
     sent = add_low(gh_two, swap(gh_three, "seq", ns, 1))
     far_got = swap(sent, "seq", ns, 2)
-    h_two, act, gu, sums_up = lax.optimization_barrier((h_two, act, gu, sums_up, sent))[:4]
+    sums_up, sent, d_down = lax.optimization_barrier((sums_up, sent, d_down))
     h_two, act, gu, gh_zero, gh_one, sums_up, x_two = feed(
-        me, o_got, x_all, g_all, vecs, 0, weights, None, (sums_up, h_two, act, gu)
+        me, o_got, x_all, g_all, vecs, 0, weights, None, sums_up
     )
     near_got = swap(gh_one, "seq", ns, 1)
-    d_down = jnp.einsum("nbk,nbc->kc", act, g_all, preferred_element_type=F32).astype(BF16)
-    d_up = jnp.einsum("nbk,nbc->kc", h_two, gu, preferred_element_type=F32).astype(BF16)
-    feeds = jnp.concatenate([d_up.reshape(nd, size, part), d_down.reshape(nd, ff_rows, dm)], 1)
-    feed_keep, feed_sent = halves(feeds, d, nd, 1)
-    feed_got = swap(feed_sent, "dp", nd, 1)
-    far_got, feed_sent = lax.optimization_barrier((far_got, feed_sent))
+    d_down = (d_down + over_rows(act, g_all[:2])).astype(BF16)
+    d_up = (over_rows(far_h, far_gu) + over_rows(h_two, gu)).astype(BF16)
+    up_keep, up_sent = halves(d_up.reshape(nd, size, part), d, nd, 1)
+    down_keep, down_sent = halves(d_down.reshape(nd, ff_rows, dm), d, nd, 2)
+    up_got, down_got = swap(up_sent, "dp", nd, 1), swap(down_sent, "dp", nd, 2)
+    far_got, up_sent, down_sent = lax.optimization_barrier((far_got, up_sent, down_sent))
     *gos, gx_two, d_out, sums_two = turn(me, o_got, gh_zero, near_got, far_got, x_two, g, w_out_all, vecs)
     go_got = [gos[0]] + [swap(gos[p], "seq", ns, p) for p in range(1, ns)]
-    outs_keep, outs_sent = halves(d_out.reshape(nd, size, dm), d, nd, 1)
-    outs_got = swap(outs_sent, "dp", nd, 1)
-    act = tie(act, gos[0])
-    out_parts = [dot_nn(act[p], w_down_own).astype(BF16) for p in range(ns)]
+    d_out, sums_two, up_got, down_got = lax.optimization_barrier((d_out, sums_two, up_got, down_got))
+    act, far_act = lax.optimization_barrier((act, far_act, gos[0]))[:2]
+    out_parts = [dot_nn(a, w_down_own).astype(BF16) for a in (act[0], act[1], far_act[0], far_act[1])]
     out_sent = add_low(out_parts[2], swap(out_parts[3], "seq", ns, 1))
     out_near = swap(out_parts[1], "seq", ns, 1)
     out_far = swap(tie(out_sent, go_got[-1]), "seq", ns, 2)
-
+    outs_keep, outs_sent = halves(d_out.reshape(nd * ns, rows, dm), s, ns, 1)
+    outs_got = swap(outs_sent, "seq", ns, 1)
+    outs_keep, outs_sent = halves(add_low(outs_keep, outs_got), s >> 1, ns // 2, 1)
+    outs_got = swap(outs_sent, "seq", ns, 2)
+
+    up_keep, up_sent = halves(add_low(up_keep, up_got), d >> 1, nd // 2, 1)
+    down_keep, down_sent = halves(add_low(down_keep, down_got), d, nd, 1)
+    up_got, down_got = swap(up_sent, "dp", nd, 2), swap(down_sent, "dp", nd, 1)
     go_all = jnp.stack(go_got)
-    go_all, feed_got = lax.optimization_barrier((go_all, feed_got))
-    feeds = add_low(feed_keep, feed_got)
-    feed_keep, feed_sent = halves(feeds, d >> 1, nd // 2, 1)
-    feed_got = swap(feed_sent, "dp", nd, 2)
-    grads = attend_back(me, qkv, go_all, o_full, lse, seg_row, seg_col, heads, hd)
-    grads, out_far, outs_got, feed_got = lax.optimization_barrier((grads, out_far, outs_got, feed_got))
-    feed_keep, feed_sent = halves(add_low(feed_keep, feed_got), d >> 2, nd // 4, 1)
+    go_all, *_ = lax.optimization_barrier((go_all, out_sent, out_parts, outs_sent, up_sent, down_sent))
+    grads, d_qkv = attend_back(me, qkv, go_all, o_full, lse, seg_row, seg_col, h_one, heads, hd)
+    grads, d_qkv, out_near, out_far, outs_got, up_got, down_got = lax.optimization_barrier(
+        (grads, d_qkv, out_near, out_far, outs_got, up_got, down_got)
+    )
+    blob_keep, blob_sent = halves(d_qkv.reshape(nd, size, 3 * width), d, nd, 1)
+    blob_got = swap(blob_sent, "dp", nd, 1)
+    feeds = jnp.concatenate([add_low(up_keep, up_got), add_low(down_keep, down_got)], 1)
+    feed_keep, feed_sent = halves(feeds, d >> 2, nd // 4, 1)
     feed_got = swap(feed_sent, "dp", nd, 4)
+    outs_keep, outs_sent = halves(add_low(outs_keep, outs_got), d, nd, 1)
+    outs_got = swap(outs_sent, "dp", nd, 1)
+    grads = lax.optimization_barrier((grads, blob_sent, feed_sent, outs_sent))[0]
+    even, odd, tile = leave(me, x_all, grads, w_qkv, vecs, sums_two, sums_up)
+    even, odd, tile, blob_got, outs_got, feed_got = lax.optimization_barrier(
+        (even, odd, tile, blob_got, outs_got, feed_got)
+    )
+    blob_keep, blob_sent = halves(add_low(blob_keep, blob_got), d >> 1, nd // 2, 1)
+    blob_got = swap(blob_sent, "dp", nd, 2)
+    tile = tile.reshape(nd // 4, 4, size, LANES)
+    tiles = [lax.dynamic_index_in_dim(tile, (d & 3) ^ p, 1, False) for p in range(4)]
+    tiles = [swap(tiles[p], "dp", nd, p) if p else tiles[0] for p in range(4)]
     outs_keep, outs_sent = halves(add_low(outs_keep, outs_got), d >> 1, nd // 2, 1)
     outs_got = swap(outs_sent, "dp", nd, 2)
-    even, odd, blob = leave(me, x_all, grads, w_qkv, vecs, sums_two, sums_up)
     keep, sent, got = collect_pairs(even, odd, ns)
-    blob_keep, blob_sent = halves(blob.reshape(nd, size, first), d, nd, 1)
-    blob_got = swap(tie(blob_sent, sent), "dp", nd, 1)
-    blob_got, feed_got, outs_got = lax.optimization_barrier((blob_got, feed_got, outs_got))
-    blob = add_low(blob_keep, blob_got)
-    blob_keep, blob_sent = halves(blob, d >> 1, nd // 2, 1)
-    blob_got = swap(blob_sent, "dp", nd, 2)
-    feeds = add_low(feed_keep, feed_got, F32 if nd == 8 else BF16)
-    outs = add_low(outs_keep, outs_got)
+    blob_got, sent, outs_got, tiles[1:] = lax.optimization_barrier((blob_got, sent, outs_got, tiles[1:]))
+    tile = sum(t.astype(F32) for t in tiles).astype(BF16)
+    blob = jnp.concatenate([add_low(blob_keep, blob_got), tile], 2)
+    blob_keep, blob_sent = halves(blob, d >> 2, nd // 4, 1)
+    blob_got = swap(blob_sent, "dp", nd, 4)
+    outs_keep, outs_sent = halves(add_low(outs_keep, outs_got), d >> 2, nd // 4, 1)
+    outs_got = swap(outs_sent, "dp", nd, 4)
+    blob_got, outs_got = lax.optimization_barrier((blob_got, outs_got))
     if nd > 8:
-        feeds = collect_dp(feeds, d >> 3, nd // 8, shift=3)
-    outs = collect_dp(outs, d >> 2, nd // 4, shift=2)
-    blob_got, got = lax.optimization_barrier((blob_got, got))
-    blob = add_low(blob_keep, blob_got)
-    blob = collect_dp(blob, d >> 2, nd // 4, shift=2)
+        rest = [(blob_keep, blob_got), (outs_keep, outs_got), (feed_keep, feed_got)]
+        rest = [collect_dp(add_low(a, b), d >> 3, nd // 8, BF16, shift=3) for a, b in rest]
+        rest = [(v, jnp.zeros_like(v)) for v in rest]
+    else:
+        rest = [(blob_keep[0], blob_got[0]), (outs_keep[0], outs_got[0]), (feed_keep[0], feed_got[0])]
+    pieces, sum_out, sum_down, last = hand_over(me, *rest, rows, ns)
     out = out_parts[0].astype(F32) + out_near.astype(F32) + out_far.astype(F32) + x_two + vecs[5:6]
-    trades = trade_seq(blob.reshape(ns, rows, first), s, ns)
-    sum_up_bias = blob[:ff_rows, 3 * width + 8]
+    trades = [pieces[0]] + [swap(pieces[p], "seq", ns, p) for p in range(1, ns)]
     gh_one = keep.astype(F32) + got.astype(F32)
     n_own, inv_own = normed_parts(x_own.astype(F32))
     grad_x = gx_two + normalize_back(gh_one, n_own, inv_own, vecs[0:1])
-    sum_q, sum_k, sum_v, vec_sum = finish(me, trades, width)
+    trades, grad_x, out, last = lax.optimization_barrier((trades, grad_x, out, last))
+    sum_q, sum_k, sum_v, vec_sum, sum_up = finish(me, trades, width, nd)
     vec_sum = vec_sum.T
-    feeds = feeds.reshape(size + ff_rows, dm)
-    sum_down = feeds[size:]
-    both = jnp.concatenate([outs, feeds[:size]], 1).reshape(ns, rows, dm + part)
-    both = trade_seq(both, s, ns)
-    sum_out = sum(b[:, :dm] for b in both)
-    sum_up = ordered([b[:, dm:] for b in both], s)
-    sum_up = sum_up.reshape(ns, rows, nd, ff_rows).transpose(1, 2, 0, 3).reshape(rows, ff)
+    sum_up_bias = last[:ff_rows, 8]
     v = [vec_sum[i] for i in range(8)]
     return (
         out.reshape(1, block, dm),

time: 291 us -> 282 us (0.969)
  waiting for transfers between devices: 82.2 us -> 65.7 us
  matrix products: 10.6 us -> 16.9 us
  local copies, waits for them, and re-layouts: 23 us -> 18.5 us
    ppermute x47 -> x51, waiting for transfers between devices: 82.2 us -> 65.7 us  [swap(): return lax.ppermute(value, axis, [(i, i ^ mask) for i in range(size)])]
    dot_general x2 -> x4, matrix products: 7.53 us -> 12.9 us  [over_rows(): return jnp.einsum('nbk,nbc->kc', a, b, preferred_element_type=F32)]
    reshape x3 -> x0, other arithmetic: 4.55 us -> none  [the longest x1 1.91 us: body(): grad_x.reshape(1, block, dm)]
    add x3 -> x2, other arithmetic: 0.13 us -> 4.55 us  [the longest x1 3.04 us: body(): grad_x = gx_two + normalize_back(gh_one, n_own, inv_own, vecs[0:1])]
    pallas_call x1, Pallas kernels: 12.8 us -> 9.18 us  [leave(): pl.pallas_call(leave_kernel, grid_spec=pltpu.PrefetchScalarGridSpec(num_s...]
    pallas_call x1, Pallas kernels: 27.1 us -> 30.5 us  [attend_back(): pl.pallas_call(functools.partial(attend_back_kernel, heads=heads, hd=hd),...]
    ppermute x47 -> x51, starting transfers between devices: 43.7 us -> 46 us  [swap(): return lax.ppermute(value, axis, [(i, i ^ mask) for i in range(size)])]
    unnamed x123 -> x127, local copies, waits for them, and re-layouts: 7.79 us -> 7.4 us
  transfers between devices with their start and end apart: 47 -> 51, of which waited for: 22 -> 16; matrix products, arithmetic and copies ran while one was open for 13% -> 16% of each run, Pallas kernels for 26% -> 31%
where the time goes in v4:
time: 282 us; the launch traced here: 277 us
  Pallas kernels  104 us (37%)
  waiting for transfers between devices  65.7 us (23%)
  starting transfers between devices  46 us (16%)
  other arithmetic  24.5 us (9%)
  local copies, waits for them, and re-layouts  18.5 us (7%)
  matrix products  16.9 us (6%)
    ppermute x51, waiting for transfers between devices, swap(): return lax.ppermute(value, axis, [(i, i ^ mask) for i in range(size)])  65.7 us
    ppermute x51, starting transfers between devices, swap(): return lax.ppermute(value, axis, [(i, i ^ mask) for i in range(size)])  46 us
    pallas_call x1, Pallas kernels, attend_back(): pl.pallas_call(functools.partial(attend_back_kernel, heads=heads, hd=hd),...  30.5 us
    pallas_call x2, Pallas kernels, feed(): pl.pallas_call(functools.partial(feed_kernel, n=n, base=base, tile=256 if...  28.1 us
    pallas_call x1, Pallas kernels, attend(): pl.pallas_call(functools.partial(attend_kernel, heads=heads, hd=hd), grid...  17.9 us
    dot_general x4, matrix products, over_rows(): return jnp.einsum('nbk,nbc->kc', a, b, preferred_element_type=F32)  12.9 us
    pallas_call x1, Pallas kernels, leave(): pl.pallas_call(leave_kernel, grid_spec=pltpu.PrefetchScalarGridSpec(num_s...  9.18 us
    pallas_call x1, Pallas kernels, turn(): pl.pallas_call(functools.partial(turn_kernel, n=n), grid_spec=pltpu.Prefe...  7.67 us
  transfers between devices with their start and end apart: 51, of which 16 were waited for; matrix products, arithmetic and copies ran while one was open for 16% of the time, Pallas kernels for 31%

profile of v4, /device:TPU:0, one launch (start us, length us, event | category | flops | bytes accessed | tf_op | source)
XLA Modules:
  0.0 277.3 jit_solution(6684008015995134575)
XLA Ops:
  7.3 2.6 collective-permute-start.1
  10.0 1.7 collective-permute-start.5
  12.2 1.8 collective-permute-done.1
  14.0 1.9 collective-permute-done
  16.5 2.7 collective-permute-start.3
  22.2 5.0 %collective-permute-done.3.refs_1_ = bf16[1,96,704]{2,1,0:T(8,128)(2,1)S(1)} collective-permute-done((bf16[1,96,704]{2,1,0:T(8,128)(2,1)S(1)}, bf16[1,96,704]{2,1,0:T(8,128)(2,1)S(1)}, u32[]{:S(2)}, u32[]{:S(2)}) %collective-permute-start.3) | collective-permute-done | bytes 135200 | tf_op jit(solution)/shard_map/ppermute | solution.py:230
  28.0 8.1 %collective-permute-done.4.refs_2_ = bf16[2,96,704]{2,1,0:T(8,128)(2,1)S(1)} collective-permute-done((bf16[2,96,704]{2,1,0:T(8,128)(2,1)S(1)}, bf16[2,96,704]{2,1,0:T(8,128)(2,1)S(1)}, u32[]{:S(2)}, u32[]{:S(2)}) %collective-permute-start.4) | collective-permute-done | bytes 270368 | tf_op jit(solution)/shard_map/ppermute | solution.py:230
  36.6 1.6 collective-permute-start.6
  38.3 1.5 collective-permute-start.9
  40.8 2.6 collective-permute-start.10
  43.8 2.0 pad_maximum_fusion.refs_4_.refs_12_.x_ref
  45.8 6.2 %collective-permute-done.6.refs_3_ = bf16[4,96,704]{2,1,0:T(8,128)(2,1)S(1)} collective-permute-done((bf16[4,96,704]{2,1,0:T(8,128)(2,1)S(1)}, bf16[4,96,704]{2,1,0:T(8,128)(2,1)S(1)}, u32[]{:S(2)}, u32[]{:S(2)}) %collective-permute-start.6) | collective-permute-done | bytes 540704 | tf_op jit(solution)/shard_map/ppermute | solution.py:230
  52.0 6.0 %enter.1 = (bf16[4,512,576]{2,1,0:T(8,128)(2,1)S(1)}, bf16[4,512,768]{2,1,0:T(8,128)(2,1)S(1)}, bf16[768,576]{1,0:T(8,128)(2,1)S(1)}, f32[16,768]{1,0:T(8,128)S(1)}) custom-call(s32[2]{0:T(128)S(1)} %pad_add_fusion.me_ref, bf16[1,96,704]{2,1,0:T(8,128)(2,1)S(1)} %fusion.45.refs_0_, bf16[1,96,704]{2,1,0:T(8,128)(2,1)S(1)} %copy-done.4, ...), custom_call_target="tpu_custom_call" | custom-call | flops 5000000000 | bytes 8000000 | tf_op jit(solution)/shard_map/enter/pallas_call | solution.py:372
  58.0 1.5 collective-permute-done.10.refs_5_
  59.6 3.5 %collective-permute-done.11.refs_9_ = bf16[1,288,384]{2,1,0:T(8,128)(2,1)S(1)} collective-permute-done((bf16[1,288,384]{2,1,0:T(8,128)(2,1)S(1)}, bf16[1,288,384]{2,1,0:T(8,128)(2,1)S(1)}, u32[]{:S(2)}, u32[]{:S(2)}) %collective-permute-start.11) | collective-permute-done | bytes 221216 | tf_op jit(solution)/shard_map/ppermute | solution.py:230
  64.4 17.9 %attend.1 = (bf16[4,192,512]{2,1,0:T(8,128)(2,1)S(1)}, f32[4,192,512]{2,1,0:T(8,128)S(1)}, f32[4,8,512]{2,1,0:T(8,128)S(1)}) custom-call(s32[2]{0:T(128)S(1)} %pad_add_fusion.me_ref, bf16[4,512,576]{2,1,0:T(8,128)(2,1)S(1)} %get-tuple-element.147.qkv_ref, s32[4,1,512]{2,1,0:T(1,128)S(1)} %maximum_convert_fusion.1.seg_row_ref, s32[4,512,1]{2,1,0:T(8,128)S(1)} %copy-done.1), custom_call_target="tpu_custom_call" | custom-call | flops 20000000000 | bytes 8000000 | tf_op jit(solution)/shard_map/attend/pallas_call | solution.py:87
  86.8 1.5 collective-permute-start.19
  88.3 15.2 %collective-permute-done.17.refs_2_ = bf16[4,192,512]{2,1,0:T(8,128)(2,1)S(1)} collective-permute-done((bf16[4,192,512]{2,1,0:T(8,128)(2,1)S(1)}, bf16[4,192,512]{2,1,0:T(8,128)(2,1)S(1)}, u32[]{:S(2)}, u32[]{:S(2)}) %collective-permute-start.17) | collective-permute-done | bytes 786464 | tf_op jit(solution)/shard_map/ppermute | solution.py:230
  103.6 2.9 %pad_maximum_fusion.1.refs_13_.refs_5_ = bf16[4,512,768]{2,1,0:T(8,128)(2,1)} fusion(bf16[1,512,768]{2,1,0:T(8,128)(2,1)S(1)} %bitcast.208, bf16[1,512,768]{2,1,0:T(8,128)(2,1)S(1)} %bitcast.206, bf16[1,512,768]{2,1,0:T(8,128)(2,1)} %bitcast.29, bf16[1,512,768]{2,1,0:T(8,128)(2,1)S(1)} %copy-done.34), kind=kLoop, calls=%fused_computation.1 | loop fusion | flops 4718592 | bytes 6291456 | tf_op jit(solution)/shard_map/stack | solution.py:835
  110.1 14.5 %feed_far.1 = (bf16[2,512,768]{2,1,0:T(8,128)(2,1)}, bf16[2,512,768]{2,1,0:T(8,128)(2,1)}, bf16[2,512,768]{2,1,0:T(8,128)(2,1)}, bf16[512,768]{1,0:T(8,128)(2,1)...) custom-call(s32[2]{0:T(128)S(1)} %pad_add_fusion.me_ref, ...), custom_call_target="tpu_custom_call" | custom-call | flops 8999999488 | bytes 16000000 | tf_op jit(solution)/shard_map/feed_far/pallas_call | solution.py:493
  124.8 3.2 %convolution_bitcast_fusion = f32[768,768]{1,0:T(8,128)S(1)} fusion(bf16[2,512,768]{2,1,0:T(8,128)(2,1)} %get-tuple-element.182, bf16[1,512,768]{2,1,0:T(8,128)(2,1)} %bitcast.209, bf16[1,512,768]{2,1,0:T(8,128)(2,1)S(1)} %bitcast.207), kind=kOutput, calls=%fused_computation.12 | convolution fusion | flops 1208745984 | bytes 5505024 | tf_op jit(solution)/shard_map/nbk,nbc->kc/dot_general | solution.py:845
  128.0 2.8 %fusion.59 = f32[768,768,1]{1,0,2:T(8,128)} fusion(bf16[2,512,768]{2,1,0:T(8,128)(2,1)S(1)} %copy-done.60, bf16[2,512,768]{2,1,0:T(8,128)(2,1)S(1)} %copy-done.61), kind=kOutput, calls=%fused_computation.151 | convolution fusion | flops 1207959552 | bytes 5505024 | tf_op jit(solution)/shard_map/nbk,nbc->kc/dot_general | solution.py:845
  132.3 1.6 collective-permute-start.23
  133.9 13.5 %feed_near.1 = (bf16[2,512,768]{2,1,0:T(8,128)(2,1)}, bf16[2,512,768]{2,1,0:T(8,128)(2,1)}, bf16[2,512,768]{2,1,0:T(8,128)(2,1)}, bf16[512,768]{1,0:T(8,128)(2,1...) custom-call(s32[2]{0:T(128)S(1)} %pad_add_fusion.me_ref, ...), custom_call_target="tpu_custom_call" | custom-call | flops 8999999488 | bytes 16000000 | tf_op jit(solution)/shard_map/feed_near/pallas_call | solution.py:493
  147.7 4.2 %fusion.1 = bf16[768,768]{1,0:T(8,128)(2,1)S(1)} fusion(f32[768,768,1]{1,0,2:T(8,128)} %fusion.59, bf16[2,512,768]{2,1,0:T(8,128)(2,1)} %get-tuple-element.172, bf16[2,512,768]{2,1,0:T(8,128)(2,1)} %get-tuple-element.173), kind=kOutput, calls=%fused_computation.5 | convolution fusion | flops 1209139200 | bytes 6684672 | tf_op jit(solution)/shard_map/nbk,nbc->kc/dot_general | solution.py:845
  152.0 1.6 collective-permute-start.28
  153.6 2.6 fusion
  157.9 7.7 %turn.1 = (bf16[192,512]{1,0:T(8,128)(2,1)S(1)}, bf16[192,512]{1,0:T(8,128)(2,1)S(1)}, bf16[192,512]{1,0:T(8,128)(2,1)S(1)}, bf16[192,512]{1,0:T(8,128)(2,1)S(1)...) custom-call(s32[2]{0:T(128)S(1)} %pad_add_fusion.me_ref, ...), custom_call_target="tpu_custom_call" | custom-call | flops 3000000000 | bytes 8000000 | tf_op jit(solution)/shard_map/turn/pallas_call | solution.py:543
  168.6 1.7 convolution_convert_fusion.1
  175.2 4.2 %collective-permute-done.25 = bf16[192,512]{1,0:T(8,128)(2,1)S(1)} collective-permute-done((bf16[192,512]{1,0:T(8,128)(2,1)S(1)}, bf16[192,512]{1,0:T(8,128)(2,1)S(1)}, u32[]{:S(2)}, u32[]{:S(2)}) %collective-permute-start.25) | collective-permute-done | bytes 196640 | tf_op jit(solution)/shard_map/ppermute | solution.py:230
  180.0 2.8 %collective-permute-done.26 = bf16[192,512]{1,0:T(8,128)(2,1)S(1)} collective-permute-done((bf16[192,512]{1,0:T(8,128)(2,1)S(1)}, bf16[192,512]{1,0:T(8,128)(2,1)S(1)}, u32[]{:S(2)}, u32[]{:S(2)}) %collective-permute-start.26) | collective-permute-done | bytes 196640 | tf_op jit(solution)/shard_map/ppermute | solution.py:230
  184.5 1.6 collective-permute-start.32
  186.0 30.5 %attend_back.1 = (bf16[4,512,576]{2,1,0:T(8,128)(2,1)S(1)}, bf16[768,576]{1,0:T(8,128)(2,1)S(1)}) custom-call(s32[2]{0:T(128)S(1)} %pad_add_fusion.me_ref, bf16[4,512,576]{2,1,0:T(8,128)(2,1)S(1)} %copy-done.18, bf16[4,192,512]{2,1,0:T(8,128)(2,1)S(1)} %pad_maximum_fusion.4.go_ref, f32[4,192,512]{2,1,0:T(8,128)S(1)} %copy-done.23, ...), custom_call_target="tpu_custom_call" | custom-call | flops 40000000000 | bytes 12000000 | tf_op jit(solution)/shard_map/attend_back/pallas_call | solution.py:177
  218.5 2.5 collective-permute-start.38
  222.6 9.2 %leave.1 = (bf16[2,512,768]{2,1,0:T(8,128)(2,1)S(1)}, bf16[2,512,768]{2,1,0:T(8,128)(2,1)}, bf16[768,128]{1,0:T(8,128)(2,1)S(1)}) custom-call(s32[2]{0:T(128)S(1)} %pad_add_fusion.me_ref, bf16[4,512,768]{2,1,0:T(8,128)(2,1)} %copy-done, bf16[4,512,576]{2,1,0:T(8,128)(2,1)} %copy-done.19, bf16[768,576]{1,0:T(8,128)(2,1)S(1)} %copy-done.21, ...), custom_call_target="tpu_custom_call" | custom-call | flops 6000000000 | bytes 10000000 | tf_op jit(solution)/shard_map/leave/pallas_call | solution.py:621
  231.8 2.4 collective-permute-done.38
  235.3 1.5 fusion.10
  238.7 1.9 collective-permute-start.44
  243.8 2.2 fusion.24
  246.6 3.4 %collective-permute-done.39 = bf16[2,96,576]{2,1,0:T(8,128)(2,1)S(1)} collective-permute-done((bf16[2,96,576]{2,1,0:T(8,128)(2,1)S(1)}, bf16[2,96,576]{2,1,0:T(8,128)(2,1)S(1)}, u32[]{:S(2)}, u32[]{:S(2)}) %collective-permute-start.39) | collective-permute-done | bytes 221216 | tf_op jit(solution)/shard_map/ppermute | solution.py:230
  250.6 3.1 %collective-permute-start.46 = (bf16[1,24,768]{2,1,0:T(8,128)(2,1)S(1)}, bf16[1,24,768]{2,1,0:T(8,128)(2,1)S(1)}, u32[]{:S(2)}, u32[]{:S(2)}) collective-permute-start(bf16[1,24,768]{2,1,0:T(8,128)(2,1)S(1)} %get-tuple-element.274), channel_id=1, source_target_pairs={{0,16},{4,20},{8,24},{12,28},{16,0},{20,4},{24,8},{28,12},{1,17},{... | collective-permute-start | bytes 110600 | tf_op jit(solution)/shard_map/ppermute | solution.py:230
  254.6 1.5 add_add_fusion
  256.1 6.4 %collective-permute-done.45 = bf16[1,96,704]{2,1,0:T(8,128)(2,1)S(1)} collective-permute-done((bf16[1,96,704]{2,1,0:T(8,128)(2,1)S(1)}, bf16[1,96,704]{2,1,0:T(8,128)(2,1)S(1)}, u32[]{:S(2)}, u32[]{:S(2)}) %collective-permute-start.45) | collective-permute-done | bytes 135200 | tf_op jit(solution)/shard_map/ppermute | solution.py:230
  263.2 2.3 hand_over.1
  267.4 2.1 fusion.19
  269.5 3.0 %fusion.9 = f32[512,768]{1,0:T(8,128)} fusion(f32[512,768]{1,0:T(8,128)S(1)} %copy-done.28, bf16[512,768]{1,0:T(8,128)(2,1)S(1)} %collective-permute-done.50, f32[512]{0:T(512)S(1)} %broadcast_multiply_fusion, f32[512]{0:T(512)S(1)} %broadcast_multiply_fusion.1, f32[768]{0:T(1024)S(1)} %get-tuple-element.246, f32[512]{0:T(512)S(1)} %add_rsqrt_fusion, ...), kind=kLoop, calls=%fused_computation.16 | loop fusion | flops 6291456 | bytes 6302720 | tf_op jit(solution)/shard_map/add | solution.py:922
  273.3 1.9 finish.1
  275.2 1.8 slice_reduce_fusion.1
  (285 shorter events, 51.0 us)
Async XLA Ops:
  6.8 5.3 %collective-permute-start.2 = (bf16[24,2368]{1,0:T(8,128)(2,1)S(1)}, bf16[24,2368]{1,0:T(8,128)(2,1)S(1)}, u32[]{:S(2)}, u32[]{:S(2)}) collective-permute-start(bf16[24,2368]{1,0:T(8,128)(2,1)S(1)} %get-tuple-element.261), channel_id=1, source_target_pairs={{0,1},{1,0},{2,3},{3,2},{4,5},{5,4},{6,7},{7,6},{8,9},{9,8},{10,11... | collective-permute-start | bytes 341000 | tf_op jit(solution)/shard_map/ppermute | solution.py:230
  7.3 6.6 %collective-permute-start.1 = (bf16[24,2368]{1,0:T(8,128)(2,1)S(1)}, bf16[24,2368]{1,0:T(8,128)(2,1)S(1)}, u32[]{:S(2)}, u32[]{:S(2)}) collective-permute-start(bf16[24,2368]{1,0:T(8,128)(2,1)S(1)} %get-tuple-element.262), channel_id=1, source_target_pairs={{0,2},{1,3},{2,0},{3,1},{4,6},{5,7},{6,4},{7,5},{8,10},{9,11},{10,... | collective-permute-start | bytes 341000 | tf_op jit(solution)/shard_map/ppermute | solution.py:230
  9.9 6.0 %collective-permute-start = (bf16[24,2368]{1,0:T(8,128)(2,1)S(1)}, bf16[24,2368]{1,0:T(8,128)(2,1)S(1)}, u32[]{:S(2)}, u32[]{:S(2)}) collective-permute-start(bf16[24,2368]{1,0:T(8,128)(2,1)S(1)} %get-tuple-element.263), channel_id=1, source_target_pairs={{0,3},{1,2},{2,1},{3,0},{4,7},{5,6},{6,5},{7,4},{8,11},{9,10},{10,... | collective-permute-start | bytes 341000 | tf_op jit(solution)/shard_map/ppermute | solution.py:230
  10.0 26.1 %collective-permute-start.5 = (bf16[512,768]{1,0:T(8,128)(2,1)S(1)}, bf16[512,768]{1,0:T(8,128)(2,1)}, u32[]{:S(2)}, u32[]{:S(2)}) collective-permute-start(bf16[512,768]{1,0:T(8,128)(2,1)S(1)} %bitcast.204), channel_id=1, source_target_pairs={{0,2},{1,3},{2,0},{3,1},{4,6},{5,7},{6,4},{7,5},{8,10},{9,11},{10,... | collective-permute-start | bytes 2359304 | tf_op jit(solution)/shard_map/ppermute | solution.py:230
  16.5 10.6 %collective-permute-start.3 = (bf16[1,96,704]{2,1,0:T(8,128)(2,1)S(1)}, bf16[1,96,704]{2,1,0:T(8,128)(2,1)S(1)}, u32[]{:S(2)}, u32[]{:S(2)}) collective-permute-start(bf16[1,96,704]{2,1,0:T(8,128)(2,1)S(1)} %fusion.45.refs_0_), channel_id=1, source_target_pairs={{0,16},{4,20},{8,24},{12,28},{16,0},{20,4},{24,8},{28,12},{1,17},{... | collective-permute-start | bytes 405512 | tf_op jit(solution)/shard_map/ppermute | solution.py:230
  27.2 8.9 %collective-permute-start.4 = (bf16[2,96,704]{2,1,0:T(8,128)(2,1)S(1)}, bf16[2,96,704]{2,1,0:T(8,128)(2,1)S(1)}, u32[]{:S(2)}, u32[]{:S(2)}) collective-permute-start(bf16[2,96,704]{2,1,0:T(8,128)(2,1)S(1)} %pad_maximum_fusion.7), channel_id=1, source_target_pairs={{0,8},{4,12},{8,0},{12,4},{16,24},{20,28},{24,16},{28,20},{1,9},{5... | collective-permute-start | bytes 811016 | tf_op jit(solution)/shard_map/ppermute | solution.py:230
  28.0 12.8 %collective-permute-start.7 = (bf16[512,768]{1,0:T(8,128)(2,1)S(1)}, bf16[512,768]{1,0:T(8,128)(2,1)}, u32[]{:S(2)}, u32[]{:S(2)}) collective-permute-start(bf16[512,768]{1,0:T(8,128)(2,1)S(1)} %bitcast.205), channel_id=1, source_target_pairs={{0,1},{1,0},{2,3},{3,2},{4,5},{5,4},{6,7},{7,6},{8,9},{9,8},{10,11... | collective-permute-start | bytes 2359304 | tf_op jit(solution)/shard_map/ppermute | solution.py:230
  36.1 7.4 %collective-permute-start.8 = (bf16[512,768]{1,0:T(8,128)(2,1)}, bf16[512,768]{1,0:T(8,128)(2,1)}, u32[]{:S(2)}, u32[]{:S(2)}) collective-permute-start(bf16[512,768]{1,0:T(8,128)(2,1)} %collective-permute-done.5), channel_id=1, source_target_pairs={{0,1},{1,0},{2,3},{3,2},{4,5},{5,4},{6,7},{7,6},{8,9},{9,8},{10,11... | collective-permute-start | bytes 2359304 | tf_op jit(solution)/shard_map/ppermute | solution.py:230
  36.1 47.5 %collective-permute-start.14 = (bf16[512,768]{1,0:T(8,128)(2,1)S(1)}, bf16[512,768]{1,0:T(8,128)(2,1)}, u32[]{:S(2)}, u32[]{:S(2)}) collective-permute-start(bf16[512,768]{1,0:T(8,128)(2,1)S(1)} %bitcast.230), channel_id=1, source_target_pairs={{0,1},{1,0},{2,3},{3,2},{4,5},{5,4},{6,7},{7,6},{8,9},{9,8},{10,11... | collective-permute-start | bytes 2359304 | tf_op jit(solution)/shard_map/ppermute | solution.py:230
  36.6 15.4 %collective-permute-start.6 = (bf16[4,96,704]{2,1,0:T(8,128)(2,1)S(1)}, bf16[4,96,704]{2,1,0:T(8,128)(2,1)S(1)}, u32[]{:S(2)}, u32[]{:S(2)}) collective-permute-start(bf16[4,96,704]{2,1,0:T(8,128)(2,1)S(1)} %pad_maximum_fusion.5), channel_id=1, source_target_pairs={{0,4},{4,0},{8,12},{12,8},{16,20},{20,16},{24,28},{28,24},{1,5},{5... | collective-permute-start | bytes 1622024 | tf_op jit(solution)/shard_map/ppermute | solution.py:230
  38.3 24.7 %collective-permute-start.9 = (bf16[512,768]{1,0:T(8,128)(2,1)S(1)}, bf16[512,768]{1,0:T(8,128)(2,1)S(1)}, u32[]{:S(2)}, u32[]{:S(2)}) collective-permute-start(bf16[512,768]{1,0:T(8,128)(2,1)S(1)} %bitcast.231), channel_id=1, source_target_pairs={{0,2},{1,3},{2,0},{3,1},{4,6},{5,7},{6,4},{7,5},{8,10},{9,11},{10,... | collective-permute-start | bytes 2359304 | tf_op jit(solution)/shard_map/ppermute | solution.py:230
  40.8 18.7 %collective-permute-start.10 = (bf16[1,288,384]{2,1,0:T(8,128)(2,1)}, bf16[1,288,384]{2,1,0:T(8,128)(2,1)S(1)}, u32[]{:S(2)}, u32[]{:S(2)}) collective-permute-start(bf16[1,288,384]{2,1,0:T(8,128)(2,1)} %bitcast.27.refs_4_), channel_id=1, source_target_pairs={{0,16},{4,20},{8,24},{12,28},{16,0},{20,4},{24,8},{28,12},{1,17},{... | collective-permute-start | bytes 663560 | tf_op jit(solution)/shard_map/ppermute | solution.py:230
  43.4 19.6 %collective-permute-start.11 = (bf16[1,288,384]{2,1,0:T(8,128)(2,1)S(1)}, bf16[1,288,384]{2,1,0:T(8,128)(2,1)S(1)}, u32[]{:S(2)}, u32[]{:S(2)}) collective-permute-start(bf16[1,288,384]{2,1,0:T(8,128)(2,1)S(1)} %bitcast.196), channel_id=1, source_target_pairs={{0,16},{4,20},{8,24},{12,28},{16,0},{20,4},{24,8},{28,12},{1,17},{... | collective-permute-start | bytes 663560 | tf_op jit(solution)/shard_map/ppermute | solution.py:230
  63.1 20.4 %collective-permute-start.13 = (bf16[2,288,384]{2,1,0:T(8,128)(2,1)S(1)}, bf16[2,288,384]{2,1,0:T(8,128)(2,1)S(1)}, u32[]{:S(2)}, u32[]{:S(2)}) collective-permute-start(bf16[2,288,384]{2,1,0:T(8,128)(2,1)S(1)} %constant_dynamic-update-slice_fusion.2), channel_id=1, source_target_pairs={{0,4},{4,0},{8,12},{12,8},{16,20},{20,16},{24,28},{28,24},{1,5},{5... | collective-permute-start | bytes 1327112 | tf_op jit(solution)/shard_map/ppermute | solution.py:230
  63.7 19.8 %collective-permute-start.12 = (bf16[2,288,384]{2,1,0:T(8,128)(2,1)S(1)}, bf16[2,288,384]{2,1,0:T(8,128)(2,1)S(1)}, u32[]{:S(2)}, u32[]{:S(2)}) collective-permute-start(bf16[2,288,384]{2,1,0:T(8,128)(2,1)S(1)} %constant_dynamic-update-slice_fusion), channel_id=1, source_target_pairs={{0,8},{4,12},{8,0},{12,4},{16,24},{20,28},{24,16},{28,20},{1,9},{5... | collective-permute-start | bytes 1327112 | tf_op jit(solution)/shard_map/ppermute | solution.py:230
  64.4 19.1 %collective-permute-start.15 = (bf16[512,768]{1,0:T(8,128)(2,1)S(1)}, bf16[512,768]{1,0:T(8,128)(2,1)S(1)}, u32[]{:S(2)}, u32[]{:S(2)}) collective-permute-start(bf16[512,768]{1,0:T(8,128)(2,1)S(1)} %collective-permute-done.9), channel_id=1, source_target_pairs={{0,1},{1,0},{2,3},{3,2},{4,5},{5,4},{6,7},{7,6},{8,9},{9,8},{10,11... | collective-permute-start | bytes 2359304 | tf_op jit(solution)/shard_map/ppermute | solution.py:230
  83.6 20.0 %collective-permute-start.17 = (bf16[4,192,512]{2,1,0:T(8,128)(2,1)S(1)}, bf16[4,192,512]{2,1,0:T(8,128)(2,1)S(1)}, u32[]{:S(2)}, u32[]{:S(2)}) collective-permute-start(bf16[4,192,512]{2,1,0:T(8,128)(2,1)S(1)} %get-tuple-element.154.refs_0_), channel_id=1, source_target_pairs={{0,2},{1,3},{2,0},{3,1},{4,6},{5,7},{6,4},{7,5},{8,10},{9,11},{10,... | collective-permute-start | bytes 2359304 | tf_op jit(solution)/shard_map/ppermute | solution.py:230
  85.3 21.8 %collective-permute-start.20 = (bf16[4,288,384]{2,1,0:T(8,128)(2,1)S(1)}, bf16[4,288,384]{2,1,0:T(8,128)(2,1)S(1)}, u32[]{:S(2)}, u32[]{:S(2)}) collective-permute-start(bf16[4,288,384]{2,1,0:T(8,128)(2,1)S(1)} %pad_maximum_fusion.3), channel_id=1, source_target_pairs={{0,8},{4,12},{8,0},{12,4},{16,24},{20,28},{24,16},{28,20},{1,9},{5... | collective-permute-start | bytes 2654216 | tf_op jit(solution)/shard_map/ppermute | solution.py:230
  86.8 21.5 %collective-permute-start.19 = (bf16[4,288,384]{2,1,0:T(8,128)(2,1)S(1)}, bf16[4,288,384]{2,1,0:T(8,128)(2,1)S(1)}, u32[]{:S(2)}, u32[]{:S(2)}) collective-permute-start(bf16[4,288,384]{2,1,0:T(8,128)(2,1)S(1)} %pad_maximum_fusion.2), channel_id=1, source_target_pairs={{0,4},{4,0},{8,12},{12,8},{16,20},{20,16},{24,28},{28,24},{1,5},{5... | collective-permute-start | bytes 2654216 | tf_op jit(solution)/shard_map/ppermute | solution.py:230
  88.3 18.2 %collective-permute-start.16 = (bf16[4,192,512]{2,1,0:T(8,128)(2,1)S(1)}, bf16[4,192,512]{2,1,0:T(8,128)(2,1)S(1)}, u32[]{:S(2)}, u32[]{:S(2)}) collective-permute-start(bf16[4,192,512]{2,1,0:T(8,128)(2,1)S(1)} %get-tuple-element.154.refs_0_), channel_id=1, source_target_pairs={{0,1},{1,0},{2,3},{3,2},{4,5},{5,4},{6,7},{7,6},{8,9},{9,8},{10,11... | collective-permute-start | bytes 2359304 | tf_op jit(solution)/shard_map/ppermute | solution.py:230
  124.7 6.2 %collective-permute-start.21 = (bf16[512,768]{1,0:T(8,128)(2,1)}, bf16[512,768]{1,0:T(8,128)(2,1)}, u32[]{:S(2)}, u32[]{:S(2)}) collective-permute-start(bf16[512,768]{1,0:T(8,128)(2,1)} %get-tuple-element.165), channel_id=1, source_target_pairs={{0,1},{1,0},{2,3},{3,2},{4,5},{5,4},{6,7},{7,6},{8,9},{9,8},{10,11... | collective-permute-start | bytes 2359304 | tf_op jit(solution)/shard_map/ppermute | solution.py:230
  132.3 24.6 %collective-permute-start.23 = (bf16[512,768]{1,0:T(8,128)(2,1)S(1)}, bf16[512,768]{1,0:T(8,128)(2,1)S(1)}, u32[]{:S(2)}, u32[]{:S(2)}) collective-permute-start(bf16[512,768]{1,0:T(8,128)(2,1)S(1)} %add_convert_fusion.3), channel_id=1, source_target_pairs={{0,2},{1,3},{2,0},{3,1},{4,6},{5,7},{6,4},{7,5},{8,10},{9,11},{10,... | collective-permute-start | bytes 2359304 | tf_op jit(solution)/shard_map/ppermute | solution.py:230
  147.5 9.5 %collective-permute-start.22 = (bf16[512,768]{1,0:T(8,128)(2,1)S(1)}, bf16[512,768]{1,0:T(8,128)(2,1)S(1)}, u32[]{:S(2)}, u32[]{:S(2)}) collective-permute-start(bf16[512,768]{1,0:T(8,128)(2,1)S(1)} %get-tuple-element.169), channel_id=1, source_target_pairs={{0,1},{1,0},{2,3},{3,2},{4,5},{5,4},{6,7},{7,6},{8,9},{9,8},{10,11... | collective-permute-start | bytes 2359304 | tf_op jit(solution)/shard_map/ppermute | solution.py:230
  152.0 18.3 %collective-permute-start.28 = (bf16[4,96,768]{2,1,0:T(8,128)(2,1)S(1)}, bf16[4,96,768]{2,1,0:T(8,128)(2,1)S(1)}, u32[]{:S(2)}, u32[]{:S(2)}) collective-permute-start(bf16[4,96,768]{2,1,0:T(8,128)(2,1)S(1)} %dynamic-slice_bitcast_fusion.1), channel_id=1, source_target_pairs={{0,4},{4,0},{8,12},{12,8},{16,20},{20,16},{24,28},{28,24},{1,5},{5... | collective-permute-start | bytes 1769480 | tf_op jit(solution)/shard_map/ppermute | solution.py:230
  156.3 15.4 %collective-permute-start.29 = (bf16[4,96,768]{2,1,0:T(8,128)(2,1)S(1)}, bf16[4,96,768]{2,1,0:T(8,128)(2,1)S(1)}, u32[]{:S(2)}, u32[]{:S(2)}) collective-permute-start(bf16[4,96,768]{2,1,0:T(8,128)(2,1)S(1)} %bitcast.236), channel_id=1, source_target_pairs={{0,8},{4,12},{8,0},{12,4},{16,24},{20,28},{24,16},{28,20},{1,9},{5... | collective-permute-start | bytes 1769480 | tf_op jit(solution)/shard_map/ppermute | solution.py:230
  171.7 7.7 %collective-permute-start.25 = (bf16[192,512]{1,0:T(8,128)(2,1)S(1)}, bf16[192,512]{1,0:T(8,128)(2,1)S(1)}, u32[]{:S(2)}, u32[]{:S(2)}) collective-permute-start(bf16[192,512]{1,0:T(8,128)(2,1)S(1)} %get-tuple-element.180), channel_id=1, source_target_pairs={{0,2},{1,3},{2,0},{3,1},{4,6},{5,7},{6,4},{7,5},{8,10},{9,11},{10,... | collective-permute-start | bytes 589832 | tf_op jit(solution)/shard_map/ppermute | solution.py:230
  172.2 10.6 %collective-permute-start.26 = (bf16[192,512]{1,0:T(8,128)(2,1)S(1)}, bf16[192,512]{1,0:T(8,128)(2,1)S(1)}, u32[]{:S(2)}, u32[]{:S(2)}) collective-permute-start(bf16[192,512]{1,0:T(8,128)(2,1)S(1)} %get-tuple-element.181), channel_id=1, source_target_pairs={{0,3},{1,2},{2,1},{3,0},{4,7},{5,6},{6,5},{7,4},{8,11},{9,10},{10,... | collective-permute-start | bytes 589832 | tf_op jit(solution)/shard_map/ppermute | solution.py:230
  173.6 9.8 %collective-permute-start.30 = (bf16[16,24,768]{2,1,0:T(8,128)(2,1)S(1)}, bf16[16,24,768]{2,1,0:T(8,128)(2,1)S(1)}, u32[]{:S(2)}, u32[]{:S(2)}) collective-permute-start(bf16[16,24,768]{2,1,0:T(8,128)(2,1)S(1)} %dynamic-slice_bitcast_fusion), channel_id=1, source_target_pairs={{0,1},{1,0},{2,3},{3,2},{4,5},{5,4},{6,7},{7,6},{8,9},{9,8},{10,11... | collective-permute-start | bytes 1769480 | tf_op jit(solution)/shard_map/ppermute | solution.py:230
  173.9 10.3 %collective-permute-start.27 = (bf16[512,768]{1,0:T(8,128)(2,1)S(1)}, bf16[512,768]{1,0:T(8,128)(2,1)S(1)}, u32[]{:S(2)}, u32[]{:S(2)}) collective-permute-start(bf16[512,768]{1,0:T(8,128)(2,1)S(1)} %convolution_convert_fusion.2), channel_id=1, source_target_pairs={{0,1},{1,0},{2,3},{3,2},{4,5},{5,4},{6,7},{7,6},{8,9},{9,8},{10,11... | collective-permute-start | bytes 2359304 | tf_op jit(solution)/shard_map/ppermute | solution.py:230
  174.6 42.0 %collective-permute-start.35 = (bf16[2,96,768]{2,1,0:T(8,128)(2,1)S(1)}, bf16[2,96,768]{2,1,0:T(8,128)(2,1)S(1)}, u32[]{:S(2)}, u32[]{:S(2)}) collective-permute-start(bf16[2,96,768]{2,1,0:T(8,128)(2,1)S(1)} %dynamic-slice_bitcast_fusion.3), channel_id=1, source_target_pairs={{0,4},{4,0},{8,12},{12,8},{16,20},{20,16},{24,28},{28,24},{1,5},{5... | collective-permute-start | bytes 884744 | tf_op jit(solution)/shard_map/ppermute | solution.py:230
  179.4 37.3 %collective-permute-start.34 = (bf16[2,96,768]{2,1,0:T(8,128)(2,1)S(1)}, bf16[2,96,768]{2,1,0:T(8,128)(2,1)S(1)}, u32[]{:S(2)}, u32[]{:S(2)}) collective-permute-start(bf16[2,96,768]{2,1,0:T(8,128)(2,1)S(1)} %dynamic-slice_bitcast_fusion.4), channel_id=1, source_target_pairs={{0,8},{4,12},{8,0},{12,4},{16,24},{20,28},{24,16},{28,20},{1,9},{5... | collective-permute-start | bytes 884744 | tf_op jit(solution)/shard_map/ppermute | solution.py:230
  182.8 33.8 %collective-permute-start.31 = (bf16[512,768]{1,0:T(8,128)(2,1)S(1)}, bf16[512,768]{1,0:T(8,128)(2,1)S(1)}, u32[]{:S(2)}, u32[]{:S(2)}) collective-permute-start(bf16[512,768]{1,0:T(8,128)(2,1)S(1)} %convolution_convert_fusion), channel_id=1, source_target_pairs={{0,1},{1,0},{2,3},{3,2},{4,5},{5,4},{6,7},{7,6},{8,9},{9,8},{10,11... | collective-permute-start | bytes 2359304 | tf_op jit(solution)/shard_map/ppermute | solution.py:230
  183.6 33.0 %collective-permute-start.33 = (bf16[8,24,768]{2,1,0:T(8,128)(2,1)S(1)}, bf16[8,24,768]{2,1,0:T(8,128)(2,1)S(1)}, u32[]{:S(2)}, u32[]{:S(2)}) collective-permute-start(bf16[8,24,768]{2,1,0:T(8,128)(2,1)S(1)} %dynamic-slice_bitcast_fusion.5), channel_id=1, source_target_pairs={{0,2},{1,3},{2,0},{3,1},{4,6},{5,7},{6,4},{7,5},{8,10},{9,11},{10,... | collective-permute-start | bytes 884744 | tf_op jit(solution)/shard_map/ppermute | solution.py:230
  184.5 32.2 %collective-permute-start.32 = (bf16[512,768]{1,0:T(8,128)(2,1)S(1)}, bf16[512,768]{1,0:T(8,128)(2,1)S(1)}, u32[]{:S(2)}, u32[]{:S(2)}) collective-permute-start(bf16[512,768]{1,0:T(8,128)(2,1)S(1)} %add_convert_fusion.2), channel_id=1, source_target_pairs={{0,2},{1,3},{2,0},{3,1},{4,6},{5,7},{6,4},{7,5},{8,10},{9,11},{10,... | collective-permute-start | bytes 2359304 | tf_op jit(solution)/shard_map/ppermute | solution.py:230
  216.8 15.0 %collective-permute-start.37 = (bf16[4,24,768]{2,1,0:T(8,128)(2,1)S(1)}, bf16[4,24,768]{2,1,0:T(8,128)(2,1)S(1)}, u32[]{:S(2)}, u32[]{:S(2)}) collective-permute-start(bf16[4,24,768]{2,1,0:T(8,128)(2,1)S(1)} %dynamic-slice_bitcast_fusion.7), channel_id=1, source_target_pairs={{0,4},{4,0},{8,12},{12,8},{16,20},{20,16},{24,28},{28,24},{1,5},{5... | collective-permute-start | bytes 442376 | tf_op jit(solution)/shard_map/ppermute | solution.py:230
  218.5 15.7 %collective-permute-start.38 = (bf16[1,192,768]{2,1,0:T(8,128)(2,1)S(1)}, bf16[1,192,768]{2,1,0:T(8,128)(2,1)S(1)}, u32[]{:S(2)}, u32[]{:S(2)}) collective-permute-start(bf16[1,192,768]{2,1,0:T(8,128)(2,1)S(1)} %get-tuple-element.258), channel_id=1, source_target_pairs={{0,16},{4,20},{8,24},{12,28},{16,0},{20,4},{24,8},{28,12},{1,17},{... | collective-permute-start | bytes 884744 | tf_op jit(solution)/shard_map/ppermute | solution.py:230
  221.1 13.1 %collective-permute-start.36 = (bf16[4,96,576]{2,1,0:T(8,128)(2,1)S(1)}, bf16[4,96,576]{2,1,0:T(8,128)(2,1)S(1)}, u32[]{:S(2)}, u32[]{:S(2)}) collective-permute-start(bf16[4,96,576]{2,1,0:T(8,128)(2,1)S(1)} %dynamic-slice_bitcast_fusion.2), channel_id=1, source_target_pairs={{0,4},{4,0},{8,12},{12,8},{16,20},{20,16},{24,28},{28,24},{1,5},{5... | collective-permute-start | bytes 1327112 | tf_op jit(solution)/shard_map/ppermute | solution.py:230
  235.1 7.4 %collective-permute-start.40 = (bf16[2,512,768]{2,1,0:T(8,128)(2,1)}, bf16[2,512,768]{2,1,0:T(8,128)(2,1)}, u32[]{:S(2)}, u32[]{:S(2)}) collective-permute-start(bf16[2,512,768]{2,1,0:T(8,128)(2,1)} %get-tuple-element.210), channel_id=1, source_target_pairs={{0,1},{1,0},{2,3},{3,2},{4,5},{5,4},{6,7},{7,6},{8,9},{9,8},{10,11... | collective-permute-start | bytes 4718600 | tf_op jit(solution)/shard_map/ppermute | solution.py:230
  237.9 8.7 %collective-permute-start.41 = (bf16[2,24,768]{2,1,0:T(8,128)(2,1)S(1)}, bf16[2,24,768]{2,1,0:T(8,128)(2,1)S(1)}, u32[]{:S(2)}, u32[]{:S(2)}) collective-permute-start(bf16[2,24,768]{2,1,0:T(8,128)(2,1)S(1)} %dynamic-slice_bitcast_fusion.13), channel_id=1, source_target_pairs={{0,8},{4,12},{8,0},{12,4},{16,24},{20,28},{24,16},{28,20},{1,9},{5... | collective-permute-start | bytes 221192 | tf_op jit(solution)/shard_map/ppermute | solution.py:230
  238.7 7.3 %collective-permute-start.44 = (bf16[2,96,128]{2,1,0:T(8,128)(2,1)S(1)}, bf16[2,96,128]{2,1,0:T(8,128)(2,1)S(1)}, u32[]{:S(2)}, u32[]{:S(2)}) collective-permute-start(bf16[2,96,128]{2,1,0:T(8,128)(2,1)S(1)} %get-tuple-element.270), channel_id=1, source_target_pairs={{0,12},{4,8},{8,4},{12,0},{16,28},{20,24},{24,20},{28,16},{1,13},{... | collective-permute-start | bytes 147464 | tf_op jit(solution)/shard_map/ppermute | solution.py:230
  240.6 6.0 %collective-permute-start.43 = (bf16[2,96,128]{2,1,0:T(8,128)(2,1)S(1)}, bf16[2,96,128]{2,1,0:T(8,128)(2,1)S(1)}, u32[]{:S(2)}, u32[]{:S(2)}) collective-permute-start(bf16[2,96,128]{2,1,0:T(8,128)(2,1)S(1)} %get-tuple-element.271), channel_id=1, source_target_pairs={{0,8},{4,12},{8,0},{12,4},{16,24},{20,28},{24,16},{28,20},{1,9},{5... | collective-permute-start | bytes 147464 | tf_op jit(solution)/shard_map/ppermute | solution.py:230
  242.5 7.5 %collective-permute-start.39 = (bf16[2,96,576]{2,1,0:T(8,128)(2,1)S(1)}, bf16[2,96,576]{2,1,0:T(8,128)(2,1)S(1)}, u32[]{:S(2)}, u32[]{:S(2)}) collective-permute-start(bf16[2,96,576]{2,1,0:T(8,128)(2,1)S(1)} %dynamic-slice_bitcast_fusion.6), channel_id=1, source_target_pairs={{0,8},{4,12},{8,0},{12,4},{16,24},{20,28},{24,16},{28,20},{1,9},{5... | collective-permute-start | bytes 663560 | tf_op jit(solution)/shard_map/ppermute | solution.py:230
  246.1 21.3 %collective-permute-start.50 = (bf16[512,768]{1,0:T(8,128)(2,1)}, bf16[512,768]{1,0:T(8,128)(2,1)S(1)}, u32[]{:S(2)}, u32[]{:S(2)}) collective-permute-start(bf16[512,768]{1,0:T(8,128)(2,1)} %fusion.24), channel_id=1, source_target_pairs={{0,2},{1,3},{2,0},{3,1},{4,6},{5,7},{6,4},{7,5},{8,10},{9,11},{10,... | collective-permute-start | bytes 2359304 | tf_op jit(solution)/shard_map/ppermute | solution.py:230
  250.6 5.5 %collective-permute-start.46 = (bf16[1,24,768]{2,1,0:T(8,128)(2,1)S(1)}, bf16[1,24,768]{2,1,0:T(8,128)(2,1)S(1)}, u32[]{:S(2)}, u32[]{:S(2)}) collective-permute-start(bf16[1,24,768]{2,1,0:T(8,128)(2,1)S(1)} %get-tuple-element.274), channel_id=1, source_target_pairs={{0,16},{4,20},{8,24},{12,28},{16,0},{20,4},{24,8},{28,12},{1,17},{... | collective-permute-start | bytes 110600 | tf_op jit(solution)/shard_map/ppermute | solution.py:230
  254.6 8.0 %collective-permute-start.45 = (bf16[1,96,704]{2,1,0:T(8,128)(2,1)S(1)}, bf16[1,96,704]{2,1,0:T(8,128)(2,1)S(1)}, u32[]{:S(2)}, u32[]{:S(2)}) collective-permute-start(bf16[1,96,704]{2,1,0:T(8,128)(2,1)S(1)} %get-tuple-element.268), channel_id=1, source_target_pairs={{0,16},{4,20},{8,24},{12,28},{16,0},{20,4},{24,8},{28,12},{1,17},{... | collective-permute-start | bytes 405512 | tf_op jit(solution)/shard_map/ppermute | solution.py:230
  265.5 7.0 %collective-permute-start.47 = (bf16[24,1472]{1,0:T(8,128)(2,1)}, bf16[24,1472]{1,0:T(8,128)(2,1)S(1)}, u32[]{:S(2)}, u32[]{:S(2)}) collective-permute-start(bf16[24,1472]{1,0:T(8,128)(2,1)} %get-tuple-element.222), channel_id=1, source_target_pairs={{0,1},{1,0},{2,3},{3,2},{4,5},{5,4},{6,7},{7,6},{8,9},{9,8},{10,11... | collective-permute-start | bytes 211976 | tf_op jit(solution)/shard_map/ppermute | solution.py:230
  265.5 7.0 %collective-permute-start.48 = (bf16[24,1472]{1,0:T(8,128)(2,1)}, bf16[24,1472]{1,0:T(8,128)(2,1)S(1)}, u32[]{:S(2)}, u32[]{:S(2)}) collective-permute-start(bf16[24,1472]{1,0:T(8,128)(2,1)} %get-tuple-element.223), channel_id=1, source_target_pairs={{0,2},{1,3},{2,0},{3,1},{4,6},{5,7},{6,4},{7,5},{8,10},{9,11},{10,... | collective-permute-start | bytes 211976 | tf_op jit(solution)/shard_map/ppermute | solution.py:230
  266.1 6.4 %collective-permute-start.49 = (bf16[24,1472]{1,0:T(8,128)(2,1)}, bf16[24,1472]{1,0:T(8,128)(2,1)S(1)}, u32[]{:S(2)}, u32[]{:S(2)}) collective-permute-start(bf16[24,1472]{1,0:T(8,128)(2,1)} %get-tuple-element.224), channel_id=1, source_target_pairs={{0,3},{1,2},{2,1},{3,0},{4,7},{5,6},{6,5},{7,4},{8,11},{9,10},{10,... | collective-permute-start | bytes 211976 | tf_op jit(solution)/shard_map/ppermute | solution.py:230
  (65 other events, 704.0 us)

commit v5 on v4

--- a/solution.py
+++ b/solution.py
@@ -107,7 +107,7 @@
 
 def attend_back_kernel(
     me_ref, qkv_ref, go_ref, full_ref, lse_ref, seg_row_ref, seg_col_ref, h_ref, grad_ref, d_w_ref,
-    gq_ref, dot_ref, total_ref, *, heads, hd
+    gq_ref, dot_ref, total_ref, gk_ref, gv_ref, *, heads, hd
 ):
     me = me_ref[0]
     kj = pl.program_id(0)
@@ -126,37 +126,46 @@
             for h in range(heads):
                 dot_ref[b, h : h + 1, :] = jnp.sum(prod[h * hd : (h + 1) * hd], 0, keepdims=True)
 
-    keys = [qkv_ref[rk, :, width + h * hd : width + (h + 1) * hd] for h in range(heads)]
-    values = [qkv_ref[rk, :, 2 * width + h * hd : 2 * width + (h + 1) * hd] for h in range(heads)]
-    seg_k = seg_col_ref[rk]
-
-    def step(rq, state, causal):
-        allowed = seg_k == seg_row_ref[rq]
-        if causal:
-            k_pos = lax.broadcasted_iota(jnp.int32, (block, block), 0)
-            q_pos = lax.broadcasted_iota(jnp.int32, (block, block), 1)
-            allowed = allowed & (k_pos <= q_pos)
-        new = []
-        for h in range(heads):
-            gk, gv = state[h]
-            query = qkv_ref[rq, :, h * hd : (h + 1) * hd] * low_scale
-            go = go_ref[rq, h * hd : (h + 1) * hd, :]
-            scores = jnp.where(allowed, dot_nt(keys[h], query), MASKED)
-            weights = jnp.exp(scores - lse_ref[rq, h : h + 1, :])
-            gw = dot_nn(values[h], go)
-            ds = (weights * (gw - dot_ref[rq, h : h + 1, :])).astype(BF16)
-            gv = gv + dot_nt(weights.astype(BF16), go)
-            gk = gk + dot_nn(ds, query)
-            gq_ref[rq, h * hd : (h + 1) * hd, :] += dot_tn(keys[h], ds)
-            new.append((gk, gv))
-        return tuple(new)
-
-    zero = jnp.zeros((block, hd), F32)
-    state = step(rk, tuple((zero, zero) for _ in range(heads)), True)
-    state = lax.fori_loop(kj + 1, n, lambda qi, c: step(qi ^ me, c, False), state)
+    def step(rq, causal):
+        for k0 in range(0, block, 512):
+            for q0 in range(0, block, 256):
+                if causal and q0 + 256 <= k0:
+                    continue
+                rows, cols = slice(k0, k0 + 512), slice(q0, q0 + 256)
+                allowed = seg_col_ref[rk, rows, :] == seg_row_ref[rq][:, cols]
+                if causal and q0 < k0 + 512:
+                    k_pos = lax.broadcasted_iota(jnp.int32, (512, 256), 0) + k0
+                    q_pos = lax.broadcasted_iota(jnp.int32, (512, 256), 1) + q0
+                    allowed = allowed & (k_pos <= q_pos)
+                for h in range(heads):
+                    head = slice(h * hd, (h + 1) * hd)
+                    query = qkv_ref[rq, cols, head] * low_scale
+                    key = qkv_ref[rk, rows, width + h * hd : width + (h + 1) * hd]
+                    value = qkv_ref[rk, rows, 2 * width + h * hd : 2 * width + (h + 1) * hd]
+                    go = go_ref[rq, head, cols]
+                    scores = jnp.where(allowed, dot_nt(key, query), MASKED)
+                    weights = jnp.exp(scores - lse_ref[rq, h : h + 1, cols])
+                    gw = dot_nn(value, go)
+                    ds = (weights * (gw - dot_ref[rq, h : h + 1, cols])).astype(BF16)
+                    gv = dot_nt(weights.astype(BF16), go)
+                    gk = dot_nn(ds, query)
+                    if causal and q0 <= k0:
+                        gv_ref[h, rows, :] = gv
+                        gk_ref[h, rows, :] = gk
+                    else:
+                        gv_ref[h, rows, :] += gv
+                        gk_ref[h, rows, :] += gk
+                    gq_ref[rq, head, cols] += dot_tn(key, ds)
+
+    step(rk, True)
+
+    @pl.loop(kj + 1, n)
+    def _(qi):
+        step(qi ^ me, False)
+
     grad_ref[0, :, :width] = (gq_ref[rk] * scale).T.astype(BF16)
     for h in range(heads):
-        gk, gv = state[h]
+        gk, gv = gk_ref[h], gv_ref[h]
         grad_ref[0, :, width + h * hd : width + (h + 1) * hd] = gk.astype(BF16)
         grad_ref[0, :, 2 * width + h * hd : 2 * width + (h + 1) * hd] = gv.astype(BF16)
     total_ref[...] += dot_tn(h_ref[0], grad_ref[0])
@@ -186,6 +195,8 @@
                 pltpu.VMEM((n, width, block), F32),
                 pltpu.VMEM((n, 8, block), F32),
                 pltpu.VMEM((dm, wide), F32),
+                pltpu.VMEM((heads, block, hd), F32),
+                pltpu.VMEM((heads, block, hd), F32),
             ],
         ),
         out_shape=[
@@ -257,8 +268,7 @@
     return lists
 
 
-def settle(parts, index, size, masks, count):
-    ids = gathered_ids(masks)
+def settle(parts, index, size, ids, count):
     rows = parts[0].shape[1] // count
     if rows % 16 == 0:
         return parts, ids
@@ -333,18 +343,22 @@
     ]
 
 
-def enter_kernel(me_ref, *refs, ids, n, width):
-    count = len(ids)
+def enter_kernel(me_ref, *refs, ids, n, width, cut):
+    count = len(ids[0]) + len(ids[1])
     pieces, (x_ref, qkv_ref, h_ref, w_ref, vec_ref, tile_ref, add_ref) = refs[:count], refs[count:]
     me = me_ref[0]
 
     @pl.when(pl.program_id(0) == 0)
     def _():
-        def put(k, where, rows):
-            w_ref[where, :] = rows[:, : 3 * width]
-            tile_ref[where, :] = rows[:, 3 * width :].astype(F32)
-
-        place(pieces, ids, me_ref[1], 1, put)
+        def put_left(k, where, rows):
+            w_ref[where, :cut] = rows
+
+        def put_right(k, where, rows):
+            w_ref[where, cut:] = rows[:, : 3 * width - cut]
+            tile_ref[where, :] = rows[:, 3 * width - cut :].astype(F32)
+
+        place(pieces[: len(ids[0])], ids[0], me_ref[1], 1, put_left)
+        place(pieces[len(ids[0]) :], ids[1], me_ref[1], 1, put_right)
         vecs = tile_ref[...].T[:16]
         vec_ref[...] = vecs
         for i, row in ((0, 6), (2, 7)):
@@ -362,6 +376,8 @@
 
 def enter(me, pieces, ids, x_all, width):
     n, block, dm = x_all.shape
+    cut = pieces[0][0].shape[2]
+    pieces = [*pieces[0], *pieces[1]]
 
     def whole(shape):
         return pl.BlockSpec(shape, lambda i, me: (0,) * len(shape))
@@ -370,7 +386,7 @@
         return pl.BlockSpec((1, block, width), lambda i, me: (i, 0, 0))
 
     return pl.pallas_call(
-        functools.partial(enter_kernel, ids=ids, n=n, width=width),
+        functools.partial(enter_kernel, ids=ids, n=n, width=width, cut=cut),
         grid_spec=pltpu.PrefetchScalarGridSpec(
             num_scalar_prefetch=1,
             grid=(n,),
@@ -395,8 +411,7 @@
     me = me_ref[0]
     i = pl.program_id(0)
     if base:
-        count = len(ids[0])
-        left, right, refs = refs[:count], refs[count : 2 * count], refs[2 * count :]
+        pieces, refs = refs[: len(ids)], refs[len(ids) :]
         x_ref, g_ref, vec_ref = refs[:3]
         h_ref, act_ref, gu_ref, low_ref, high_ref, sum_ref, out_w_ref, up_ref, down_ref = refs[3:]
     else:
@@ -409,12 +424,11 @@
     def _():
         if base:
             sum_ref[...] = jnp.zeros_like(sum_ref)
-            for first, pieces, held in ((0, left, ids[0]), (part // 2, right, ids[1])):
-
-                def put(k, where, rows, first=first):
-                    (out_w_ref, up_ref, down_ref)[k][where, first : first + part // 2] = rows
-
-                place(pieces, held, me_ref[1], 3, put)
+
+            def put(k, where, rows):
+                (out_w_ref, up_ref, down_ref)[k][where, :] = rows
+
+            place(pieces, ids, me_ref[1], 3, put)
         else:
             sum_ref[...] = sum_in_ref[...]
 
@@ -472,8 +486,7 @@
         return pl.BlockSpec((1, width, block), lambda i, me: ((i + base) ^ p, 0, 0))
 
     if base:
-        part = 2 * weights[0][0].shape[2]
-        weights = [*weights[0], *weights[1]]
+        part = weights[0].shape[2]
     wide = jax.ShapeDtypeStruct((2, block, dm), BF16)
     hidden = jax.ShapeDtypeStruct((2, block, part), BF16)
     low = jax.ShapeDtypeStruct((block, dm), BF16)
@@ -642,16 +655,16 @@
     )(me, x_all, grads, w, vecs, sums_two, sums_up)
 
 
-def hand_over_kernel(me_ref, *refs, n, rows):
-    blob_a, blob_b, outs_a, outs_b, feed_a, feed_b = refs[:6]
-    pieces, (out_ref, down_ref, last_ref) = refs[6 : 6 + n], refs[6 + n :]
+def hand_over_kernel(me_ref, *refs, n, rows, first):
+    blob_a, blob_b, feed_a, feed_b = refs[:4]
+    pieces, (out_ref, down_ref, last_ref) = refs[4 : 4 + n], refs[4 + n :]
     size = n * rows
     blob = blob_a[...].astype(F32) + blob_b[...].astype(F32)
     feed = feed_a[...].astype(F32) + feed_b[...].astype(F32)
-    out_ref[...] = outs_a[...].astype(F32) + outs_b[...].astype(F32)
+    out_ref[...] = blob[size:]
     down_ref[...] = feed[size:]
-    last_ref[...] = blob[:, -LANES:]
-    both = jnp.concatenate([blob, feed[:size]], 1)
+    last_ref[...] = blob[:size, first - LANES : first]
+    both = jnp.concatenate([blob[:size, :first], feed[:size]], 1)
     parts = [both[t * rows : (t + 1) * rows] for t in range(n)]
     for p, ref in enumerate(pieces):
         chosen = parts[0]
@@ -660,23 +673,23 @@
         ref[...] = chosen.astype(BF16)
 
 
-def hand_over(me, blob, outs, feeds, rows, n):
-    args = [*blob, *outs, *feeds]
-    wide = blob[0].shape[1] + feeds[0].shape[1]
-    size = blob[0].shape[0]
+def hand_over(me, blob, feeds, rows, n, first):
+    dm = blob[0].shape[1]
+    part = feeds[0].shape[1]
+    size = n * rows
     vmem = pl.BlockSpec(memory_space=pltpu.VMEM)
     *pieces, out, down, last = pl.pallas_call(
-        functools.partial(hand_over_kernel, n=n, rows=rows),
-        in_specs=[pl.BlockSpec(memory_space=pltpu.SMEM)] + [vmem] * 6,
+        functools.partial(hand_over_kernel, n=n, rows=rows, first=first),
+        in_specs=[pl.BlockSpec(memory_space=pltpu.SMEM)] + [vmem] * 4,
         out_specs=[vmem] * (n + 3),
-        out_shape=[jax.ShapeDtypeStruct((rows, wide), BF16)] * n
+        out_shape=[jax.ShapeDtypeStruct((rows, first + part), BF16)] * n
         + [
-            jax.ShapeDtypeStruct(outs[0].shape, F32),
-            jax.ShapeDtypeStruct((feeds[0].shape[0] - size, feeds[0].shape[1]), F32),
+            jax.ShapeDtypeStruct((rows, dm), F32),
+            jax.ShapeDtypeStruct((feeds[0].shape[0] - size, part), F32),
             jax.ShapeDtypeStruct((size, LANES), F32),
         ],
         name="hand_over",
-    )(me, *args)
+    )(me, *blob, *feeds)
     return pieces, out, down, last
 
 
@@ -780,64 +793,59 @@
     lane = lax.broadcasted_iota(jnp.int32, (size, first), 1)
     one = jnp.where(lane == 3 * width + 8, jnp.pad(up_bias, (0, size - ff_rows))[:, None], pieces[:, :first])
     two = jnp.concatenate([pieces[:, first:start], pieces[:, start + lanes :], w_down], 0)
-    left, right = two[:, : dm // 2], two[:, dm // 2 :]
 
     turned = masks[:-2] + masks[:-3:-1]
-    ones, lefts, rights = [one[None]], None, None
-    for step, mask in enumerate(masks):
-        both = jnp.concatenate(ones, 0)
-        if step == len(masks) - 2:
-            both, left, right, seg_row, seg_col = lax.optimization_barrier((both, left, right, seg_row, seg_col))
-            lefts, rights = [left[None]], [right[None]]
-        got = swap(both, "dp", nd, mask)
-        if step == len(masks) - 2:
-            got, x_far = lax.optimization_barrier((got, x_far))
-            g_far = swap(tie(g, x_far), "seq", ns, far)
-            lefts[0], rights[0] = tie(lefts[0], got), tie(rights[0], got)
-        ones.append(got)
-
-    for step in range(len(masks) - 2):
-        lefts.append(swap(jnp.concatenate(lefts, 0), "dp", nd, masks[step]))
-        rights.append(swap(jnp.concatenate(rights, 0), "dp", nd, turned[step]))
+    ones = [one[None]]
+    for mask in masks[:-2]:
+        ones.append(swap(jnp.concatenate(ones, 0), "dp", nd, mask))
+    ones = jnp.concatenate(ones, 0)
+    cut = -(-(first // 2) // LANES) * LANES
+    ones = [ones[:, :, :cut]], [ones[:, :, cut:]]
+    ones[0][0], ones[1][0], two, seg_row, seg_col = lax.optimization_barrier(
+        (ones[0][0], ones[1][0], two, seg_row, seg_col)
+    )
+    for parts, order in zip(ones, (masks, turned)):
+        parts.append(swap(parts[0], "dp", nd, order[-2]))
+    ones[0][1], ones[1][1], x_far = lax.optimization_barrier((ones[0][1], ones[1][1], x_far))
+    g_far = swap(tie(g, x_far), "seq", ns, far)
+    last = [jnp.concatenate(parts, 0) for parts in ones]
+    twos = [tie(two, *last)[None]]
+    for parts, held, order in zip(ones, last, (masks, turned)):
+        parts.append(swap(held, "dp", nd, order[-1]))
+
+    for mask in masks[:-2]:
+        twos.append(swap(jnp.concatenate(twos, 0), "dp", nd, mask))
     parts = {0: x_own, far: x_far}
     for mask in bits_of(ns)[-2::-1]:
         for p in list(parts):
             parts[p | mask] = swap(parts[p], "seq", ns, mask)
     x_all = jnp.stack([parts[p] for p in range(ns)])
 
-    ones, ids = settle(ones, d, nd, masks, 1)
-    ones[-1], x_all = lax.optimization_barrier((ones[-1], x_all))
+    ids = [gathered_ids(order) for order in (masks, turned)]
+    ids = [[sum(i[:-2], [])] + i[-2:] for i in ids]
+    ones, ids = zip(*[settle(p, d, nd, i, 1) for p, i in zip(ones, ids)])
+    ones, x_all = lax.optimization_barrier((ones, x_all))
     qkv, h_one, w_qkv, vecs = enter(me, ones, ids, x_all, width)
-    qkv, h_one, w_qkv, vecs, g_far, lefts[-1], rights[-1] = lax.optimization_barrier(
-        (qkv, h_one, w_qkv, vecs, g_far, lefts[-1], rights[-1])
-    )
-
-    def onward(parts, mask):
-        held = jnp.concatenate(parts, 0)
-        return held, swap(held, "dp", nd, mask)
-
-    left_held, left_got = onward(lefts, masks[-2])
-    right_held, right_got = onward(rights, turned[-2])
+    qkv, h_one, w_qkv, vecs, g_far, twos = lax.optimization_barrier((qkv, h_one, w_qkv, vecs, g_far, twos))
+    two = jnp.concatenate(twos, 0)
+    twos = [two] + [swap(two, "dp", nd, p) for p in (1, 2)]
+
     g_parts = {0: g, far: g_far}
     for mask in bits_of(ns)[-2::-1]:
         for p in list(g_parts):
             g_parts[p | mask] = swap(g_parts[p], "seq", ns, mask)
-    qkv, left_held, right_held = lax.optimization_barrier((qkv, left_held, right_held))
+    qkv, two = lax.optimization_barrier((qkv, two))
     o_low, o_full, lse = attend(me, qkv, seg_row, seg_col, heads, hd)
-    o_low, o_full, lse, left_got, right_got, *g_last = lax.optimization_barrier(
-        (o_low, o_full, lse, left_got, right_got, g_parts[1], g_parts[ns - 1])
+    o_low, o_full, lse, twos[1:], *g_last = lax.optimization_barrier(
+        (o_low, o_full, lse, twos[1:], g_parts[1], g_parts[ns - 1])
     )
-    o_got = spread_seq(o_low, ns)
-    lefts.append(left_got)
-    rights.append(right_got)
-    lefts.append(onward(lefts, masks[-1])[1])
-    rights.append(onward(rights, turned[-1])[1])
     g_all = jnp.stack([g, g_last[0], g_far, g_last[1]])
-    lefts, left_ids = settle(lefts, d, nd, masks, 3)
-    rights, right_ids = settle(rights, d, nd, turned, 3)
-    ids = (left_ids, right_ids)
+    o_got = spread_seq(o_low, ns, (g_all,))
+    twos.append(swap(tie(two, o_low), "dp", nd, 3))
+    ids = sum(gathered_ids(masks[:-2]), [])
+    twos, ids = settle(twos, d, nd, [[r ^ p for r in ids] for p in range(4)], 3)
     far_h, far_act, far_gu, gh_two, gh_three, sums_up, *weights = feed(
-        me, o_got, x_all, g_all, vecs, 2, (lefts, rights), ids
+        me, o_got, x_all, g_all, vecs, 2, twos, ids
     )
     w_out_all, _, w_down_own = weights
 
@@ -860,9 +868,10 @@
     far_got, up_sent, down_sent = lax.optimization_barrier((far_got, up_sent, down_sent))
     *gos, gx_two, d_out, sums_two = turn(me, o_got, gh_zero, near_got, far_got, x_two, g, w_out_all, vecs)
     go_got = [gos[0]] + [swap(gos[p], "seq", ns, p) for p in range(1, ns)]
-    d_out, sums_two, up_got, down_got = lax.optimization_barrier((d_out, sums_two, up_got, down_got))
-    act, far_act = lax.optimization_barrier((act, far_act, gos[0]))[:2]
+    go_got[1], d_out, sums_two = lax.optimization_barrier((go_got[1], d_out, sums_two))
+    act, far_act = lax.optimization_barrier((act, far_act, go_got[1]))[:2]
     out_parts = [dot_nn(a, w_down_own).astype(BF16) for a in (act[0], act[1], far_act[0], far_act[1])]
+    up_got, down_got = lax.optimization_barrier((up_got, down_got, out_parts))[:2]
     out_sent = add_low(out_parts[2], swap(out_parts[3], "seq", ns, 1))
     out_near = swap(out_parts[1], "seq", ns, 1)
     out_far = swap(tie(out_sent, go_got[-1]), "seq", ns, 2)
@@ -880,45 +889,46 @@
     grads, d_qkv, out_near, out_far, outs_got, up_got, down_got = lax.optimization_barrier(
         (grads, d_qkv, out_near, out_far, outs_got, up_got, down_got)
     )
-    blob_keep, blob_sent = halves(d_qkv.reshape(nd, size, 3 * width), d, nd, 1)
+    blob = jnp.concatenate(
+        [
+            jnp.pad(d_qkv.reshape(nd, size, 3 * width), ((0, 0), (0, 0), (0, dm - 3 * width))),
+            add_low(outs_keep, outs_got),
+        ],
+        1,
+    )
+    blob_keep, blob_sent = halves(blob, d, nd, 1)
     blob_got = swap(blob_sent, "dp", nd, 1)
     feeds = jnp.concatenate([add_low(up_keep, up_got), add_low(down_keep, down_got)], 1)
     feed_keep, feed_sent = halves(feeds, d >> 2, nd // 4, 1)
     feed_got = swap(feed_sent, "dp", nd, 4)
-    outs_keep, outs_sent = halves(add_low(outs_keep, outs_got), d, nd, 1)
-    outs_got = swap(outs_sent, "dp", nd, 1)
-    grads = lax.optimization_barrier((grads, blob_sent, feed_sent, outs_sent))[0]
+    grads = lax.optimization_barrier((grads, blob_sent, feed_sent))[0]
     even, odd, tile = leave(me, x_all, grads, w_qkv, vecs, sums_two, sums_up)
-    even, odd, tile, blob_got, outs_got, feed_got = lax.optimization_barrier(
-        (even, odd, tile, blob_got, outs_got, feed_got)
-    )
-    blob_keep, blob_sent = halves(add_low(blob_keep, blob_got), d >> 1, nd // 2, 1)
-    blob_got = swap(blob_sent, "dp", nd, 2)
+    even, odd, tile, blob_got, feed_got = lax.optimization_barrier((even, odd, tile, blob_got, feed_got))
     tile = tile.reshape(nd // 4, 4, size, LANES)
     tiles = [lax.dynamic_index_in_dim(tile, (d & 3) ^ p, 1, False) for p in range(4)]
-    tiles = [swap(tiles[p], "dp", nd, p) if p else tiles[0] for p in range(4)]
-    outs_keep, outs_sent = halves(add_low(outs_keep, outs_got), d >> 1, nd // 2, 1)
-    outs_got = swap(outs_sent, "dp", nd, 2)
+    tiles = [jnp.pad(t, ((0, 0), (0, rows), (3 * width, dm - first))) for t in tiles[::2]] + tiles[1::2]
+    blob_keep, blob_sent = halves(add_low(blob_keep, blob_got), d >> 1, nd // 2, 1)
+    blob_keep, blob_sent = blob_keep + tiles[0], blob_sent + tiles[1]
+    blob_got = swap(blob_sent, "dp", nd, 2)
+    tiles = [swap(t, "dp", nd, p) for t, p in zip(tie(tiles[2:], blob_sent), (1, 3))]
     keep, sent, got = collect_pairs(even, odd, ns)
-    blob_got, sent, outs_got, tiles[1:] = lax.optimization_barrier((blob_got, sent, outs_got, tiles[1:]))
-    tile = sum(t.astype(F32) for t in tiles).astype(BF16)
-    blob = jnp.concatenate([add_low(blob_keep, blob_got), tile], 2)
+    blob_got, sent, tiles = lax.optimization_barrier((blob_got, sent, tiles))
+    tile = jnp.pad(tiles[0].astype(F32) + tiles[1].astype(F32), ((0, 0), (0, rows), (3 * width, dm - first)))
+    blob = (blob_keep.astype(F32) + blob_got.astype(F32) + tile).astype(BF16)
     blob_keep, blob_sent = halves(blob, d >> 2, nd // 4, 1)
     blob_got = swap(blob_sent, "dp", nd, 4)
-    outs_keep, outs_sent = halves(add_low(outs_keep, outs_got), d >> 2, nd // 4, 1)
-    outs_got = swap(outs_sent, "dp", nd, 4)
-    blob_got, outs_got = lax.optimization_barrier((blob_got, outs_got))
+    blob_got, sent = lax.optimization_barrier((blob_got, sent))
     if nd > 8:
-        rest = [(blob_keep, blob_got), (outs_keep, outs_got), (feed_keep, feed_got)]
+        rest = [(blob_keep, blob_got), (feed_keep, feed_got)]
         rest = [collect_dp(add_low(a, b), d >> 3, nd // 8, BF16, shift=3) for a, b in rest]
         rest = [(v, jnp.zeros_like(v)) for v in rest]
     else:
-        rest = [(blob_keep[0], blob_got[0]), (outs_keep[0], outs_got[0]), (feed_keep[0], feed_got[0])]
-    pieces, sum_out, sum_down, last = hand_over(me, *rest, rows, ns)
+        rest = [(blob_keep[0], blob_got[0]), (feed_keep[0], feed_got[0])]
+    pieces, sum_out, sum_down, last = hand_over(me, *rest, rows, ns, first)
     out = out_parts[0].astype(F32) + out_near.astype(F32) + out_far.astype(F32) + x_two + vecs[5:6]
     trades = [pieces[0]] + [swap(pieces[p], "seq", ns, p) for p in range(1, ns)]
     gh_one = keep.astype(F32) + got.astype(F32)
-    n_own, inv_own = normed_parts(x_own.astype(F32))
+    n_own, inv_own = normed_parts(tie(x_own, pieces[0]).astype(F32))
     grad_x = gx_two + normalize_back(gh_one, n_own, inv_own, vecs[0:1])
     trades, grad_x, out, last = lax.optimization_barrier((trades, grad_x, out, last))
     sum_q, sum_k, sum_v, vec_sum, sum_up = finish(me, trades, width, nd)

time: 282 us -> 278 us (0.986)
  Pallas kernels: 104 us -> 98.3 us
    pallas_call x1, Pallas kernels: 30.5 us -> 26.8 us  [attend_back(): pl.pallas_call(functools.partial(attend_back_kernel, heads=heads, hd=hd),...]
    unnamed x127 -> x124, local copies, waits for them, and re-layouts: 7.4 us -> 8.79 us
    ppermute x51 -> x47, starting transfers between devices: 46 us -> 46.3 us  [swap(): return lax.ppermute(value, axis, [(i, i ^ mask) for i in range(size)])]
    ppermute x51 -> x47, waiting for transfers between devices: 65.7 us -> 65.7 us  [swap(): return lax.ppermute(value, axis, [(i, i ^ mask) for i in range(size)])]
  transfers between devices with their start and end apart: 51 -> 47, of which waited for: 16 -> 14; matrix products, arithmetic and copies ran while one was open for 16% -> 16% of each run, Pallas kernels for 31% -> 27%
where the time goes in v5:
time: 278 us; the launch traced here: 274 us
  Pallas kernels  98.3 us (35%)
  waiting for transfers between devices  65.7 us (24%)
  starting transfers between devices  46.3 us (17%)
  other arithmetic  23.5 us (8%)
  local copies, waits for them, and re-layouts  21.2 us (8%)
  matrix products  16.9 us (6%)
    ppermute x47, waiting for transfers between devices, swap(): return lax.ppermute(value, axis, [(i, i ^ mask) for i in range(size)])  65.7 us
    ppermute x47, starting transfers between devices, swap(): return lax.ppermute(value, axis, [(i, i ^ mask) for i in range(size)])  46.3 us
    pallas_call x2, Pallas kernels, feed(): pl.pallas_call(functools.partial(feed_kernel, n=n, base=base, tile=256 if...  27.8 us
    pallas_call x1, Pallas kernels, attend_back(): pl.pallas_call(functools.partial(attend_back_kernel, heads=heads, hd=hd),...  26.8 us
    pallas_call x1, Pallas kernels, attend(): pl.pallas_call(functools.partial(attend_kernel, heads=heads, hd=hd), grid...  18 us
    dot_general x4, matrix products, over_rows(): return jnp.einsum('nbk,nbc->kc', a, b, preferred_element_type=F32)  11.2 us
    unnamed x124, local copies, waits for them, and re-layouts  8.79 us
    pallas_call x1, Pallas kernels, leave(): pl.pallas_call(leave_kernel, grid_spec=pltpu.PrefetchScalarGridSpec(num_s...  8.14 us
  transfers between devices with their start and end apart: 47, of which 14 were waited for; matrix products, arithmetic and copies ran while one was open for 16% of the time, Pallas kernels for 27%

profile of v5, /device:TPU:0, one launch (start us, length us, event | category | flops | bytes accessed | tf_op | source)
XLA Modules:
  0.0 273.9 jit_solution(2420320897995890365)
XLA Ops:
  7.3 2.6 collective-permute-start.1
  9.9 1.7 collective-permute-start.6
  12.2 1.8 collective-permute-done.1
  13.9 2.0 collective-permute-done
  17.4 2.7 collective-permute-start.3
  22.2 5.8 %collective-permute-done.3 = bf16[1,96,704]{2,1,0:T(8,128)(2,1)S(1)} collective-permute-done((bf16[1,96,704]{2,1,0:T(8,128)(2,1)S(1)}, bf16[1,96,704]{2,1,0:T(8,128)(2,1)S(1)}, u32[]{:S(2)}, u32[]{:S(2)}) %collective-permute-start.3) | collective-permute-done | bytes 135200 | tf_op jit(solution)/shard_map/ppermute | solution.py:241
  28.9 1.5 collective-permute-start.5
  30.4 4.0 %collective-permute-done.5.refs_4_ = bf16[2,96,320]{2,1,0:T(8,128)(2,1)S(1)} collective-permute-done((bf16[2,96,320]{2,1,0:T(8,128)(2,1)S(1)}, bf16[2,96,320]{2,1,0:T(8,128)(2,1)S(1)}, u32[]{:S(2)}, u32[]{:S(2)}) %collective-permute-start.5) | collective-permute-done | bytes 122912 | tf_op jit(solution)/shard_map/ppermute | solution.py:241
  35.2 1.6 collective-permute-start.7
  36.8 1.5 collective-permute-start.11
  39.5 2.6 collective-permute-start.12
  42.2 2.2 pad_maximum_fusion.refs_6_.refs_8_.refs_4_.x_ref
  44.4 9.6 %collective-permute-done.8.refs_5_ = bf16[4,96,320]{2,1,0:T(8,128)(2,1)S(1)} collective-permute-done((bf16[4,96,320]{2,1,0:T(8,128)(2,1)S(1)}, bf16[4,96,320]{2,1,0:T(8,128)(2,1)S(1)}, u32[]{:S(2)}, u32[]{:S(2)}) %collective-permute-start.8) | collective-permute-done | bytes 245792 | tf_op jit(solution)/shard_map/ppermute | solution.py:241
  54.1 6.0 %enter.1 = (bf16[4,512,576]{2,1,0:T(8,128)(2,1)S(1)}, bf16[4,512,768]{2,1,0:T(8,128)(2,1)S(1)}, bf16[768,576]{1,0:T(8,128)(2,1)S(1)}, f32[16,768]{1,0:T(8,128)S(1)}) custom-call(s32[2]{0:T(128)S(1)} %pad_add_fusion.me_ref, bf16[2,96,384]{2,1,0:T(8,128)(2,1)S(1)} %fusion.42.refs_0_, bf16[2,96,384]{2,1,0:T(8,128)(2,1)S(1)} %copy-done.4, ...), custom_call_target="tpu_custom_call" | custom-call | flops 5000000000 | bytes 8000000 | tf_op jit(solution)/shard_map/enter/pallas_call | solution.py:388
  64.4 18.0 %attend.1 = (bf16[4,192,512]{2,1,0:T(8,128)(2,1)S(1)}, f32[4,192,512]{2,1,0:T(8,128)S(1)}, f32[4,8,512]{2,1,0:T(8,128)S(1)}) custom-call(s32[2]{0:T(128)S(1)} %pad_add_fusion.me_ref, bf16[4,512,576]{2,1,0:T(8,128)(2,1)S(1)} %get-tuple-element.159.qkv_ref, s32[4,1,512]{2,1,0:T(1,128)S(1)} %maximum_convert_fusion.1.seg_row_ref, s32[4,512,1]{2,1,0:T(8,128)S(1)} %copy-done.1), custom_call_target="tpu_custom_call" | custom-call | flops 20000000000 | bytes 8000000 | tf_op jit(solution)/shard_map/attend/pallas_call | solution.py:87
  85.0 2.7 collective-permute-start.20
  87.7 3.0 %pad_maximum_fusion.1.refs_9_.refs_5_ = bf16[4,512,768]{2,1,0:T(8,128)(2,1)} fusion(bf16[1,512,768]{2,1,0:T(8,128)(2,1)S(1)} %bitcast.190, bf16[1,512,768]{2,1,0:T(8,128)(2,1)S(1)} %bitcast.188, bf16[1,512,768]{2,1,0:T(8,128)(2,1)} %bitcast.28, bf16[1,512,768]{2,1,0:T(8,128)(2,1)} %param.19), kind=kLoop, calls=%fused_computation.1 | loop fusion | flops 4718592 | bytes 6291456 | tf_op jit(solution)/shard_map/stack | solution.py:842
  90.7 13.1 %collective-permute-done.18.refs_2_ = bf16[4,192,512]{2,1,0:T(8,128)(2,1)S(1)} collective-permute-done((bf16[4,192,512]{2,1,0:T(8,128)(2,1)S(1)}, bf16[4,192,512]{2,1,0:T(8,128)(2,1)S(1)}, u32[]{:S(2)}, u32[]{:S(2)}) %collective-permute-start.18) | collective-permute-done | bytes 786464 | tf_op jit(solution)/shard_map/ppermute | solution.py:241
  103.8 4.2 %collective-permute-done.20.refs_7_ = bf16[2,288,768]{2,1,0:T(8,128)(2,1)S(1)} collective-permute-done((bf16[2,288,768]{2,1,0:T(8,128)(2,1)S(1)}, bf16[2,288,768]{2,1,0:T(8,128)(2,1)S(1)}, u32[]{:S(2)}, u32[]{:S(2)}) %collective-permute-start.20) | collective-permute-done | bytes 884768 | tf_op jit(solution)/shard_map/ppermute | solution.py:241
  108.9 14.3 %feed_far.1 = (bf16[2,512,768]{2,1,0:T(8,128)(2,1)}, bf16[2,512,768]{2,1,0:T(8,128)(2,1)}, bf16[2,512,768]{2,1,0:T(8,128)(2,1)}, bf16[512,768]{1,0:T(8,128)(2,1)...) custom-call(s32[2]{0:T(128)S(1)} %pad_add_fusion.me_ref, ...), custom_call_target="tpu_custom_call" | custom-call | flops 8999999488 | bytes 16000000 | tf_op jit(solution)/shard_map/feed_far/pallas_call | solution.py:506
  123.4 3.4 %convolution_bitcast_fusion = f32[768,768]{1,0:T(8,128)S(1)} fusion(bf16[2,512,768]{2,1,0:T(8,128)(2,1)} %get-tuple-element.200, bf16[1,512,768]{2,1,0:T(8,128)(2,1)} %bitcast.191, bf16[1,512,768]{2,1,0:T(8,128)(2,1)} %bitcast.189), kind=kOutput, calls=%fused_computation.14 | convolution fusion | flops 1208745984 | bytes 5505024 | tf_op jit(solution)/shard_map/nbk,nbc->kc/dot_general | solution.py:853
  126.9 1.5 fusion.50
  130.6 13.5 %feed_near.1 = (bf16[2,512,768]{2,1,0:T(8,128)(2,1)}, bf16[2,512,768]{2,1,0:T(8,128)(2,1)}, bf16[2,512,768]{2,1,0:T(8,128)(2,1)}, bf16[512,768]{1,0:T(8,128)(2,1...) custom-call(s32[2]{0:T(128)S(1)} %pad_add_fusion.me_ref, ...), custom_call_target="tpu_custom_call" | custom-call | flops 8999999488 | bytes 16000000 | tf_op jit(solution)/shard_map/feed_near/pallas_call | solution.py:506
  144.4 3.5 %fusion.2 = bf16[768,768]{1,0:T(8,128)(2,1)S(1)} fusion(f32[768,768,1]{1,0,2:T(8,128)S(1)} %fusion.50, bf16[2,512,768]{2,1,0:T(8,128)(2,1)} %get-tuple-element.187, bf16[2,512,768]{2,1,0:T(8,128)(2,1)} %get-tuple-element.188), kind=kOutput, calls=%fused_computation.7 | convolution fusion | flops 1209139200 | bytes 6684672 | tf_op jit(solution)/shard_map/nbk,nbc->kc/dot_general | solution.py:853
  149.1 2.8 %fusion.15 = f32[768,768,1]{1,0,2:T(8,128)S(1)} fusion(bf16[2,512,768]{2,1,0:T(8,128)(2,1)S(1)} %copy-done.31, bf16[1,512,768]{2,1,0:T(8,128)(2,1)} %bitcast.28, bf16[1,512,768]{2,1,0:T(8,128)(2,1)} %param.19), kind=kOutput, calls=%fused_computation.23 | convolution fusion | flops 1208745984 | bytes 5505024 | tf_op jit(solution)/shard_map/nbk,nbc->kc/dot_general | solution.py:853
  154.3 7.4 %turn.1 = (bf16[192,512]{1,0:T(8,128)(2,1)S(1)}, bf16[192,512]{1,0:T(8,128)(2,1)S(1)}, bf16[192,512]{1,0:T(8,128)(2,1)S(1)}, bf16[192,512]{1,0:T(8,128)(2,1)S(1)...) custom-call(s32[2]{0:T(128)S(1)} %pad_add_fusion.me_ref, ...), custom_call_target="tpu_custom_call" | custom-call | flops 3000000000 | bytes 8000000 | tf_op jit(solution)/shard_map/turn/pallas_call | solution.py:556
  162.1 1.5 collective-permute-start.29
  164.7 1.8 collective-permute-start.25
  166.5 2.4 convolution_convert_fusion.2
  171.6 1.7 convolution_convert_fusion.1
  173.3 4.4 %collective-permute-done.29 = bf16[4,96,768]{2,1,0:T(8,128)(2,1)S(1)} collective-permute-done((bf16[4,96,768]{2,1,0:T(8,128)(2,1)}, bf16[4,96,768]{2,1,0:T(8,128)(2,1)S(1)}, u32[]{:S(2)}, u32[]{:S(2)}) %collective-permute-start.29) | collective-permute-done | bytes 589856 | tf_op jit(solution)/shard_map/ppermute | solution.py:241
  179.4 1.5 collective-permute-start.34
  182.0 1.6 collective-permute-start.33
  184.4 26.8 %attend_back.1 = (bf16[4,512,576]{2,1,0:T(8,128)(2,1)S(1)}, bf16[768,576]{1,0:T(8,128)(2,1)S(1)}) custom-call(s32[2]{0:T(128)S(1)} %pad_add_fusion.me_ref, bf16[4,512,576]{2,1,0:T(8,128)(2,1)S(1)} %copy-done.14, bf16[4,192,512]{2,1,0:T(8,128)(2,1)S(1)} %pad_maximum_fusion.2.go_ref, f32[4,192,512]{2,1,0:T(8,128)S(1)} %copy-done.19, ...), custom_call_target="tpu_custom_call" | custom-call | flops 40000000000 | bytes 12000000 | tf_op jit(solution)/shard_map/attend_back/pallas_call | solution.py:186
  215.4 2.2 collective-permute-start.37
  217.6 8.1 %leave.1 = (bf16[2,512,768]{2,1,0:T(8,128)(2,1)S(1)}, bf16[2,512,768]{2,1,0:T(8,128)(2,1)S(1)}, bf16[768,128]{1,0:T(8,128)(2,1)S(1)}) custom-call(s32[2]{0:T(128)S(1)} %pad_add_fusion.me_ref, bf16[4,512,768]{2,1,0:T(8,128)(2,1)} %copy-done, bf16[4,512,576]{2,1,0:T(8,128)(2,1)} %copy-done.15, bf16[768,576]{1,0:T(8,128)(2,1)S(1)} %copy-done.17, ...), custom_call_target="tpu_custom_call" | custom-call | flops 6000000000 | bytes 10000000 | tf_op jit(solution)/shard_map/leave/pallas_call | solution.py:634
  225.8 5.1 %collective-permute-done.37 = bf16[1,192,768]{2,1,0:T(8,128)(2,1)S(1)} collective-permute-done((bf16[1,192,768]{2,1,0:T(8,128)(2,1)S(1)}, bf16[1,192,768]{2,1,0:T(8,128)(2,1)S(1)}, u32[]{:S(2)}, u32[]{:S(2)}) %collective-permute-start.37) | collective-permute-done | bytes 294944 | tf_op jit(solution)/shard_map/ppermute | solution.py:241
  232.0 1.5 fusion.21
  237.2 2.4 fusion.26
  241.1 5.5 %collective-permute-done.41 = bf16[2,96,128]{2,1,0:T(8,128)(2,1)S(1)} collective-permute-done((bf16[2,96,128]{2,1,0:T(8,128)(2,1)S(1)}, bf16[2,96,128]{2,1,0:T(8,128)(2,1)S(1)}, u32[]{:S(2)}, u32[]{:S(2)}) %collective-permute-start.41) | collective-permute-done | bytes 49184 | tf_op jit(solution)/shard_map/ppermute | solution.py:241
  247.6 2.2 collective-permute-start.42
  249.8 1.5 add_add_fusion
  251.4 7.3 %collective-permute-done.42 = bf16[1,120,768]{2,1,0:T(8,128)(2,1)S(1)} collective-permute-done((bf16[1,120,768]{2,1,0:T(8,128)(2,1)S(1)}, bf16[1,120,768]{2,1,0:T(8,128)(2,1)S(1)}, u32[]{:S(2)}, u32[]{:S(2)}) %collective-permute-start.42) | collective-permute-done | bytes 184352 | tf_op jit(solution)/shard_map/ppermute | solution.py:241
  259.4 2.3 hand_over.1
  264.1 2.0 fusion.22
  266.1 3.0 %fusion.10 = f32[512,768]{1,0:T(8,128)} fusion(f32[512,768]{1,0:T(8,128)S(1)} %copy-done.28, bf16[512,768]{1,0:T(8,128)(2,1)S(1)} %bitcast.184, bf16[512,768]{1,0:T(8,128)(2,1)S(1)} %collective-permute-done.46, f32[512]{0:T(512)S(1)} %get-tuple-element.286, f32[512]{0:T(512)S(1)} %get-tuple-element.287, f32[768]{0:T(1024)S(1)} %get-tuple-element.260, ...), kind=kLoop, calls=%fused_computation.18 | loop fusion | flops 6291456 | bytes 6302720 | tf_op jit(solution)/shard_map/add | solution.py:932
  269.9 1.9 finish.1
  271.9 1.8 slice_reduce_fusion.1
  (269 shorter events, 50.1 us)
Async XLA Ops:
  6.8 5.3 %collective-permute-start.2 = (bf16[24,2368]{1,0:T(8,128)(2,1)S(1)}, bf16[24,2368]{1,0:T(8,128)(2,1)S(1)}, u32[]{:S(2)}, u32[]{:S(2)}) collective-permute-start(bf16[24,2368]{1,0:T(8,128)(2,1)S(1)} %get-tuple-element.275), channel_id=1, source_target_pairs={{0,1},{1,0},{2,3},{3,2},{4,5},{5,4},{6,7},{7,6},{8,9},{9,8},{10,11... | collective-permute-start | bytes 341000 | tf_op jit(solution)/shard_map/ppermute | solution.py:241
  7.3 6.6 %collective-permute-start.1 = (bf16[24,2368]{1,0:T(8,128)(2,1)S(1)}, bf16[24,2368]{1,0:T(8,128)(2,1)S(1)}, u32[]{:S(2)}, u32[]{:S(2)}) collective-permute-start(bf16[24,2368]{1,0:T(8,128)(2,1)S(1)} %get-tuple-element.276), channel_id=1, source_target_pairs={{0,2},{1,3},{2,0},{3,1},{4,6},{5,7},{6,4},{7,5},{8,10},{9,11},{10,... | collective-permute-start | bytes 341000 | tf_op jit(solution)/shard_map/ppermute | solution.py:241
  9.9 6.0 %collective-permute-start = (bf16[24,2368]{1,0:T(8,128)(2,1)S(1)}, bf16[24,2368]{1,0:T(8,128)(2,1)S(1)}, u32[]{:S(2)}, u32[]{:S(2)}) collective-permute-start(bf16[24,2368]{1,0:T(8,128)(2,1)S(1)} %get-tuple-element.277), channel_id=1, source_target_pairs={{0,3},{1,2},{2,1},{3,0},{4,7},{5,6},{6,5},{7,4},{8,11},{9,10},{10,... | collective-permute-start | bytes 341000 | tf_op jit(solution)/shard_map/ppermute | solution.py:241
  9.9 24.5 %collective-permute-start.6 = (bf16[512,768]{1,0:T(8,128)(2,1)S(1)}, bf16[512,768]{1,0:T(8,128)(2,1)S(1)}, u32[]{:S(2)}, u32[]{:S(2)}) collective-permute-start(bf16[512,768]{1,0:T(8,128)(2,1)S(1)} %bitcast.179), channel_id=1, source_target_pairs={{0,2},{1,3},{2,0},{3,1},{4,6},{5,7},{6,4},{7,5},{8,10},{9,11},{10,... | collective-permute-start | bytes 2359304 | tf_op jit(solution)/shard_map/ppermute | solution.py:241
  17.4 10.6 %collective-permute-start.3 = (bf16[1,96,704]{2,1,0:T(8,128)(2,1)S(1)}, bf16[1,96,704]{2,1,0:T(8,128)(2,1)S(1)}, u32[]{:S(2)}, u32[]{:S(2)}) collective-permute-start(bf16[1,96,704]{2,1,0:T(8,128)(2,1)S(1)} %fusion.43), channel_id=1, source_target_pairs={{0,16},{4,20},{8,24},{12,28},{16,0},{20,4},{24,8},{28,12},{1,17},{... | collective-permute-start | bytes 405512 | tf_op jit(solution)/shard_map/ppermute | solution.py:241
  28.1 6.4 %collective-permute-start.4 = (bf16[2,96,384]{2,1,0:T(8,128)(2,1)S(1)}, bf16[2,96,384]{2,1,0:T(8,128)(2,1)S(1)}, u32[]{:S(2)}, u32[]{:S(2)}) collective-permute-start(bf16[2,96,384]{2,1,0:T(8,128)(2,1)S(1)} %fusion.42.refs_0_), channel_id=1, source_target_pairs={{0,8},{4,12},{8,0},{12,4},{16,24},{20,28},{24,16},{28,20},{1,9},{5... | collective-permute-start | bytes 442376 | tf_op jit(solution)/shard_map/ppermute | solution.py:241
  28.9 5.6 %collective-permute-start.5 = (bf16[2,96,320]{2,1,0:T(8,128)(2,1)S(1)}, bf16[2,96,320]{2,1,0:T(8,128)(2,1)S(1)}, u32[]{:S(2)}, u32[]{:S(2)}) collective-permute-start(bf16[2,96,320]{2,1,0:T(8,128)(2,1)S(1)} %pad_maximum_fusion.4.refs_3_), channel_id=1, source_target_pairs={{0,4},{4,0},{8,12},{12,8},{16,20},{20,16},{24,28},{28,24},{1,5},{5... | collective-permute-start | bytes 368648 | tf_op jit(solution)/shard_map/ppermute | solution.py:241
  30.4 7.9 %collective-permute-start.9 = (bf16[512,768]{1,0:T(8,128)(2,1)S(1)}, bf16[512,768]{1,0:T(8,128)(2,1)S(1)}, u32[]{:S(2)}, u32[]{:S(2)}) collective-permute-start(bf16[512,768]{1,0:T(8,128)(2,1)S(1)} %bitcast.180), channel_id=1, source_target_pairs={{0,1},{1,0},{2,3},{3,2},{4,5},{5,4},{6,7},{7,6},{8,9},{9,8},{10,11... | collective-permute-start | bytes 2359304 | tf_op jit(solution)/shard_map/ppermute | solution.py:241
  34.5 5.1 %collective-permute-start.10 = (bf16[512,768]{1,0:T(8,128)(2,1)S(1)}, bf16[512,768]{1,0:T(8,128)(2,1)}, u32[]{:S(2)}, u32[]{:S(2)}) collective-permute-start(bf16[512,768]{1,0:T(8,128)(2,1)S(1)} %collective-permute-done.6), channel_id=1, source_target_pairs={{0,1},{1,0},{2,3},{3,2},{4,5},{5,4},{6,7},{7,6},{8,9},{9,8},{10,11... | collective-permute-start | bytes 2359304 | tf_op jit(solution)/shard_map/ppermute | solution.py:241
  34.6 49.1 %collective-permute-start.15 = (bf16[512,768]{1,0:T(8,128)(2,1)}, bf16[512,768]{1,0:T(8,128)(2,1)}, u32[]{:S(2)}, u32[]{:S(2)}) collective-permute-start(bf16[512,768]{1,0:T(8,128)(2,1)} %bitcast.26.refs_8_), channel_id=1, source_target_pairs={{0,1},{1,0},{2,3},{3,2},{4,5},{5,4},{6,7},{7,6},{8,9},{9,8},{10,11... | collective-permute-start | bytes 2359304 | tf_op jit(solution)/shard_map/ppermute | solution.py:241
  35.1 182.5 %copy-start.7 = (s32[2]{0:T(128)}, s32[2]{0:T(128)S(1)}, u32[]{:S(2)}) copy-start(s32[2]{0:T(128)S(1)} %pad_add_fusion.me_ref) | copy-start | bytes 28
  35.2 18.9 %collective-permute-start.7 = (bf16[4,96,384]{2,1,0:T(8,128)(2,1)S(1)}, bf16[4,96,384]{2,1,0:T(8,128)(2,1)S(1)}, u32[]{:S(2)}, u32[]{:S(2)}) collective-permute-start(bf16[4,96,384]{2,1,0:T(8,128)(2,1)S(1)} %constant_dynamic-update-slice_fusion), channel_id=1, source_target_pairs={{0,4},{4,0},{8,12},{12,8},{16,20},{20,16},{24,28},{28,24},{1,5},{5... | collective-permute-start | bytes 884744 | tf_op jit(solution)/shard_map/ppermute | solution.py:241
  36.8 24.7 %collective-permute-start.11 = (bf16[512,768]{1,0:T(8,128)(2,1)}, bf16[512,768]{1,0:T(8,128)(2,1)S(1)}, u32[]{:S(2)}, u32[]{:S(2)}) collective-permute-start(bf16[512,768]{1,0:T(8,128)(2,1)} %bitcast.26.refs_8_), channel_id=1, source_target_pairs={{0,2},{1,3},{2,0},{3,1},{4,6},{5,7},{6,4},{7,5},{8,10},{9,11},{10,... | collective-permute-start | bytes 2359304 | tf_op jit(solution)/shard_map/ppermute | solution.py:241
  38.3 15.7 %collective-permute-start.8 = (bf16[4,96,320]{2,1,0:T(8,128)(2,1)S(1)}, bf16[4,96,320]{2,1,0:T(8,128)(2,1)S(1)}, u32[]{:S(2)}, u32[]{:S(2)}) collective-permute-start(bf16[4,96,320]{2,1,0:T(8,128)(2,1)S(1)} %constant_dynamic-update-slice_fusion.2), channel_id=1, source_target_pairs={{0,8},{4,12},{8,0},{12,4},{16,24},{20,28},{24,16},{28,20},{1,9},{5... | collective-permute-start | bytes 737288 | tf_op jit(solution)/shard_map/ppermute | solution.py:241
  39.5 21.9 %collective-permute-start.12 = (bf16[1,288,768]{2,1,0:T(8,128)(2,1)}, bf16[1,288,768]{2,1,0:T(8,128)(2,1)S(1)}, u32[]{:S(2)}, u32[]{:S(2)}) collective-permute-start(bf16[1,288,768]{2,1,0:T(8,128)(2,1)} %bitcast.27), channel_id=1, source_target_pairs={{0,16},{4,20},{8,24},{12,28},{16,0},{20,4},{24,8},{28,12},{1,17},{... | collective-permute-start | bytes 1327112 | tf_op jit(solution)/shard_map/ppermute | solution.py:241
  62.9 20.8 %collective-permute-start.14 = (bf16[2,288,768]{2,1,0:T(8,128)(2,1)S(1)}, bf16[2,288,768]{2,1,0:T(8,128)(2,1)S(1)}, u32[]{:S(2)}, u32[]{:S(2)}) collective-permute-start(bf16[2,288,768]{2,1,0:T(8,128)(2,1)S(1)} %constant_dynamic-update-slice_fusion.4.refs_4_), channel_id=1, source_target_pairs={{0,8},{4,12},{8,0},{12,4},{16,24},{20,28},{24,16},{28,20},{1,9},{5... | collective-permute-start | bytes 2654216 | tf_op jit(solution)/shard_map/ppermute | solution.py:241
  63.9 19.8 %collective-permute-start.13 = (bf16[2,288,768]{2,1,0:T(8,128)(2,1)S(1)}, bf16[2,288,768]{2,1,0:T(8,128)(2,1)S(1)}, u32[]{:S(2)}, u32[]{:S(2)}) collective-permute-start(bf16[2,288,768]{2,1,0:T(8,128)(2,1)S(1)} %constant_dynamic-update-slice_fusion.4.refs_4_), channel_id=1, source_target_pairs={{0,4},{4,0},{8,12},{12,8},{16,20},{20,16},{24,28},{28,24},{1,5},{5... | collective-permute-start | bytes 2654216 | tf_op jit(solution)/shard_map/ppermute | solution.py:241
  64.4 19.2 %collective-permute-start.16 = (bf16[512,768]{1,0:T(8,128)(2,1)S(1)}, bf16[512,768]{1,0:T(8,128)(2,1)S(1)}, u32[]{:S(2)}, u32[]{:S(2)}) collective-permute-start(bf16[512,768]{1,0:T(8,128)(2,1)S(1)} %collective-permute-done.11), channel_id=1, source_target_pairs={{0,1},{1,0},{2,3},{3,2},{4,5},{5,4},{6,7},{7,6},{8,9},{9,8},{10,11... | collective-permute-start | bytes 2359304 | tf_op jit(solution)/shard_map/ppermute | solution.py:241
  83.7 20.0 %collective-permute-start.18 = (bf16[4,192,512]{2,1,0:T(8,128)(2,1)S(1)}, bf16[4,192,512]{2,1,0:T(8,128)(2,1)S(1)}, u32[]{:S(2)}, u32[]{:S(2)}) collective-permute-start(bf16[4,192,512]{2,1,0:T(8,128)(2,1)S(1)} %get-tuple-element.166.refs_0_), channel_id=1, source_target_pairs={{0,2},{1,3},{2,0},{3,1},{4,6},{5,7},{6,4},{7,5},{8,10},{9,11},{10,... | collective-permute-start | bytes 2359304 | tf_op jit(solution)/shard_map/ppermute | solution.py:241
  84.8 18.9 %collective-permute-start.17 = (bf16[4,192,512]{2,1,0:T(8,128)(2,1)S(1)}, bf16[4,192,512]{2,1,0:T(8,128)(2,1)S(1)}, u32[]{:S(2)}, u32[]{:S(2)}) collective-permute-start(bf16[4,192,512]{2,1,0:T(8,128)(2,1)S(1)} %get-tuple-element.166.refs_0_), channel_id=1, source_target_pairs={{0,1},{1,0},{2,3},{3,2},{4,5},{5,4},{6,7},{7,6},{8,9},{9,8},{10,11... | collective-permute-start | bytes 2359304 | tf_op jit(solution)/shard_map/ppermute | solution.py:241
  85.0 23.0 %collective-permute-start.20 = (bf16[2,288,768]{2,1,0:T(8,128)(2,1)S(1)}, bf16[2,288,768]{2,1,0:T(8,128)(2,1)S(1)}, u32[]{:S(2)}, u32[]{:S(2)}) collective-permute-start(bf16[2,288,768]{2,1,0:T(8,128)(2,1)S(1)} %constant_dynamic-update-slice_fusion.4.refs_4_), channel_id=1, source_target_pairs={{0,12},{4,8},{8,4},{12,0},{16,28},{20,24},{24,20},{28,16},{1,13},{... | collective-permute-start | bytes 2654216 | tf_op jit(solution)/shard_map/ppermute | solution.py:241
  103.8 4.3 %collective-permute-start.19 = (bf16[4,192,512]{2,1,0:T(8,128)(2,1)S(1)}, bf16[4,192,512]{2,1,0:T(8,128)(2,1)S(1)}, u32[]{:S(2)}, u32[]{:S(2)}) collective-permute-start(bf16[4,192,512]{2,1,0:T(8,128)(2,1)S(1)} %collective-permute-done.18.refs_2_), channel_id=1, source_target_pairs={{0,1},{1,0},{2,3},{3,2},{4,5},{5,4},{6,7},{7,6},{8,9},{9,8},{10,11... | collective-permute-start | bytes 2359304 | tf_op jit(solution)/shard_map/ppermute | solution.py:241
  123.3 5.1 %collective-permute-start.21 = (bf16[512,768]{1,0:T(8,128)(2,1)}, bf16[512,768]{1,0:T(8,128)(2,1)}, u32[]{:S(2)}, u32[]{:S(2)}) collective-permute-start(bf16[512,768]{1,0:T(8,128)(2,1)} %get-tuple-element.180), channel_id=1, source_target_pairs={{0,1},{1,0},{2,3},{3,2},{4,5},{5,4},{6,7},{7,6},{8,9},{9,8},{10,11... | collective-permute-start | bytes 2359304 | tf_op jit(solution)/shard_map/ppermute | solution.py:241
  129.8 23.6 %collective-permute-start.23 = (bf16[512,768]{1,0:T(8,128)(2,1)S(1)}, bf16[512,768]{1,0:T(8,128)(2,1)S(1)}, u32[]{:S(2)}, u32[]{:S(2)}) collective-permute-start(bf16[512,768]{1,0:T(8,128)(2,1)S(1)} %add_convert_fusion.3), channel_id=1, source_target_pairs={{0,2},{1,3},{2,0},{3,1},{4,6},{5,7},{6,4},{7,5},{8,10},{9,11},{10,... | collective-permute-start | bytes 2359304 | tf_op jit(solution)/shard_map/ppermute | solution.py:241
  144.1 9.3 %collective-permute-start.22 = (bf16[512,768]{1,0:T(8,128)(2,1)S(1)}, bf16[512,768]{1,0:T(8,128)(2,1)S(1)}, u32[]{:S(2)}, u32[]{:S(2)}) collective-permute-start(bf16[512,768]{1,0:T(8,128)(2,1)S(1)} %get-tuple-element.184), channel_id=1, source_target_pairs={{0,1},{1,0},{2,3},{3,2},{4,5},{5,4},{6,7},{7,6},{8,9},{9,8},{10,11... | collective-permute-start | bytes 2359304 | tf_op jit(solution)/shard_map/ppermute | solution.py:241
  161.7 4.8 %collective-permute-start.24 = (bf16[192,512]{1,0:T(8,128)(2,1)S(1)}, bf16[192,512]{1,0:T(8,128)(2,1)S(1)}, u32[]{:S(2)}, u32[]{:S(2)}) collective-permute-start(bf16[192,512]{1,0:T(8,128)(2,1)S(1)} %get-tuple-element.194), channel_id=1, source_target_pairs={{0,1},{1,0},{2,3},{3,2},{4,5},{5,4},{6,7},{7,6},{8,9},{9,8},{10,11... | collective-permute-start | bytes 589832 | tf_op jit(solution)/shard_map/ppermute | solution.py:241
  162.1 15.6 %collective-permute-start.29 = (bf16[4,96,768]{2,1,0:T(8,128)(2,1)}, bf16[4,96,768]{2,1,0:T(8,128)(2,1)S(1)}, u32[]{:S(2)}, u32[]{:S(2)}) collective-permute-start(bf16[4,96,768]{2,1,0:T(8,128)(2,1)} %dynamic-slice_bitcast_fusion.2), channel_id=1, source_target_pairs={{0,4},{4,0},{8,12},{12,8},{16,20},{20,16},{24,28},{28,24},{1,5},{5... | collective-permute-start | bytes 1769480 | tf_op jit(solution)/shard_map/ppermute | solution.py:241
  163.6 15.3 %collective-permute-start.30 = (bf16[4,96,768]{2,1,0:T(8,128)(2,1)}, bf16[4,96,768]{2,1,0:T(8,128)(2,1)S(1)}, u32[]{:S(2)}, u32[]{:S(2)}) collective-permute-start(bf16[4,96,768]{2,1,0:T(8,128)(2,1)} %bitcast.212), channel_id=1, source_target_pairs={{0,8},{4,12},{8,0},{12,4},{16,24},{20,28},{24,16},{28,20},{1,9},{5... | collective-permute-start | bytes 1769480 | tf_op jit(solution)/shard_map/ppermute | solution.py:241
  164.7 14.7 %collective-permute-start.25 = (bf16[192,512]{1,0:T(8,128)(2,1)S(1)}, bf16[192,512]{1,0:T(8,128)(2,1)S(1)}, u32[]{:S(2)}, u32[]{:S(2)}) collective-permute-start(bf16[192,512]{1,0:T(8,128)(2,1)S(1)} %get-tuple-element.198), channel_id=1, source_target_pairs={{0,2},{1,3},{2,0},{3,1},{4,6},{5,7},{6,4},{7,5},{8,10},{9,11},{10,... | collective-permute-start | bytes 589832 | tf_op jit(solution)/shard_map/ppermute | solution.py:241
  166.5 14.4 %collective-permute-start.26 = (bf16[192,512]{1,0:T(8,128)(2,1)S(1)}, bf16[192,512]{1,0:T(8,128)(2,1)S(1)}, u32[]{:S(2)}, u32[]{:S(2)}) collective-permute-start(bf16[192,512]{1,0:T(8,128)(2,1)S(1)} %get-tuple-element.199), channel_id=1, source_target_pairs={{0,3},{1,2},{2,1},{3,0},{4,7},{5,6},{6,5},{7,4},{8,11},{9,10},{10,... | collective-permute-start | bytes 589832 | tf_op jit(solution)/shard_map/ppermute | solution.py:241
  170.3 11.5 %collective-permute-start.28 = (bf16[16,24,768]{2,1,0:T(8,128)(2,1)S(1)}, bf16[16,24,768]{2,1,0:T(8,128)(2,1)S(1)}, u32[]{:S(2)}, u32[]{:S(2)}) collective-permute-start(bf16[16,24,768]{2,1,0:T(8,128)(2,1)S(1)} %dynamic-slice_bitcast_fusion.1), channel_id=1, source_target_pairs={{0,1},{1,0},{2,3},{3,2},{4,5},{5,4},{6,7},{7,6},{8,9},{9,8},{10,11... | collective-permute-start | bytes 1769480 | tf_op jit(solution)/shard_map/ppermute | solution.py:241
  177.7 33.5 %collective-permute-start.31 = (bf16[512,768]{1,0:T(8,128)(2,1)S(1)}, bf16[512,768]{1,0:T(8,128)(2,1)S(1)}, u32[]{:S(2)}, u32[]{:S(2)}) collective-permute-start(bf16[512,768]{1,0:T(8,128)(2,1)S(1)} %convolution_convert_fusion), channel_id=1, source_target_pairs={{0,1},{1,0},{2,3},{3,2},{4,5},{5,4},{6,7},{7,6},{8,9},{9,8},{10,11... | collective-permute-start | bytes 2359304 | tf_op jit(solution)/shard_map/ppermute | solution.py:241
  178.9 4.7 %collective-permute-start.27 = (bf16[512,768]{1,0:T(8,128)(2,1)S(1)}, bf16[512,768]{1,0:T(8,128)(2,1)S(1)}, u32[]{:S(2)}, u32[]{:S(2)}) collective-permute-start(bf16[512,768]{1,0:T(8,128)(2,1)S(1)} %convolution_convert_fusion.2), channel_id=1, source_target_pairs={{0,1},{1,0},{2,3},{3,2},{4,5},{5,4},{6,7},{7,6},{8,9},{9,8},{10,11... | collective-permute-start | bytes 2359304 | tf_op jit(solution)/shard_map/ppermute | solution.py:241
  179.4 31.8 %collective-permute-start.34 = (bf16[2,96,768]{2,1,0:T(8,128)(2,1)S(1)}, bf16[2,96,768]{2,1,0:T(8,128)(2,1)S(1)}, u32[]{:S(2)}, u32[]{:S(2)}) collective-permute-start(bf16[2,96,768]{2,1,0:T(8,128)(2,1)S(1)} %dynamic-slice_bitcast_fusion.4), channel_id=1, source_target_pairs={{0,8},{4,12},{8,0},{12,4},{16,24},{20,28},{24,16},{28,20},{1,9},{5... | collective-permute-start | bytes 884744 | tf_op jit(solution)/shard_map/ppermute | solution.py:241
  180.9 30.3 %collective-permute-start.35 = (bf16[2,96,768]{2,1,0:T(8,128)(2,1)S(1)}, bf16[2,96,768]{2,1,0:T(8,128)(2,1)S(1)}, u32[]{:S(2)}, u32[]{:S(2)}) collective-permute-start(bf16[2,96,768]{2,1,0:T(8,128)(2,1)S(1)} %dynamic-slice_bitcast_fusion.3), channel_id=1, source_target_pairs={{0,4},{4,0},{8,12},{12,8},{16,20},{20,16},{24,28},{28,24},{1,5},{5... | collective-permute-start | bytes 884744 | tf_op jit(solution)/shard_map/ppermute | solution.py:241
  182.0 29.2 %collective-permute-start.33 = (bf16[8,24,768]{2,1,0:T(8,128)(2,1)S(1)}, bf16[8,24,768]{2,1,0:T(8,128)(2,1)S(1)}, u32[]{:S(2)}, u32[]{:S(2)}) collective-permute-start(bf16[8,24,768]{2,1,0:T(8,128)(2,1)S(1)} %dynamic-slice_bitcast_fusion.5), channel_id=1, source_target_pairs={{0,2},{1,3},{2,0},{3,1},{4,6},{5,7},{6,4},{7,5},{8,10},{9,11},{10,... | collective-permute-start | bytes 884744 | tf_op jit(solution)/shard_map/ppermute | solution.py:241
  183.8 27.4 %collective-permute-start.32 = (bf16[512,768]{1,0:T(8,128)(2,1)S(1)}, bf16[512,768]{1,0:T(8,128)(2,1)S(1)}, u32[]{:S(2)}, u32[]{:S(2)}) collective-permute-start(bf16[512,768]{1,0:T(8,128)(2,1)S(1)} %add_convert_fusion.2), channel_id=1, source_target_pairs={{0,2},{1,3},{2,0},{3,1},{4,6},{5,7},{6,4},{7,5},{8,10},{9,11},{10,... | collective-permute-start | bytes 2359304 | tf_op jit(solution)/shard_map/ppermute | solution.py:241
  213.3 17.8 %collective-permute-start.36 = (bf16[4,120,768]{2,1,0:T(8,128)(2,1)S(1)}, bf16[4,120,768]{2,1,0:T(8,128)(2,1)S(1)}, u32[]{:S(2)}, u32[]{:S(2)}) collective-permute-start(bf16[4,120,768]{2,1,0:T(8,128)(2,1)S(1)} %dynamic-slice_bitcast_fusion), channel_id=1, source_target_pairs={{0,4},{4,0},{8,12},{12,8},{16,20},{20,16},{24,28},{28,24},{1,5},{5... | collective-permute-start | bytes 2211848 | tf_op jit(solution)/shard_map/ppermute | solution.py:241
  215.4 15.4 %collective-permute-start.37 = (bf16[1,192,768]{2,1,0:T(8,128)(2,1)S(1)}, bf16[1,192,768]{2,1,0:T(8,128)(2,1)S(1)}, u32[]{:S(2)}, u32[]{:S(2)}) collective-permute-start(bf16[1,192,768]{2,1,0:T(8,128)(2,1)S(1)} %get-tuple-element.272), channel_id=1, source_target_pairs={{0,16},{4,20},{8,24},{12,28},{16,0},{20,4},{24,8},{28,12},{1,17},{... | collective-permute-start | bytes 884744 | tf_op jit(solution)/shard_map/ppermute | solution.py:241
  231.9 5.3 %collective-permute-start.39 = (bf16[2,512,768]{2,1,0:T(8,128)(2,1)S(1)}, bf16[2,512,768]{2,1,0:T(8,128)(2,1)}, u32[]{:S(2)}, u32[]{:S(2)}) collective-permute-start(bf16[2,512,768]{2,1,0:T(8,128)(2,1)S(1)} %get-tuple-element.227), channel_id=1, source_target_pairs={{0,1},{1,0},{2,3},{3,2},{4,5},{5,4},{6,7},{7,6},{8,9},{9,8},{10,11... | collective-permute-start | bytes 4718600 | tf_op jit(solution)/shard_map/ppermute | solution.py:241
  233.6 13.0 %collective-permute-start.38 = (bf16[2,120,768]{2,1,0:T(8,128)(2,1)S(1)}, bf16[2,120,768]{2,1,0:T(8,128)(2,1)S(1)}, u32[]{:S(2)}, u32[]{:S(2)}) collective-permute-start(bf16[2,120,768]{2,1,0:T(8,128)(2,1)S(1)} %bitcast_add_fusion.2), channel_id=1, source_target_pairs={{0,8},{4,12},{8,0},{12,4},{16,24},{20,28},{24,16},{28,20},{1,9},{5... | collective-permute-start | bytes 1105928 | tf_op jit(solution)/shard_map/ppermute | solution.py:241
  234.6 6.5 %collective-permute-start.40 = (bf16[2,96,128]{2,1,0:T(8,128)(2,1)S(1)}, bf16[2,96,128]{2,1,0:T(8,128)(2,1)S(1)}, u32[]{:S(2)}, u32[]{:S(2)}) collective-permute-start(bf16[2,96,128]{2,1,0:T(8,128)(2,1)S(1)} %get-tuple-element.228), channel_id=1, source_target_pairs={{0,4},{4,0},{8,12},{12,8},{16,20},{20,16},{24,28},{28,24},{1,5},{5... | collective-permute-start | bytes 147464 | tf_op jit(solution)/shard_map/ppermute | solution.py:241
  235.8 10.8 %collective-permute-start.41 = (bf16[2,96,128]{2,1,0:T(8,128)(2,1)S(1)}, bf16[2,96,128]{2,1,0:T(8,128)(2,1)S(1)}, u32[]{:S(2)}, u32[]{:S(2)}) collective-permute-start(bf16[2,96,128]{2,1,0:T(8,128)(2,1)S(1)} %get-tuple-element.229), channel_id=1, source_target_pairs={{0,12},{4,8},{8,4},{12,0},{16,28},{20,24},{24,20},{28,16},{1,13},{... | collective-permute-start | bytes 147464 | tf_op jit(solution)/shard_map/ppermute | solution.py:241
  239.6 24.4 %collective-permute-start.46 = (bf16[512,768]{1,0:T(8,128)(2,1)}, bf16[512,768]{1,0:T(8,128)(2,1)S(1)}, u32[]{:S(2)}, u32[]{:S(2)}) collective-permute-start(bf16[512,768]{1,0:T(8,128)(2,1)} %fusion.26), channel_id=1, source_target_pairs={{0,2},{1,3},{2,0},{3,1},{4,6},{5,7},{6,4},{7,5},{8,10},{9,11},{10,... | collective-permute-start | bytes 2359304 | tf_op jit(solution)/shard_map/ppermute | solution.py:241
  247.6 11.1 %collective-permute-start.42 = (bf16[1,120,768]{2,1,0:T(8,128)(2,1)S(1)}, bf16[1,120,768]{2,1,0:T(8,128)(2,1)S(1)}, u32[]{:S(2)}, u32[]{:S(2)}) collective-permute-start(bf16[1,120,768]{2,1,0:T(8,128)(2,1)S(1)} %get-tuple-element.280), channel_id=1, source_target_pairs={{0,16},{4,20},{8,24},{12,28},{16,0},{20,4},{24,8},{28,12},{1,17},{... | collective-permute-start | bytes 552968 | tf_op jit(solution)/shard_map/ppermute | solution.py:241
  261.6 7.5 %collective-permute-start.43 = (bf16[24,1472]{1,0:T(8,128)(2,1)}, bf16[24,1472]{1,0:T(8,128)(2,1)S(1)}, u32[]{:S(2)}, u32[]{:S(2)}) collective-permute-start(bf16[24,1472]{1,0:T(8,128)(2,1)} %get-tuple-element.235), channel_id=1, source_target_pairs={{0,1},{1,0},{2,3},{3,2},{4,5},{5,4},{6,7},{7,6},{8,9},{9,8},{10,11... | collective-permute-start | bytes 211976 | tf_op jit(solution)/shard_map/ppermute | solution.py:241
  261.6 7.5 %collective-permute-start.44 = (bf16[24,1472]{1,0:T(8,128)(2,1)}, bf16[24,1472]{1,0:T(8,128)(2,1)S(1)}, u32[]{:S(2)}, u32[]{:S(2)}) collective-permute-start(bf16[24,1472]{1,0:T(8,128)(2,1)} %get-tuple-element.236), channel_id=1, source_target_pairs={{0,2},{1,3},{2,0},{3,1},{4,6},{5,7},{6,4},{7,5},{8,10},{9,11},{10,... | collective-permute-start | bytes 211976 | tf_op jit(solution)/shard_map/ppermute | solution.py:241
  263.1 6.1 %collective-permute-start.45 = (bf16[24,1472]{1,0:T(8,128)(2,1)}, bf16[24,1472]{1,0:T(8,128)(2,1)S(1)}, u32[]{:S(2)}, u32[]{:S(2)}) collective-permute-start(bf16[24,1472]{1,0:T(8,128)(2,1)} %get-tuple-element.237), channel_id=1, source_target_pairs={{0,3},{1,2},{2,1},{3,0},{4,7},{5,6},{6,5},{7,4},{8,11},{9,10},{10,... | collective-permute-start | bytes 211976 | tf_op jit(solution)/shard_map/ppermute | solution.py:241
  (59 other events, 403.0 us)

commit v6 on v5

--- a/solution.py
+++ b/solution.py
@@ -799,7 +799,7 @@
     for mask in masks[:-2]:
         ones.append(swap(jnp.concatenate(ones, 0), "dp", nd, mask))
     ones = jnp.concatenate(ones, 0)
-    cut = -(-(first // 2) // LANES) * LANES
+    cut = -(-(first // 2) // LANES) * LANES + LANES
     ones = [ones[:, :, :cut]], [ones[:, :, cut:]]
     ones[0][0], ones[1][0], two, seg_row, seg_col = lax.optimization_barrier(
         (ones[0][0], ones[1][0], two, seg_row, seg_col)
@@ -862,16 +862,15 @@
     near_got = swap(gh_one, "seq", ns, 1)
     d_down = (d_down + over_rows(act, g_all[:2])).astype(BF16)
     d_up = (over_rows(far_h, far_gu) + over_rows(h_two, gu)).astype(BF16)
-    up_keep, up_sent = halves(d_up.reshape(nd, size, part), d, nd, 1)
-    down_keep, down_sent = halves(d_down.reshape(nd, ff_rows, dm), d, nd, 2)
-    up_got, down_got = swap(up_sent, "dp", nd, 1), swap(down_sent, "dp", nd, 2)
-    far_got, up_sent, down_sent = lax.optimization_barrier((far_got, up_sent, down_sent))
+    feeds = jnp.concatenate([d_up.reshape(nd, size, part), d_down.reshape(nd, ff_rows, dm)], 1)
+    feed_keep, feed_sent = halves(feeds, d, nd, 1)
+    feed_got = swap(feed_sent, "dp", nd, 1)
+    far_got, feed_sent = lax.optimization_barrier((far_got, feed_sent))
     *gos, gx_two, d_out, sums_two = turn(me, o_got, gh_zero, near_got, far_got, x_two, g, w_out_all, vecs)
     go_got = [gos[0]] + [swap(gos[p], "seq", ns, p) for p in range(1, ns)]
     go_got[1], d_out, sums_two = lax.optimization_barrier((go_got[1], d_out, sums_two))
     act, far_act = lax.optimization_barrier((act, far_act, go_got[1]))[:2]
     out_parts = [dot_nn(a, w_down_own).astype(BF16) for a in (act[0], act[1], far_act[0], far_act[1])]
-    up_got, down_got = lax.optimization_barrier((up_got, down_got, out_parts))[:2]
     out_sent = add_low(out_parts[2], swap(out_parts[3], "seq", ns, 1))
     out_near = swap(out_parts[1], "seq", ns, 1)
     out_far = swap(tie(out_sent, go_got[-1]), "seq", ns, 2)
@@ -880,14 +879,11 @@
     outs_keep, outs_sent = halves(add_low(outs_keep, outs_got), s >> 1, ns // 2, 1)
     outs_got = swap(outs_sent, "seq", ns, 2)
 
-    up_keep, up_sent = halves(add_low(up_keep, up_got), d >> 1, nd // 2, 1)
-    down_keep, down_sent = halves(add_low(down_keep, down_got), d, nd, 1)
-    up_got, down_got = swap(up_sent, "dp", nd, 2), swap(down_sent, "dp", nd, 1)
     go_all = jnp.stack(go_got)
-    go_all, *_ = lax.optimization_barrier((go_all, out_sent, out_parts, outs_sent, up_sent, down_sent))
+    go_all, *_ = lax.optimization_barrier((go_all, out_sent, out_parts, outs_sent))
     grads, d_qkv = attend_back(me, qkv, go_all, o_full, lse, seg_row, seg_col, h_one, heads, hd)
-    grads, d_qkv, out_near, out_far, outs_got, up_got, down_got = lax.optimization_barrier(
-        (grads, d_qkv, out_near, out_far, outs_got, up_got, down_got)
+    grads, d_qkv, out_near, out_far, outs_got, feed_got = lax.optimization_barrier(
+        (grads, d_qkv, out_near, out_far, outs_got, feed_got)
     )
     blob = jnp.concatenate(
         [
@@ -898,9 +894,8 @@
     )
     blob_keep, blob_sent = halves(blob, d, nd, 1)
     blob_got = swap(blob_sent, "dp", nd, 1)
-    feeds = jnp.concatenate([add_low(up_keep, up_got), add_low(down_keep, down_got)], 1)
-    feed_keep, feed_sent = halves(feeds, d >> 2, nd // 4, 1)
-    feed_got = swap(feed_sent, "dp", nd, 4)
+    feed_keep, feed_sent = halves(add_low(feed_keep, feed_got), d >> 1, nd // 2, 1)
+    feed_got = swap(feed_sent, "dp", nd, 2)
     grads = lax.optimization_barrier((grads, blob_sent, feed_sent))[0]
     even, odd, tile = leave(me, x_all, grads, w_qkv, vecs, sums_two, sums_up)
     even, odd, tile, blob_got, feed_got = lax.optimization_barrier((even, odd, tile, blob_got, feed_got))
@@ -911,13 +906,15 @@
     blob_keep, blob_sent = blob_keep + tiles[0], blob_sent + tiles[1]
     blob_got = swap(blob_sent, "dp", nd, 2)
     tiles = [swap(t, "dp", nd, p) for t, p in zip(tie(tiles[2:], blob_sent), (1, 3))]
+    feed_keep, feed_sent = halves(tie(add_low(feed_keep, feed_got), blob_sent), d >> 2, nd // 4, 1)
+    feed_got = swap(feed_sent, "dp", nd, 4)
     keep, sent, got = collect_pairs(even, odd, ns)
     blob_got, sent, tiles = lax.optimization_barrier((blob_got, sent, tiles))
     tile = jnp.pad(tiles[0].astype(F32) + tiles[1].astype(F32), ((0, 0), (0, rows), (3 * width, dm - first)))
     blob = (blob_keep.astype(F32) + blob_got.astype(F32) + tile).astype(BF16)
     blob_keep, blob_sent = halves(blob, d >> 2, nd // 4, 1)
     blob_got = swap(blob_sent, "dp", nd, 4)
-    blob_got, sent = lax.optimization_barrier((blob_got, sent))
+    blob_got, sent, feed_got = lax.optimization_barrier((blob_got, sent, feed_got))
     if nd > 8:
         rest = [(blob_keep, blob_got), (feed_keep, feed_got)]
         rest = [collect_dp(add_low(a, b), d >> 3, nd // 8, BF16, shift=3) for a, b in rest]

time: 278 us -> 275 us (0.989)
  starting transfers between devices: 46.3 us -> 43.3 us
    ppermute x47 -> x45, starting transfers between devices: 46.3 us -> 43.3 us  [swap(): return lax.ppermute(value, axis, [(i, i ^ mask) for i in range(size)])]
    ppermute x47 -> x45, waiting for transfers between devices: 65.7 us -> 67.9 us  [swap(): return lax.ppermute(value, axis, [(i, i ^ mask) for i in range(size)])]
    unnamed x124 -> x130, local copies, waits for them, and re-layouts: 8.79 us -> 9.97 us
  transfers between devices with their start and end apart: 47 -> 45, of which waited for: 14 -> 16; matrix products, arithmetic and copies ran while one was open for 16% -> 15% of each run, Pallas kernels for 27% -> 27%
where the time goes in v6:
time: 275 us; the launch traced here: 271 us
  Pallas kernels  97.9 us (36%)
  waiting for transfers between devices  67.9 us (25%)
  starting transfers between devices  43.3 us (16%)
  other arithmetic  23 us (8%)
  local copies, waits for them, and re-layouts  22 us (8%)
  matrix products  14.9 us (5%)
    ppermute x45, waiting for transfers between devices, swap(): return lax.ppermute(value, axis, [(i, i ^ mask) for i in range(size)])  67.9 us
    ppermute x45, starting transfers between devices, swap(): return lax.ppermute(value, axis, [(i, i ^ mask) for i in range(size)])  43.3 us
    pallas_call x2, Pallas kernels, feed(): pl.pallas_call(functools.partial(feed_kernel, n=n, base=base, tile=256 if...  27.9 us
    pallas_call x1, Pallas kernels, attend_back(): pl.pallas_call(functools.partial(attend_back_kernel, heads=heads, hd=hd),...  26.7 us
    pallas_call x1, Pallas kernels, attend(): pl.pallas_call(functools.partial(attend_kernel, heads=heads, hd=hd), grid...  17.7 us
    unnamed x130, local copies, waits for them, and re-layouts  9.97 us
    dot_general x4, matrix products, over_rows(): return jnp.einsum('nbk,nbc->kc', a, b, preferred_element_type=F32)  9.36 us
    pallas_call x1, Pallas kernels, leave(): pl.pallas_call(leave_kernel, grid_spec=pltpu.PrefetchScalarGridSpec(num_s...  8.14 us
  transfers between devices with their start and end apart: 45, of which 16 were waited for; matrix products, arithmetic and copies ran while one was open for 15% of the time, Pallas kernels for 27%

profile of v6, /device:TPU:0, one launch (start us, length us, event | category | flops | bytes accessed | tf_op | source)
XLA Modules:
  0.0 271.0 jit_solution(3845925101168687833)
XLA Ops:
  6.8 2.4 collective-permute-start
  9.9 1.7 collective-permute-start.6
  13.2 2.8 %collective-permute-done.1 = bf16[24,2368]{1,0:T(8,128)(2,1)S(1)} collective-permute-done((bf16[24,2368]{1,0:T(8,128)(2,1)S(1)}, bf16[24,2368]{1,0:T(8,128)(2,1)S(1)}, u32[]{:S(2)}, u32[]{:S(2)}) %collective-permute-start.1) | collective-permute-done | bytes 113696 | tf_op jit(solution)/shard_map/ppermute | solution.py:241
  17.2 3.0 %collective-permute-start.3 = (bf16[1,96,704]{2,1,0:T(8,128)(2,1)S(1)}, bf16[1,96,704]{2,1,0:T(8,128)(2,1)S(1)}, u32[]{:S(2)}, u32[]{:S(2)}) collective-permute-start(bf16[1,96,704]{2,1,0:T(8,128)(2,1)S(1)} %fusion.42), channel_id=1, source_target_pairs={{0,16},{4,20},{8,24},{12,28},{16,0},{20,4},{24,8},{28,12},{1,17},{... | collective-permute-start | bytes 405512 | tf_op jit(solution)/shard_map/ppermute | solution.py:241
  21.5 5.9 %collective-permute-done.3 = bf16[1,96,704]{2,1,0:T(8,128)(2,1)S(1)} collective-permute-done((bf16[1,96,704]{2,1,0:T(8,128)(2,1)S(1)}, bf16[1,96,704]{2,1,0:T(8,128)(2,1)S(1)}, u32[]{:S(2)}, u32[]{:S(2)}) %collective-permute-start.3) | collective-permute-done | bytes 135200 | tf_op jit(solution)/shard_map/ppermute | solution.py:241
  28.3 1.5 collective-permute-start.5
  29.8 3.1 %collective-permute-done.5.refs_4_ = bf16[2,96,192]{2,1,0:T(8,128)(2,1)S(1)} collective-permute-done((bf16[2,96,192]{2,1,0:T(8,128)(2,1)S(1)}, bf16[2,96,192]{2,1,0:T(8,128)(2,1)S(1)}, u32[]{:S(2)}, u32[]{:S(2)}) %collective-permute-start.5) | collective-permute-done | bytes 73760 | tf_op jit(solution)/shard_map/ppermute | solution.py:241
  35.8 1.6 collective-permute-start.11
  37.4 1.5 collective-permute-start.8
  39.0 3.4 %collective-permute-start.12 = (bf16[1,288,768]{2,1,0:T(8,128)(2,1)S(1)}, bf16[1,288,768]{2,1,0:T(8,128)(2,1)S(1)}, u32[]{:S(2)}, u32[]{:S(2)}) collective-permute-start(bf16[1,288,768]{2,1,0:T(8,128)(2,1)S(1)} %bitcast.197), channel_id=1, source_target_pairs={{0,16},{4,20},{8,24},{12,28},{16,0},{20,4},{24,8},{28,12},{1,17},{... | collective-permute-start | bytes 1327112 | tf_op jit(solution)/shard_map/ppermute | solution.py:241
  42.3 2.0 pad_maximum_fusion.refs_6_.refs_8_.refs_4_.x_ref
  44.3 3.2 %collective-permute-done.8.refs_5_ = bf16[4,96,192]{2,1,0:T(8,128)(2,1)S(1)} collective-permute-done((bf16[4,96,192]{2,1,0:T(8,128)(2,1)S(1)}, bf16[4,96,192]{2,1,0:T(8,128)(2,1)S(1)}, u32[]{:S(2)}, u32[]{:S(2)}) %collective-permute-start.8) | collective-permute-done | bytes 147488 | tf_op jit(solution)/shard_map/ppermute | solution.py:241
  47.5 5.8 %enter.1 = (bf16[4,512,576]{2,1,0:T(8,128)(2,1)S(1)}, bf16[4,512,768]{2,1,0:T(8,128)(2,1)S(1)}, bf16[768,576]{1,0:T(8,128)(2,1)S(1)}, f32[16,768]{1,0:T(8,128)S(1)}) custom-call(s32[2]{0:T(128)S(1)} %pad_add_fusion.me_ref, bf16[2,96,512]{2,1,0:T(8,128)(2,1)S(1)} %fusion.41.refs_0_, bf16[2,96,512]{2,1,0:T(8,128)(2,1)S(1)} %copy-done.4, ...), custom_call_target="tpu_custom_call" | custom-call | flops 5000000000 | bytes 8000000 | tf_op jit(solution)/shard_map/enter/pallas_call | solution.py:388
  53.4 8.0 %collective-permute-done.12 = bf16[1,288,768]{2,1,0:T(8,128)(2,1)S(1)} collective-permute-done((bf16[1,288,768]{2,1,0:T(8,128)(2,1)S(1)}, bf16[1,288,768]{2,1,0:T(8,128)(2,1)S(1)}, u32[]{:S(2)}, u32[]{:S(2)}) %collective-permute-start.12) | collective-permute-done | bytes 442400 | tf_op jit(solution)/shard_map/ppermute | solution.py:241
  62.2 17.7 %attend.1 = (bf16[4,192,512]{2,1,0:T(8,128)(2,1)S(1)}, f32[4,192,512]{2,1,0:T(8,128)S(1)}, f32[4,8,512]{2,1,0:T(8,128)S(1)}) custom-call(s32[2]{0:T(128)S(1)} %pad_add_fusion.me_ref, bf16[4,512,576]{2,1,0:T(8,128)(2,1)S(1)} %get-tuple-element.159.qkv_ref, s32[4,1,512]{2,1,0:T(1,128)S(1)} %maximum_convert_fusion.1.seg_row_ref, s32[4,512,1]{2,1,0:T(8,128)S(1)} %copy-done.1), custom_call_target="tpu_custom_call" | custom-call | flops 20000000000 | bytes 8000000 | tf_op jit(solution)/shard_map/attend/pallas_call | solution.py:87
  82.1 1.4 collective-permute-start.18
  83.7 1.9 collective-permute-start.20
  85.6 3.0 %pad_maximum_fusion.1.refs_9_.refs_5_ = bf16[4,512,768]{2,1,0:T(8,128)(2,1)} fusion(bf16[1,512,768]{2,1,0:T(8,128)(2,1)S(1)} %bitcast.189, bf16[1,512,768]{2,1,0:T(8,128)(2,1)S(1)} %bitcast.187, bf16[1,512,768]{2,1,0:T(8,128)(2,1)} %bitcast.185, bf16[1,512,768]{2,1,0:T(8,128)(2,1)} %param.19), kind=kLoop, calls=%fused_computation.1 | loop fusion | flops 4718592 | bytes 6291456 | tf_op jit(solution)/shard_map/stack | solution.py:842
  88.6 13.4 %collective-permute-done.18.refs_2_ = bf16[4,192,512]{2,1,0:T(8,128)(2,1)S(1)} collective-permute-done((bf16[4,192,512]{2,1,0:T(8,128)(2,1)S(1)}, bf16[4,192,512]{2,1,0:T(8,128)(2,1)S(1)}, u32[]{:S(2)}, u32[]{:S(2)}) %collective-permute-start.18) | collective-permute-done | bytes 786464 | tf_op jit(solution)/shard_map/ppermute | solution.py:241
  102.0 4.4 %collective-permute-done.20.refs_7_ = bf16[2,288,768]{2,1,0:T(8,128)(2,1)S(1)} collective-permute-done((bf16[2,288,768]{2,1,0:T(8,128)(2,1)S(1)}, bf16[2,288,768]{2,1,0:T(8,128)(2,1)S(1)}, u32[]{:S(2)}, u32[]{:S(2)}) %collective-permute-start.20) | collective-permute-done | bytes 884768 | tf_op jit(solution)/shard_map/ppermute | solution.py:241
  107.4 14.3 %feed_far.1 = (bf16[2,512,768]{2,1,0:T(8,128)(2,1)}, bf16[2,512,768]{2,1,0:T(8,128)(2,1)}, bf16[2,512,768]{2,1,0:T(8,128)(2,1)}, bf16[512,768]{1,0:T(8,128)(2,1)...) custom-call(s32[2]{0:T(128)S(1)} %pad_add_fusion.me_ref, ...), custom_call_target="tpu_custom_call" | custom-call | flops 8999999488 | bytes 16000000 | tf_op jit(solution)/shard_map/feed_far/pallas_call | solution.py:506
  121.8 3.4 %convolution_bitcast_fusion = f32[768,768]{1,0:T(8,128)S(1)} fusion(bf16[2,512,768]{2,1,0:T(8,128)(2,1)} %get-tuple-element.200, bf16[1,512,768]{2,1,0:T(8,128)(2,1)} %bitcast.190, bf16[1,512,768]{2,1,0:T(8,128)(2,1)} %bitcast.188), kind=kOutput, calls=%fused_computation.20 | convolution fusion | flops 1208745984 | bytes 5505024 | tf_op jit(solution)/shard_map/nbk,nbc->kc/dot_general | solution.py:853
  125.3 1.4 fusion.49
  126.8 1.5 add_convert_fusion.3
  129.1 13.6 %feed_near.1 = (bf16[2,512,768]{2,1,0:T(8,128)(2,1)}, bf16[2,512,768]{2,1,0:T(8,128)(2,1)}, bf16[2,512,768]{2,1,0:T(8,128)(2,1)}, bf16[512,768]{1,0:T(8,128)(2,1...) custom-call(s32[2]{0:T(128)S(1)} %pad_add_fusion.me_ref, ...), custom_call_target="tpu_custom_call" | custom-call | flops 8999999488 | bytes 16000000 | tf_op jit(solution)/shard_map/feed_near/pallas_call | solution.py:506
  143.0 3.0 %fusion.16 = f32[768,768,1]{1,0,2:T(8,128)S(1)} fusion(bf16[2,512,768]{2,1,0:T(8,128)(2,1)} %get-tuple-element.201, bf16[1,512,768]{2,1,0:T(8,128)(2,1)S(1)} %bitcast.186, bf16[1,512,768]{2,1,0:T(8,128)(2,1)} %param.19), kind=kOutput, calls=%fused_computation.29 | convolution fusion | flops 1208745984 | bytes 5505024 | tf_op jit(solution)/shard_map/nbk,nbc->kc/dot_general | solution.py:853
  148.3 1.4 fusion.3
  152.1 7.4 %turn.1 = (bf16[192,512]{1,0:T(8,128)(2,1)S(1)}, bf16[192,512]{1,0:T(8,128)(2,1)S(1)}, bf16[192,512]{1,0:T(8,128)(2,1)S(1)}, bf16[192,512]{1,0:T(8,128)(2,1)S(1)...) custom-call(s32[2]{0:T(128)S(1)} %pad_add_fusion.me_ref, ...), custom_call_target="tpu_custom_call" | custom-call | flops 3000000000 | bytes 8000000 | tf_op jit(solution)/shard_map/turn/pallas_call | solution.py:556
  164.5 2.3 convolution_convert_fusion.2
  169.3 1.7 collective-permute-done.26
  171.1 1.7 convolution_convert_fusion.1
  175.4 26.7 %attend_back.1 = (bf16[4,512,576]{2,1,0:T(8,128)(2,1)S(1)}, bf16[768,576]{1,0:T(8,128)(2,1)S(1)}) custom-call(s32[2]{0:T(128)S(1)} %pad_add_fusion.me_ref, bf16[4,512,576]{2,1,0:T(8,128)(2,1)S(1)} %copy-done.14, bf16[4,192,512]{2,1,0:T(8,128)(2,1)S(1)} %pad_maximum_fusion.2.go_ref, f32[4,192,512]{2,1,0:T(8,128)S(1)} %copy-done.19, ...), custom_call_target="tpu_custom_call" | custom-call | flops 40000000000 | bytes 12000000 | tf_op jit(solution)/shard_map/attend_back/pallas_call | solution.py:186
  206.0 2.0 collective-permute-start.34
  208.0 8.1 %leave.1 = (bf16[2,512,768]{2,1,0:T(8,128)(2,1)S(1)}, bf16[2,512,768]{2,1,0:T(8,128)(2,1)S(1)}, bf16[768,128]{1,0:T(8,128)(2,1)S(1)}) custom-call(s32[2]{0:T(128)S(1)} %pad_add_fusion.me_ref, bf16[4,512,768]{2,1,0:T(8,128)(2,1)} %copy-done, bf16[4,512,576]{2,1,0:T(8,128)(2,1)} %copy-done.15, bf16[768,576]{1,0:T(8,128)(2,1)S(1)} %copy-done.17, ...), custom_call_target="tpu_custom_call" | custom-call | flops 6000000000 | bytes 10000000 | tf_op jit(solution)/shard_map/leave/pallas_call | solution.py:634
  216.2 5.8 %collective-permute-done.34 = bf16[2,192,768]{2,1,0:T(8,128)(2,1)S(1)} collective-permute-done((bf16[2,192,768]{2,1,0:T(8,128)(2,1)S(1)}, bf16[2,192,768]{2,1,0:T(8,128)(2,1)S(1)}, u32[]{:S(2)}, u32[]{:S(2)}) %collective-permute-start.34) | collective-permute-done | bytes 589856 | tf_op jit(solution)/shard_map/ppermute | solution.py:241
  224.3 1.6 fusion.22
  226.1 2.0 collective-permute-start.35
  230.7 2.9 %collective-permute-start.40 = (bf16[1,192,768]{2,1,0:T(8,128)(2,1)S(1)}, bf16[1,192,768]{2,1,0:T(8,128)(2,1)}, u32[]{:S(2)}, u32[]{:S(2)}) collective-permute-start(bf16[1,192,768]{2,1,0:T(8,128)(2,1)S(1)} %get-tuple-element.270), channel_id=1, source_target_pairs={{0,16},{4,20},{8,24},{12,28},{16,0},{20,4},{24,8},{28,12},{1,17},{... | collective-permute-start | bytes 884744 | tf_op jit(solution)/shard_map/ppermute | solution.py:241
  233.6 2.4 fusion.30
  236.0 1.6 collective-permute-start.44
  237.6 7.0 %collective-permute-done.38 = bf16[2,96,128]{2,1,0:T(8,128)(2,1)S(1)} collective-permute-done((bf16[2,96,128]{2,1,0:T(8,128)(2,1)S(1)}, bf16[2,96,128]{2,1,0:T(8,128)(2,1)S(1)}, u32[]{:S(2)}, u32[]{:S(2)}) %collective-permute-start.38) | collective-permute-done | bytes 49184 | tf_op jit(solution)/shard_map/ppermute | solution.py:241
  245.6 1.5 add_add_fusion
  247.1 8.7 %collective-permute-done.39 = bf16[1,120,768]{2,1,0:T(8,128)(2,1)S(1)} collective-permute-done((bf16[1,120,768]{2,1,0:T(8,128)(2,1)S(1)}, bf16[1,120,768]{2,1,0:T(8,128)(2,1)S(1)}, u32[]{:S(2)}, u32[]{:S(2)}) %collective-permute-start.39) | collective-permute-done | bytes 184352 | tf_op jit(solution)/shard_map/ppermute | solution.py:241
  256.5 2.3 hand_over.1
  261.2 2.0 fusion.23
  263.3 3.0 %fusion.11 = f32[512,768]{1,0:T(8,128)} fusion(f32[512,768]{1,0:T(8,128)S(1)} %copy-done.33, bf16[512,768]{1,0:T(8,128)(2,1)S(1)} %bitcast.176, bf16[512,768]{1,0:T(8,128)(2,1)S(1)} %collective-permute-done.44, f32[512]{0:T(512)S(1)} %get-tuple-element.284, f32[512]{0:T(512)S(1)} %get-tuple-element.285, f32[768]{0:T(1024)S(1)} %get-tuple-element.260, ...), kind=kLoop, calls=%fused_computation.24 | loop fusion | flops 6291456 | bytes 6302720 | tf_op jit(solution)/shard_map/add | solution.py:929
  267.1 1.9 finish.1
  269.0 1.8 slice_reduce_fusion.1
  (267 shorter events, 47.6 us)
Async XLA Ops:
  6.8 6.0 %collective-permute-start = (bf16[24,2368]{1,0:T(8,128)(2,1)S(1)}, bf16[24,2368]{1,0:T(8,128)(2,1)S(1)}, u32[]{:S(2)}, u32[]{:S(2)}) collective-permute-start(bf16[24,2368]{1,0:T(8,128)(2,1)S(1)} %get-tuple-element.275), channel_id=1, source_target_pairs={{0,3},{1,2},{2,1},{3,0},{4,7},{5,6},{6,5},{7,4},{8,11},{9,10},{10,... | collective-permute-start | bytes 341000 | tf_op jit(solution)/shard_map/ppermute | solution.py:241
  9.2 6.7 %collective-permute-start.1 = (bf16[24,2368]{1,0:T(8,128)(2,1)S(1)}, bf16[24,2368]{1,0:T(8,128)(2,1)S(1)}, u32[]{:S(2)}, u32[]{:S(2)}) collective-permute-start(bf16[24,2368]{1,0:T(8,128)(2,1)S(1)} %get-tuple-element.274), channel_id=1, source_target_pairs={{0,2},{1,3},{2,0},{3,1},{4,6},{5,7},{6,4},{7,5},{8,10},{9,11},{10,... | collective-permute-start | bytes 341000 | tf_op jit(solution)/shard_map/ppermute | solution.py:241
  9.9 6.4 %collective-permute-start.2 = (bf16[24,2368]{1,0:T(8,128)(2,1)S(1)}, bf16[24,2368]{1,0:T(8,128)(2,1)S(1)}, u32[]{:S(2)}, u32[]{:S(2)}) collective-permute-start(bf16[24,2368]{1,0:T(8,128)(2,1)S(1)} %get-tuple-element.273), channel_id=1, source_target_pairs={{0,1},{1,0},{2,3},{3,2},{4,5},{5,4},{6,7},{7,6},{8,9},{9,8},{10,11... | collective-permute-start | bytes 341000 | tf_op jit(solution)/shard_map/ppermute | solution.py:241
  9.9 24.0 %collective-permute-start.6 = (bf16[512,768]{1,0:T(8,128)(2,1)S(1)}, bf16[512,768]{1,0:T(8,128)(2,1)S(1)}, u32[]{:S(2)}, u32[]{:S(2)}) collective-permute-start(bf16[512,768]{1,0:T(8,128)(2,1)S(1)} %bitcast.171), channel_id=1, source_target_pairs={{0,2},{1,3},{2,0},{3,1},{4,6},{5,7},{6,4},{7,5},{8,10},{9,11},{10,... | collective-permute-start | bytes 2359304 | tf_op jit(solution)/shard_map/ppermute | solution.py:241
  17.2 10.3 %collective-permute-start.3 = (bf16[1,96,704]{2,1,0:T(8,128)(2,1)S(1)}, bf16[1,96,704]{2,1,0:T(8,128)(2,1)S(1)}, u32[]{:S(2)}, u32[]{:S(2)}) collective-permute-start(bf16[1,96,704]{2,1,0:T(8,128)(2,1)S(1)} %fusion.42), channel_id=1, source_target_pairs={{0,16},{4,20},{8,24},{12,28},{16,0},{20,4},{24,8},{28,12},{1,17},{... | collective-permute-start | bytes 405512 | tf_op jit(solution)/shard_map/ppermute | solution.py:241
  27.5 6.4 %collective-permute-start.4 = (bf16[2,96,512]{2,1,0:T(8,128)(2,1)S(1)}, bf16[2,96,512]{2,1,0:T(8,128)(2,1)S(1)}, u32[]{:S(2)}, u32[]{:S(2)}) collective-permute-start(bf16[2,96,512]{2,1,0:T(8,128)(2,1)S(1)} %fusion.41.refs_0_), channel_id=1, source_target_pairs={{0,8},{4,12},{8,0},{12,4},{16,24},{20,28},{24,16},{28,20},{1,9},{5... | collective-permute-start | bytes 589832 | tf_op jit(solution)/shard_map/ppermute | solution.py:241
  28.3 4.6 %collective-permute-start.5 = (bf16[2,96,192]{2,1,0:T(8,128)(2,1)S(1)}, bf16[2,96,192]{2,1,0:T(8,128)(2,1)S(1)}, u32[]{:S(2)}, u32[]{:S(2)}) collective-permute-start(bf16[2,96,192]{2,1,0:T(8,128)(2,1)S(1)} %pad_maximum_fusion.4.refs_3_), channel_id=1, source_target_pairs={{0,4},{4,0},{8,12},{12,8},{16,20},{20,16},{24,28},{28,24},{1,5},{5... | collective-permute-start | bytes 221192 | tf_op jit(solution)/shard_map/ppermute | solution.py:241
  29.8 7.6 %collective-permute-start.9 = (bf16[512,768]{1,0:T(8,128)(2,1)S(1)}, bf16[512,768]{1,0:T(8,128)(2,1)}, u32[]{:S(2)}, u32[]{:S(2)}) collective-permute-start(bf16[512,768]{1,0:T(8,128)(2,1)S(1)} %bitcast.172), channel_id=1, source_target_pairs={{0,1},{1,0},{2,3},{3,2},{4,5},{5,4},{6,7},{7,6},{8,9},{9,8},{10,11... | collective-permute-start | bytes 2359304 | tf_op jit(solution)/shard_map/ppermute | solution.py:241
  33.9 5.1 %collective-permute-start.10 = (bf16[512,768]{1,0:T(8,128)(2,1)S(1)}, bf16[512,768]{1,0:T(8,128)(2,1)}, u32[]{:S(2)}, u32[]{:S(2)}) collective-permute-start(bf16[512,768]{1,0:T(8,128)(2,1)S(1)} %collective-permute-done.6), channel_id=1, source_target_pairs={{0,1},{1,0},{2,3},{3,2},{4,5},{5,4},{6,7},{7,6},{8,9},{9,8},{10,11... | collective-permute-start | bytes 2359304 | tf_op jit(solution)/shard_map/ppermute | solution.py:241
  33.9 47.3 %collective-permute-start.15 = (bf16[512,768]{1,0:T(8,128)(2,1)}, bf16[512,768]{1,0:T(8,128)(2,1)S(1)}, u32[]{:S(2)}, u32[]{:S(2)}) collective-permute-start(bf16[512,768]{1,0:T(8,128)(2,1)} %bitcast.26.refs_8_), channel_id=1, source_target_pairs={{0,1},{1,0},{2,3},{3,2},{4,5},{5,4},{6,7},{7,6},{8,9},{9,8},{10,11... | collective-permute-start | bytes 2359304 | tf_op jit(solution)/shard_map/ppermute | solution.py:241
  34.5 173.5 %copy-start.5 = (s32[2]{0:T(128)}, s32[2]{0:T(128)S(1)}, u32[]{:S(2)}) copy-start(s32[2]{0:T(128)S(1)} %pad_add_fusion.me_ref) | copy-start | bytes 28
  34.5 13.0 %collective-permute-start.7 = (bf16[4,96,512]{2,1,0:T(8,128)(2,1)S(1)}, bf16[4,96,512]{2,1,0:T(8,128)(2,1)S(1)}, u32[]{:S(2)}, u32[]{:S(2)}) collective-permute-start(bf16[4,96,512]{2,1,0:T(8,128)(2,1)S(1)} %constant_dynamic-update-slice_fusion), channel_id=1, source_target_pairs={{0,4},{4,0},{8,12},{12,8},{16,20},{20,16},{24,28},{28,24},{1,5},{5... | collective-permute-start | bytes 1179656 | tf_op jit(solution)/shard_map/ppermute | solution.py:241
  35.8 25.6 %collective-permute-start.11 = (bf16[512,768]{1,0:T(8,128)(2,1)}, bf16[512,768]{1,0:T(8,128)(2,1)S(1)}, u32[]{:S(2)}, u32[]{:S(2)}) collective-permute-start(bf16[512,768]{1,0:T(8,128)(2,1)} %bitcast.26.refs_8_), channel_id=1, source_target_pairs={{0,2},{1,3},{2,0},{3,1},{4,6},{5,7},{6,4},{7,5},{8,10},{9,11},{10,... | collective-permute-start | bytes 2359304 | tf_op jit(solution)/shard_map/ppermute | solution.py:241
  37.4 10.1 %collective-permute-start.8 = (bf16[4,96,192]{2,1,0:T(8,128)(2,1)S(1)}, bf16[4,96,192]{2,1,0:T(8,128)(2,1)S(1)}, u32[]{:S(2)}, u32[]{:S(2)}) collective-permute-start(bf16[4,96,192]{2,1,0:T(8,128)(2,1)S(1)} %constant_dynamic-update-slice_fusion.2), channel_id=1, source_target_pairs={{0,8},{4,12},{8,0},{12,4},{16,24},{20,28},{24,16},{28,20},{1,9},{5... | collective-permute-start | bytes 442376 | tf_op jit(solution)/shard_map/ppermute | solution.py:241
  39.0 22.5 %collective-permute-start.12 = (bf16[1,288,768]{2,1,0:T(8,128)(2,1)S(1)}, bf16[1,288,768]{2,1,0:T(8,128)(2,1)S(1)}, u32[]{:S(2)}, u32[]{:S(2)}) collective-permute-start(bf16[1,288,768]{2,1,0:T(8,128)(2,1)S(1)} %bitcast.197), channel_id=1, source_target_pairs={{0,16},{4,20},{8,24},{12,28},{16,0},{20,4},{24,8},{28,12},{1,17},{... | collective-permute-start | bytes 1327112 | tf_op jit(solution)/shard_map/ppermute | solution.py:241
  53.4 26.6 %copy-start.11 = (bf16[4,512,768]{2,1,0:T(8,128)(2,1)}, bf16[4,512,768]{2,1,0:T(8,128)(2,1)S(1)}, u32[]{:S(2)}) copy-start(bf16[4,512,768]{2,1,0:T(8,128)(2,1)S(1)} %get-tuple-element.206.h_ref) | copy-start | bytes 9437188
  53.4 53.1 %copy-start.6 = (f32[16,768]{1,0:T(8,128)}, f32[16,768]{1,0:T(8,128)S(1)}, u32[]{:S(2)}) copy-start(f32[16,768]{1,0:T(8,128)S(1)} %get-tuple-element.170.refs_10_.refs_6_.vec_ref) | copy-start | bytes 147460
  61.5 20.3 %collective-permute-start.14 = (bf16[2,288,768]{2,1,0:T(8,128)(2,1)S(1)}, bf16[2,288,768]{2,1,0:T(8,128)(2,1)S(1)}, u32[]{:S(2)}, u32[]{:S(2)}) collective-permute-start(bf16[2,288,768]{2,1,0:T(8,128)(2,1)S(1)} %constant_dynamic-update-slice_fusion.4.refs_4_), channel_id=1, source_target_pairs={{0,8},{4,12},{8,0},{12,4},{16,24},{20,28},{24,16},{28,20},{1,9},{5... | collective-permute-start | bytes 2654216 | tf_op jit(solution)/shard_map/ppermute | solution.py:241
  61.6 20.3 %collective-permute-start.13 = (bf16[2,288,768]{2,1,0:T(8,128)(2,1)S(1)}, bf16[2,288,768]{2,1,0:T(8,128)(2,1)S(1)}, u32[]{:S(2)}, u32[]{:S(2)}) collective-permute-start(bf16[2,288,768]{2,1,0:T(8,128)(2,1)S(1)} %constant_dynamic-update-slice_fusion.4.refs_4_), channel_id=1, source_target_pairs={{0,4},{4,0},{8,12},{12,8},{16,20},{20,16},{24,28},{28,24},{1,5},{5... | collective-permute-start | bytes 2654216 | tf_op jit(solution)/shard_map/ppermute | solution.py:241
  62.2 19.0 %collective-permute-start.16 = (bf16[512,768]{1,0:T(8,128)(2,1)S(1)}, bf16[512,768]{1,0:T(8,128)(2,1)S(1)}, u32[]{:S(2)}, u32[]{:S(2)}) collective-permute-start(bf16[512,768]{1,0:T(8,128)(2,1)S(1)} %collective-permute-done.11), channel_id=1, source_target_pairs={{0,1},{1,0},{2,3},{3,2},{4,5},{5,4},{6,7},{7,6},{8,9},{9,8},{10,11... | collective-permute-start | bytes 2359304 | tf_op jit(solution)/shard_map/ppermute | solution.py:241
  82.1 20.0 %collective-permute-start.18 = (bf16[4,192,512]{2,1,0:T(8,128)(2,1)S(1)}, bf16[4,192,512]{2,1,0:T(8,128)(2,1)S(1)}, u32[]{:S(2)}, u32[]{:S(2)}) collective-permute-start(bf16[4,192,512]{2,1,0:T(8,128)(2,1)S(1)} %get-tuple-element.166.refs_0_), channel_id=1, source_target_pairs={{0,2},{1,3},{2,0},{3,1},{4,6},{5,7},{6,4},{7,5},{8,10},{9,11},{10,... | collective-permute-start | bytes 2359304 | tf_op jit(solution)/shard_map/ppermute | solution.py:241
  83.5 18.5 %collective-permute-start.17 = (bf16[4,192,512]{2,1,0:T(8,128)(2,1)S(1)}, bf16[4,192,512]{2,1,0:T(8,128)(2,1)S(1)}, u32[]{:S(2)}, u32[]{:S(2)}) collective-permute-start(bf16[4,192,512]{2,1,0:T(8,128)(2,1)S(1)} %get-tuple-element.166.refs_0_), channel_id=1, source_target_pairs={{0,1},{1,0},{2,3},{3,2},{4,5},{5,4},{6,7},{7,6},{8,9},{9,8},{10,11... | collective-permute-start | bytes 2359304 | tf_op jit(solution)/shard_map/ppermute | solution.py:241
  83.7 22.7 %collective-permute-start.20 = (bf16[2,288,768]{2,1,0:T(8,128)(2,1)S(1)}, bf16[2,288,768]{2,1,0:T(8,128)(2,1)S(1)}, u32[]{:S(2)}, u32[]{:S(2)}) collective-permute-start(bf16[2,288,768]{2,1,0:T(8,128)(2,1)S(1)} %constant_dynamic-update-slice_fusion.4.refs_4_), channel_id=1, source_target_pairs={{0,12},{4,8},{8,4},{12,0},{16,28},{20,24},{24,20},{28,16},{1,13},{... | collective-permute-start | bytes 2654216 | tf_op jit(solution)/shard_map/ppermute | solution.py:241
  102.0 4.4 %collective-permute-start.19 = (bf16[4,192,512]{2,1,0:T(8,128)(2,1)S(1)}, bf16[4,192,512]{2,1,0:T(8,128)(2,1)S(1)}, u32[]{:S(2)}, u32[]{:S(2)}) collective-permute-start(bf16[4,192,512]{2,1,0:T(8,128)(2,1)S(1)} %collective-permute-done.18.refs_2_), channel_id=1, source_target_pairs={{0,1},{1,0},{2,3},{3,2},{4,5},{5,4},{6,7},{7,6},{8,9},{9,8},{10,11... | collective-permute-start | bytes 2359304 | tf_op jit(solution)/shard_map/ppermute | solution.py:241
  121.7 5.0 %collective-permute-start.21 = (bf16[512,768]{1,0:T(8,128)(2,1)}, bf16[512,768]{1,0:T(8,128)(2,1)}, u32[]{:S(2)}, u32[]{:S(2)}) collective-permute-start(bf16[512,768]{1,0:T(8,128)(2,1)} %get-tuple-element.180), channel_id=1, source_target_pairs={{0,1},{1,0},{2,3},{3,2},{4,5},{5,4},{6,7},{7,6},{8,9},{9,8},{10,11... | collective-permute-start | bytes 2359304 | tf_op jit(solution)/shard_map/ppermute | solution.py:241
  128.3 23.0 %collective-permute-start.23 = (bf16[512,768]{1,0:T(8,128)(2,1)S(1)}, bf16[512,768]{1,0:T(8,128)(2,1)S(1)}, u32[]{:S(2)}, u32[]{:S(2)}) collective-permute-start(bf16[512,768]{1,0:T(8,128)(2,1)S(1)} %add_convert_fusion.3), channel_id=1, source_target_pairs={{0,2},{1,3},{2,0},{3,1},{4,6},{5,7},{6,4},{7,5},{8,10},{9,11},{10,... | collective-permute-start | bytes 2359304 | tf_op jit(solution)/shard_map/ppermute | solution.py:241
  142.7 8.5 %collective-permute-start.22 = (bf16[512,768]{1,0:T(8,128)(2,1)S(1)}, bf16[512,768]{1,0:T(8,128)(2,1)S(1)}, u32[]{:S(2)}, u32[]{:S(2)}) collective-permute-start(bf16[512,768]{1,0:T(8,128)(2,1)S(1)} %get-tuple-element.184), channel_id=1, source_target_pairs={{0,1},{1,0},{2,3},{3,2},{4,5},{5,4},{6,7},{7,6},{8,9},{9,8},{10,11... | collective-permute-start | bytes 2359304 | tf_op jit(solution)/shard_map/ppermute | solution.py:241
  159.6 2.8 %collective-permute-start.24 = (bf16[192,512]{1,0:T(8,128)(2,1)S(1)}, bf16[192,512]{1,0:T(8,128)(2,1)S(1)}, u32[]{:S(2)}, u32[]{:S(2)}) collective-permute-start(bf16[192,512]{1,0:T(8,128)(2,1)S(1)} %get-tuple-element.194), channel_id=1, source_target_pairs={{0,1},{1,0},{2,3},{3,2},{4,5},{5,4},{6,7},{7,6},{8,9},{9,8},{10,11... | collective-permute-start | bytes 589832 | tf_op jit(solution)/shard_map/ppermute | solution.py:241
  159.9 42.2 %collective-permute-start.32 = (bf16[4,192,768]{2,1,0:T(8,128)(2,1)}, bf16[4,192,768]{2,1,0:T(8,128)(2,1)S(1)}, u32[]{:S(2)}, u32[]{:S(2)}) collective-permute-start(bf16[4,192,768]{2,1,0:T(8,128)(2,1)} %fusion.27), channel_id=1, source_target_pairs={{0,4},{4,0},{8,12},{12,8},{16,20},{20,16},{24,28},{28,24},{1,5},{5... | collective-permute-start | bytes 3538952 | tf_op jit(solution)/shard_map/ppermute | solution.py:241
  161.2 7.9 %collective-permute-start.25 = (bf16[192,512]{1,0:T(8,128)(2,1)S(1)}, bf16[192,512]{1,0:T(8,128)(2,1)S(1)}, u32[]{:S(2)}, u32[]{:S(2)}) collective-permute-start(bf16[192,512]{1,0:T(8,128)(2,1)S(1)} %get-tuple-element.198), channel_id=1, source_target_pairs={{0,2},{1,3},{2,0},{3,1},{4,6},{5,7},{6,4},{7,5},{8,10},{9,11},{10,... | collective-permute-start | bytes 589832 | tf_op jit(solution)/shard_map/ppermute | solution.py:241
  162.3 8.7 %collective-permute-start.26 = (bf16[192,512]{1,0:T(8,128)(2,1)S(1)}, bf16[192,512]{1,0:T(8,128)(2,1)S(1)}, u32[]{:S(2)}, u32[]{:S(2)}) collective-permute-start(bf16[192,512]{1,0:T(8,128)(2,1)S(1)} %get-tuple-element.199), channel_id=1, source_target_pairs={{0,3},{1,2},{2,1},{3,0},{4,7},{5,6},{6,5},{7,4},{8,11},{9,10},{10,... | collective-permute-start | bytes 589832 | tf_op jit(solution)/shard_map/ppermute | solution.py:241
  163.5 9.3 %collective-permute-start.28 = (bf16[16,24,768]{2,1,0:T(8,128)(2,1)S(1)}, bf16[16,24,768]{2,1,0:T(8,128)(2,1)S(1)}, u32[]{:S(2)}, u32[]{:S(2)}) collective-permute-start(bf16[16,24,768]{2,1,0:T(8,128)(2,1)S(1)} %dynamic-slice_bitcast_fusion.2), channel_id=1, source_target_pairs={{0,1},{1,0},{2,3},{3,2},{4,5},{5,4},{6,7},{7,6},{8,9},{9,8},{10,11... | collective-permute-start | bytes 1769480 | tf_op jit(solution)/shard_map/ppermute | solution.py:241
  167.6 34.5 %collective-permute-start.29 = (bf16[512,768]{1,0:T(8,128)(2,1)S(1)}, bf16[512,768]{1,0:T(8,128)(2,1)S(1)}, u32[]{:S(2)}, u32[]{:S(2)}) collective-permute-start(bf16[512,768]{1,0:T(8,128)(2,1)S(1)} %convolution_convert_fusion), channel_id=1, source_target_pairs={{0,1},{1,0},{2,3},{3,2},{4,5},{5,4},{6,7},{7,6},{8,9},{9,8},{10,11... | collective-permute-start | bytes 2359304 | tf_op jit(solution)/shard_map/ppermute | solution.py:241
  169.0 5.2 %collective-permute-start.27 = (bf16[512,768]{1,0:T(8,128)(2,1)S(1)}, bf16[512,768]{1,0:T(8,128)(2,1)S(1)}, u32[]{:S(2)}, u32[]{:S(2)}) collective-permute-start(bf16[512,768]{1,0:T(8,128)(2,1)S(1)} %convolution_convert_fusion.2), channel_id=1, source_target_pairs={{0,1},{1,0},{2,3},{3,2},{4,5},{5,4},{6,7},{7,6},{8,9},{9,8},{10,11... | collective-permute-start | bytes 2359304 | tf_op jit(solution)/shard_map/ppermute | solution.py:241
  173.0 29.1 %collective-permute-start.31 = (bf16[8,24,768]{2,1,0:T(8,128)(2,1)S(1)}, bf16[8,24,768]{2,1,0:T(8,128)(2,1)S(1)}, u32[]{:S(2)}, u32[]{:S(2)}) collective-permute-start(bf16[8,24,768]{2,1,0:T(8,128)(2,1)S(1)} %dynamic-slice_bitcast_fusion.4), channel_id=1, source_target_pairs={{0,2},{1,3},{2,0},{3,1},{4,6},{5,7},{6,4},{7,5},{8,10},{9,11},{10,... | collective-permute-start | bytes 884744 | tf_op jit(solution)/shard_map/ppermute | solution.py:241
  174.4 27.7 %collective-permute-start.30 = (bf16[512,768]{1,0:T(8,128)(2,1)S(1)}, bf16[512,768]{1,0:T(8,128)(2,1)S(1)}, u32[]{:S(2)}, u32[]{:S(2)}) collective-permute-start(bf16[512,768]{1,0:T(8,128)(2,1)S(1)} %add_convert_fusion.2), channel_id=1, source_target_pairs={{0,2},{1,3},{2,0},{3,1},{4,6},{5,7},{6,4},{7,5},{8,10},{9,11},{10,... | collective-permute-start | bytes 2359304 | tf_op jit(solution)/shard_map/ppermute | solution.py:241
  203.9 19.4 %collective-permute-start.33 = (bf16[4,120,768]{2,1,0:T(8,128)(2,1)S(1)}, bf16[4,120,768]{2,1,0:T(8,128)(2,1)S(1)}, u32[]{:S(2)}, u32[]{:S(2)}) collective-permute-start(bf16[4,120,768]{2,1,0:T(8,128)(2,1)S(1)} %dynamic-slice_bitcast_fusion), channel_id=1, source_target_pairs={{0,4},{4,0},{8,12},{12,8},{16,20},{20,16},{24,28},{28,24},{1,5},{5... | collective-permute-start | bytes 2211848 | tf_op jit(solution)/shard_map/ppermute | solution.py:241
  206.0 16.0 %collective-permute-start.34 = (bf16[2,192,768]{2,1,0:T(8,128)(2,1)S(1)}, bf16[2,192,768]{2,1,0:T(8,128)(2,1)S(1)}, u32[]{:S(2)}, u32[]{:S(2)}) collective-permute-start(bf16[2,192,768]{2,1,0:T(8,128)(2,1)S(1)} %dynamic-slice_bitcast_fusion.1), channel_id=1, source_target_pairs={{0,8},{4,12},{8,0},{12,4},{16,24},{20,28},{24,16},{28,20},{1,9},{5... | collective-permute-start | bytes 1769480 | tf_op jit(solution)/shard_map/ppermute | solution.py:241
  224.1 9.4 %collective-permute-start.36 = (bf16[2,512,768]{2,1,0:T(8,128)(2,1)S(1)}, bf16[2,512,768]{2,1,0:T(8,128)(2,1)}, u32[]{:S(2)}, u32[]{:S(2)}) collective-permute-start(bf16[2,512,768]{2,1,0:T(8,128)(2,1)S(1)} %get-tuple-element.224), channel_id=1, source_target_pairs={{0,1},{1,0},{2,3},{3,2},{4,5},{5,4},{6,7},{7,6},{8,9},{9,8},{10,11... | collective-permute-start | bytes 4718600 | tf_op jit(solution)/shard_map/ppermute | solution.py:241
  226.1 18.5 %collective-permute-start.35 = (bf16[2,120,768]{2,1,0:T(8,128)(2,1)S(1)}, bf16[2,120,768]{2,1,0:T(8,128)(2,1)S(1)}, u32[]{:S(2)}, u32[]{:S(2)}) collective-permute-start(bf16[2,120,768]{2,1,0:T(8,128)(2,1)S(1)} %bitcast_add_fusion.2), channel_id=1, source_target_pairs={{0,8},{4,12},{8,0},{12,4},{16,24},{20,28},{24,16},{28,20},{1,9},{5... | collective-permute-start | bytes 1105928 | tf_op jit(solution)/shard_map/ppermute | solution.py:241
  228.3 9.3 %collective-permute-start.37 = (bf16[2,96,128]{2,1,0:T(8,128)(2,1)S(1)}, bf16[2,96,128]{2,1,0:T(8,128)(2,1)S(1)}, u32[]{:S(2)}, u32[]{:S(2)}) collective-permute-start(bf16[2,96,128]{2,1,0:T(8,128)(2,1)S(1)} %get-tuple-element.225), channel_id=1, source_target_pairs={{0,4},{4,0},{8,12},{12,8},{16,20},{20,16},{24,28},{28,24},{1,5},{5... | collective-permute-start | bytes 147464 | tf_op jit(solution)/shard_map/ppermute | solution.py:241
  228.8 15.8 %collective-permute-start.38 = (bf16[2,96,128]{2,1,0:T(8,128)(2,1)S(1)}, bf16[2,96,128]{2,1,0:T(8,128)(2,1)S(1)}, u32[]{:S(2)}, u32[]{:S(2)}) collective-permute-start(bf16[2,96,128]{2,1,0:T(8,128)(2,1)S(1)} %get-tuple-element.226), channel_id=1, source_target_pairs={{0,12},{4,8},{8,4},{12,0},{16,28},{20,24},{24,20},{28,16},{1,13},{... | collective-permute-start | bytes 147464 | tf_op jit(solution)/shard_map/ppermute | solution.py:241
  230.7 16.4 %collective-permute-start.40 = (bf16[1,192,768]{2,1,0:T(8,128)(2,1)S(1)}, bf16[1,192,768]{2,1,0:T(8,128)(2,1)}, u32[]{:S(2)}, u32[]{:S(2)}) collective-permute-start(bf16[1,192,768]{2,1,0:T(8,128)(2,1)S(1)} %get-tuple-element.270), channel_id=1, source_target_pairs={{0,16},{4,20},{8,24},{12,28},{16,0},{20,4},{24,8},{28,12},{1,17},{... | collective-permute-start | bytes 884744 | tf_op jit(solution)/shard_map/ppermute | solution.py:241
  236.0 25.1 %collective-permute-start.44 = (bf16[512,768]{1,0:T(8,128)(2,1)}, bf16[512,768]{1,0:T(8,128)(2,1)S(1)}, u32[]{:S(2)}, u32[]{:S(2)}) collective-permute-start(bf16[512,768]{1,0:T(8,128)(2,1)} %fusion.30), channel_id=1, source_target_pairs={{0,2},{1,3},{2,0},{3,1},{4,6},{5,7},{6,4},{7,5},{8,10},{9,11},{10,... | collective-permute-start | bytes 2359304 | tf_op jit(solution)/shard_map/ppermute | solution.py:241
  245.5 10.3 %collective-permute-start.39 = (bf16[1,120,768]{2,1,0:T(8,128)(2,1)S(1)}, bf16[1,120,768]{2,1,0:T(8,128)(2,1)S(1)}, u32[]{:S(2)}, u32[]{:S(2)}) collective-permute-start(bf16[1,120,768]{2,1,0:T(8,128)(2,1)S(1)} %get-tuple-element.278), channel_id=1, source_target_pairs={{0,16},{4,20},{8,24},{12,28},{16,0},{20,4},{24,8},{28,12},{1,17},{... | collective-permute-start | bytes 552968 | tf_op jit(solution)/shard_map/ppermute | solution.py:241
  258.8 7.6 %collective-permute-start.41 = (bf16[24,1472]{1,0:T(8,128)(2,1)}, bf16[24,1472]{1,0:T(8,128)(2,1)S(1)}, u32[]{:S(2)}, u32[]{:S(2)}) collective-permute-start(bf16[24,1472]{1,0:T(8,128)(2,1)} %get-tuple-element.235), channel_id=1, source_target_pairs={{0,1},{1,0},{2,3},{3,2},{4,5},{5,4},{6,7},{7,6},{8,9},{9,8},{10,11... | collective-permute-start | bytes 211976 | tf_op jit(solution)/shard_map/ppermute | solution.py:241
  258.8 7.6 %collective-permute-start.42 = (bf16[24,1472]{1,0:T(8,128)(2,1)}, bf16[24,1472]{1,0:T(8,128)(2,1)S(1)}, u32[]{:S(2)}, u32[]{:S(2)}) collective-permute-start(bf16[24,1472]{1,0:T(8,128)(2,1)} %get-tuple-element.236), channel_id=1, source_target_pairs={{0,2},{1,3},{2,0},{3,1},{4,6},{5,7},{6,4},{7,5},{8,10},{9,11},{10,... | collective-permute-start | bytes 211976 | tf_op jit(solution)/shard_map/ppermute | solution.py:241
  259.5 6.8 %collective-permute-start.43 = (bf16[24,1472]{1,0:T(8,128)(2,1)}, bf16[24,1472]{1,0:T(8,128)(2,1)S(1)}, u32[]{:S(2)}, u32[]{:S(2)}) collective-permute-start(bf16[24,1472]{1,0:T(8,128)(2,1)} %get-tuple-element.237), channel_id=1, source_target_pairs={{0,3},{1,2},{2,1},{3,0},{4,7},{5,6},{6,5},{7,4},{8,11},{9,10},{10,... | collective-permute-start | bytes 211976 | tf_op jit(solution)/shard_map/ppermute | solution.py:241
  (60 other events, 335.8 us)

commit v7 on v6

--- a/solution.py
+++ b/solution.py
@@ -809,7 +809,7 @@
     ones[0][1], ones[1][1], x_far = lax.optimization_barrier((ones[0][1], ones[1][1], x_far))
     g_far = swap(tie(g, x_far), "seq", ns, far)
     last = [jnp.concatenate(parts, 0) for parts in ones]
-    twos = [tie(two, *last)[None]]
+    twos = [tie(two, ones[0][1])[None]]
     for parts, held, order in zip(ones, last, (masks, turned)):
         parts.append(swap(held, "dp", nd, order[-1]))
 

time: 275 us -> 276 us (level)
    unnamed x130 -> x134, local copies, waits for them, and re-layouts: 9.97 us -> 10.1 us
  transfers between devices with their start and end apart: 45 -> 45, of which waited for: 16 -> 16; matrix products, arithmetic and copies ran while one was open for 15% -> 15% of each run, Pallas kernels for 27% -> 28%
where the time goes in v7:
time: 276 us; the launch traced here: 272 us
  Pallas kernels  98.6 us (36%)
  waiting for transfers between devices  67.5 us (24%)
  starting transfers between devices  43.2 us (16%)
  other arithmetic  23.3 us (8%)
  local copies, waits for them, and re-layouts  22.2 us (8%)
  matrix products  14.8 us (5%)
    ppermute x45, waiting for transfers between devices, swap(): return lax.ppermute(value, axis, [(i, i ^ mask) for i in range(size)])  67.5 us
    ppermute x45, starting transfers between devices, swap(): return lax.ppermute(value, axis, [(i, i ^ mask) for i in range(size)])  43.2 us
    pallas_call x2, Pallas kernels, feed(): pl.pallas_call(functools.partial(feed_kernel, n=n, base=base, tile=256 if...  27.9 us
    pallas_call x1, Pallas kernels, attend_back(): pl.pallas_call(functools.partial(attend_back_kernel, heads=heads, hd=hd),...  26.9 us
    pallas_call x1, Pallas kernels, attend(): pl.pallas_call(functools.partial(attend_kernel, heads=heads, hd=hd), grid...  17.9 us
    unnamed x134, local copies, waits for them, and re-layouts  10.1 us
    dot_general x4, matrix products, over_rows(): return jnp.einsum('nbk,nbc->kc', a, b, preferred_element_type=F32)  9.31 us
    pallas_call x1, Pallas kernels, leave(): pl.pallas_call(leave_kernel, grid_spec=pltpu.PrefetchScalarGridSpec(num_s...  8.21 us
  transfers between devices with their start and end apart: 45, of which 16 were waited for; matrix products, arithmetic and copies ran while one was open for 15% of the time, Pallas kernels for 28%

profile of v7, /device:TPU:0, one launch (start us, length us, event | category | flops | bytes accessed | tf_op | source)
XLA Modules:
  0.0 271.5 jit_solution(5311162310205354767)
XLA Ops:
  6.8 2.4 collective-permute-start
  9.9 1.7 collective-permute-start.6
  13.2 2.8 %collective-permute-done.1 = bf16[24,2368]{1,0:T(8,128)(2,1)S(1)} collective-permute-done((bf16[24,2368]{1,0:T(8,128)(2,1)S(1)}, bf16[24,2368]{1,0:T(8,128)(2,1)S(1)}, u32[]{:S(2)}, u32[]{:S(2)}) %collective-permute-start.1) | collective-permute-done | bytes 113696 | tf_op jit(solution)/shard_map/ppermute | solution.py:241
  17.2 3.0 %collective-permute-start.3 = (bf16[1,96,704]{2,1,0:T(8,128)(2,1)S(1)}, bf16[1,96,704]{2,1,0:T(8,128)(2,1)S(1)}, u32[]{:S(2)}, u32[]{:S(2)}) collective-permute-start(bf16[1,96,704]{2,1,0:T(8,128)(2,1)S(1)} %fusion.42), channel_id=1, source_target_pairs={{0,16},{4,20},{8,24},{12,28},{16,0},{20,4},{24,8},{28,12},{1,17},{... | collective-permute-start | bytes 405512 | tf_op jit(solution)/shard_map/ppermute | solution.py:241
  21.5 5.9 %collective-permute-done.3 = bf16[1,96,704]{2,1,0:T(8,128)(2,1)S(1)} collective-permute-done((bf16[1,96,704]{2,1,0:T(8,128)(2,1)S(1)}, bf16[1,96,704]{2,1,0:T(8,128)(2,1)S(1)}, u32[]{:S(2)}, u32[]{:S(2)}) %collective-permute-start.3) | collective-permute-done | bytes 135200 | tf_op jit(solution)/shard_map/ppermute | solution.py:241
  28.3 1.5 collective-permute-start.5
  29.8 3.1 %collective-permute-done.5.refs_4_ = bf16[2,96,192]{2,1,0:T(8,128)(2,1)S(1)} collective-permute-done((bf16[2,96,192]{2,1,0:T(8,128)(2,1)S(1)}, bf16[2,96,192]{2,1,0:T(8,128)(2,1)S(1)}, u32[]{:S(2)}, u32[]{:S(2)}) %collective-permute-start.5) | collective-permute-done | bytes 73760 | tf_op jit(solution)/shard_map/ppermute | solution.py:241
  35.8 1.6 collective-permute-start.11
  37.4 1.5 collective-permute-start.8
  39.0 3.4 %collective-permute-start.12 = (bf16[1,288,768]{2,1,0:T(8,128)(2,1)S(1)}, bf16[1,288,768]{2,1,0:T(8,128)(2,1)S(1)}, u32[]{:S(2)}, u32[]{:S(2)}) collective-permute-start(bf16[1,288,768]{2,1,0:T(8,128)(2,1)S(1)} %bitcast.200), channel_id=1, source_target_pairs={{0,16},{4,20},{8,24},{12,28},{16,0},{20,4},{24,8},{28,12},{1,17},{... | collective-permute-start | bytes 1327112 | tf_op jit(solution)/shard_map/ppermute | solution.py:241
  42.4 2.2 pad_maximum_fusion.refs_6_.refs_8_.refs_4_.x_ref
  44.6 3.0 %collective-permute-done.8.refs_5_ = bf16[4,96,192]{2,1,0:T(8,128)(2,1)S(1)} collective-permute-done((bf16[4,96,192]{2,1,0:T(8,128)(2,1)S(1)}, bf16[4,96,192]{2,1,0:T(8,128)(2,1)S(1)}, u32[]{:S(2)}, u32[]{:S(2)}) %collective-permute-start.8) | collective-permute-done | bytes 147488 | tf_op jit(solution)/shard_map/ppermute | solution.py:241
  47.6 5.9 %enter.1 = (bf16[4,512,576]{2,1,0:T(8,128)(2,1)S(1)}, bf16[4,512,768]{2,1,0:T(8,128)(2,1)S(1)}, bf16[768,576]{1,0:T(8,128)(2,1)S(1)}, f32[16,768]{1,0:T(8,128)S(1)}) custom-call(s32[2]{0:T(128)S(1)} %pad_add_fusion.me_ref, bf16[2,96,512]{2,1,0:T(8,128)(2,1)S(1)} %fusion.41.refs_0_, bf16[2,96,512]{2,1,0:T(8,128)(2,1)S(1)} %copy-done.4, ...), custom_call_target="tpu_custom_call" | custom-call | flops 5000000000 | bytes 8000000 | tf_op jit(solution)/shard_map/enter/pallas_call | solution.py:388
  53.6 7.9 %collective-permute-done.12 = bf16[1,288,768]{2,1,0:T(8,128)(2,1)S(1)} collective-permute-done((bf16[1,288,768]{2,1,0:T(8,128)(2,1)S(1)}, bf16[1,288,768]{2,1,0:T(8,128)(2,1)S(1)}, u32[]{:S(2)}, u32[]{:S(2)}) %collective-permute-start.12) | collective-permute-done | bytes 442400 | tf_op jit(solution)/shard_map/ppermute | solution.py:241
  62.3 17.9 %attend.1 = (bf16[4,192,512]{2,1,0:T(8,128)(2,1)S(1)}, f32[4,192,512]{2,1,0:T(8,128)S(1)}, f32[4,8,512]{2,1,0:T(8,128)S(1)}) custom-call(s32[2]{0:T(128)S(1)} %pad_add_fusion.me_ref, bf16[4,512,576]{2,1,0:T(8,128)(2,1)S(1)} %get-tuple-element.159.qkv_ref, s32[4,1,512]{2,1,0:T(1,128)S(1)} %maximum_convert_fusion.1.seg_row_ref, s32[4,512,1]{2,1,0:T(8,128)S(1)} %copy-done.1), custom_call_target="tpu_custom_call" | custom-call | flops 20000000000 | bytes 8000000 | tf_op jit(solution)/shard_map/attend/pallas_call | solution.py:87
  82.3 1.4 collective-permute-start.18
  84.0 1.9 collective-permute-start.20
  85.8 2.9 %pad_maximum_fusion.1.refs_9_.refs_5_ = bf16[4,512,768]{2,1,0:T(8,128)(2,1)} fusion(bf16[1,512,768]{2,1,0:T(8,128)(2,1)S(1)} %bitcast.192, bf16[1,512,768]{2,1,0:T(8,128)(2,1)S(1)} %bitcast.190, bf16[1,512,768]{2,1,0:T(8,128)(2,1)} %bitcast.188, bf16[1,512,768]{2,1,0:T(8,128)(2,1)S(1)} %copy-done.30), kind=kLoop, calls=%fused_computation.1 | loop fusion | flops 4718592 | bytes 6291456 | tf_op jit(solution)/shard_map/stack | solution.py:842
  88.7 13.6 %collective-permute-done.18.refs_2_ = bf16[4,192,512]{2,1,0:T(8,128)(2,1)S(1)} collective-permute-done((bf16[4,192,512]{2,1,0:T(8,128)(2,1)S(1)}, bf16[4,192,512]{2,1,0:T(8,128)(2,1)S(1)}, u32[]{:S(2)}, u32[]{:S(2)}) %collective-permute-start.18) | collective-permute-done | bytes 786464 | tf_op jit(solution)/shard_map/ppermute | solution.py:241
  102.3 4.4 %collective-permute-done.20.refs_7_ = bf16[2,288,768]{2,1,0:T(8,128)(2,1)S(1)} collective-permute-done((bf16[2,288,768]{2,1,0:T(8,128)(2,1)S(1)}, bf16[2,288,768]{2,1,0:T(8,128)(2,1)S(1)}, u32[]{:S(2)}, u32[]{:S(2)}) %collective-permute-start.20) | collective-permute-done | bytes 884768 | tf_op jit(solution)/shard_map/ppermute | solution.py:241
  107.6 14.3 %feed_far.1 = (bf16[2,512,768]{2,1,0:T(8,128)(2,1)}, bf16[2,512,768]{2,1,0:T(8,128)(2,1)}, bf16[2,512,768]{2,1,0:T(8,128)(2,1)}, bf16[512,768]{1,0:T(8,128)(2,1)...) custom-call(s32[2]{0:T(128)S(1)} %pad_add_fusion.me_ref, ...), custom_call_target="tpu_custom_call" | custom-call | flops 8999999488 | bytes 16000000 | tf_op jit(solution)/shard_map/feed_far/pallas_call | solution.py:506
  122.1 3.4 %convolution_bitcast_fusion = f32[768,768]{1,0:T(8,128)S(1)} fusion(bf16[2,512,768]{2,1,0:T(8,128)(2,1)} %get-tuple-element.200, bf16[1,512,768]{2,1,0:T(8,128)(2,1)} %bitcast.193, bf16[1,512,768]{2,1,0:T(8,128)(2,1)} %bitcast.191), kind=kOutput, calls=%fused_computation.20 | convolution fusion | flops 1208745984 | bytes 5505024 | tf_op jit(solution)/shard_map/nbk,nbc->kc/dot_general | solution.py:853
  125.6 1.5 fusion.49
  127.1 1.5 add_convert_fusion.3
  129.4 13.6 %feed_near.1 = (bf16[2,512,768]{2,1,0:T(8,128)(2,1)}, bf16[2,512,768]{2,1,0:T(8,128)(2,1)}, bf16[2,512,768]{2,1,0:T(8,128)(2,1)}, bf16[512,768]{1,0:T(8,128)(2,1...) custom-call(s32[2]{0:T(128)S(1)} %pad_add_fusion.me_ref, ...), custom_call_target="tpu_custom_call" | custom-call | flops 8999999488 | bytes 16000000 | tf_op jit(solution)/shard_map/feed_near/pallas_call | solution.py:506
  143.2 2.9 %fusion.16 = f32[768,768,1]{1,0,2:T(8,128)S(1)} fusion(bf16[2,512,768]{2,1,0:T(8,128)(2,1)} %get-tuple-element.201, bf16[1,512,768]{2,1,0:T(8,128)(2,1)S(1)} %bitcast.189, bf16[1,512,768]{2,1,0:T(8,128)(2,1)S(1)} %copy-done.31), kind=kOutput, calls=%fused_computation.29 | convolution fusion | flops 1208745984 | bytes 5505024 | tf_op jit(solution)/shard_map/nbk,nbc->kc/dot_general | solution.py:853
  148.4 1.5 fusion.3
  152.2 7.5 %turn.1 = (bf16[192,512]{1,0:T(8,128)(2,1)S(1)}, bf16[192,512]{1,0:T(8,128)(2,1)S(1)}, bf16[192,512]{1,0:T(8,128)(2,1)S(1)}, bf16[192,512]{1,0:T(8,128)(2,1)S(1)...) custom-call(s32[2]{0:T(128)S(1)} %pad_add_fusion.me_ref, ...), custom_call_target="tpu_custom_call" | custom-call | flops 3000000000 | bytes 8000000 | tf_op jit(solution)/shard_map/turn/pallas_call | solution.py:556
  164.7 2.3 convolution_convert_fusion.2
  169.4 1.8 collective-permute-done.26
  171.3 1.7 convolution_convert_fusion.1
  175.6 26.9 %attend_back.1 = (bf16[4,512,576]{2,1,0:T(8,128)(2,1)S(1)}, bf16[768,576]{1,0:T(8,128)(2,1)S(1)}) custom-call(s32[2]{0:T(128)S(1)} %pad_add_fusion.me_ref, bf16[4,512,576]{2,1,0:T(8,128)(2,1)S(1)} %copy-done.14, bf16[4,192,512]{2,1,0:T(8,128)(2,1)S(1)} %pad_maximum_fusion.2.go_ref, f32[4,192,512]{2,1,0:T(8,128)S(1)} %copy-done.19, ...), custom_call_target="tpu_custom_call" | custom-call | flops 40000000000 | bytes 12000000 | tf_op jit(solution)/shard_map/attend_back/pallas_call | solution.py:186
  206.4 2.0 collective-permute-start.34
  208.4 8.2 %leave.1 = (bf16[2,512,768]{2,1,0:T(8,128)(2,1)S(1)}, bf16[2,512,768]{2,1,0:T(8,128)(2,1)S(1)}, bf16[768,128]{1,0:T(8,128)(2,1)S(1)}) custom-call(s32[2]{0:T(128)S(1)} %pad_add_fusion.me_ref, bf16[4,512,768]{2,1,0:T(8,128)(2,1)} %copy-done, bf16[4,512,576]{2,1,0:T(8,128)(2,1)} %copy-done.15, bf16[768,576]{1,0:T(8,128)(2,1)S(1)} %copy-done.17, ...), custom_call_target="tpu_custom_call" | custom-call | flops 6000000000 | bytes 10000000 | tf_op jit(solution)/shard_map/leave/pallas_call | solution.py:634
  216.6 5.8 %collective-permute-done.34 = bf16[2,192,768]{2,1,0:T(8,128)(2,1)S(1)} collective-permute-done((bf16[2,192,768]{2,1,0:T(8,128)(2,1)S(1)}, bf16[2,192,768]{2,1,0:T(8,128)(2,1)S(1)}, u32[]{:S(2)}, u32[]{:S(2)}) %collective-permute-start.34) | collective-permute-done | bytes 589856 | tf_op jit(solution)/shard_map/ppermute | solution.py:241
  224.8 1.6 fusion.22
  226.5 2.0 collective-permute-start.35
  231.1 3.0 %collective-permute-start.40 = (bf16[1,192,768]{2,1,0:T(8,128)(2,1)S(1)}, bf16[1,192,768]{2,1,0:T(8,128)(2,1)}, u32[]{:S(2)}, u32[]{:S(2)}) collective-permute-start(bf16[1,192,768]{2,1,0:T(8,128)(2,1)S(1)} %get-tuple-element.270), channel_id=1, source_target_pairs={{0,16},{4,20},{8,24},{12,28},{16,0},{20,4},{24,8},{28,12},{1,17},{... | collective-permute-start | bytes 884744 | tf_op jit(solution)/shard_map/ppermute | solution.py:241
  234.1 2.4 fusion.30
  236.5 1.4 collective-permute-start.44
  237.9 7.1 %collective-permute-done.38 = bf16[2,96,128]{2,1,0:T(8,128)(2,1)S(1)} collective-permute-done((bf16[2,96,128]{2,1,0:T(8,128)(2,1)S(1)}, bf16[2,96,128]{2,1,0:T(8,128)(2,1)S(1)}, u32[]{:S(2)}, u32[]{:S(2)}) %collective-permute-start.38) | collective-permute-done | bytes 49184 | tf_op jit(solution)/shard_map/ppermute | solution.py:241
  246.0 1.5 add_add_fusion
  247.5 8.7 %collective-permute-done.39 = bf16[1,120,768]{2,1,0:T(8,128)(2,1)S(1)} collective-permute-done((bf16[1,120,768]{2,1,0:T(8,128)(2,1)S(1)}, bf16[1,120,768]{2,1,0:T(8,128)(2,1)S(1)}, u32[]{:S(2)}, u32[]{:S(2)}) %collective-permute-start.39) | collective-permute-done | bytes 184352 | tf_op jit(solution)/shard_map/ppermute | solution.py:241
  256.9 2.3 hand_over.1
  261.7 2.0 fusion.23
  263.7 3.1 %fusion.11 = f32[512,768]{1,0:T(8,128)} fusion(f32[512,768]{1,0:T(8,128)S(1)} %copy-done.36, bf16[512,768]{1,0:T(8,128)(2,1)S(1)} %bitcast.176, bf16[512,768]{1,0:T(8,128)(2,1)S(1)} %collective-permute-done.44, f32[512]{0:T(512)S(1)} %get-tuple-element.284, f32[512]{0:T(512)S(1)} %get-tuple-element.285, f32[768]{0:T(1024)S(1)} %get-tuple-element.260, ...), kind=kLoop, calls=%fused_computation.24 | loop fusion | flops 6291456 | bytes 6302720 | tf_op jit(solution)/shard_map/add | solution.py:929
  267.6 1.9 finish.1
  269.5 1.8 slice_reduce_fusion.1
  (271 shorter events, 47.7 us)
Async XLA Ops:
  6.8 6.0 %collective-permute-start = (bf16[24,2368]{1,0:T(8,128)(2,1)S(1)}, bf16[24,2368]{1,0:T(8,128)(2,1)S(1)}, u32[]{:S(2)}, u32[]{:S(2)}) collective-permute-start(bf16[24,2368]{1,0:T(8,128)(2,1)S(1)} %get-tuple-element.275), channel_id=1, source_target_pairs={{0,3},{1,2},{2,1},{3,0},{4,7},{5,6},{6,5},{7,4},{8,11},{9,10},{10,... | collective-permute-start | bytes 341000 | tf_op jit(solution)/shard_map/ppermute | solution.py:241
  9.2 6.7 %collective-permute-start.1 = (bf16[24,2368]{1,0:T(8,128)(2,1)S(1)}, bf16[24,2368]{1,0:T(8,128)(2,1)S(1)}, u32[]{:S(2)}, u32[]{:S(2)}) collective-permute-start(bf16[24,2368]{1,0:T(8,128)(2,1)S(1)} %get-tuple-element.274), channel_id=1, source_target_pairs={{0,2},{1,3},{2,0},{3,1},{4,6},{5,7},{6,4},{7,5},{8,10},{9,11},{10,... | collective-permute-start | bytes 341000 | tf_op jit(solution)/shard_map/ppermute | solution.py:241
  9.9 6.4 %collective-permute-start.2 = (bf16[24,2368]{1,0:T(8,128)(2,1)S(1)}, bf16[24,2368]{1,0:T(8,128)(2,1)S(1)}, u32[]{:S(2)}, u32[]{:S(2)}) collective-permute-start(bf16[24,2368]{1,0:T(8,128)(2,1)S(1)} %get-tuple-element.273), channel_id=1, source_target_pairs={{0,1},{1,0},{2,3},{3,2},{4,5},{5,4},{6,7},{7,6},{8,9},{9,8},{10,11... | collective-permute-start | bytes 341000 | tf_op jit(solution)/shard_map/ppermute | solution.py:241
  9.9 24.0 %collective-permute-start.6 = (bf16[512,768]{1,0:T(8,128)(2,1)S(1)}, bf16[512,768]{1,0:T(8,128)(2,1)}, u32[]{:S(2)}, u32[]{:S(2)}) collective-permute-start(bf16[512,768]{1,0:T(8,128)(2,1)S(1)} %bitcast.171), channel_id=1, source_target_pairs={{0,2},{1,3},{2,0},{3,1},{4,6},{5,7},{6,4},{7,5},{8,10},{9,11},{10,... | collective-permute-start | bytes 2359304 | tf_op jit(solution)/shard_map/ppermute | solution.py:241
  17.2 10.3 %collective-permute-start.3 = (bf16[1,96,704]{2,1,0:T(8,128)(2,1)S(1)}, bf16[1,96,704]{2,1,0:T(8,128)(2,1)S(1)}, u32[]{:S(2)}, u32[]{:S(2)}) collective-permute-start(bf16[1,96,704]{2,1,0:T(8,128)(2,1)S(1)} %fusion.42), channel_id=1, source_target_pairs={{0,16},{4,20},{8,24},{12,28},{16,0},{20,4},{24,8},{28,12},{1,17},{... | collective-permute-start | bytes 405512 | tf_op jit(solution)/shard_map/ppermute | solution.py:241
  27.5 6.4 %collective-permute-start.4 = (bf16[2,96,512]{2,1,0:T(8,128)(2,1)S(1)}, bf16[2,96,512]{2,1,0:T(8,128)(2,1)S(1)}, u32[]{:S(2)}, u32[]{:S(2)}) collective-permute-start(bf16[2,96,512]{2,1,0:T(8,128)(2,1)S(1)} %fusion.41.refs_0_), channel_id=1, source_target_pairs={{0,8},{4,12},{8,0},{12,4},{16,24},{20,28},{24,16},{28,20},{1,9},{5... | collective-permute-start | bytes 589832 | tf_op jit(solution)/shard_map/ppermute | solution.py:241
  28.3 4.6 %collective-permute-start.5 = (bf16[2,96,192]{2,1,0:T(8,128)(2,1)S(1)}, bf16[2,96,192]{2,1,0:T(8,128)(2,1)S(1)}, u32[]{:S(2)}, u32[]{:S(2)}) collective-permute-start(bf16[2,96,192]{2,1,0:T(8,128)(2,1)S(1)} %pad_maximum_fusion.6.refs_3_), channel_id=1, source_target_pairs={{0,4},{4,0},{8,12},{12,8},{16,20},{20,16},{24,28},{28,24},{1,5},{5... | collective-permute-start | bytes 221192 | tf_op jit(solution)/shard_map/ppermute | solution.py:241
  29.8 7.6 %collective-permute-start.9 = (bf16[512,768]{1,0:T(8,128)(2,1)S(1)}, bf16[512,768]{1,0:T(8,128)(2,1)}, u32[]{:S(2)}, u32[]{:S(2)}) collective-permute-start(bf16[512,768]{1,0:T(8,128)(2,1)S(1)} %bitcast.172), channel_id=1, source_target_pairs={{0,1},{1,0},{2,3},{3,2},{4,5},{5,4},{6,7},{7,6},{8,9},{9,8},{10,11... | collective-permute-start | bytes 2359304 | tf_op jit(solution)/shard_map/ppermute | solution.py:241
  33.9 5.1 %collective-permute-start.10 = (bf16[512,768]{1,0:T(8,128)(2,1)}, bf16[512,768]{1,0:T(8,128)(2,1)}, u32[]{:S(2)}, u32[]{:S(2)}) collective-permute-start(bf16[512,768]{1,0:T(8,128)(2,1)} %collective-permute-done.6), channel_id=1, source_target_pairs={{0,1},{1,0},{2,3},{3,2},{4,5},{5,4},{6,7},{7,6},{8,9},{9,8},{10,11... | collective-permute-start | bytes 2359304 | tf_op jit(solution)/shard_map/ppermute | solution.py:241
  33.9 47.6 %collective-permute-start.15 = (bf16[512,768]{1,0:T(8,128)(2,1)S(1)}, bf16[512,768]{1,0:T(8,128)(2,1)S(1)}, u32[]{:S(2)}, u32[]{:S(2)}) collective-permute-start(bf16[512,768]{1,0:T(8,128)(2,1)S(1)} %bitcast.186), channel_id=1, source_target_pairs={{0,1},{1,0},{2,3},{3,2},{4,5},{5,4},{6,7},{7,6},{8,9},{9,8},{10,11... | collective-permute-start | bytes 2359304 | tf_op jit(solution)/shard_map/ppermute | solution.py:241
  34.5 174.0 %copy-start.5 = (s32[2]{0:T(128)}, s32[2]{0:T(128)S(1)}, u32[]{:S(2)}) copy-start(s32[2]{0:T(128)S(1)} %pad_add_fusion.me_ref) | copy-start | bytes 28
  34.5 13.1 %collective-permute-start.7 = (bf16[4,96,512]{2,1,0:T(8,128)(2,1)S(1)}, bf16[4,96,512]{2,1,0:T(8,128)(2,1)S(1)}, u32[]{:S(2)}, u32[]{:S(2)}) collective-permute-start(bf16[4,96,512]{2,1,0:T(8,128)(2,1)S(1)} %pad_maximum_fusion.4), channel_id=1, source_target_pairs={{0,4},{4,0},{8,12},{12,8},{16,20},{20,16},{24,28},{28,24},{1,5},{5... | collective-permute-start | bytes 1179656 | tf_op jit(solution)/shard_map/ppermute | solution.py:241
  35.8 25.6 %collective-permute-start.11 = (bf16[512,768]{1,0:T(8,128)(2,1)S(1)}, bf16[512,768]{1,0:T(8,128)(2,1)S(1)}, u32[]{:S(2)}, u32[]{:S(2)}) collective-permute-start(bf16[512,768]{1,0:T(8,128)(2,1)S(1)} %bitcast.187), channel_id=1, source_target_pairs={{0,2},{1,3},{2,0},{3,1},{4,6},{5,7},{6,4},{7,5},{8,10},{9,11},{10,... | collective-permute-start | bytes 2359304 | tf_op jit(solution)/shard_map/ppermute | solution.py:241
  37.4 10.1 %collective-permute-start.8 = (bf16[4,96,192]{2,1,0:T(8,128)(2,1)S(1)}, bf16[4,96,192]{2,1,0:T(8,128)(2,1)S(1)}, u32[]{:S(2)}, u32[]{:S(2)}) collective-permute-start(bf16[4,96,192]{2,1,0:T(8,128)(2,1)S(1)} %pad_maximum_fusion.5), channel_id=1, source_target_pairs={{0,8},{4,12},{8,0},{12,4},{16,24},{20,28},{24,16},{28,20},{1,9},{5... | collective-permute-start | bytes 442376 | tf_op jit(solution)/shard_map/ppermute | solution.py:241
  39.0 22.5 %collective-permute-start.12 = (bf16[1,288,768]{2,1,0:T(8,128)(2,1)S(1)}, bf16[1,288,768]{2,1,0:T(8,128)(2,1)S(1)}, u32[]{:S(2)}, u32[]{:S(2)}) collective-permute-start(bf16[1,288,768]{2,1,0:T(8,128)(2,1)S(1)} %bitcast.200), channel_id=1, source_target_pairs={{0,16},{4,20},{8,24},{12,28},{16,0},{20,4},{24,8},{28,12},{1,17},{... | collective-permute-start | bytes 1327112 | tf_op jit(solution)/shard_map/ppermute | solution.py:241
  53.5 26.8 %copy-start.11 = (bf16[4,512,768]{2,1,0:T(8,128)(2,1)}, bf16[4,512,768]{2,1,0:T(8,128)(2,1)S(1)}, u32[]{:S(2)}) copy-start(bf16[4,512,768]{2,1,0:T(8,128)(2,1)S(1)} %get-tuple-element.206.h_ref) | copy-start | bytes 9437188
  53.5 53.2 %copy-start.6 = (f32[16,768]{1,0:T(8,128)}, f32[16,768]{1,0:T(8,128)S(1)}, u32[]{:S(2)}) copy-start(f32[16,768]{1,0:T(8,128)S(1)} %get-tuple-element.170.refs_10_.refs_6_.vec_ref) | copy-start | bytes 147460
  61.5 20.3 %collective-permute-start.14 = (bf16[2,288,768]{2,1,0:T(8,128)(2,1)S(1)}, bf16[2,288,768]{2,1,0:T(8,128)(2,1)S(1)}, u32[]{:S(2)}, u32[]{:S(2)}) collective-permute-start(bf16[2,288,768]{2,1,0:T(8,128)(2,1)S(1)} %constant_dynamic-update-slice_fusion.refs_4_), channel_id=1, source_target_pairs={{0,8},{4,12},{8,0},{12,4},{16,24},{20,28},{24,16},{28,20},{1,9},{5... | collective-permute-start | bytes 2654216 | tf_op jit(solution)/shard_map/ppermute | solution.py:241
  61.6 20.3 %collective-permute-start.13 = (bf16[2,288,768]{2,1,0:T(8,128)(2,1)S(1)}, bf16[2,288,768]{2,1,0:T(8,128)(2,1)S(1)}, u32[]{:S(2)}, u32[]{:S(2)}) collective-permute-start(bf16[2,288,768]{2,1,0:T(8,128)(2,1)S(1)} %constant_dynamic-update-slice_fusion.refs_4_), channel_id=1, source_target_pairs={{0,4},{4,0},{8,12},{12,8},{16,20},{20,16},{24,28},{28,24},{1,5},{5... | collective-permute-start | bytes 2654216 | tf_op jit(solution)/shard_map/ppermute | solution.py:241
  62.3 19.1 %collective-permute-start.16 = (bf16[512,768]{1,0:T(8,128)(2,1)S(1)}, bf16[512,768]{1,0:T(8,128)(2,1)S(1)}, u32[]{:S(2)}, u32[]{:S(2)}) collective-permute-start(bf16[512,768]{1,0:T(8,128)(2,1)S(1)} %collective-permute-done.11), channel_id=1, source_target_pairs={{0,1},{1,0},{2,3},{3,2},{4,5},{5,4},{6,7},{7,6},{8,9},{9,8},{10,11... | collective-permute-start | bytes 2359304 | tf_op jit(solution)/shard_map/ppermute | solution.py:241
  82.3 20.0 %collective-permute-start.18 = (bf16[4,192,512]{2,1,0:T(8,128)(2,1)S(1)}, bf16[4,192,512]{2,1,0:T(8,128)(2,1)S(1)}, u32[]{:S(2)}, u32[]{:S(2)}) collective-permute-start(bf16[4,192,512]{2,1,0:T(8,128)(2,1)S(1)} %get-tuple-element.166.refs_0_), channel_id=1, source_target_pairs={{0,2},{1,3},{2,0},{3,1},{4,6},{5,7},{6,4},{7,5},{8,10},{9,11},{10,... | collective-permute-start | bytes 2359304 | tf_op jit(solution)/shard_map/ppermute | solution.py:241
  83.8 18.5 %collective-permute-start.17 = (bf16[4,192,512]{2,1,0:T(8,128)(2,1)S(1)}, bf16[4,192,512]{2,1,0:T(8,128)(2,1)S(1)}, u32[]{:S(2)}, u32[]{:S(2)}) collective-permute-start(bf16[4,192,512]{2,1,0:T(8,128)(2,1)S(1)} %get-tuple-element.166.refs_0_), channel_id=1, source_target_pairs={{0,1},{1,0},{2,3},{3,2},{4,5},{5,4},{6,7},{7,6},{8,9},{9,8},{10,11... | collective-permute-start | bytes 2359304 | tf_op jit(solution)/shard_map/ppermute | solution.py:241
  84.0 22.7 %collective-permute-start.20 = (bf16[2,288,768]{2,1,0:T(8,128)(2,1)S(1)}, bf16[2,288,768]{2,1,0:T(8,128)(2,1)S(1)}, u32[]{:S(2)}, u32[]{:S(2)}) collective-permute-start(bf16[2,288,768]{2,1,0:T(8,128)(2,1)S(1)} %constant_dynamic-update-slice_fusion.refs_4_), channel_id=1, source_target_pairs={{0,12},{4,8},{8,4},{12,0},{16,28},{20,24},{24,20},{28,16},{1,13},{... | collective-permute-start | bytes 2654216 | tf_op jit(solution)/shard_map/ppermute | solution.py:241
  102.3 4.4 %collective-permute-start.19 = (bf16[4,192,512]{2,1,0:T(8,128)(2,1)S(1)}, bf16[4,192,512]{2,1,0:T(8,128)(2,1)S(1)}, u32[]{:S(2)}, u32[]{:S(2)}) collective-permute-start(bf16[4,192,512]{2,1,0:T(8,128)(2,1)S(1)} %collective-permute-done.18.refs_2_), channel_id=1, source_target_pairs={{0,1},{1,0},{2,3},{3,2},{4,5},{5,4},{6,7},{7,6},{8,9},{9,8},{10,11... | collective-permute-start | bytes 2359304 | tf_op jit(solution)/shard_map/ppermute | solution.py:241
  122.0 5.1 %collective-permute-start.21 = (bf16[512,768]{1,0:T(8,128)(2,1)}, bf16[512,768]{1,0:T(8,128)(2,1)}, u32[]{:S(2)}, u32[]{:S(2)}) collective-permute-start(bf16[512,768]{1,0:T(8,128)(2,1)} %get-tuple-element.180), channel_id=1, source_target_pairs={{0,1},{1,0},{2,3},{3,2},{4,5},{5,4},{6,7},{7,6},{8,9},{9,8},{10,11... | collective-permute-start | bytes 2359304 | tf_op jit(solution)/shard_map/ppermute | solution.py:241
  128.5 22.8 %collective-permute-start.23 = (bf16[512,768]{1,0:T(8,128)(2,1)S(1)}, bf16[512,768]{1,0:T(8,128)(2,1)S(1)}, u32[]{:S(2)}, u32[]{:S(2)}) collective-permute-start(bf16[512,768]{1,0:T(8,128)(2,1)S(1)} %add_convert_fusion.3), channel_id=1, source_target_pairs={{0,2},{1,3},{2,0},{3,1},{4,6},{5,7},{6,4},{7,5},{8,10},{9,11},{10,... | collective-permute-start | bytes 2359304 | tf_op jit(solution)/shard_map/ppermute | solution.py:241
  142.9 8.4 %collective-permute-start.22 = (bf16[512,768]{1,0:T(8,128)(2,1)S(1)}, bf16[512,768]{1,0:T(8,128)(2,1)S(1)}, u32[]{:S(2)}, u32[]{:S(2)}) collective-permute-start(bf16[512,768]{1,0:T(8,128)(2,1)S(1)} %get-tuple-element.184), channel_id=1, source_target_pairs={{0,1},{1,0},{2,3},{3,2},{4,5},{5,4},{6,7},{7,6},{8,9},{9,8},{10,11... | collective-permute-start | bytes 2359304 | tf_op jit(solution)/shard_map/ppermute | solution.py:241
  159.7 2.8 %collective-permute-start.24 = (bf16[192,512]{1,0:T(8,128)(2,1)S(1)}, bf16[192,512]{1,0:T(8,128)(2,1)S(1)}, u32[]{:S(2)}, u32[]{:S(2)}) collective-permute-start(bf16[192,512]{1,0:T(8,128)(2,1)S(1)} %get-tuple-element.194), channel_id=1, source_target_pairs={{0,1},{1,0},{2,3},{3,2},{4,5},{5,4},{6,7},{7,6},{8,9},{9,8},{10,11... | collective-permute-start | bytes 589832 | tf_op jit(solution)/shard_map/ppermute | solution.py:241
  160.1 42.4 %collective-permute-start.32 = (bf16[4,192,768]{2,1,0:T(8,128)(2,1)}, bf16[4,192,768]{2,1,0:T(8,128)(2,1)S(1)}, u32[]{:S(2)}, u32[]{:S(2)}) collective-permute-start(bf16[4,192,768]{2,1,0:T(8,128)(2,1)} %fusion.27), channel_id=1, source_target_pairs={{0,4},{4,0},{8,12},{12,8},{16,20},{20,16},{24,28},{28,24},{1,5},{5... | collective-permute-start | bytes 3538952 | tf_op jit(solution)/shard_map/ppermute | solution.py:241
  161.3 7.9 %collective-permute-start.25 = (bf16[192,512]{1,0:T(8,128)(2,1)S(1)}, bf16[192,512]{1,0:T(8,128)(2,1)S(1)}, u32[]{:S(2)}, u32[]{:S(2)}) collective-permute-start(bf16[192,512]{1,0:T(8,128)(2,1)S(1)} %get-tuple-element.198), channel_id=1, source_target_pairs={{0,2},{1,3},{2,0},{3,1},{4,6},{5,7},{6,4},{7,5},{8,10},{9,11},{10,... | collective-permute-start | bytes 589832 | tf_op jit(solution)/shard_map/ppermute | solution.py:241
  162.4 8.8 %collective-permute-start.26 = (bf16[192,512]{1,0:T(8,128)(2,1)S(1)}, bf16[192,512]{1,0:T(8,128)(2,1)S(1)}, u32[]{:S(2)}, u32[]{:S(2)}) collective-permute-start(bf16[192,512]{1,0:T(8,128)(2,1)S(1)} %get-tuple-element.199), channel_id=1, source_target_pairs={{0,3},{1,2},{2,1},{3,0},{4,7},{5,6},{6,5},{7,4},{8,11},{9,10},{10,... | collective-permute-start | bytes 589832 | tf_op jit(solution)/shard_map/ppermute | solution.py:241
  163.7 9.3 %collective-permute-start.28 = (bf16[16,24,768]{2,1,0:T(8,128)(2,1)S(1)}, bf16[16,24,768]{2,1,0:T(8,128)(2,1)S(1)}, u32[]{:S(2)}, u32[]{:S(2)}) collective-permute-start(bf16[16,24,768]{2,1,0:T(8,128)(2,1)S(1)} %dynamic-slice_bitcast_fusion.2), channel_id=1, source_target_pairs={{0,1},{1,0},{2,3},{3,2},{4,5},{5,4},{6,7},{7,6},{8,9},{9,8},{10,11... | collective-permute-start | bytes 1769480 | tf_op jit(solution)/shard_map/ppermute | solution.py:241
  167.8 34.7 %collective-permute-start.29 = (bf16[512,768]{1,0:T(8,128)(2,1)S(1)}, bf16[512,768]{1,0:T(8,128)(2,1)S(1)}, u32[]{:S(2)}, u32[]{:S(2)}) collective-permute-start(bf16[512,768]{1,0:T(8,128)(2,1)S(1)} %convolution_convert_fusion), channel_id=1, source_target_pairs={{0,1},{1,0},{2,3},{3,2},{4,5},{5,4},{6,7},{7,6},{8,9},{9,8},{10,11... | collective-permute-start | bytes 2359304 | tf_op jit(solution)/shard_map/ppermute | solution.py:241
  169.2 5.1 %collective-permute-start.27 = (bf16[512,768]{1,0:T(8,128)(2,1)S(1)}, bf16[512,768]{1,0:T(8,128)(2,1)S(1)}, u32[]{:S(2)}, u32[]{:S(2)}) collective-permute-start(bf16[512,768]{1,0:T(8,128)(2,1)S(1)} %convolution_convert_fusion.2), channel_id=1, source_target_pairs={{0,1},{1,0},{2,3},{3,2},{4,5},{5,4},{6,7},{7,6},{8,9},{9,8},{10,11... | collective-permute-start | bytes 2359304 | tf_op jit(solution)/shard_map/ppermute | solution.py:241
  173.2 29.3 %collective-permute-start.31 = (bf16[8,24,768]{2,1,0:T(8,128)(2,1)S(1)}, bf16[8,24,768]{2,1,0:T(8,128)(2,1)S(1)}, u32[]{:S(2)}, u32[]{:S(2)}) collective-permute-start(bf16[8,24,768]{2,1,0:T(8,128)(2,1)S(1)} %dynamic-slice_bitcast_fusion.4), channel_id=1, source_target_pairs={{0,2},{1,3},{2,0},{3,1},{4,6},{5,7},{6,4},{7,5},{8,10},{9,11},{10,... | collective-permute-start | bytes 884744 | tf_op jit(solution)/shard_map/ppermute | solution.py:241
  174.5 28.0 %collective-permute-start.30 = (bf16[512,768]{1,0:T(8,128)(2,1)S(1)}, bf16[512,768]{1,0:T(8,128)(2,1)S(1)}, u32[]{:S(2)}, u32[]{:S(2)}) collective-permute-start(bf16[512,768]{1,0:T(8,128)(2,1)S(1)} %add_convert_fusion.2), channel_id=1, source_target_pairs={{0,2},{1,3},{2,0},{3,1},{4,6},{5,7},{6,4},{7,5},{8,10},{9,11},{10,... | collective-permute-start | bytes 2359304 | tf_op jit(solution)/shard_map/ppermute | solution.py:241
  204.3 19.4 %collective-permute-start.33 = (bf16[4,120,768]{2,1,0:T(8,128)(2,1)S(1)}, bf16[4,120,768]{2,1,0:T(8,128)(2,1)S(1)}, u32[]{:S(2)}, u32[]{:S(2)}) collective-permute-start(bf16[4,120,768]{2,1,0:T(8,128)(2,1)S(1)} %dynamic-slice_bitcast_fusion), channel_id=1, source_target_pairs={{0,4},{4,0},{8,12},{12,8},{16,20},{20,16},{24,28},{28,24},{1,5},{5... | collective-permute-start | bytes 2211848 | tf_op jit(solution)/shard_map/ppermute | solution.py:241
  206.4 16.0 %collective-permute-start.34 = (bf16[2,192,768]{2,1,0:T(8,128)(2,1)S(1)}, bf16[2,192,768]{2,1,0:T(8,128)(2,1)S(1)}, u32[]{:S(2)}, u32[]{:S(2)}) collective-permute-start(bf16[2,192,768]{2,1,0:T(8,128)(2,1)S(1)} %dynamic-slice_bitcast_fusion.1), channel_id=1, source_target_pairs={{0,8},{4,12},{8,0},{12,4},{16,24},{20,28},{24,16},{28,20},{1,9},{5... | collective-permute-start | bytes 1769480 | tf_op jit(solution)/shard_map/ppermute | solution.py:241
  224.6 9.5 %collective-permute-start.36 = (bf16[2,512,768]{2,1,0:T(8,128)(2,1)S(1)}, bf16[2,512,768]{2,1,0:T(8,128)(2,1)}, u32[]{:S(2)}, u32[]{:S(2)}) collective-permute-start(bf16[2,512,768]{2,1,0:T(8,128)(2,1)S(1)} %get-tuple-element.224), channel_id=1, source_target_pairs={{0,1},{1,0},{2,3},{3,2},{4,5},{5,4},{6,7},{7,6},{8,9},{9,8},{10,11... | collective-permute-start | bytes 4718600 | tf_op jit(solution)/shard_map/ppermute | solution.py:241
  226.5 18.5 %collective-permute-start.35 = (bf16[2,120,768]{2,1,0:T(8,128)(2,1)S(1)}, bf16[2,120,768]{2,1,0:T(8,128)(2,1)S(1)}, u32[]{:S(2)}, u32[]{:S(2)}) collective-permute-start(bf16[2,120,768]{2,1,0:T(8,128)(2,1)S(1)} %bitcast_add_fusion.2), channel_id=1, source_target_pairs={{0,8},{4,12},{8,0},{12,4},{16,24},{20,28},{24,16},{28,20},{1,9},{5... | collective-permute-start | bytes 1105928 | tf_op jit(solution)/shard_map/ppermute | solution.py:241
  228.7 9.2 %collective-permute-start.37 = (bf16[2,96,128]{2,1,0:T(8,128)(2,1)S(1)}, bf16[2,96,128]{2,1,0:T(8,128)(2,1)S(1)}, u32[]{:S(2)}, u32[]{:S(2)}) collective-permute-start(bf16[2,96,128]{2,1,0:T(8,128)(2,1)S(1)} %get-tuple-element.225), channel_id=1, source_target_pairs={{0,4},{4,0},{8,12},{12,8},{16,20},{20,16},{24,28},{28,24},{1,5},{5... | collective-permute-start | bytes 147464 | tf_op jit(solution)/shard_map/ppermute | solution.py:241
  229.3 15.7 %collective-permute-start.38 = (bf16[2,96,128]{2,1,0:T(8,128)(2,1)S(1)}, bf16[2,96,128]{2,1,0:T(8,128)(2,1)S(1)}, u32[]{:S(2)}, u32[]{:S(2)}) collective-permute-start(bf16[2,96,128]{2,1,0:T(8,128)(2,1)S(1)} %get-tuple-element.226), channel_id=1, source_target_pairs={{0,12},{4,8},{8,4},{12,0},{16,28},{20,24},{24,20},{28,16},{1,13},{... | collective-permute-start | bytes 147464 | tf_op jit(solution)/shard_map/ppermute | solution.py:241
  231.1 16.5 %collective-permute-start.40 = (bf16[1,192,768]{2,1,0:T(8,128)(2,1)S(1)}, bf16[1,192,768]{2,1,0:T(8,128)(2,1)}, u32[]{:S(2)}, u32[]{:S(2)}) collective-permute-start(bf16[1,192,768]{2,1,0:T(8,128)(2,1)S(1)} %get-tuple-element.270), channel_id=1, source_target_pairs={{0,16},{4,20},{8,24},{12,28},{16,0},{20,4},{24,8},{28,12},{1,17},{... | collective-permute-start | bytes 884744 | tf_op jit(solution)/shard_map/ppermute | solution.py:241
  236.5 25.2 %collective-permute-start.44 = (bf16[512,768]{1,0:T(8,128)(2,1)}, bf16[512,768]{1,0:T(8,128)(2,1)S(1)}, u32[]{:S(2)}, u32[]{:S(2)}) collective-permute-start(bf16[512,768]{1,0:T(8,128)(2,1)} %fusion.30), channel_id=1, source_target_pairs={{0,2},{1,3},{2,0},{3,1},{4,6},{5,7},{6,4},{7,5},{8,10},{9,11},{10,... | collective-permute-start | bytes 2359304 | tf_op jit(solution)/shard_map/ppermute | solution.py:241
  246.0 10.2 %collective-permute-start.39 = (bf16[1,120,768]{2,1,0:T(8,128)(2,1)S(1)}, bf16[1,120,768]{2,1,0:T(8,128)(2,1)S(1)}, u32[]{:S(2)}, u32[]{:S(2)}) collective-permute-start(bf16[1,120,768]{2,1,0:T(8,128)(2,1)S(1)} %get-tuple-element.278), channel_id=1, source_target_pairs={{0,16},{4,20},{8,24},{12,28},{16,0},{20,4},{24,8},{28,12},{1,17},{... | collective-permute-start | bytes 552968 | tf_op jit(solution)/shard_map/ppermute | solution.py:241
  259.2 7.6 %collective-permute-start.41 = (bf16[24,1472]{1,0:T(8,128)(2,1)}, bf16[24,1472]{1,0:T(8,128)(2,1)S(1)}, u32[]{:S(2)}, u32[]{:S(2)}) collective-permute-start(bf16[24,1472]{1,0:T(8,128)(2,1)} %get-tuple-element.235), channel_id=1, source_target_pairs={{0,1},{1,0},{2,3},{3,2},{4,5},{5,4},{6,7},{7,6},{8,9},{9,8},{10,11... | collective-permute-start | bytes 211976 | tf_op jit(solution)/shard_map/ppermute | solution.py:241
  259.2 7.6 %collective-permute-start.42 = (bf16[24,1472]{1,0:T(8,128)(2,1)}, bf16[24,1472]{1,0:T(8,128)(2,1)S(1)}, u32[]{:S(2)}, u32[]{:S(2)}) collective-permute-start(bf16[24,1472]{1,0:T(8,128)(2,1)} %get-tuple-element.236), channel_id=1, source_target_pairs={{0,2},{1,3},{2,0},{3,1},{4,6},{5,7},{6,4},{7,5},{8,10},{9,11},{10,... | collective-permute-start | bytes 211976 | tf_op jit(solution)/shard_map/ppermute | solution.py:241
  260.1 6.8 %collective-permute-start.43 = (bf16[24,1472]{1,0:T(8,128)(2,1)}, bf16[24,1472]{1,0:T(8,128)(2,1)S(1)}, u32[]{:S(2)}, u32[]{:S(2)}) collective-permute-start(bf16[24,1472]{1,0:T(8,128)(2,1)} %get-tuple-element.237), channel_id=1, source_target_pairs={{0,3},{1,2},{2,1},{3,0},{4,7},{5,6},{6,5},{7,4},{8,11},{9,10},{10,... | collective-permute-start | bytes 211976 | tf_op jit(solution)/shard_map/ppermute | solution.py:241
  (63 other events, 387.6 us)
